TPU v7x, 32 devices: a whole 2x2x4 slice. The times are simulated.
32 devices in a mesh: rep: 2 (over x), ep: 4 (over y, core), grp: 4 (over z).
Axes of the slice: x: 2, y: 2, z: 4, core: 2. Of those that a mesh axis runs over, the one named last changes fastest.
Arguments:
- tokens: bfloat16 [4096, 4096], P(('rep', 'ep'), 'grp'), parts along dimension 0, may hold values from -6 to 6
- proj_in: bfloat16 [1024, 4096], P('ep', 'grp'), may hold values from -0.09375 to 0.09375
- proj_out: bfloat16 [1024, 4096], P('ep', 'grp'), may hold values from -0.1875 to 0.1875
- expert_up: bfloat16 [16, 1024, 2688], P(('ep', 'grp')), may hold values from -0.1875 to 0.1875
- expert_down: bfloat16 [16, 2688, 1024], P(('ep', 'grp')), may hold values from -0.125 to 0.125
- expert_ids: int32 [4096, 6], P(('rep', 'ep')), parts along dimension 0, may hold values from 0 to 15, as said below
- weight_codes: int32 [4096, 6], P(('rep', 'ep')), parts along dimension 0, may hold values from 1 to 64
Outputs:
- mixed: bfloat16 [4096, 4096], P(('rep', 'ep'), 'grp'), parts along dimension 0
There are 2 independent parts, one for each index of `rep`. A program takes and returns all parts, laid end to end along the dimension named above; an argument that names none is the same for every part. Nothing has to cross between parts.
Inputs may be any that keep to these rules, and one draw needn't show every extreme that they name: `expert_ids`: expert e belongs to group e % 4. Each token picks 6 distinct experts, two in each of 3 distinct groups. Within each aligned block of 128 tokens (the tokens of one device), every group is picked from by exactly 96 tokens, no expert is picked by more than 64 tokens, and in every block each group has an expert picked by exactly 64.
All inputs are finite; a program needn't handle non-finite values.
Results may differ from a plain program's by a relative error of at most 0.012.
Values may be sent and summed in bfloat16 or wider, within the bound.
No kernel may reach another device: no remote copies, remote signals or barrier semaphores. Data moves between devices by JAX's collectives and lax.ppermute only.
A program may use at most 64 MiB of HBM per device.

v0:
```python
import jax
import jax.numpy as jnp
from jax import lax
from jax.sharding import PartitionSpec as P


def expert_block(arrived, expert_up, expert_down):
    width = arrived.shape[-1]
    flat_rows = arrived.reshape(-1, width)
    hidden = jnp.dot(flat_rows, expert_up[0], preferred_element_type=jnp.float32)
    hidden = jnp.square(jnp.maximum(hidden, 0.0)).astype(jnp.bfloat16)
    result = jnp.dot(hidden, expert_down[0], preferred_element_type=jnp.float32)
    return result.astype(jnp.bfloat16).reshape(arrived.shape)


def slot_positions(bucket, live, buckets):
    labels = jnp.arange(buckets, dtype=jnp.int32)
    onehot = jnp.logical_and(bucket[:, :, None] == labels, live[:, :, None]).astype(jnp.int32)
    per_row = jnp.sum(onehot, axis=1)
    before = jnp.cumsum(per_row, axis=0) - per_row
    return jnp.take_along_axis(before, bucket, axis=1)


def per_device(tokens, proj_in, proj_out, expert_up, expert_down, expert_ids, weight_codes):
    ep_count = lax.axis_size("ep")
    group_count = lax.axis_size("grp")
    experts = ep_count * group_count
    tok_block = tokens.shape[0]
    tok_dev = tok_block // group_count
    picks = expert_ids.shape[1]
    width = expert_up.shape[1]
    capacity = max(2, (4 * tok_dev * picks + 3 * experts - 1) // (3 * experts))
    in_rows, out_rows = (
        lax.all_gather(proj_in, "ep", axis=0, tiled=True),
        lax.all_gather(proj_out, "ep", axis=0, tiled=True),
    )
    latent = lax.psum_scatter(
        lax.dot_general(
            tokens, in_rows, (((1,), (1,)), ((), ())), preferred_element_type=jnp.float32
        ),
        "grp",
        scatter_dimension=0,
        tiled=True,
    ).astype(jnp.bfloat16)
    codes = weight_codes.astype(jnp.float32)
    route_weights = codes / jnp.sum(codes, axis=1, keepdims=True)
    group_index = lax.axis_index("grp")
    my_ids = lax.dynamic_slice_in_dim(expert_ids, group_index * tok_dev, tok_dev, 0)
    my_weights = lax.dynamic_slice_in_dim(route_weights, group_index * tok_dev, tok_dev, 0)
    position = slot_positions(my_ids, jnp.ones(my_ids.shape, jnp.bool_), experts)
    spread = jnp.broadcast_to(latent[:, None, :], (tok_dev, picks, width))
    outgoing = jnp.zeros((experts, capacity, width), jnp.bfloat16).at[my_ids, position].set(spread)
    computed = expert_block(
        lax.all_to_all(outgoing, ("ep", "grp"), split_axis=0, concat_axis=0, tiled=True),
        expert_up,
        expert_down,
    )
    returned = lax.all_to_all(computed, ("ep", "grp"), split_axis=0, concat_axis=0, tiled=True)
    picked = returned[my_ids, position]
    combined = jnp.sum(my_weights[:, :, None] * picked.astype(jnp.float32), axis=1)
    latent_out = combined.astype(jnp.bfloat16)
    mixed = jnp.dot(
        lax.all_gather(latent_out, "grp", axis=0, tiled=True),
        out_rows,
        preferred_element_type=jnp.float32,
    )
    return mixed.astype(jnp.bfloat16)


def solution(mesh):
    in_specs = (
        P(("rep", "ep"), "grp"),
        P("ep", "grp"),
        P("ep", "grp"),
        P(("ep", "grp"), None, None),
        P(("ep", "grp"), None, None),
        P(("rep", "ep"), None),
        P(("rep", "ep"), None),
    )
    out_specs = P(("rep", "ep"), "grp")
    return jax.shard_map(
        per_device, mesh=mesh, in_specs=in_specs, out_specs=out_specs, check_vma=False
    )
```

profile of v0, /device:TPU:0, one launch (start us, length us, event | category | flops | bytes accessed | tf_op | source)
XLA Modules:
  0.0 341.0 jit_solution(4923864919701778482)
XLA Ops:
  6.5 0.0 copy-start
  6.5 0.0 all-gather.4.cloned.1.call-start
  6.5 0.7 all-gather.4.cloned.1.call-update
  7.3 0.0 reduce-scatter.2.cloned.1.call-start
  7.3 26.9 %all-gather.4.cloned.1.call-done = bf16[1024,1024]{1,0:T(8,128)(2,1)} async-done(((bf16[256,1024]{1,0:T(8,128)(2,1)}), bf16[1024,1024]{1,0:T(8,128)(2,1)}) %all-gather.4.cloned.1.call-update) | async-done | bytes 2097168 | tf_op jit(solution)/shard_map/all_gather | solution.py:34
  34.2 0.0 copy-done
  34.2 4.2 %fusion.16 = f32[512,1024]{1,0:T(8,128)} fusion(bf16[512,1024]{1,0:T(8,128)(2,1)S(1)} %copy-done, bf16[1024,1024]{1,0:T(8,128)(2,1)} %all-gather.4.cloned.1.call-done), kind=kOutput, calls=%fused_computation.29 | convolution fusion | flops 1073741824 | bytes 5242880 | tf_op jit(solution)/shard_map/dot_general | solution.py:38
  38.5 0.0 reduce-scatter.2.cloned.1.call-update
  38.5 0.7 constant_dynamic-slice_fusion
  39.2 0.1 copy.17
  39.3 0.1 copy.15
  39.4 0.2 reduce_window_sum.11
  39.6 0.1 reshape.29
  39.8 5.1 %gather_fusion.1 = s32[768]{0:T(1024)S(1)} fusion(s32[128,16]{1,0:T(8,128)S(1)} %sub.3, s32[768]{0:T(1024)S(1)} %reshape.29), kind=kCustom, calls=%fused_computation.1 | custom fusion | bytes 12288 | tf_op jit(solution)/shard_map/jit(take_along_axis)/gather | solution.py:21
  44.9 0.1 reshape.32
  45.1 0.1 fusion.10
  45.1 0.1 reshape.35
  45.3 37.3 %reduce-scatter.2.cloned.1.call-done = f32[128,1024]{1,0:T(8,128)} async-done(((f32[512,1024]{1,0:T(8,128)}), f32[128,1024]{1,0:T(8,128)}) %reduce-scatter.2.cloned.1.call-update) | async-done | bytes 524304 | tf_op jit(solution)/shard_map/reduce_scatter | solution.py:37
  82.6 1.1 convert_element_type.26
  83.6 0.3 broadcast_in_dim.13
  84.0 1.4 reshape.37
  85.4 0.3 broadcast_in_dim.10
  85.7 75.1 %scatter_fusion = bf16[16,64,1024]{2,1,0:T(8,128)(2,1)S(1)} fusion(bf16[16,64,1024]{2,1,0:T(8,128)(2,1)S(1)} %broadcast_in_dim.10, s32[768]{0:T(1024)S(1)} %reshape.35, bf16[768,1024]{1,0:T(8,128)(2,1)} %reshape.37), kind=kCustom, calls=%fused_computation.2 | custom fusion | bytes 4724736 | tf_op jit(solution)/shard_map/scatter | solution.py:52
  160.8 53.4 %all_to_all.10 = bf16[16,64,1024]{2,1,0:T(8,128)(2,1)} all-to-all(bf16[16,64,1024]{2,1,0:T(8,128)(2,1)S(1)} %scatter_fusion), channel_id=1, replica_groups=mesh['rep'=2,'ep'=4,'grp'=4] {'ep','grp'}, dimensions={0} | all-to-all | bytes 4194304 | tf_op jit(solution)/shard_map/all_to_all | solution.py:54
  214.2 18.2 %fusion.5 = bf16[1024,1024]{1,0:T(8,128)(2,1)} fusion(bf16[1,2688,1024]{2,1,0:T(8,128)(2,1)} %param.11, bf16[1024,1024]{1,0:T(8,128)(2,1)} %bitcast.43, bf16[1,1024,2688]{2,1,0:T(8,128)(2,1)} %param.10), kind=kOutput, calls=%fused_computation.9 | convolution fusion | flops 11283595264 | bytes 15204352 | tf_op jit(solution)/shard_map/dot_general | solution.py:12
  232.4 0.0 copy-start.1
  232.4 3.8 %all-to-all-start.1 = ((bf16[16,64,1024]{2,1,0:T(8,128)(2,1)}), bf16[16,64,1024]{2,1,0:T(8,128)(2,1)S(1)}, u32[]{:S(2)}, u32[]{:S(2)}) async-start(bf16[16,64,1024]{2,1,0:T(8,128)(2,1)} %bitcast.42), calls=%async_computation.2 | async-start | bytes 4194304 | tf_op jit(solution)/shard_map/all_to_all | solution.py:58
  236.2 0.0 all-gather.8.cloned.1.call-start
  236.3 0.7 all-gather.8.cloned.1.call-update
  237.0 0.3 all-gather.6.cloned.1.call-start
  237.3 0.1 reshape.23
  237.4 0.0 copy-done.1
  237.4 0.1 dynamic-slice
  237.5 0.1 copy.12
  237.6 48.0 %all-to-all-done.1 = bf16[16,64,1024]{2,1,0:T(8,128)(2,1)S(1)} async-done(((bf16[16,64,1024]{2,1,0:T(8,128)(2,1)}), bf16[16,64,1024]{2,1,0:T(8,128)(2,1)S(1)}, u32[]{:S(2)}, u32[]{:S(2)}) %all-to-all-start.1) | async-done | bytes 2097184 | tf_op jit(solution)/shard_map/all_to_all | solution.py:58
  285.6 9.8 %gather_fusion = bf16[768,1024]{1,0:T(8,128)(2,1)} fusion(bf16[16,64,1024]{2,1,0:T(8,128)(2,1)S(1)} %all-to-all-done.1, s32[768]{0:T(1024)S(1)} %reshape.23), kind=kCustom, calls=%fused_computation | custom fusion | bytes 3151872 | tf_op jit(solution)/shard_map/gather | solution.py:59
  295.4 3.9 %reshape.41 = f32[128,6,1024]{2,1,0:T(8,128)} reshape(bf16[768,1024]{1,0:T(8,128)(2,1)} %gather_fusion) | data formatting | bytes 4718592 | tf_op jit(solution)/shard_map/convert_element_type | solution.py:60
  299.3 4.3 %multiply_reduce_fusion = bf16[128,1024]{1,0:T(8,128)(2,1)} fusion(f32[128,6,1024]{2,1,0:T(8,128)} %reshape.41, f32[128,6]{1,0:T(8,128)S(1)} %copy.12), kind=kLoop, calls=%fused_computation.8 | loop fusion | flops 1441792 | bytes 3410944 | tf_op jit(solution)/shard_map/reduce_sum | solution.py:60
  303.6 0.0 all-gather.6.cloned.1.call-update
  303.6 0.0 all-gather.8.cloned.1.call-done
  303.7 26.7 %all-gather.6.cloned.1.call-done = bf16[512,1024]{1,0:T(8,128)(2,1)} async-done(((bf16[128,1024]{1,0:T(8,128)(2,1)}), bf16[512,1024]{1,0:T(8,128)(2,1)}) %all-gather.6.cloned.1.call-update) | async-done | bytes 1048592 | tf_op jit(solution)/shard_map/all_gather | solution.py:63
  330.4 4.1 %convolution_convert_fusion = bf16[512,1024]{1,0:T(8,128)(2,1)} fusion(bf16[512,1024]{1,0:T(8,128)(2,1)} %all-gather.6.cloned.1.call-done, bf16[1024,1024]{1,0:T(8,128)(2,1)} %all-gather.8.cloned.1.call-done), kind=kOutput, calls=%fused_computation.10 | convolution fusion | flops 1074266112 | bytes 4194304 | tf_op jit(solution)/shard_map/dot_general | solution.py:62
  (6 shorter events, 0.1 us)
Async XLA Ops:
  6.5 27.7 %copy-start = (bf16[512,1024]{1,0:T(8,128)(2,1)S(1)}, bf16[512,1024]{1,0:T(8,128)(2,1)}, u32[]{:S(2)}) copy-start(bf16[512,1024]{1,0:T(8,128)(2,1)} %param.7) | copy-start | bytes 3145732
  6.5 27.7 %all-gather.4.cloned.1.call-start = ((), (), s32[]{:S(2)}) async-start(), calls=%async_computation.3 | async-start | bytes 2621440 | tf_op jit(solution)/shard_map/all_gather | solution.py:34
  7.3 75.3 %reduce-scatter.2.cloned.1.call-start = ((), (), s32[]{:S(2)}) async-start(), calls=%async_computation.4 | async-start | bytes 2621440 | tf_op jit(solution)/shard_map/reduce_scatter | solution.py:37
  232.4 5.0 %copy-start.1 = (s32[512,6]{0,1:T(8,128)S(1)}, s32[512,6]{0,1:T(8,128)}, u32[]{:S(2)}) copy-start(s32[512,6]{0,1:T(8,128)} %param.13) | copy-start | bytes 36868
  232.4 53.2 %all-to-all-start.1 = ((bf16[16,64,1024]{2,1,0:T(8,128)(2,1)}), bf16[16,64,1024]{2,1,0:T(8,128)(2,1)S(1)}, u32[]{:S(2)}, u32[]{:S(2)}) async-start(bf16[16,64,1024]{2,1,0:T(8,128)(2,1)} %bitcast.42), calls=%async_computation.2 | async-start | bytes 4194304 | tf_op jit(solution)/shard_map/all_to_all | solution.py:58
  236.2 67.4 %all-gather.8.cloned.1.call-start = ((), (), s32[]{:S(2)}) async-start(), calls=%async_computation.6 | async-start | bytes 2621440 | tf_op jit(solution)/shard_map/all_gather | solution.py:35
  237.0 93.4 %all-gather.6.cloned.1.call-start = ((), (), s32[]{:S(2)}) async-start(), calls=%async_computation.5 | async-start | bytes 1310720 | tf_op jit(solution)/shard_map/all_gather | solution.py:63
Sparse Core Ops, SparseCore 0:
  8.9 25.2 all-gather.3
  38.6 43.8 reduce-scatter.1
  238.7 34.3 all-gather.7
  303.7 26.5 all-gather.5
where the time goes:
time: 345 us; the launch traced here: 341 us
  waiting for transfers between devices  140 us (41%)
  local copies, waits for them, and re-layouts  97.6 us (28%)
  blocking collectives  53.4 us (15%)
  matrix products  26.6 us (8%)
  between operations  13.3 us (4%)
  other arithmetic  5.68 us (2%)
  starting transfers between devices  4.19 us (1%)
    scatter x1, local copies, waits for them, and re-layouts, per_device(): jnp.zeros((experts, capacity, width), jnp.bfloat16).at[my_ids, position]  75.1 us
    all_to_all x1, blocking collectives, per_device(): lax.all_to_all(outgoing, ('ep', 'grp'), split_axis=0, concat_axis=0, tile...  53.4 us
    all_to_all x1, waiting for transfers between devices, per_device(): lax.all_to_all(computed, ('ep', 'grp'), split_axis=0, concat_axis=0, tile...  48 us
    reduce_scatter x1, waiting for transfers between devices, per_device(): lax.psum_scatter(lax.dot_general(tokens, in_rows, (((1,), (1,)), ((), ())...  37.3 us
    all_gather x1, waiting for transfers between devices, per_device(): lax.all_gather(proj_in, 'ep', axis=0, tiled=True)  26.9 us
    all_gather x1, waiting for transfers between devices, per_device(): lax.all_gather(latent_out, 'grp', axis=0, tiled=True)  26.7 us
    dot_general x1, matrix products, expert_block(): result = jnp.dot(hidden, expert_down[0], preferred_element_type=jnp.float32)  18.2 us
    gather x1, local copies, waits for them, and re-layouts, per_device(): picked = returned[my_ids, position]  9.77 us
  transfers between devices with their start and end apart: 5, of which 4 were waited for; matrix products, arithmetic and copies ran while one was open for 7% of the time, Pallas kernels for 0%

commit v1 on v0

v1 whole, which is shorter than its diff:
```python
import functools

import jax
import jax.numpy as jnp
from jax import lax
from jax.experimental import pallas as pl
from jax.experimental.pallas import tpu as pltpu
from jax.sharding import PartitionSpec as P

BF16, F32, I32 = jnp.bfloat16, jnp.float32, jnp.int32
VMEM_LIMIT = 56 * 2**20


def hop(x, axis, step):
    count = lax.axis_size(axis)
    return lax.ppermute(x, axis, [(i, i ^ step) for i in range(count)])


def xor_order(x, axis, me, count):
    bit = 1
    while bit < count:
        parts = jnp.split(x, count // bit, axis=axis)
        swapped = jnp.concatenate([parts[i ^ 1] for i in range(len(parts))], axis=axis)
        x = jnp.where((me & bit) != 0, swapped, x)
        bit *= 2
    return x


def call(kernel, me, operands, outs, scratch=(), flops=0):
    vmem = pl.BlockSpec(memory_space=pltpu.VMEM)
    moved = sum(o.size * o.dtype.itemsize for o in (*operands, *outs))
    return pl.pallas_call(
        kernel,
        out_shape=tuple(outs),
        in_specs=[pl.BlockSpec(memory_space=pltpu.SMEM)] + [vmem] * len(operands),
        out_specs=tuple(vmem for _ in outs),
        scratch_shapes=list(scratch),
        cost_estimate=pl.CostEstimate(flops=flops, bytes_accessed=moved, transcendentals=0),
        compiler_params=pltpu.CompilerParams(vmem_limit_bytes=VMEM_LIMIT),
    )(me, *operands)


def tiles(total, tile, body):
    whole = total // tile

    def step(i, carry):
        body(pl.multiple_of(i * tile, tile), tile)
        return carry

    if whole:
        lax.fori_loop(0, whole, step, 0)
    if total % tile:
        body(whole * tile, total % tile)


def partial_kernel(n_rows, me_ref, tokens_ref, *refs):
    n_blocks = len(refs) - 2 - n_rows
    rows, outs, (weights, product) = refs[:n_rows], refs[n_rows:-2], refs[-2:]
    high = rows[0].shape[0]
    core, grp = me_ref[0] & 1, me_ref[1]
    for q in range(n_rows):
        place = (q // 2) * 2 * high + (core ^ (q % 2)) * high
        weights[pl.ds(pl.multiple_of(place, high), high), :] = rows[q][...]

    def body(start, width):
        product[:, pl.ds(start, width)] = lax.dot_general(
            tokens_ref[...], weights[pl.ds(start, width), :], (((1,), (1,)), ((), ())), preferred_element_type=F32
        ).astype(BF16)

    tiles(product.shape[1], min(256, product.shape[1]), body)
    block = product.shape[0] // n_blocks
    for k, out in enumerate(outs):
        out[...] = product[pl.ds(pl.multiple_of((grp ^ k) * block, block), block), :]


def one_hot(codes, height):
    at = lax.broadcasted_iota(I32, (height, codes.shape[1]), 0)
    return jnp.where(at == codes, 1.0, 0.0).astype(BF16)


def dispatch_kernel(me_ref, ranks_ref, *refs):
    n = len(refs) // 2
    parts, outs = refs[:n], refs[n:]
    total = parts[0][...].astype(F32)
    for part in parts[1:]:
        total += part[...].astype(F32)
    latent = total.astype(BF16)
    for k, out in enumerate(outs):
        pick = one_hot(ranks_ref[k], out.shape[0])
        out[...] = jnp.dot(pick, latent, preferred_element_type=F32).astype(BF16)


def up_kernel(sources, slots, me_ref, slot_ref, *refs):
    n = len(sources)
    near, far, (up_ref, hidden_ref, placed) = refs[:n], refs[n : 2 * n], refs[2 * n :]
    pair = near[0].shape[1]
    chip = me_ref[0] // 2
    for i, r in enumerate(sources):
        pick = one_hot(slot_ref[r], slots)
        for j in range(up_ref.shape[0] // pair):
            part = near[i][...] if j == 0 else far[i][:, (j - 1) * pair : j * pair]
            column = pl.multiple_of((chip ^ (r // 2) ^ j) * pair, pair)
            placed[i * slots : (i + 1) * slots, pl.ds(column, pair)] = jnp.dot(
                pick, part, preferred_element_type=F32
            ).astype(BF16)

    def body(start, width):
        hidden = jnp.dot(placed[...], up_ref[:, pl.ds(start, width)], preferred_element_type=F32)
        hidden_ref[:, pl.ds(start, width)] = jnp.square(jnp.maximum(hidden, 0.0)).astype(BF16)

    tiles(hidden_ref.shape[1], 512, body)


def down_kernel(sources, slots, first, me_ref, slot_ref, weight_ref, hidden_ref, down_ref, *refs):
    outs, scaled = refs[:-1], refs[-1]
    picks = [one_hot(slot_ref[r], slots) for r in sources]
    scale = jnp.concatenate(
        [jnp.sum(pick.astype(F32) * weight_ref[r], axis=1, keepdims=True) for pick, r in zip(picks, sources)], axis=0
    )
    width = scaled.shape[1]
    result = jnp.dot(hidden_ref[...], down_ref[:, first : first + width], preferred_element_type=F32)
    scaled[...] = (result * scale).astype(BF16)
    for i, out in enumerate(outs):
        out[...] = lax.dot_general(
            picks[i], scaled[i * slots : (i + 1) * slots, :], (((0,), (0,)), ((), ())), preferred_element_type=F32
        ).astype(BF16)


def join_kernel(n_in, me_ref, *refs):
    parts, outs = refs[:n_in], refs[n_in:]
    height = outs[0].shape[0]
    for k, out in enumerate(outs):
        rows = slice(k * height, (k + 1) * height)
        total = parts[0][rows, :].astype(F32)
        for part in parts[1:]:
            total += part[rows, :].astype(F32)
        out[...] = total.astype(BF16)


def combine_kernel(me_ref, ranks_ref, *refs):
    parts, out = refs[:-1], refs[-1]
    total = jnp.zeros(out.shape, F32)
    for k, part in enumerate(parts):
        pick = one_hot(ranks_ref[k], part.shape[0])
        total += lax.dot_general(pick, part[...], (((0,), (0,)), ((), ())), preferred_element_type=F32)
    out[...] = total.astype(BF16)


def mixed_kernel(n_rows, halves, me_ref, *refs):
    rows, latents, (out_ref, weights, gathered) = refs[:n_rows], refs[n_rows:-3], refs[-3:]
    ep, grp = me_ref[0], me_ref[1]
    high = rows[0].shape[0]
    for q in range(n_rows):
        weights[pl.ds(pl.multiple_of((ep ^ q) * high, high), high), :] = rows[q][...]
    block, width = latents[0].shape
    for i, part in enumerate(latents):
        k, h = i // halves, i % halves
        place = pl.ds(pl.multiple_of((grp ^ k) * block, block), block)
        gathered[place, h * width : (h + 1) * width] = part[...]

    def body(start, size):
        out_ref[:, pl.ds(start, size)] = jnp.dot(
            gathered[...], weights[:, pl.ds(start, size)], preferred_element_type=F32
        ).astype(BF16)

    tiles(out_ref.shape[1], min(256, out_ref.shape[1]), body)


def spread_ep(x):
    count = lax.axis_size("ep")
    near = [x] + [hop(x, "ep", 2 * k) for k in range(1, count // 2)]
    out = []
    for part in near:
        out += [part, hop(part, "ep", 1)]
    return out


def per_device(tokens, proj_in, proj_out, expert_up, expert_down, expert_ids, weight_codes):
    n_ep, n_grp = lax.axis_size("ep"), lax.axis_size("grp")
    ep, grp = lax.axis_index("ep"), lax.axis_index("grp")
    experts = n_ep * n_grp
    picks = expert_ids.shape[1]
    block = tokens.shape[0] // n_grp
    width, wide = expert_up.shape[1], expert_up.shape[2]
    high, depth = proj_in.shape
    hits = block * (picks // 2) // n_grp
    cap = max(2, (4 * block * picks + 3 * experts - 1) // (3 * experts))
    slots, lines = n_grp * cap, n_grp * hits
    me = jnp.stack([ep, grp]).astype(I32)
    shape = jax.ShapeDtypeStruct

    meta_own = jnp.concatenate([expert_ids.T, weight_codes.T], axis=0)
    before = (jnp.arange(block)[:, None] < jnp.arange(block)[None, :]).astype(BF16)

    def rank_of(hit):
        return jnp.dot(hit.astype(BF16), before, preferred_element_type=F32).astype(I32)

    own = lax.dynamic_slice_in_dim(expert_ids.T, grp * block, block, 1)
    group_of = grp ^ jnp.arange(n_grp, dtype=I32)
    own_hit = jnp.any((own % n_grp)[None] == group_of[:, None, None], axis=1)
    ranks = jnp.where(own_hit, rank_of(own_hit), -1)[:, None, :]

    rows_in = spread_ep(proj_in)

    def partial(rows):
        columns = high * len(rows)
        return call(
            functools.partial(partial_kernel, len(rows)),
            me,
            [tokens, *rows],
            [shape((block, columns), BF16)] * n_grp,
            [pltpu.VMEM((columns, depth), BF16), pltpu.VMEM((tokens.shape[0], columns), BF16)],
            flops=2 * tokens.shape[0] * columns * depth,
        )

    def latents(rows):
        cut = partial(rows)
        arrived = [cut[0]] + [hop(cut[k], "grp", k) for k in range(1, n_grp)]
        columns = cut[0].shape[1]
        chosen = call(dispatch_kernel, me, [ranks, *arrived], [shape((hits, columns), BF16)] * n_grp)
        arrived = [chosen[0]] + [hop(chosen[k], "grp", k) for k in range(1, n_grp)]
        return spread_ep(jnp.concatenate(arrived, axis=0))

    near = latents(rows_in[:2])
    far = latents(rows_in[2:])

    meta = jnp.stack(spread_ep(meta_own)).reshape(n_ep, 2 * picks, n_grp, block)
    meta = xor_order(meta, 2, grp, n_grp)
    ids, codes = meta[:, :picks], meta[:, picks:].astype(F32)
    mine = ids == ep * n_grp + grp
    picked = jnp.any(mine, axis=1)
    weight = jnp.sum(jnp.where(mine, codes, 0.0), axis=1) / jnp.sum(codes, axis=1)
    hit = jnp.any(ids % n_grp == grp, axis=1)
    flat = (n_ep * n_grp, block)
    rank = jnp.where(hit, rank_of(hit.reshape(flat)).reshape(hit.shape), -1)
    slot = rank_of(picked.reshape(flat)).reshape(hit.shape) + cap * jnp.arange(n_grp, dtype=I32)[None, :, None]
    at = rank[:, :, None, :] == jnp.arange(hits, dtype=I32)[None, None, :, None]
    line_slot = jnp.sum(jnp.where(at & picked[:, :, None, :], slot[:, :, None, :] + 1, 0), axis=3) - 1
    line_weight = jnp.sum(jnp.where(at, weight[:, :, None, :], 0.0), axis=3)
    line_slot = line_slot.reshape(n_ep, 1, lines)
    line_weight = line_weight.reshape(n_ep, 1, lines)

    half = width // 2
    results = []
    for sources in (range(2), range(2, n_ep)):
        sources = list(sources)
        n = len(sources) * slots
        [hidden] = call(
            functools.partial(up_kernel, sources, slots),
            me,
            [line_slot, *[near[r] for r in sources], *[far[r] for r in sources], expert_up[0]],
            [shape((n, wide), BF16)],
            [pltpu.VMEM((n, width), BF16)],
            flops=2 * n * width * wide,
        )
        results.append(
            [
                call(
                    functools.partial(down_kernel, sources, slots, first),
                    me,
                    [line_slot, line_weight, hidden, expert_down[0]],
                    [shape((lines, half), BF16)] * len(sources),
                    [pltpu.VMEM((n, half), BF16)],
                    flops=2 * n * half * wide,
                )
                for first in (0, half)
            ]
        )

    rows_out = spread_ep(proj_out)
    gathered = []
    for h in range(2):
        local, remote = results[0][h], results[1][h]
        parts = [local[0], hop(local[1], "ep", 1)]
        for k in range(1, n_ep // 2):
            both = remote[2 * k - 2].astype(F32) + hop(remote[2 * k - 1], "ep", 1).astype(F32)
            parts.append(hop(both.astype(BF16), "ep", 2 * k))
        cut = call(functools.partial(join_kernel, len(parts)), me, parts, [shape((hits, half), BF16)] * n_grp)
        arrived = [cut[0]] + [hop(cut[k], "grp", k) for k in range(1, n_grp)]
        [latent_out] = call(combine_kernel, me, [ranks, *arrived], [shape((block, half), BF16)])
        blocks = {0: latent_out}
        for k in range(1, n_grp):
            low = k & -k
            blocks[k] = hop(blocks[k ^ low], "grp", low)
        gathered.append(blocks)
    pieces = [gathered[h][k] for k in range(n_grp) for h in range(2)]
    [mixed] = call(
        functools.partial(mixed_kernel, n_ep, 2),
        me,
        [*rows_out, *pieces],
        [shape((tokens.shape[0], depth), BF16)],
        [pltpu.VMEM((width, depth), BF16), pltpu.VMEM((tokens.shape[0], width), BF16)],
        flops=2 * tokens.shape[0] * width * depth,
    )
    return mixed


def solution(mesh):
    in_specs = (
        P(("rep", "ep"), "grp"),
        P("ep", "grp"),
        P("ep", "grp"),
        P(("ep", "grp"), None, None),
        P(("ep", "grp"), None, None),
        P(("rep", "ep"), None),
        P(("rep", "ep"), None),
    )
    out_specs = P(("rep", "ep"), "grp")
    return jax.shard_map(
        per_device, mesh=mesh, in_specs=in_specs, out_specs=out_specs, check_vma=False
    )
```

time: 345 us -> 200 us (0.58)
  local copies, waits for them, and re-layouts: 97.6 us -> 9.39 us
  waiting for transfers between devices: 140 us -> 62.6 us
  Pallas kernels: 0 us -> 67.4 us
  blocking collectives: 53.4 us -> 0 us
  starting transfers between devices: 4.19 us -> 54.8 us
  matrix products: 26.6 us -> 0.99 us
  between operations: 13.3 us -> 0.45 us
    scatter x1 -> x0, local copies, waits for them, and re-layouts: 75.1 us -> none  [per_device(): jnp.zeros((experts, capacity, width), jnp.bfloat16).at[my_ids, position]]
    pallas_call x0 -> x15, Pallas kernels: none -> 67.4 us  [call(): pl.pallas_call(kernel, out_shape=tuple(outs), in_specs=[pl.BlockSpec(memo...]
    ppermute x0 -> x45, waiting for transfers between devices: none -> 62.6 us  [hop(): return lax.ppermute(x, axis, [(i, i ^ step) for i in range(count)])]
    ppermute x0 -> x45, starting transfers between devices: none -> 54.8 us  [hop(): return lax.ppermute(x, axis, [(i, i ^ step) for i in range(count)])]
    all_gather x3 -> x0, waiting for transfers between devices: 53.7 us -> none  [the longest x1 26.9 us: per_device(): lax.all_gather(proj_in, 'ep', axis=0, tiled=True)]
    all_to_all x1 -> x0, blocking collectives: 53.4 us -> none  [per_device(): lax.all_to_all(outgoing, ('ep', 'grp'), split_axis=0, concat_axis=0, tile...]
    all_to_all x1 -> x0, waiting for transfers between devices: 48 us -> none  [per_device(): lax.all_to_all(computed, ('ep', 'grp'), split_axis=0, concat_axis=0, tile...]
    reduce_scatter x1 -> x0, waiting for transfers between devices: 37.3 us -> none  [per_device(): lax.psum_scatter(lax.dot_general(tokens, in_rows, (((1,), (1,)), ((), ())...]
  transfers between devices with their start and end apart: 5 -> 45, of which waited for: 4 -> 17; matrix products, arithmetic and copies ran while one was open for 7% -> 4% of each run, Pallas kernels for 0% -> 31%
where the time goes in v1:
time: 200 us; the launch traced here: 199 us
  Pallas kernels  67.4 us (34%)
  waiting for transfers between devices  62.6 us (31%)
  starting transfers between devices  54.8 us (27%)
  local copies, waits for them, and re-layouts  9.39 us (5%)
  other arithmetic  3.56 us (2%)
    pallas_call x15, Pallas kernels, call(): pl.pallas_call(kernel, out_shape=tuple(outs), in_specs=[pl.BlockSpec(memo...  67.4 us
    ppermute x45, waiting for transfers between devices, hop(): return lax.ppermute(x, axis, [(i, i ^ step) for i in range(count)])  62.6 us
    ppermute x45, starting transfers between devices, hop(): return lax.ppermute(x, axis, [(i, i ^ step) for i in range(count)])  54.8 us
    unnamed x83, local copies, waits for them, and re-layouts  7.82 us
  transfers between devices with their start and end apart: 45, of which 17 were waited for; matrix products, arithmetic and copies ran while one was open for 4% of the time, Pallas kernels for 31%

profile of v1, /device:TPU:0, one launch (start us, length us, event | category | flops | bytes accessed | tf_op | source)
XLA Modules:
  0.0 199.2 jit_solution(3784733401895646722)
XLA Ops:
  0.0 3.0 %collective-permute-start.14 = (bf16[256,1024]{1,0:T(8,128)(2,1)}, bf16[256,1024]{1,0:T(8,128)(2,1)S(1)}, u32[]{:S(2)}, u32[]{:S(2)}) collective-permute-start(bf16[256,1024]{1,0:T(8,128)(2,1)} %refs_0_.2), channel_id=1, source_target_pairs={{0,8},{4,12},{8,0},{12,4},{1,9},{5,13},{9,1},{13,5},{2,10},{6,14},... | collective-permute-start | bytes 1572872 | tf_op jit(solution)/shard_map/ppermute | solution.py:16
  3.0 0.7 pad_add_fusion
  4.3 2.0 %collective-permute-start.1 = (bf16[256,1024]{1,0:T(8,128)(2,1)}, bf16[256,1024]{1,0:T(8,128)(2,1)S(1)}, u32[]{:S(2)}, u32[]{:S(2)}) collective-permute-start(bf16[256,1024]{1,0:T(8,128)(2,1)} %refs_0_.3), channel_id=1, source_target_pairs={{0,8},{4,12},{8,0},{12,4},{1,9},{5,13},{9,1},{13,5},{2,10},{6,14},... | collective-permute-start | bytes 1572872 | tf_op jit(solution)/shard_map/ppermute | solution.py:16
  6.4 0.7 add_select_fusion.3
  7.1 0.7 fusion
  8.5 8.1 %collective-permute-done.4 = s32[12,512]{1,0:T(8,128)S(1)} collective-permute-done((s32[12,512]{1,0:T(8,128)S(1)}, s32[12,512]{1,0:T(8,128)S(1)}, u32[]{:S(2)}, u32[]{:S(2)}) %collective-permute-start.4) | collective-permute-done | bytes 24608 | tf_op jit(solution)/shard_map/ppermute | solution.py:16
  16.7 1.2 collective-permute-done.5
  18.8 0.8 copy-done.5
  19.6 3.4 %shard_map.73 = (bf16[128,512]{1,0:T(8,128)(2,1)}, bf16[128,512]{1,0:T(8,128)(2,1)}, bf16[128,512]{1,0:T(8,128)(2,1)}, bf16[128,512]{1,0:T(8,128)(2,1)}) custom-call(s32[2]{0:T(128)} %pad_add_fusion.1.me_ref, bf16[512,1024]{1,0:T(8,128)(2,1)} %tokens_ref.3, bf16[256,1024]{1,0:T(8,128)(2,1)} %refs_0_.2, bf16[256,1024]{1,0:T(8,128)(2,1)} %copy-done.5), custom_call_target="tpu_custom_call" | custom-call | flops 536870912 | bytes 2621440 | tf_op jit(solution)/shard_map/pallas_call | solution.py:32
  23.0 2.1 %collective-permute-start.7 = (bf16[128,512]{1,0:T(8,128)(2,1)}, bf16[128,512]{1,0:T(8,128)(2,1)S(1)}, u32[]{:S(2)}, u32[]{:S(2)}) collective-permute-start(bf16[128,512]{1,0:T(8,128)(2,1)} %get-tuple-element.38), channel_id=1, source_target_pairs={{0,1},{1,0},{2,3},{3,2},{4,5},{5,4},{6,7},{7,6},{8,9},{9,8},{10,11... | collective-permute-start | bytes 393224 | tf_op jit(solution)/shard_map/ppermute | solution.py:16
  25.1 2.6 %collective-permute-start.8 = (bf16[128,512]{1,0:T(8,128)(2,1)}, bf16[128,512]{1,0:T(8,128)(2,1)S(1)}, u32[]{:S(2)}, u32[]{:S(2)}) collective-permute-start(bf16[128,512]{1,0:T(8,128)(2,1)} %get-tuple-element.39), channel_id=1, source_target_pairs={{0,2},{1,3},{2,0},{3,1},{4,6},{5,7},{6,4},{7,5},{8,10},{9,11},{10,... | collective-permute-start | bytes 393224 | tf_op jit(solution)/shard_map/ppermute | solution.py:16
  27.9 3.6 %collective-permute-done.7.refs_1_ = bf16[128,512]{1,0:T(8,128)(2,1)S(1)} collective-permute-done((bf16[128,512]{1,0:T(8,128)(2,1)}, bf16[128,512]{1,0:T(8,128)(2,1)S(1)}, u32[]{:S(2)}, u32[]{:S(2)}) %collective-permute-start.7) | collective-permute-done | bytes 131104 | tf_op jit(solution)/shard_map/ppermute | solution.py:16
  31.4 6.8 %collective-permute-done.8.refs_2_ = bf16[128,512]{1,0:T(8,128)(2,1)S(1)} collective-permute-done((bf16[128,512]{1,0:T(8,128)(2,1)}, bf16[128,512]{1,0:T(8,128)(2,1)S(1)}, u32[]{:S(2)}, u32[]{:S(2)}) %collective-permute-start.8) | collective-permute-done | bytes 131104 | tf_op jit(solution)/shard_map/ppermute | solution.py:16
  39.0 2.1 %shard_map.74 = (bf16[96,512]{1,0:T(8,128)(2,1)}, bf16[96,512]{1,0:T(8,128)(2,1)}, bf16[96,512]{1,0:T(8,128)(2,1)}, bf16[96,512]{1,0:T(8,128)(2,1)}) custom-call(s32[2]{0:T(128)} %pad_add_fusion.1.me_ref, s32[4,1,128]{2,1,0:T(1,128)} %bitcast.22, bf16[128,512]{1,0:T(8,128)(2,1)} %get-tuple-element.37.refs_0_, bf16[128,512]{1,0:T(8,128)(2,1)} %copy-done.21, ...), custom_call_target="tpu_custom_call" | custom-call | bytes 919552 | tf_op jit(solution)/shard_map/pallas_call | solution.py:32
  41.0 2.4 %collective-permute-start.10 = (bf16[96,512]{1,0:T(8,128)(2,1)}, bf16[96,512]{1,0:T(8,128)(2,1)S(1)}, u32[]{:S(2)}, u32[]{:S(2)}) collective-permute-start(bf16[96,512]{1,0:T(8,128)(2,1)} %get-tuple-element.42), channel_id=1, source_target_pairs={{0,1},{1,0},{2,3},{3,2},{4,5},{5,4},{6,7},{7,6},{8,9},{9,8},{10,11... | collective-permute-start | bytes 294920 | tf_op jit(solution)/shard_map/ppermute | solution.py:16
  43.5 1.0 collective-permute-start.11
  44.5 1.4 collective-permute-start.12
  45.9 0.9 constant_dynamic-update-slice_fusion.7
  47.3 0.8 copy-done.6
  48.1 3.4 %shard_map.75 = (bf16[128,512]{1,0:T(8,128)(2,1)}, bf16[128,512]{1,0:T(8,128)(2,1)}, bf16[128,512]{1,0:T(8,128)(2,1)}, bf16[128,512]{1,0:T(8,128)(2,1)}) custom-call(s32[2]{0:T(128)} %pad_add_fusion.1.me_ref, bf16[512,1024]{1,0:T(8,128)(2,1)} %tokens_ref.3, bf16[256,1024]{1,0:T(8,128)(2,1)} %copy-done.2, bf16[256,1024]{1,0:T(8,128)(2,1)} %copy-done.6), custom_call_target="tpu_custom_call" | custom-call | flops 536870912 | bytes 2621440 | tf_op jit(solution)/shard_map/pallas_call | solution.py:32
  51.4 2.1 %collective-permute-start.16 = (bf16[128,512]{1,0:T(8,128)(2,1)}, bf16[128,512]{1,0:T(8,128)(2,1)S(1)}, u32[]{:S(2)}, u32[]{:S(2)}) collective-permute-start(bf16[128,512]{1,0:T(8,128)(2,1)} %get-tuple-element.46), channel_id=1, source_target_pairs={{0,1},{1,0},{2,3},{3,2},{4,5},{5,4},{6,7},{7,6},{8,9},{9,8},{10,11... | collective-permute-start | bytes 393224 | tf_op jit(solution)/shard_map/ppermute | solution.py:16
  53.6 1.0 collective-permute-start.17
  54.6 1.5 collective-permute-start.18
  56.1 1.6 collective-permute-start.24
  57.7 6.3 %collective-permute-done.17.refs_2_ = bf16[128,512]{1,0:T(8,128)(2,1)S(1)} collective-permute-done((bf16[128,512]{1,0:T(8,128)(2,1)}, bf16[128,512]{1,0:T(8,128)(2,1)S(1)}, u32[]{:S(2)}, u32[]{:S(2)}) %collective-permute-start.17) | collective-permute-done | bytes 131104 | tf_op jit(solution)/shard_map/ppermute | solution.py:16
  64.7 2.1 %shard_map.76 = (bf16[96,512]{1,0:T(8,128)(2,1)}, bf16[96,512]{1,0:T(8,128)(2,1)}, bf16[96,512]{1,0:T(8,128)(2,1)}, bf16[96,512]{1,0:T(8,128)(2,1)}) custom-call(s32[2]{0:T(128)} %pad_add_fusion.1.me_ref, s32[4,1,128]{2,1,0:T(1,128)} %bitcast.23, bf16[128,512]{1,0:T(8,128)(2,1)} %get-tuple-element.45.refs_0_, bf16[128,512]{1,0:T(8,128)(2,1)} %copy-done.15, ...), custom_call_target="tpu_custom_call" | custom-call | bytes 919552 | tf_op jit(solution)/shard_map/pallas_call | solution.py:32
  66.8 2.2 %collective-permute-start.19 = (bf16[96,512]{1,0:T(8,128)(2,1)}, bf16[96,512]{1,0:T(8,128)(2,1)S(1)}, u32[]{:S(2)}, u32[]{:S(2)}) collective-permute-start(bf16[96,512]{1,0:T(8,128)(2,1)} %get-tuple-element.50), channel_id=1, source_target_pairs={{0,1},{1,0},{2,3},{3,2},{4,5},{5,4},{6,7},{7,6},{8,9},{9,8},{10,11... | collective-permute-start | bytes 294920 | tf_op jit(solution)/shard_map/ppermute | solution.py:16
  69.1 0.8 collective-permute-start.20
  69.9 1.5 collective-permute-start.21
  71.5 0.9 constant_dynamic-update-slice_fusion.11
  72.6 6.1 %collective-permute-done.20 = bf16[96,512]{1,0:T(8,128)(2,1)S(1)} collective-permute-done((bf16[96,512]{1,0:T(8,128)(2,1)}, bf16[96,512]{1,0:T(8,128)(2,1)S(1)}, u32[]{:S(2)}, u32[]{:S(2)}) %collective-permute-start.20) | collective-permute-done | bytes 98336 | tf_op jit(solution)/shard_map/ppermute | solution.py:16
  78.8 1.6 collective-permute-start.26
  81.4 0.7 sub.7.slot_ref
  82.2 4.5 %collective-permute-done.26.refs_2_ = bf16[384,512]{1,0:T(8,128)(2,1)S(1)} collective-permute-done((bf16[384,512]{1,0:T(8,128)(2,1)S(1)}, bf16[384,512]{1,0:T(8,128)(2,1)S(1)}, u32[]{:S(2)}, u32[]{:S(2)}) %collective-permute-start.26) | collective-permute-done | bytes 393248 | tf_op jit(solution)/shard_map/ppermute | solution.py:16
  87.1 0.7 reshape.71.weight_ref
  87.8 0.7 copy-done.35
  88.6 9.3 %shard_map.77.hidden_ref = bf16[512,2688]{1,0:T(8,128)(2,1)} custom-call(s32[2]{0:T(128)} %pad_add_fusion.1.me_ref, s32[4,1,384]{2,1,0:T(1,128)} %sub.7.slot_ref, bf16[384,512]{1,0:T(8,128)(2,1)} %copy-done.31, bf16[384,512]{1,0:T(8,128)(2,1)} %copy-done.35, bf16[384,512]{1,0:T(8,128)(2,1)} %copy-done.32, bf16[384,512]{1,0:T(8,128)(2,1)} %copy-done.36, ...), custom_call_target="tpu_custom_call" | custom-call | flops 2818572288 | bytes 9836544 | tf_op jit(solution)/shard_map/pallas_call | solution.py:32
  98.0 9.5 %shard_map.79.hidden_ref = bf16[512,2688]{1,0:T(8,128)(2,1)} custom-call(s32[2]{0:T(128)} %pad_add_fusion.1.me_ref, s32[4,1,384]{2,1,0:T(1,128)} %sub.7.slot_ref, bf16[384,512]{1,0:T(8,128)(2,1)} %copy-done.33, bf16[384,512]{1,0:T(8,128)(2,1)} %collective-permute-done.25.refs_1_, bf16[384,512]{1,0:T(8,128)(2,1)} %copy-done.34, ...), custom_call_target="tpu_custom_call" | custom-call | flops 2818572288 | bytes 9836544 | tf_op jit(solution)/shard_map/pallas_call | solution.py:32
  107.5 6.2 %shard_map.84 = (bf16[384,512]{1,0:T(8,128)(2,1)}, bf16[384,512]{1,0:T(8,128)(2,1)}) custom-call(s32[2]{0:T(128)} %pad_add_fusion.1.me_ref, s32[4,1,384]{2,1,0:T(1,128)} %sub.7.slot_ref, f32[4,1,384]{2,1,0:T(1,128)} %reshape.71.weight_ref, bf16[512,2688]{1,0:T(8,128)(2,1)} %shard_map.79.hidden_ref, bf16[2688,1024]{1,0:T(8,128)(2,1)} %bitcast.18), custom_call_target="tpu_custom_call" | custom-call | flops 1409286144 | bytes 9056256 | tf_op jit(solution)/shard_map/pallas_call | solution.py:32
  114.2 6.2 %shard_map.80 = (bf16[384,512]{1,0:T(8,128)(2,1)}, bf16[384,512]{1,0:T(8,128)(2,1)}) custom-call(s32[2]{0:T(128)} %pad_add_fusion.1.me_ref, s32[4,1,384]{2,1,0:T(1,128)} %sub.7.slot_ref, f32[4,1,384]{2,1,0:T(1,128)} %reshape.71.weight_ref, bf16[512,2688]{1,0:T(8,128)(2,1)} %shard_map.79.hidden_ref, bf16[2688,1024]{1,0:T(8,128)(2,1)} %bitcast.19), custom_call_target="tpu_custom_call" | custom-call | flops 1409286144 | bytes 9056256 | tf_op jit(solution)/shard_map/pallas_call | solution.py:32
  120.4 6.2 %shard_map.83 = (bf16[384,512]{1,0:T(8,128)(2,1)}, bf16[384,512]{1,0:T(8,128)(2,1)}) custom-call(s32[2]{0:T(128)} %pad_add_fusion.1.me_ref, s32[4,1,384]{2,1,0:T(1,128)} %sub.7.slot_ref, f32[4,1,384]{2,1,0:T(1,128)} %reshape.71.weight_ref, bf16[512,2688]{1,0:T(8,128)(2,1)} %shard_map.77.hidden_ref, bf16[2688,1024]{1,0:T(8,128)(2,1)} %bitcast.20), custom_call_target="tpu_custom_call" | custom-call | flops 1409286144 | bytes 9056256 | tf_op jit(solution)/shard_map/pallas_call | solution.py:32
  127.2 6.2 %shard_map.78 = (bf16[384,512]{1,0:T(8,128)(2,1)}, bf16[384,512]{1,0:T(8,128)(2,1)}) custom-call(s32[2]{0:T(128)} %pad_add_fusion.1.me_ref, s32[4,1,384]{2,1,0:T(1,128)} %sub.7.slot_ref, f32[4,1,384]{2,1,0:T(1,128)} %reshape.71.weight_ref, bf16[512,2688]{1,0:T(8,128)(2,1)} %shard_map.77.hidden_ref, bf16[2688,1024]{1,0:T(8,128)(2,1)} %bitcast.21), custom_call_target="tpu_custom_call" | custom-call | flops 1409286144 | bytes 9056256 | tf_op jit(solution)/shard_map/pallas_call | solution.py:32
  133.6 1.6 collective-permute-start.35
  136.4 9.1 %collective-permute-done.35.refs_2_ = bf16[384,512]{1,0:T(8,128)(2,1)S(1)} collective-permute-done((bf16[384,512]{1,0:T(8,128)(2,1)S(1)}, bf16[384,512]{1,0:T(8,128)(2,1)S(1)}, u32[]{:S(2)}, u32[]{:S(2)}) %collective-permute-start.35) | collective-permute-done | bytes 393248 | tf_op jit(solution)/shard_map/ppermute | solution.py:16
  145.6 0.7 copy-done.11
  146.3 2.0 %shard_map.85 = (bf16[96,512]{1,0:T(8,128)(2,1)}, bf16[96,512]{1,0:T(8,128)(2,1)}, bf16[96,512]{1,0:T(8,128)(2,1)}, bf16[96,512]{1,0:T(8,128)(2,1)}) custom-call(s32[2]{0:T(128)} %pad_add_fusion.1.me_ref, bf16[384,512]{1,0:T(8,128)(2,1)} %get-tuple-element.61.refs_0_, bf16[384,512]{1,0:T(8,128)(2,1)} %copy-done.8, bf16[384,512]{1,0:T(8,128)(2,1)} %copy-done.11), custom_call_target="tpu_custom_call" | custom-call | bytes 1572864 | tf_op jit(solution)/shard_map/pallas_call | solution.py:32
  148.3 4.1 %collective-permute-start.36 = (bf16[96,512]{1,0:T(8,128)(2,1)}, bf16[96,512]{1,0:T(8,128)(2,1)S(1)}, u32[]{:S(2)}, u32[]{:S(2)}) collective-permute-start(bf16[96,512]{1,0:T(8,128)(2,1)} %get-tuple-element.66), channel_id=1, source_target_pairs={{0,1},{1,0},{2,3},{3,2},{4,5},{5,4},{6,7},{7,6},{8,9},{9,8},{10,11... | collective-permute-start | bytes 294920 | tf_op jit(solution)/shard_map/ppermute | solution.py:16
  152.5 0.8 collective-permute-start.37
  153.5 3.7 %collective-permute-start.38 = (bf16[96,512]{1,0:T(8,128)(2,1)}, bf16[96,512]{1,0:T(8,128)(2,1)S(1)}, u32[]{:S(2)}, u32[]{:S(2)}) collective-permute-start(bf16[96,512]{1,0:T(8,128)(2,1)} %get-tuple-element.68), channel_id=1, source_target_pairs={{0,3},{1,2},{2,1},{3,0},{4,7},{5,6},{6,5},{7,4},{8,11},{9,10},{10,... | collective-permute-start | bytes 294920 | tf_op jit(solution)/shard_map/ppermute | solution.py:16
  157.2 2.0 %shard_map.81 = (bf16[96,512]{1,0:T(8,128)(2,1)}, bf16[96,512]{1,0:T(8,128)(2,1)}, bf16[96,512]{1,0:T(8,128)(2,1)}, bf16[96,512]{1,0:T(8,128)(2,1)}) custom-call(s32[2]{0:T(128)} %pad_add_fusion.1.me_ref, bf16[384,512]{1,0:T(8,128)(2,1)} %get-tuple-element.53.refs_0_, bf16[384,512]{1,0:T(8,128)(2,1)} %copy-done.7, bf16[384,512]{1,0:T(8,128)(2,1)} %copy-done.9), custom_call_target="tpu_custom_call" | custom-call | bytes 1572864 | tf_op jit(solution)/shard_map/pallas_call | solution.py:32
  159.3 1.8 collective-permute-start.30
  161.7 2.3 %collective-permute-start.32 = (bf16[96,512]{1,0:T(8,128)(2,1)}, bf16[96,512]{1,0:T(8,128)(2,1)S(1)}, u32[]{:S(2)}, u32[]{:S(2)}) collective-permute-start(bf16[96,512]{1,0:T(8,128)(2,1)} %get-tuple-element.60), channel_id=1, source_target_pairs={{0,3},{1,2},{2,1},{3,0},{4,7},{5,6},{6,5},{7,4},{8,11},{9,10},{10,... | collective-permute-start | bytes 294920 | tf_op jit(solution)/shard_map/ppermute | solution.py:16
  164.0 2.0 %shard_map.86.refs_5_ = bf16[128,512]{1,0:T(8,128)(2,1)} custom-call(s32[2]{0:T(128)} %pad_add_fusion.1.me_ref, s32[4,1,128]{2,1,0:T(1,128)} %bitcast.24, bf16[96,512]{1,0:T(8,128)(2,1)} %get-tuple-element.65.refs_0_, bf16[96,512]{1,0:T(8,128)(2,1)} %copy-done.25, bf16[96,512]{1,0:T(8,128)(2,1)} %copy-done.26, bf16[96,512]{1,0:T(8,128)(2,1)} %copy-done.28), custom_call_target="tpu_custom_call" | custom-call | bytes 526336 | tf_op jit(solution)/shard_map/pallas_call | solution.py:32
  166.0 1.6 collective-permute-start.42
  167.6 6.7 %collective-permute-done.31.refs_2_ = bf16[96,512]{1,0:T(8,128)(2,1)S(1)} collective-permute-done((bf16[96,512]{1,0:T(8,128)(2,1)}, bf16[96,512]{1,0:T(8,128)(2,1)S(1)}, u32[]{:S(2)}, u32[]{:S(2)}) %collective-permute-start.31) | collective-permute-done | bytes 98336 | tf_op jit(solution)/shard_map/ppermute | solution.py:16
  174.9 2.0 %shard_map.82.refs_4_ = bf16[128,512]{1,0:T(8,128)(2,1)} custom-call(s32[2]{0:T(128)} %pad_add_fusion.1.me_ref, s32[4,1,128]{2,1,0:T(1,128)} %bitcast.25, bf16[96,512]{1,0:T(8,128)(2,1)} %get-tuple-element.57.refs_0_, bf16[96,512]{1,0:T(8,128)(2,1)} %copy-done.27, bf16[96,512]{1,0:T(8,128)(2,1)} %copy-done.29, bf16[96,512]{1,0:T(8,128)(2,1)} %copy-done.30), custom_call_target="tpu_custom_call" | custom-call | bytes 526336 | tf_op jit(solution)/shard_map/pallas_call | solution.py:32
  176.9 2.6 %collective-permute-start.41 = (bf16[128,512]{1,0:T(8,128)(2,1)}, bf16[128,512]{1,0:T(8,128)(2,1)S(1)}, u32[]{:S(2)}, u32[]{:S(2)}) collective-permute-start(bf16[128,512]{1,0:T(8,128)(2,1)} %shard_map.82.refs_4_), channel_id=1, source_target_pairs={{0,2},{1,3},{2,0},{3,1},{4,6},{5,7},{6,4},{7,5},{8,10},{9,11},{10,... | collective-permute-start | bytes 393224 | tf_op jit(solution)/shard_map/ppermute | solution.py:16
  179.6 2.0 collective-permute-start.39
  181.6 2.1 %collective-permute-done.41.refs_8_ = bf16[128,512]{1,0:T(8,128)(2,1)S(1)} collective-permute-done((bf16[128,512]{1,0:T(8,128)(2,1)}, bf16[128,512]{1,0:T(8,128)(2,1)S(1)}, u32[]{:S(2)}, u32[]{:S(2)}) %collective-permute-start.41) | collective-permute-done | bytes 131104 | tf_op jit(solution)/shard_map/ppermute | solution.py:16
  183.8 3.3 %collective-permute-start.43 = (bf16[128,512]{1,0:T(8,128)(2,1)S(1)}, bf16[128,512]{1,0:T(8,128)(2,1)S(1)}, u32[]{:S(2)}, u32[]{:S(2)}) collective-permute-start(bf16[128,512]{1,0:T(8,128)(2,1)S(1)} %collective-permute-done.41.refs_8_), channel_id=1, source_target_pairs={{0,1},{1,0},{2,3},{3,2},{4,5},{5,4},{6,7},{7,6},{8,9},{9,8},{10,11... | collective-permute-start | bytes 393224 | tf_op jit(solution)/shard_map/ppermute | solution.py:16
  187.1 2.3 %collective-permute-done.39.refs_6_ = bf16[128,512]{1,0:T(8,128)(2,1)S(1)} collective-permute-done((bf16[128,512]{1,0:T(8,128)(2,1)}, bf16[128,512]{1,0:T(8,128)(2,1)S(1)}, u32[]{:S(2)}, u32[]{:S(2)}) %collective-permute-start.39) | collective-permute-done | bytes 131104 | tf_op jit(solution)/shard_map/ppermute | solution.py:16
  189.4 2.6 %collective-permute-done.44.refs_11_ = bf16[128,512]{1,0:T(8,128)(2,1)S(1)} collective-permute-done((bf16[128,512]{1,0:T(8,128)(2,1)S(1)}, bf16[128,512]{1,0:T(8,128)(2,1)S(1)}, u32[]{:S(2)}, u32[]{:S(2)}) %collective-permute-start.44) | collective-permute-done | bytes 131104 | tf_op jit(solution)/shard_map/ppermute | solution.py:16
  192.0 1.6 collective-permute-done.43.refs_10_
  194.4 4.8 %shard_map.87 = bf16[512,1024]{1,0:T(8,128)(2,1)} custom-call(s32[2]{0:T(128)} %pad_add_fusion.1.me_ref, bf16[256,1024]{1,0:T(8,128)(2,1)} %refs_0_.3, bf16[256,1024]{1,0:T(8,128)(2,1)} %copy-done.3, bf16[256,1024]{1,0:T(8,128)(2,1)} %copy-done.1, bf16[256,1024]{1,0:T(8,128)(2,1)} %copy-done.4, bf16[128,512]{1,0:T(8,128)(2,1)} %shard_map.82.refs_4_, ...), custom_call_target="tpu_custom_call" | custom-call | flops 1073741824 | bytes 4194304 | tf_op jit(solution)/shard_map/pallas_call | solution.py:32
  (156 shorter events, 11.1 us)
Async XLA Ops:
  0.0 18.5 %collective-permute-start.14 = (bf16[256,1024]{1,0:T(8,128)(2,1)}, bf16[256,1024]{1,0:T(8,128)(2,1)S(1)}, u32[]{:S(2)}, u32[]{:S(2)}) collective-permute-start(bf16[256,1024]{1,0:T(8,128)(2,1)} %refs_0_.2), channel_id=1, source_target_pairs={{0,8},{4,12},{8,0},{12,4},{1,9},{5,13},{9,1},{13,5},{2,10},{6,14},... | collective-permute-start | bytes 1572872 | tf_op jit(solution)/shard_map/ppermute | solution.py:16
  3.0 15.9 %collective-permute-start.6 = (bf16[256,1024]{1,0:T(8,128)(2,1)}, bf16[256,1024]{1,0:T(8,128)(2,1)S(1)}, u32[]{:S(2)}, u32[]{:S(2)}) collective-permute-start(bf16[256,1024]{1,0:T(8,128)(2,1)} %refs_0_.2), channel_id=1, source_target_pairs={{0,4},{4,0},{8,12},{12,8},{1,5},{5,1},{9,13},{13,9},{2,6},{6,2},{1... | collective-permute-start | bytes 1572872 | tf_op jit(solution)/shard_map/ppermute | solution.py:16
  3.7 4.8 %collective-permute-start.3 = (s32[12,512]{1,0:T(8,128)S(1)}, s32[12,512]{1,0:T(8,128)S(1)}, u32[]{:S(2)}, u32[]{:S(2)}) collective-permute-start(s32[12,512]{1,0:T(8,128)S(1)} %pad_add_fusion), channel_id=1, source_target_pairs={{0,4},{4,0},{8,12},{12,8},{1,5},{5,1},{9,13},{13,9},{2,6},{6,2},{1... | collective-permute-start | bytes 73736 | tf_op jit(solution)/shard_map/ppermute | solution.py:16
  4.3 12.3 %collective-permute-start.4 = (s32[12,512]{1,0:T(8,128)S(1)}, s32[12,512]{1,0:T(8,128)S(1)}, u32[]{:S(2)}, u32[]{:S(2)}) collective-permute-start(s32[12,512]{1,0:T(8,128)S(1)} %pad_add_fusion), channel_id=1, source_target_pairs={{0,8},{4,12},{8,0},{12,4},{1,9},{5,13},{9,1},{13,5},{2,10},{6,14},... | collective-permute-start | bytes 73736 | tf_op jit(solution)/shard_map/ppermute | solution.py:16
  4.3 131.5 %collective-permute-start.1 = (bf16[256,1024]{1,0:T(8,128)(2,1)}, bf16[256,1024]{1,0:T(8,128)(2,1)S(1)}, u32[]{:S(2)}, u32[]{:S(2)}) collective-permute-start(bf16[256,1024]{1,0:T(8,128)(2,1)} %refs_0_.3), channel_id=1, source_target_pairs={{0,8},{4,12},{8,0},{12,4},{1,9},{5,13},{9,1},{13,5},{2,10},{6,14},... | collective-permute-start | bytes 1572872 | tf_op jit(solution)/shard_map/ppermute | solution.py:16
  16.6 1.3 collective-permute-start.5
  18.5 28.7 %copy-start.2 = (bf16[256,1024]{1,0:T(8,128)(2,1)}, bf16[256,1024]{1,0:T(8,128)(2,1)S(1)}, u32[]{:S(2)}) copy-start(bf16[256,1024]{1,0:T(8,128)(2,1)S(1)} %collective-permute-done.14.refs_0_) | copy-start | bytes 1572868
  18.5 28.7 %collective-permute-start.15 = (bf16[256,1024]{1,0:T(8,128)(2,1)S(1)}, bf16[256,1024]{1,0:T(8,128)(2,1)S(1)}, u32[]{:S(2)}, u32[]{:S(2)}) collective-permute-start(bf16[256,1024]{1,0:T(8,128)(2,1)S(1)} %collective-permute-done.14.refs_0_), channel_id=1, source_target_pairs={{0,4},{4,0},{8,12},{12,8},{1,5},{5,1},{9,13},{13,9},{2,6},{6,2},{1... | collective-permute-start | bytes 1572872 | tf_op jit(solution)/shard_map/ppermute | solution.py:16
  23.0 8.4 %collective-permute-start.7 = (bf16[128,512]{1,0:T(8,128)(2,1)}, bf16[128,512]{1,0:T(8,128)(2,1)S(1)}, u32[]{:S(2)}, u32[]{:S(2)}) collective-permute-start(bf16[128,512]{1,0:T(8,128)(2,1)} %get-tuple-element.38), channel_id=1, source_target_pairs={{0,1},{1,0},{2,3},{3,2},{4,5},{5,4},{6,7},{7,6},{8,9},{9,8},{10,11... | collective-permute-start | bytes 393224 | tf_op jit(solution)/shard_map/ppermute | solution.py:16
  25.1 13.1 %collective-permute-start.8 = (bf16[128,512]{1,0:T(8,128)(2,1)}, bf16[128,512]{1,0:T(8,128)(2,1)S(1)}, u32[]{:S(2)}, u32[]{:S(2)}) collective-permute-start(bf16[128,512]{1,0:T(8,128)(2,1)} %get-tuple-element.39), channel_id=1, source_target_pairs={{0,2},{1,3},{2,0},{3,1},{4,6},{5,7},{6,4},{7,5},{8,10},{9,11},{10,... | collective-permute-start | bytes 393224 | tf_op jit(solution)/shard_map/ppermute | solution.py:16
  27.7 10.5 %collective-permute-start.9 = (bf16[128,512]{1,0:T(8,128)(2,1)}, bf16[128,512]{1,0:T(8,128)(2,1)S(1)}, u32[]{:S(2)}, u32[]{:S(2)}) collective-permute-start(bf16[128,512]{1,0:T(8,128)(2,1)} %get-tuple-element.40), channel_id=1, source_target_pairs={{0,3},{1,2},{2,1},{3,0},{4,7},{5,6},{6,5},{7,4},{8,11},{9,10},{10,... | collective-permute-start | bytes 393224 | tf_op jit(solution)/shard_map/ppermute | solution.py:16
  31.4 6.8 %copy-start.21 = (bf16[128,512]{1,0:T(8,128)(2,1)}, bf16[128,512]{1,0:T(8,128)(2,1)S(1)}, u32[]{:S(2)}) copy-start(bf16[128,512]{1,0:T(8,128)(2,1)S(1)} %collective-permute-done.7.refs_1_) | copy-start | bytes 393220
  41.0 6.2 %collective-permute-start.10 = (bf16[96,512]{1,0:T(8,128)(2,1)}, bf16[96,512]{1,0:T(8,128)(2,1)S(1)}, u32[]{:S(2)}, u32[]{:S(2)}) collective-permute-start(bf16[96,512]{1,0:T(8,128)(2,1)} %get-tuple-element.42), channel_id=1, source_target_pairs={{0,1},{1,0},{2,3},{3,2},{4,5},{5,4},{6,7},{7,6},{8,9},{9,8},{10,11... | collective-permute-start | bytes 294920 | tf_op jit(solution)/shard_map/ppermute | solution.py:16
  43.5 11.2 %collective-permute-start.11 = (bf16[96,512]{1,0:T(8,128)(2,1)}, bf16[96,512]{1,0:T(8,128)(2,1)S(1)}, u32[]{:S(2)}, u32[]{:S(2)}) collective-permute-start(bf16[96,512]{1,0:T(8,128)(2,1)} %get-tuple-element.43), channel_id=1, source_target_pairs={{0,2},{1,3},{2,0},{3,1},{4,6},{5,7},{6,4},{7,5},{8,10},{9,11},{10,... | collective-permute-start | bytes 294920 | tf_op jit(solution)/shard_map/ppermute | solution.py:16
  44.5 11.6 %collective-permute-start.12 = (bf16[96,512]{1,0:T(8,128)(2,1)}, bf16[96,512]{1,0:T(8,128)(2,1)S(1)}, u32[]{:S(2)}, u32[]{:S(2)}) collective-permute-start(bf16[96,512]{1,0:T(8,128)(2,1)} %get-tuple-element.44), channel_id=1, source_target_pairs={{0,3},{1,2},{2,1},{3,0},{4,7},{5,6},{6,5},{7,4},{8,11},{9,10},{10,... | collective-permute-start | bytes 294920 | tf_op jit(solution)/shard_map/ppermute | solution.py:16
  51.4 6.3 %collective-permute-start.16 = (bf16[128,512]{1,0:T(8,128)(2,1)}, bf16[128,512]{1,0:T(8,128)(2,1)S(1)}, u32[]{:S(2)}, u32[]{:S(2)}) collective-permute-start(bf16[128,512]{1,0:T(8,128)(2,1)} %get-tuple-element.46), channel_id=1, source_target_pairs={{0,1},{1,0},{2,3},{3,2},{4,5},{5,4},{6,7},{7,6},{8,9},{9,8},{10,11... | collective-permute-start | bytes 393224 | tf_op jit(solution)/shard_map/ppermute | solution.py:16
  53.6 10.4 %collective-permute-start.17 = (bf16[128,512]{1,0:T(8,128)(2,1)}, bf16[128,512]{1,0:T(8,128)(2,1)S(1)}, u32[]{:S(2)}, u32[]{:S(2)}) collective-permute-start(bf16[128,512]{1,0:T(8,128)(2,1)} %get-tuple-element.47), channel_id=1, source_target_pairs={{0,2},{1,3},{2,0},{3,1},{4,6},{5,7},{6,4},{7,5},{8,10},{9,11},{10,... | collective-permute-start | bytes 393224 | tf_op jit(solution)/shard_map/ppermute | solution.py:16
  54.6 9.4 %collective-permute-start.18 = (bf16[128,512]{1,0:T(8,128)(2,1)}, bf16[128,512]{1,0:T(8,128)(2,1)S(1)}, u32[]{:S(2)}, u32[]{:S(2)}) collective-permute-start(bf16[128,512]{1,0:T(8,128)(2,1)} %get-tuple-element.48), channel_id=1, source_target_pairs={{0,3},{1,2},{2,1},{3,0},{4,7},{5,6},{6,5},{7,4},{8,11},{9,10},{10,... | collective-permute-start | bytes 393224 | tf_op jit(solution)/shard_map/ppermute | solution.py:16
  56.1 31.7 %copy-start.31 = (bf16[384,512]{1,0:T(8,128)(2,1)}, bf16[384,512]{1,0:T(8,128)(2,1)S(1)}, u32[]{:S(2)}) copy-start(bf16[384,512]{1,0:T(8,128)(2,1)S(1)} %constant_dynamic-update-slice_fusion.4.refs_0_) | copy-start | bytes 1179652
  56.1 26.0 %collective-permute-start.24 = (bf16[384,512]{1,0:T(8,128)(2,1)S(1)}, bf16[384,512]{1,0:T(8,128)(2,1)S(1)}, u32[]{:S(2)}, u32[]{:S(2)}) collective-permute-start(bf16[384,512]{1,0:T(8,128)(2,1)S(1)} %constant_dynamic-update-slice_fusion.4.refs_0_), channel_id=1, source_target_pairs={{0,8},{4,12},{8,0},{12,4},{1,9},{5,13},{9,1},{13,5},{2,10},{6,14},... | collective-permute-start | bytes 1179656 | tf_op jit(solution)/shard_map/ppermute | solution.py:16
  57.7 6.3 %copy-start.15 = (bf16[128,512]{1,0:T(8,128)(2,1)}, bf16[128,512]{1,0:T(8,128)(2,1)S(1)}, u32[]{:S(2)}) copy-start(bf16[128,512]{1,0:T(8,128)(2,1)S(1)} %collective-permute-done.16.refs_1_) | copy-start | bytes 393220
  66.8 5.8 %collective-permute-start.19 = (bf16[96,512]{1,0:T(8,128)(2,1)}, bf16[96,512]{1,0:T(8,128)(2,1)S(1)}, u32[]{:S(2)}, u32[]{:S(2)}) collective-permute-start(bf16[96,512]{1,0:T(8,128)(2,1)} %get-tuple-element.50), channel_id=1, source_target_pairs={{0,1},{1,0},{2,3},{3,2},{4,5},{5,4},{6,7},{7,6},{8,9},{9,8},{10,11... | collective-permute-start | bytes 294920 | tf_op jit(solution)/shard_map/ppermute | solution.py:16
  69.1 9.7 %collective-permute-start.20 = (bf16[96,512]{1,0:T(8,128)(2,1)}, bf16[96,512]{1,0:T(8,128)(2,1)S(1)}, u32[]{:S(2)}, u32[]{:S(2)}) collective-permute-start(bf16[96,512]{1,0:T(8,128)(2,1)} %get-tuple-element.51), channel_id=1, source_target_pairs={{0,2},{1,3},{2,0},{3,1},{4,6},{5,7},{6,4},{7,5},{8,10},{9,11},{10,... | collective-permute-start | bytes 294920 | tf_op jit(solution)/shard_map/ppermute | solution.py:16
  69.9 8.9 %collective-permute-start.21 = (bf16[96,512]{1,0:T(8,128)(2,1)}, bf16[96,512]{1,0:T(8,128)(2,1)S(1)}, u32[]{:S(2)}, u32[]{:S(2)}) collective-permute-start(bf16[96,512]{1,0:T(8,128)(2,1)} %get-tuple-element.52), channel_id=1, source_target_pairs={{0,3},{1,2},{2,1},{3,0},{4,7},{5,6},{6,5},{7,4},{8,11},{9,10},{10,... | collective-permute-start | bytes 294920 | tf_op jit(solution)/shard_map/ppermute | solution.py:16
  78.8 9.0 %copy-start.32 = (bf16[384,512]{1,0:T(8,128)(2,1)}, bf16[384,512]{1,0:T(8,128)(2,1)S(1)}, u32[]{:S(2)}) copy-start(bf16[384,512]{1,0:T(8,128)(2,1)S(1)} %constant_dynamic-update-slice_fusion.8.refs_2_) | copy-start | bytes 1179652
  78.8 7.8 %collective-permute-start.26 = (bf16[384,512]{1,0:T(8,128)(2,1)S(1)}, bf16[384,512]{1,0:T(8,128)(2,1)S(1)}, u32[]{:S(2)}, u32[]{:S(2)}) collective-permute-start(bf16[384,512]{1,0:T(8,128)(2,1)S(1)} %constant_dynamic-update-slice_fusion.8.refs_2_), channel_id=1, source_target_pairs={{0,8},{4,12},{8,0},{12,4},{1,9},{5,13},{9,1},{13,5},{2,10},{6,14},... | collective-permute-start | bytes 1179656 | tf_op jit(solution)/shard_map/ppermute | solution.py:16
  80.5 7.3 %collective-permute-start.13 = (bf16[384,512]{1,0:T(8,128)(2,1)S(1)}, bf16[384,512]{1,0:T(8,128)(2,1)S(1)}, u32[]{:S(2)}, u32[]{:S(2)}) collective-permute-start(bf16[384,512]{1,0:T(8,128)(2,1)S(1)} %constant_dynamic-update-slice_fusion.4.refs_0_), channel_id=1, source_target_pairs={{0,4},{4,0},{8,12},{12,8},{1,5},{5,1},{9,13},{13,9},{2,6},{6,2},{1... | collective-permute-start | bytes 1179656 | tf_op jit(solution)/shard_map/ppermute | solution.py:16
  80.5 7.3 %collective-permute-start.22 = (bf16[384,512]{1,0:T(8,128)(2,1)S(1)}, bf16[384,512]{1,0:T(8,128)(2,1)S(1)}, u32[]{:S(2)}, u32[]{:S(2)}) collective-permute-start(bf16[384,512]{1,0:T(8,128)(2,1)S(1)} %constant_dynamic-update-slice_fusion.8.refs_2_), channel_id=1, source_target_pairs={{0,4},{4,0},{8,12},{12,8},{1,5},{5,1},{9,13},{13,9},{2,6},{6,2},{1... | collective-permute-start | bytes 1179656 | tf_op jit(solution)/shard_map/ppermute | solution.py:16
  82.1 15.9 %copy-start.33 = (bf16[384,512]{1,0:T(8,128)(2,1)}, bf16[384,512]{1,0:T(8,128)(2,1)S(1)}, u32[]{:S(2)}) copy-start(bf16[384,512]{1,0:T(8,128)(2,1)S(1)} %collective-permute-done.24.refs_0_) | copy-start | bytes 1179652
  82.1 15.9 %collective-permute-start.25 = (bf16[384,512]{1,0:T(8,128)(2,1)S(1)}, bf16[384,512]{1,0:T(8,128)(2,1)}, u32[]{:S(2)}, u32[]{:S(2)}) collective-permute-start(bf16[384,512]{1,0:T(8,128)(2,1)S(1)} %collective-permute-done.24.refs_0_), channel_id=1, source_target_pairs={{0,4},{4,0},{8,12},{12,8},{1,5},{5,1},{9,13},{13,9},{2,6},{6,2},{1... | collective-permute-start | bytes 1179656 | tf_op jit(solution)/shard_map/ppermute | solution.py:16
  86.7 11.3 %copy-start.34 = (bf16[384,512]{1,0:T(8,128)(2,1)}, bf16[384,512]{1,0:T(8,128)(2,1)S(1)}, u32[]{:S(2)}) copy-start(bf16[384,512]{1,0:T(8,128)(2,1)S(1)} %collective-permute-done.26.refs_2_) | copy-start | bytes 1179652
  86.7 11.3 %collective-permute-start.27 = (bf16[384,512]{1,0:T(8,128)(2,1)S(1)}, bf16[384,512]{1,0:T(8,128)(2,1)}, u32[]{:S(2)}, u32[]{:S(2)}) collective-permute-start(bf16[384,512]{1,0:T(8,128)(2,1)S(1)} %collective-permute-done.26.refs_2_), channel_id=1, source_target_pairs={{0,4},{4,0},{8,12},{12,8},{1,5},{5,1},{9,13},{13,9},{2,6},{6,2},{1... | collective-permute-start | bytes 1179656 | tf_op jit(solution)/shard_map/ppermute | solution.py:16
  113.7 19.8 %collective-permute-start.34 = (bf16[384,512]{1,0:T(8,128)(2,1)}, bf16[384,512]{1,0:T(8,128)(2,1)S(1)}, u32[]{:S(2)}, u32[]{:S(2)}) collective-permute-start(bf16[384,512]{1,0:T(8,128)(2,1)} %get-tuple-element.64), channel_id=1, source_target_pairs={{0,4},{4,0},{8,12},{12,8},{1,5},{5,1},{9,13},{13,9},{2,6},{6,2},{1... | collective-permute-start | bytes 1179656 | tf_op jit(solution)/shard_map/ppermute | solution.py:16
  120.4 14.7 %collective-permute-start.28 = (bf16[384,512]{1,0:T(8,128)(2,1)}, bf16[384,512]{1,0:T(8,128)(2,1)S(1)}, u32[]{:S(2)}, u32[]{:S(2)}) collective-permute-start(bf16[384,512]{1,0:T(8,128)(2,1)} %get-tuple-element.56), channel_id=1, source_target_pairs={{0,4},{4,0},{8,12},{12,8},{1,5},{5,1},{9,13},{13,9},{2,6},{6,2},{1... | collective-permute-start | bytes 1179656 | tf_op jit(solution)/shard_map/ppermute | solution.py:16
  126.6 6.9 %copy-start.12 = (bf16[384,512]{1,0:T(8,128)(2,1)S(1)}, bf16[384,512]{1,0:T(8,128)(2,1)}, u32[]{:S(2)}) copy-start(bf16[384,512]{1,0:T(8,128)(2,1)} %get-tuple-element.63) | copy-start | bytes 1179652
  126.6 8.5 %copy-start.10 = (bf16[384,512]{1,0:T(8,128)(2,1)S(1)}, bf16[384,512]{1,0:T(8,128)(2,1)}, u32[]{:S(2)}) copy-start(bf16[384,512]{1,0:T(8,128)(2,1)} %get-tuple-element.55) | copy-start | bytes 1179652
  126.6 9.2 %copy-start = (bf16[256,1024]{1,0:T(8,128)(2,1)S(1)}, bf16[256,1024]{1,0:T(8,128)(2,1)}, u32[]{:S(2)}) copy-start(bf16[256,1024]{1,0:T(8,128)(2,1)} %refs_0_.3) | copy-start | bytes 1572868
  126.6 9.3 %collective-permute-start.33 = (bf16[384,512]{1,0:T(8,128)(2,1)}, bf16[384,512]{1,0:T(8,128)(2,1)S(1)}, u32[]{:S(2)}, u32[]{:S(2)}) collective-permute-start(bf16[384,512]{1,0:T(8,128)(2,1)} %get-tuple-element.62), channel_id=1, source_target_pairs={{0,4},{4,0},{8,12},{12,8},{1,5},{5,1},{9,13},{13,9},{2,6},{6,2},{1... | collective-permute-start | bytes 1179656 | tf_op jit(solution)/shard_map/ppermute | solution.py:16
  133.4 19.1 %collective-permute-start.23 = (bf16[384,512]{1,0:T(8,128)(2,1)}, bf16[384,512]{1,0:T(8,128)(2,1)S(1)}, u32[]{:S(2)}, u32[]{:S(2)}) collective-permute-start(bf16[384,512]{1,0:T(8,128)(2,1)} %get-tuple-element.54), channel_id=1, source_target_pairs={{0,4},{4,0},{8,12},{12,8},{1,5},{5,1},{9,13},{13,9},{2,6},{6,2},{1... | collective-permute-start | bytes 1179656 | tf_op jit(solution)/shard_map/ppermute | solution.py:16
  133.6 12.0 %collective-permute-start.35 = (bf16[384,512]{1,0:T(8,128)(2,1)S(1)}, bf16[384,512]{1,0:T(8,128)(2,1)S(1)}, u32[]{:S(2)}, u32[]{:S(2)}) collective-permute-start(bf16[384,512]{1,0:T(8,128)(2,1)S(1)} %add_convert_fusion), channel_id=1, source_target_pairs={{0,8},{4,12},{8,0},{12,4},{1,9},{5,13},{9,1},{13,5},{2,10},{6,14},... | collective-permute-start | bytes 1179656 | tf_op jit(solution)/shard_map/ppermute | solution.py:16
  135.2 18.3 %collective-permute-start.29 = (bf16[384,512]{1,0:T(8,128)(2,1)S(1)}, bf16[384,512]{1,0:T(8,128)(2,1)S(1)}, u32[]{:S(2)}, u32[]{:S(2)}) collective-permute-start(bf16[384,512]{1,0:T(8,128)(2,1)S(1)} %add_convert_fusion.1), channel_id=1, source_target_pairs={{0,8},{4,12},{8,0},{12,4},{1,9},{5,13},{9,1},{13,5},{2,10},{6,14},... | collective-permute-start | bytes 1179656 | tf_op jit(solution)/shard_map/ppermute | solution.py:16
  135.8 57.8 %copy-start.1 = (bf16[256,1024]{1,0:T(8,128)(2,1)}, bf16[256,1024]{1,0:T(8,128)(2,1)S(1)}, u32[]{:S(2)}) copy-start(bf16[256,1024]{1,0:T(8,128)(2,1)S(1)} %collective-permute-done.1.refs_2_) | copy-start | bytes 1572868
  135.8 43.7 %collective-permute-start = (bf16[256,1024]{1,0:T(8,128)(2,1)S(1)}, bf16[256,1024]{1,0:T(8,128)(2,1)S(1)}, u32[]{:S(2)}, u32[]{:S(2)}) collective-permute-start(bf16[256,1024]{1,0:T(8,128)(2,1)S(1)} %copy-done), channel_id=1, source_target_pairs={{0,4},{4,0},{8,12},{12,8},{1,5},{5,1},{9,13},{13,9},{2,6},{6,2},{1... | collective-permute-start | bytes 1572872 | tf_op jit(solution)/shard_map/ppermute | solution.py:16
  135.9 9.6 %copy-start.8 = (bf16[384,512]{1,0:T(8,128)(2,1)}, bf16[384,512]{1,0:T(8,128)(2,1)S(1)}, u32[]{:S(2)}) copy-start(bf16[384,512]{1,0:T(8,128)(2,1)S(1)} %collective-permute-done.33.refs_1_) | copy-start | bytes 1179652
  135.9 51.2 %collective-permute-start.2 = (bf16[256,1024]{1,0:T(8,128)(2,1)S(1)}, bf16[256,1024]{1,0:T(8,128)(2,1)S(1)}, u32[]{:S(2)}, u32[]{:S(2)}) collective-permute-start(bf16[256,1024]{1,0:T(8,128)(2,1)S(1)} %collective-permute-done.1.refs_2_), channel_id=1, source_target_pairs={{0,4},{4,0},{8,12},{12,8},{1,5},{5,1},{9,13},{13,9},{2,6},{6,2},{1... | collective-permute-start | bytes 1572872 | tf_op jit(solution)/shard_map/ppermute | solution.py:16
  148.3 10.9 %collective-permute-start.36 = (bf16[96,512]{1,0:T(8,128)(2,1)}, bf16[96,512]{1,0:T(8,128)(2,1)S(1)}, u32[]{:S(2)}, u32[]{:S(2)}) collective-permute-start(bf16[96,512]{1,0:T(8,128)(2,1)} %get-tuple-element.66), channel_id=1, source_target_pairs={{0,1},{1,0},{2,3},{3,2},{4,5},{5,4},{6,7},{7,6},{8,9},{9,8},{10,11... | collective-permute-start | bytes 294920 | tf_op jit(solution)/shard_map/ppermute | solution.py:16
  152.5 4.8 %copy-start.7 = (bf16[384,512]{1,0:T(8,128)(2,1)}, bf16[384,512]{1,0:T(8,128)(2,1)S(1)}, u32[]{:S(2)}) copy-start(bf16[384,512]{1,0:T(8,128)(2,1)S(1)} %collective-permute-done.23.refs_1_) | copy-start | bytes 1179652
  152.5 9.2 %collective-permute-start.37 = (bf16[96,512]{1,0:T(8,128)(2,1)}, bf16[96,512]{1,0:T(8,128)(2,1)S(1)}, u32[]{:S(2)}, u32[]{:S(2)}) collective-permute-start(bf16[96,512]{1,0:T(8,128)(2,1)} %get-tuple-element.67), channel_id=1, source_target_pairs={{0,2},{1,3},{2,0},{3,1},{4,6},{5,7},{6,4},{7,5},{8,10},{9,11},{10,... | collective-permute-start | bytes 294920 | tf_op jit(solution)/shard_map/ppermute | solution.py:16
  153.5 8.2 %collective-permute-start.38 = (bf16[96,512]{1,0:T(8,128)(2,1)}, bf16[96,512]{1,0:T(8,128)(2,1)S(1)}, u32[]{:S(2)}, u32[]{:S(2)}) collective-permute-start(bf16[96,512]{1,0:T(8,128)(2,1)} %get-tuple-element.68), channel_id=1, source_target_pairs={{0,3},{1,2},{2,1},{3,0},{4,7},{5,6},{6,5},{7,4},{8,11},{9,10},{10,... | collective-permute-start | bytes 294920 | tf_op jit(solution)/shard_map/ppermute | solution.py:16
  159.3 6.7 %collective-permute-start.30 = (bf16[96,512]{1,0:T(8,128)(2,1)}, bf16[96,512]{1,0:T(8,128)(2,1)S(1)}, u32[]{:S(2)}, u32[]{:S(2)}) collective-permute-start(bf16[96,512]{1,0:T(8,128)(2,1)} %get-tuple-element.58), channel_id=1, source_target_pairs={{0,1},{1,0},{2,3},{3,2},{4,5},{5,4},{6,7},{7,6},{8,9},{9,8},{10,11... | collective-permute-start | bytes 294920 | tf_op jit(solution)/shard_map/ppermute | solution.py:16
  161.7 12.6 %collective-permute-start.31 = (bf16[96,512]{1,0:T(8,128)(2,1)}, bf16[96,512]{1,0:T(8,128)(2,1)S(1)}, u32[]{:S(2)}, u32[]{:S(2)}) collective-permute-start(bf16[96,512]{1,0:T(8,128)(2,1)} %get-tuple-element.59), channel_id=1, source_target_pairs={{0,2},{1,3},{2,0},{3,1},{4,6},{5,7},{6,4},{7,5},{8,10},{9,11},{10,... | collective-permute-start | bytes 294920 | tf_op jit(solution)/shard_map/ppermute | solution.py:16
  161.7 12.6 %collective-permute-start.32 = (bf16[96,512]{1,0:T(8,128)(2,1)}, bf16[96,512]{1,0:T(8,128)(2,1)S(1)}, u32[]{:S(2)}, u32[]{:S(2)}) collective-permute-start(bf16[96,512]{1,0:T(8,128)(2,1)} %get-tuple-element.60), channel_id=1, source_target_pairs={{0,3},{1,2},{2,1},{3,0},{4,7},{5,6},{6,5},{7,4},{8,11},{9,10},{10,... | collective-permute-start | bytes 294920 | tf_op jit(solution)/shard_map/ppermute | solution.py:16
  166.0 8.2 %copy-start.27 = (bf16[96,512]{1,0:T(8,128)(2,1)}, bf16[96,512]{1,0:T(8,128)(2,1)S(1)}, u32[]{:S(2)}) copy-start(bf16[96,512]{1,0:T(8,128)(2,1)S(1)} %collective-permute-done.30.refs_1_) | copy-start | bytes 294916
  166.0 15.5 %collective-permute-start.42 = (bf16[128,512]{1,0:T(8,128)(2,1)}, bf16[128,512]{1,0:T(8,128)(2,1)S(1)}, u32[]{:S(2)}, u32[]{:S(2)}) collective-permute-start(bf16[128,512]{1,0:T(8,128)(2,1)} %shard_map.86.refs_5_), channel_id=1, source_target_pairs={{0,2},{1,3},{2,0},{3,1},{4,6},{5,7},{6,4},{7,5},{8,10},{9,11},{10,... | collective-permute-start | bytes 393224 | tf_op jit(solution)/shard_map/ppermute | solution.py:16
  176.9 6.8 %collective-permute-start.41 = (bf16[128,512]{1,0:T(8,128)(2,1)}, bf16[128,512]{1,0:T(8,128)(2,1)S(1)}, u32[]{:S(2)}, u32[]{:S(2)}) collective-permute-start(bf16[128,512]{1,0:T(8,128)(2,1)} %shard_map.82.refs_4_), channel_id=1, source_target_pairs={{0,2},{1,3},{2,0},{3,1},{4,6},{5,7},{6,4},{7,5},{8,10},{9,11},{10,... | collective-permute-start | bytes 393224 | tf_op jit(solution)/shard_map/ppermute | solution.py:16
  179.5 7.6 %collective-permute-start.40 = (bf16[128,512]{1,0:T(8,128)(2,1)}, bf16[128,512]{1,0:T(8,128)(2,1)S(1)}, u32[]{:S(2)}, u32[]{:S(2)}) collective-permute-start(bf16[128,512]{1,0:T(8,128)(2,1)} %shard_map.86.refs_5_), channel_id=1, source_target_pairs={{0,1},{1,0},{2,3},{3,2},{4,5},{5,4},{6,7},{7,6},{8,9},{9,8},{10,11... | collective-permute-start | bytes 393224 | tf_op jit(solution)/shard_map/ppermute | solution.py:16
  179.6 14.1 %copy-start.3 = (bf16[256,1024]{1,0:T(8,128)(2,1)}, bf16[256,1024]{1,0:T(8,128)(2,1)S(1)}, u32[]{:S(2)}) copy-start(bf16[256,1024]{1,0:T(8,128)(2,1)S(1)} %collective-permute-done.refs_1_) | copy-start | bytes 1572868
  179.6 9.8 %collective-permute-start.39 = (bf16[128,512]{1,0:T(8,128)(2,1)}, bf16[128,512]{1,0:T(8,128)(2,1)S(1)}, u32[]{:S(2)}, u32[]{:S(2)}) collective-permute-start(bf16[128,512]{1,0:T(8,128)(2,1)} %shard_map.82.refs_4_), channel_id=1, source_target_pairs={{0,1},{1,0},{2,3},{3,2},{4,5},{5,4},{6,7},{7,6},{8,9},{9,8},{10,11... | collective-permute-start | bytes 393224 | tf_op jit(solution)/shard_map/ppermute | solution.py:16
  181.5 12.1 %copy-start.13 = (bf16[128,512]{1,0:T(8,128)(2,1)}, bf16[128,512]{1,0:T(8,128)(2,1)S(1)}, u32[]{:S(2)}) copy-start(bf16[128,512]{1,0:T(8,128)(2,1)S(1)} %collective-permute-done.42.refs_9_) | copy-start | bytes 393220
  181.5 10.5 %collective-permute-start.44 = (bf16[128,512]{1,0:T(8,128)(2,1)S(1)}, bf16[128,512]{1,0:T(8,128)(2,1)S(1)}, u32[]{:S(2)}, u32[]{:S(2)}) collective-permute-start(bf16[128,512]{1,0:T(8,128)(2,1)S(1)} %collective-permute-done.42.refs_9_), channel_id=1, source_target_pairs={{0,1},{1,0},{2,3},{3,2},{4,5},{5,4},{6,7},{7,6},{8,9},{9,8},{10,11... | collective-permute-start | bytes 393224 | tf_op jit(solution)/shard_map/ppermute | solution.py:16
  183.8 9.9 %copy-start.14 = (bf16[128,512]{1,0:T(8,128)(2,1)}, bf16[128,512]{1,0:T(8,128)(2,1)S(1)}, u32[]{:S(2)}) copy-start(bf16[128,512]{1,0:T(8,128)(2,1)S(1)} %collective-permute-done.41.refs_8_) | copy-start | bytes 393220
  183.8 9.9 %collective-permute-start.43 = (bf16[128,512]{1,0:T(8,128)(2,1)S(1)}, bf16[128,512]{1,0:T(8,128)(2,1)S(1)}, u32[]{:S(2)}, u32[]{:S(2)}) collective-permute-start(bf16[128,512]{1,0:T(8,128)(2,1)S(1)} %collective-permute-done.41.refs_8_), channel_id=1, source_target_pairs={{0,1},{1,0},{2,3},{3,2},{4,5},{5,4},{6,7},{7,6},{8,9},{9,8},{10,11... | collective-permute-start | bytes 393224 | tf_op jit(solution)/shard_map/ppermute | solution.py:16
  187.1 6.6 %copy-start.4 = (bf16[256,1024]{1,0:T(8,128)(2,1)}, bf16[256,1024]{1,0:T(8,128)(2,1)S(1)}, u32[]{:S(2)}) copy-start(bf16[256,1024]{1,0:T(8,128)(2,1)S(1)} %collective-permute-done.2.refs_3_) | copy-start | bytes 1572868
  187.1 6.6 %copy-start.16 = (bf16[128,512]{1,0:T(8,128)(2,1)}, bf16[128,512]{1,0:T(8,128)(2,1)S(1)}, u32[]{:S(2)}) copy-start(bf16[128,512]{1,0:T(8,128)(2,1)S(1)} %collective-permute-done.40.refs_7_) | copy-start | bytes 393220
  (18 other events, 27.6 us)

commit v2 on v1

v2 whole, which is shorter than its diff:
```python
import functools
import math

import jax
import jax.numpy as jnp
from jax import lax
from jax.experimental import pallas as pl
from jax.experimental.pallas import tpu as pltpu
from jax.sharding import PartitionSpec as P

BF16, F32, I32 = jnp.bfloat16, jnp.float32, jnp.int32


def hop(x, axis, step):
    count = lax.axis_size(axis)
    return lax.ppermute(x, axis, [(i, i ^ step) for i in range(count)])


def after(x, *earlier):
    return lax.optimization_barrier((x, *earlier))[0]


def call(kernel, me, operands, outs, scratch=(), flops=1, room=4):
    vmem = pl.BlockSpec(memory_space=pltpu.VMEM)
    def size(arrays):
        return sum(math.prod(x.shape) * jnp.dtype(x.dtype).itemsize for x in arrays)

    moved = size(operands) + size(outs)
    limit = min(56 * 2**20, moved + size(scratch) + room * 2**20)
    return pl.pallas_call(
        kernel,
        out_shape=tuple(outs),
        in_specs=[pl.BlockSpec(memory_space=pltpu.SMEM)] + [vmem] * len(operands),
        out_specs=tuple(vmem for _ in outs),
        scratch_shapes=list(scratch),
        cost_estimate=pl.CostEstimate(
            flops=flops, bytes_accessed=moved, transcendentals=0
        ),
        compiler_params=pltpu.CompilerParams(vmem_limit_bytes=limit),
    )(me, *operands)


def partial_kernel(n_rows, me_ref, tokens_ref, *refs):
    n_blocks = len(refs) - 2 - n_rows
    rows, outs, (weights, product) = refs[:n_rows], refs[n_rows:-2], refs[-2:]
    high = rows[0].shape[0]
    core, grp = me_ref[0] & 1, me_ref[1]
    for q in range(n_rows):
        place = pl.multiple_of((q // 2) * 2 * high + (core ^ (q % 2)) * high, high)
        weights[pl.ds(place, high), :] = rows[q][...]
    tile = min(256, product.shape[1])
    for start in range(0, product.shape[1], tile):
        product[:, start : start + tile] = lax.dot_general(
            tokens_ref[...], weights[start : start + tile, :], (((1,), (1,)), ((), ())), preferred_element_type=F32
        ).astype(BF16)
    block = product.shape[0] // n_blocks
    for k, out in enumerate(outs):
        out[...] = product[pl.ds(pl.multiple_of((grp ^ k) * block, block), block), :]


def one_hot(codes, height):
    at = lax.broadcasted_iota(I32, (height, codes.shape[1]), 0)
    return jnp.where(at == codes, 1.0, 0.0).astype(BF16)


def earlier(hits):
    n = hits.shape[1]
    before = lax.broadcasted_iota(I32, (n, n), 0) < lax.broadcasted_iota(I32, (n, n), 1)
    return jnp.dot(hits.astype(BF16), jnp.where(before, 1.0, 0.0).astype(BF16), preferred_element_type=F32)


def ranks_kernel(me_ref, ids_ref, out_ref):
    groups = out_ref.shape[0]
    block = out_ref.shape[2]
    ids = ids_ref[:, pl.ds(pl.multiple_of(me_ref[1] * block, block), block)] & (groups - 1)
    hits = jnp.concatenate(
        [jnp.max(jnp.where(ids == (me_ref[1] ^ k), 1.0, 0.0), axis=0, keepdims=True) for k in range(groups)], axis=0
    )
    ranks = jnp.where(hits > 0.0, earlier(hits), -1.0).astype(I32)
    for k in range(groups):
        out_ref[k] = ranks[k : k + 1, :]


def route_kernel(groups, picks, cap, me_ref, *refs):
    metas, slot_ref, weight_ref = refs[:-2], refs[-2], refs[-1]
    block = metas[0].shape[1] // groups
    lines = slot_ref.shape[2]
    hits, picked, weights = [], [], []
    expert = me_ref[0] * groups + me_ref[1]
    for meta in metas:
        for k in range(groups):
            place = pl.ds(pl.multiple_of((me_ref[1] ^ k) * block, block), block)
            ids, codes = meta[:picks, place], meta[picks:, place].astype(F32)
            mine = jnp.where(ids == expert, 1.0, 0.0)
            hits.append(jnp.max(jnp.where((ids & (groups - 1)) == me_ref[1], 1.0, 0.0), axis=0, keepdims=True))
            picked.append(jnp.max(mine, axis=0, keepdims=True))
            weights.append(
                jnp.sum(mine * codes, axis=0, keepdims=True) / jnp.sum(codes, axis=0, keepdims=True)
            )
    ranks = earlier(jnp.concatenate(hits, axis=0))
    slots = earlier(jnp.concatenate(picked, axis=0))
    for r in range(len(metas)):
        rows = range(r * groups, (r + 1) * groups)
        height = lines // groups
        line = jnp.concatenate(
            [jnp.where(hits[i] > 0.0, ranks[i : i + 1, :] + k * height, -1.0) for k, i in enumerate(rows)], axis=1
        ).astype(I32)
        slot = jnp.concatenate(
            [jnp.where(picked[i] > 0.0, slots[i : i + 1, :] + (k * cap + 1), 0.0) for k, i in enumerate(rows)], axis=1
        )
        weight = jnp.concatenate([weights[i] for i in rows], axis=1)
        at = jnp.where(lax.broadcasted_iota(I32, (lines, line.shape[1]), 0) == line, 1.0, 0.0)
        moved = lax.dot_general(
            jnp.concatenate([slot, weight], axis=0), at, (((1,), (1,)), ((), ())),
            precision=lax.Precision.HIGHEST, preferred_element_type=F32,
        )
        slot_ref[r] = moved[:1, :].astype(I32) - 1
        weight_ref[r] = moved[1:, :]


def dispatch_kernel(me_ref, ranks_ref, *refs):
    n = len(refs) // 2
    parts, outs = refs[:n], refs[n:]
    total = parts[0][...].astype(F32)
    for part in parts[1:]:
        total += part[...].astype(F32)
    latent = total.astype(BF16)
    for k, out in enumerate(outs):
        pick = one_hot(ranks_ref[k], out.shape[0])
        out[...] = jnp.dot(pick, latent, preferred_element_type=F32).astype(BF16)


def up_kernel(sources, slots, tile, me_ref, slot_ref, *refs):
    n = len(sources)
    near, far, (up_ref, hidden_ref, placed) = refs[:n], refs[n : 2 * n], refs[2 * n :]
    pair = near[0].shape[1]
    chip = me_ref[0] // 2
    for i, r in enumerate(sources):
        pick = one_hot(slot_ref[r], slots)
        for j in range(up_ref.shape[0] // pair):
            part = near[i][...] if j == 0 else far[i][:, (j - 1) * pair : j * pair]
            column = pl.multiple_of((chip ^ (r // 2) ^ j) * pair, pair)
            placed[i * slots : (i + 1) * slots, pl.ds(column, pair)] = jnp.dot(
                pick, part, preferred_element_type=F32
            ).astype(BF16)
    total = hidden_ref.shape[1]
    for start in range(0, total, tile):
        span = slice(start, min(start + tile, total))
        hidden = jnp.dot(placed[...], up_ref[:, span], preferred_element_type=F32)
        hidden_ref[:, span] = jnp.square(jnp.maximum(hidden, 0.0)).astype(BF16)


def down_kernel(sources, slots, tile, first, stride, me_ref, slot_ref, weight_ref, hidden_ref, down_ref, *refs):
    outs, picked, scaled = refs[:-2], refs[-2], refs[-1]
    picks = [one_hot(slot_ref[r], slots) for r in sources]
    scale = jnp.concatenate(
        [jnp.sum(pick.astype(F32) * weight_ref[r], axis=1, keepdims=True) for pick, r in zip(picks, sources)], axis=0
    )
    for i in range(len(sources)):
        at = (first + i * stride) * slots
        picked[i * slots : (i + 1) * slots, :] = hidden_ref[at : at + slots, :]
    for start in range(0, scaled.shape[1], tile):
        span = slice(start, start + tile)
        result = jnp.dot(picked[...], down_ref[:, span], preferred_element_type=F32)
        scaled[:, span] = (result * scale).astype(BF16)
        for i, out in enumerate(outs):
            out[:, span] = lax.dot_general(
                picks[i], scaled[i * slots : (i + 1) * slots, span], (((0,), (0,)), ((), ())), preferred_element_type=F32
            ).astype(BF16)


def add_kernel(me_ref, *refs):
    n = len(refs) // 4
    half = refs[0].shape[1] // 2
    for i in range(n):
        for h in range(2):
            span = slice(h * half, (h + 1) * half)
            refs[2 * n + 2 * i + h][...] = (
                refs[i][:, span].astype(F32) + refs[n + i][:, span].astype(F32)
            ).astype(BF16)


def join_kernel(n_in, h, me_ref, *refs):
    parts, outs = refs[:n_in], refs[n_in:]
    height, width = outs[0].shape
    for k, out in enumerate(outs):
        rows = slice(k * height, (k + 1) * height)
        total = jnp.zeros((height, width), F32)
        for part in parts:
            first = h * width if part.shape[1] > width else 0
            total += part[rows, first : first + width].astype(F32)
        out[...] = total.astype(BF16)


def combine_kernel(me_ref, ranks_ref, *refs):
    parts, out = refs[:-1], refs[-1]
    total = jnp.zeros(out.shape, F32)
    for k, part in enumerate(parts):
        pick = one_hot(ranks_ref[k], part.shape[0])
        total += lax.dot_general(pick, part[...], (((0,), (0,)), ((), ())), preferred_element_type=F32)
    out[...] = total.astype(BF16)


def rows_kernel(me_ref, *refs):
    rows, out_ref = refs[:-1], refs[-1]
    high = rows[0].shape[0]
    for q, row in enumerate(rows):
        out_ref[pl.ds(pl.multiple_of((me_ref[0] ^ q) * high, high), high), :] = row[...]


def mixed_kernel(h, me_ref, weights_ref, *refs):
    latents, out_ref, gathered = refs[: -2 - h], refs[-2], refs[-1]
    block, width = latents[0].shape
    for k, part in enumerate(latents):
        gathered[pl.ds(pl.multiple_of((me_ref[1] ^ k) * block, block), block), :] = part[...]
    tile = min(256, out_ref.shape[1])
    for start in range(0, out_ref.shape[1], tile):
        span = slice(start, start + tile)
        total = jnp.dot(
            gathered[...], weights_ref[h * width : (h + 1) * width, span], preferred_element_type=F32
        )
        if h:
            total += refs[-3][:, span]
        out_ref[:, span] = total.astype(out_ref.dtype)


def spread_ep(x):
    count = lax.axis_size("ep")
    near = [x] + [hop(x, "ep", 2 * k) for k in range(1, count // 2)]
    out = []
    for part in near:
        out += [part, hop(part, "ep", 1)]
    return out


def per_device(tokens, proj_in, proj_out, expert_up, expert_down, expert_ids, weight_codes):
    n_ep, n_grp = lax.axis_size("ep"), lax.axis_size("grp")
    ep, grp = lax.axis_index("ep"), lax.axis_index("grp")
    experts = n_ep * n_grp
    picks = expert_ids.shape[1]
    block = tokens.shape[0] // n_grp
    width, wide = expert_up.shape[1], expert_up.shape[2]
    high, depth = proj_in.shape
    hits = block * (picks // 2) // n_grp
    cap = max(2, (4 * block * picks + 3 * experts - 1) // (3 * experts))
    slots, lines = n_grp * cap, n_grp * hits
    me = jnp.stack([ep, grp]).astype(I32)
    shape = jax.ShapeDtypeStruct

    ids = expert_ids.T
    meta_own = jnp.concatenate([ids, weight_codes.T], axis=0)
    [ranks] = call(ranks_kernel, me, [ids], [shape((n_grp, 1, block), I32)])

    steps = range(1, n_ep // 2)
    rows_near = [proj_in, hop(proj_in, "ep", 1)]
    rows_far = [hop(proj_in, "ep", 2 * k) for k in steps]

    def partial(rows):
        columns = high * len(rows)
        return call(
            functools.partial(partial_kernel, len(rows)),
            me,
            [tokens, *rows],
            [shape((block, columns), BF16)] * n_grp,
            [pltpu.VMEM((columns, depth), BF16), pltpu.VMEM((tokens.shape[0], columns), BF16)],
            flops=2 * tokens.shape[0] * columns * depth,
        )

    def swap(cut):
        return [cut[0]] + [hop(cut[k], "grp", k) for k in range(1, n_grp)]

    def choose(ranks, arrived):
        columns = arrived[0].shape[1]
        return call(dispatch_kernel, me, [ranks, *arrived], [shape((hits, columns), BF16)] * n_grp)

    cut_near = partial(rows_near)
    meta_own = after(meta_own, cut_near[0])
    arrived_near = swap(cut_near)
    rows_far = [after(part, *arrived_near) for part in rows_far]
    metas = [meta_own, hop(meta_own, "ep", 1)]
    for k in steps:
        part = after(hop(meta_own, "ep", 2 * k), *arrived_near)
        metas += [part, hop(part, "ep", 1)]
    crossed_out = [hop(after(proj_out, *rows_far), "ep", 2 * k) for k in steps]
    cut_far = partial([x for part in rows_far for x in (part, hop(part, "ep", 1))])
    chosen_near = choose(after(ranks, cut_far[0]), arrived_near)
    arrived_far, near_own = swap(cut_far), jnp.concatenate(swap(chosen_near), axis=0)
    near = [near_own, hop(near_own, "ep", 1)]
    crossed_near = [hop(near_own, "ep", 2 * k) for k in steps]
    line_slot, line_weight = call(
        functools.partial(route_kernel, n_grp, picks, cap),
        after(me, chosen_near[0]),
        metas,
        [shape((n_ep, 1, lines), I32), shape((n_ep, 1, lines), F32)],
        room=3 * n_ep,
    )
    chosen_far = choose(after(ranks, near_own, line_slot, *crossed_out), arrived_far)
    far_own = jnp.concatenate(swap(chosen_far), axis=0)
    crossed_side = [hop(part, "ep", 1) for part in crossed_near]
    far = [far_own, hop(far_own, "ep", 1)]
    crossed_far = [hop(far_own, "ep", 2 * k) for k in steps]

    def up(sources, *deps):
        n = len(sources) * slots
        return call(
            functools.partial(up_kernel, sources, slots, 512),
            me,
            [after(line_slot, *deps), *[near[r] for r in sources], *[far[r] for r in sources], expert_up[0]],
            [shape((n, wide), BF16)],
            [pltpu.VMEM((n, width), BF16)],
            flops=2 * n * width * wide,
        )[0]

    def down(sources, hidden, first, stride, *deps, hides=1):
        n = len(sources) * slots
        return call(
            functools.partial(down_kernel, sources, slots, width // 2, first, stride),
            me,
            [after(line_slot, *deps), line_weight, hidden, expert_down[0]],
            [shape((lines, width), BF16)] * len(sources),
            [pltpu.VMEM((n, wide), BF16), pltpu.VMEM((n, width), BF16)],
            flops=hides * 2 * n * width * wide,
        )

    here, there = list(range(2)), list(range(2, n_ep))
    hidden_here = up(here, *crossed_side)
    local = down(here, hidden_here, 0, 1)
    crossed_far = [after(part, *local) for part in crossed_far]
    local = [local[0], hop(local[1], "ep", 1)]
    for k in steps:
        near += [crossed_near[k - 1], crossed_side[k - 1]]
        far += [crossed_far[k - 1], hop(crossed_far[k - 1], "ep", 1)]
    hidden_there = up(there)
    rows_out = [proj_out, hop(proj_out, "ep", 1)]
    for part in crossed_out:
        rows_out += [part, hop(part, "ep", 1)]
    odd = down(there[1::2], hidden_there, 1, 2)
    other = [hop(part, "ep", 1) for part in odd]
    even = down(there[::2], hidden_there, 0, 2, *odd)
    sums = call(add_kernel, me, [*even, *other], [shape((lines, width // 2), BF16)] * (2 * len(even)))
    half = width // 2
    returned = [[hop(sums[2 * k + h], "ep", 2 * k + 2) for k in range(len(even))] for h in range(2)]
    [rows_out] = call(rows_kernel, me, rows_out, [shape((width, depth), BF16)])

    def join(h, arrived):
        parts = [*local, *returned[h]]
        kernel = functools.partial(join_kernel, len(parts), h)
        return call(kernel, after(me, *arrived), parts, [shape((hits, half), BF16)] * n_grp)

    def combine(arrived):
        return call(combine_kernel, me, [ranks, *arrived], [shape((block, half), BF16)])[0]

    def gather(latent_out):
        blocks = [latent_out]
        for k in range(1, n_grp):
            low = k & -k
            blocks.append(hop(blocks[k ^ low], "grp", low))
        return blocks

    def mix(h, blocks, total):
        return call(
            functools.partial(mixed_kernel, h),
            me,
            [rows_out, *blocks, *total],
            [shape((tokens.shape[0], depth), BF16 if h else F32)],
            [pltpu.VMEM((tokens.shape[0], half), BF16)],
            flops=2 * tokens.shape[0] * half * depth,
        )

    arrived = swap(join(0, ()))
    latent_out = combine(arrived)
    cut = join(1, (latent_out,))
    total = mix(0, gather(latent_out), ())
    return mix(1, gather(combine(swap(cut))), total)[0]


def solution(mesh):
    in_specs = (
        P(("rep", "ep"), "grp"),
        P("ep", "grp"),
        P("ep", "grp"),
        P(("ep", "grp"), None, None),
        P(("ep", "grp"), None, None),
        P(("rep", "ep"), None),
        P(("rep", "ep"), None),
    )
    out_specs = P(("rep", "ep"), "grp")
    return jax.shard_map(
        per_device, mesh=mesh, in_specs=in_specs, out_specs=out_specs, check_vma=False
    )
```

time: 200 us -> 158 us (0.79)
  Pallas kernels: 67.4 us -> 35.4 us
  starting transfers between devices: 54.8 us -> 51.1 us
  other arithmetic: 3.56 us -> 0.82 us
  local copies, waits for them, and re-layouts: 9.39 us -> 6.86 us
    pallas_call x15 -> x19, Pallas kernels: 67.4 us -> 35.4 us  [call(): pl.pallas_call(kernel, out_shape=tuple(outs), in_specs=[pl.BlockSpec(memo...]
    ppermute x45 -> x43, starting transfers between devices: 54.8 us -> 51.1 us  [hop(): return lax.ppermute(x, axis, [(i, i ^ step) for i in range(count)])]
    unnamed x83 -> x26, local copies, waits for them, and re-layouts: 7.82 us -> 6.84 us
    ppermute x45 -> x43, waiting for transfers between devices: 62.6 us -> 62.8 us  [hop(): return lax.ppermute(x, axis, [(i, i ^ step) for i in range(count)])]
  transfers between devices with their start and end apart: 45 -> 43, of which waited for: 17 -> 20; matrix products, arithmetic and copies ran while one was open for 4% -> 1% of each run, Pallas kernels for 31% -> 16%
where the time goes in v2:
time: 158 us; the launch traced here: 157 us
  waiting for transfers between devices  62.8 us (40%)
  starting transfers between devices  51.1 us (32%)
  Pallas kernels  35.4 us (22%)
  local copies, waits for them, and re-layouts  6.86 us (4%)
    ppermute x43, waiting for transfers between devices, hop(): return lax.ppermute(x, axis, [(i, i ^ step) for i in range(count)])  62.8 us
    ppermute x43, starting transfers between devices, hop(): return lax.ppermute(x, axis, [(i, i ^ step) for i in range(count)])  51.1 us
    pallas_call x19, Pallas kernels, call(): pl.pallas_call(kernel, out_shape=tuple(outs), in_specs=[pl.BlockSpec(memo...  35.4 us
    unnamed x26, local copies, waits for them, and re-layouts  6.84 us
  transfers between devices with their start and end apart: 43, of which 20 were waited for; matrix products, arithmetic and copies ran while one was open for 1% of the time, Pallas kernels for 16%

profile of v2, /device:TPU:0, one launch (start us, length us, event | category | flops | bytes accessed | tf_op | source)
XLA Modules:
  0.0 157.3 jit_solution(4070404984143888093)
XLA Ops:
  0.5 2.5 %collective-permute-start.1 = (bf16[256,1024]{1,0:T(8,128)(2,1)}, bf16[256,1024]{1,0:T(8,128)(2,1)S(1)}, u32[]{:S(2)}, u32[]{:S(2)}) collective-permute-start(bf16[256,1024]{1,0:T(8,128)(2,1)} %refs_0_.2), channel_id=1, source_target_pairs={{0,8},{4,12},{8,0},{12,4},{1,9},{5,13},{9,1},{13,5},{2,10},{6,14},... | collective-permute-start | bytes 1572872 | tf_op jit(solution)/shard_map/ppermute | solution.py:16
  3.1 1.2 copy-done
  4.3 1.0 copy-done.2
  5.3 1.4 shard_map.73
  6.7 2.2 %collective-permute-start.3 = (bf16[128,512]{1,0:T(8,128)(2,1)S(1)}, bf16[128,512]{1,0:T(8,128)(2,1)S(1)}, u32[]{:S(2)}, u32[]{:S(2)}) collective-permute-start(bf16[128,512]{1,0:T(8,128)(2,1)S(1)} %get-tuple-element.47), channel_id=1, source_target_pairs={{0,1},{1,0},{2,3},{3,2},{4,5},{5,4},{6,7},{7,6},{8,9},{9,8},{10,11... | collective-permute-start | bytes 393224 | tf_op jit(solution)/shard_map/ppermute | solution.py:16
  8.9 2.6 %collective-permute-start.4 = (bf16[128,512]{1,0:T(8,128)(2,1)S(1)}, bf16[128,512]{1,0:T(8,128)(2,1)S(1)}, u32[]{:S(2)}, u32[]{:S(2)}) collective-permute-start(bf16[128,512]{1,0:T(8,128)(2,1)S(1)} %get-tuple-element.48), channel_id=1, source_target_pairs={{0,2},{1,3},{2,0},{3,1},{4,6},{5,7},{6,4},{7,5},{8,10},{9,11},{10,... | collective-permute-start | bytes 393224 | tf_op jit(solution)/shard_map/ppermute | solution.py:16
  11.5 4.3 %collective-permute-done.1.refs_0_ = bf16[256,1024]{1,0:T(8,128)(2,1)S(1)} collective-permute-done((bf16[256,1024]{1,0:T(8,128)(2,1)}, bf16[256,1024]{1,0:T(8,128)(2,1)S(1)}, u32[]{:S(2)}, u32[]{:S(2)}) %collective-permute-start.1) | collective-permute-done | bytes 524320 | tf_op jit(solution)/shard_map/ppermute | solution.py:16
  15.8 6.0 %collective-permute-done.4.refs_2_ = bf16[128,512]{1,0:T(8,128)(2,1)S(1)} collective-permute-done((bf16[128,512]{1,0:T(8,128)(2,1)S(1)}, bf16[128,512]{1,0:T(8,128)(2,1)S(1)}, u32[]{:S(2)}, u32[]{:S(2)}) %collective-permute-start.4) | collective-permute-done | bytes 131104 | tf_op jit(solution)/shard_map/ppermute | solution.py:16
  21.8 0.7 pad_add_fusion.refs_0_
  22.5 1.6 %collective-permute-start.10 = (s32[12,512]{1,0:T(8,128)S(1)}, s32[12,512]{1,0:T(8,128)S(1)}, u32[]{:S(2)}, u32[]{:S(2)}) collective-permute-start(s32[12,512]{1,0:T(8,128)S(1)} %pad_add_fusion.refs_0_), channel_id=1, source_target_pairs={{0,8},{4,12},{8,0},{12,4},{1,9},{5,13},{9,1},{13,5},{2,10},{6,14},... | collective-permute-start | bytes 73736 | tf_op jit(solution)/shard_map/ppermute | solution.py:16
  24.1 0.7 copy-done.4
  25.7 0.8 collective-permute-done.10.refs_2_
  26.5 1.5 collective-permute-start.6
  28.1 1.2 copy-done.1
  29.3 1.4 shard_map.76
  30.7 0.8 shard_map.77
  31.5 2.3 %collective-permute-start.12 = (bf16[96,512]{1,0:T(8,128)(2,1)S(1)}, bf16[96,512]{1,0:T(8,128)(2,1)S(1)}, u32[]{:S(2)}, u32[]{:S(2)}) collective-permute-start(bf16[96,512]{1,0:T(8,128)(2,1)S(1)} %get-tuple-element.60), channel_id=1, source_target_pairs={{0,1},{1,0},{2,3},{3,2},{4,5},{5,4},{6,7},{7,6},{8,9},{9,8},{10,11... | collective-permute-start | bytes 294920 | tf_op jit(solution)/shard_map/ppermute | solution.py:16
  33.9 1.1 collective-permute-start.13
  35.0 2.1 %collective-permute-done.12 = bf16[96,512]{1,0:T(8,128)(2,1)S(1)} collective-permute-done((bf16[96,512]{1,0:T(8,128)(2,1)S(1)}, bf16[96,512]{1,0:T(8,128)(2,1)S(1)}, u32[]{:S(2)}, u32[]{:S(2)}) %collective-permute-start.12) | collective-permute-done | bytes 98336 | tf_op jit(solution)/shard_map/ppermute | solution.py:16
  37.1 2.5 %collective-permute-start.14 = (bf16[96,512]{1,0:T(8,128)(2,1)S(1)}, bf16[96,512]{1,0:T(8,128)(2,1)S(1)}, u32[]{:S(2)}, u32[]{:S(2)}) collective-permute-start(bf16[96,512]{1,0:T(8,128)(2,1)S(1)} %get-tuple-element.62), channel_id=1, source_target_pairs={{0,3},{1,2},{2,1},{3,0},{4,7},{5,6},{6,5},{7,4},{8,11},{9,10},{10,... | collective-permute-start | bytes 294920 | tf_op jit(solution)/shard_map/ppermute | solution.py:16
  39.5 4.2 %collective-permute-done.13 = bf16[96,512]{1,0:T(8,128)(2,1)S(1)} collective-permute-done((bf16[96,512]{1,0:T(8,128)(2,1)S(1)}, bf16[96,512]{1,0:T(8,128)(2,1)S(1)}, u32[]{:S(2)}, u32[]{:S(2)}) %collective-permute-start.13) | collective-permute-done | bytes 98336 | tf_op jit(solution)/shard_map/ppermute | solution.py:16
  43.8 3.5 %collective-permute-start.19 = (bf16[128,512]{1,0:T(8,128)(2,1)S(1)}, bf16[128,512]{1,0:T(8,128)(2,1)S(1)}, u32[]{:S(2)}, u32[]{:S(2)}) collective-permute-start(bf16[128,512]{1,0:T(8,128)(2,1)S(1)} %get-tuple-element.66), channel_id=1, source_target_pairs={{0,2},{1,3},{2,0},{3,1},{4,6},{5,7},{6,4},{7,5},{8,10},{9,11},{10,... | collective-permute-start | bytes 393224 | tf_op jit(solution)/shard_map/ppermute | solution.py:16
  47.3 0.9 collective-permute-start.20
  48.8 3.5 %shard_map.78 = (s32[4,1,384]{2,1,0:T(1,128)S(1)}, f32[4,1,384]{2,1,0:T(1,128)S(1)}) custom-call(s32[2]{0:T(128)S(1)} %pad_add_fusion.1.me_ref, s32[12,512]{1,0:T(8,128)S(1)} %pad_add_fusion.refs_0_, s32[12,512]{1,0:T(8,128)S(1)} %collective-permute-done.9.refs_1_, s32[12,512]{1,0:T(8,128)S(1)} %collective-permute-done.10.refs_2_, ...), custom_call_target="tpu_custom_call" | custom-call | flops 1 | bytes 110592 | tf_op jit(solution)/shard_map/pallas_call | solution.py:30
  52.4 3.0 %collective-permute-done.19.refs_2_ = bf16[128,512]{1,0:T(8,128)(2,1)S(1)} collective-permute-done((bf16[128,512]{1,0:T(8,128)(2,1)S(1)}, bf16[128,512]{1,0:T(8,128)(2,1)S(1)}, u32[]{:S(2)}, u32[]{:S(2)}) %collective-permute-start.19) | collective-permute-done | bytes 131104 | tf_op jit(solution)/shard_map/ppermute | solution.py:16
  55.4 0.8 shard_map.79
  56.3 2.2 %collective-permute-start.21 = (bf16[96,512]{1,0:T(8,128)(2,1)S(1)}, bf16[96,512]{1,0:T(8,128)(2,1)S(1)}, u32[]{:S(2)}, u32[]{:S(2)}) collective-permute-start(bf16[96,512]{1,0:T(8,128)(2,1)S(1)} %get-tuple-element.69), channel_id=1, source_target_pairs={{0,1},{1,0},{2,3},{3,2},{4,5},{5,4},{6,7},{7,6},{8,9},{9,8},{10,11... | collective-permute-start | bytes 294920 | tf_op jit(solution)/shard_map/ppermute | solution.py:16
  58.5 1.1 collective-permute-start.22
  59.6 1.4 collective-permute-start.23
  61.0 1.1 collective-permute-done.21
  62.1 5.9 %collective-permute-done.22 = bf16[96,512]{1,0:T(8,128)(2,1)S(1)} collective-permute-done((bf16[96,512]{1,0:T(8,128)(2,1)S(1)}, bf16[96,512]{1,0:T(8,128)(2,1)S(1)}, u32[]{:S(2)}, u32[]{:S(2)}) %collective-permute-start.22) | collective-permute-done | bytes 98336 | tf_op jit(solution)/shard_map/ppermute | solution.py:16
  70.4 2.6 %copy-done.5 = bf16[1,1024,2688]{2,1,0:T(8,128)(2,1)S(1)} copy-done((bf16[1,1024,2688]{2,1,0:T(8,128)(2,1)S(1)}, bf16[1,1024,2688]{2,1,0:T(8,128)(2,1)}, u32[]{:S(2)}) %copy-start.5) | copy-done | bytes 5505048
  72.9 4.4 %shard_map.80.hidden_ref = bf16[512,2688]{1,0:T(8,128)(2,1)S(1)} custom-call(s32[2]{0:T(128)S(1)} %pad_add_fusion.1.me_ref, s32[4,1,384]{2,1,0:T(1,128)S(1)} %get-tuple-element.75.slot_ref, bf16[384,512]{1,0:T(8,128)(2,1)S(1)} %constant_dynamic-update-slice_fusion.refs_0_, bf16[384,512]{1,0:T(8,128)(2,1)S(1)} %collective-permute-done.17.refs_1_, ...), custom_call_target="tpu_custom_call" | custom-call | flops 2818572288 | bytes 9836544 | tf_op jit(solution)/shard_map/pallas_call | solution.py:30
  77.4 4.3 %shard_map.81 = (bf16[384,1024]{1,0:T(8,128)(2,1)S(1)}, bf16[384,1024]{1,0:T(8,128)(2,1)S(1)}) custom-call(s32[2]{0:T(128)S(1)} %pad_add_fusion.1.me_ref, s32[4,1,384]{2,1,0:T(1,128)S(1)} %get-tuple-element.75.slot_ref, f32[4,1,384]{2,1,0:T(1,128)S(1)} %get-tuple-element.59.weight_ref, bf16[512,2688]{1,0:T(8,128)(2,1)S(1)} %shard_map.80.hidden_ref, ...), custom_call_target="tpu_custom_call" | custom-call | flops 2818572288 | bytes 9842688 | tf_op jit(solution)/shard_map/pallas_call | solution.py:30
  82.0 1.6 %collective-permute-done.27.refs_3_ = bf16[384,512]{1,0:T(8,128)(2,1)S(1)} collective-permute-done((bf16[384,512]{1,0:T(8,128)(2,1)S(1)}, bf16[384,512]{1,0:T(8,128)(2,1)S(1)}, u32[]{:S(2)}, u32[]{:S(2)}) %collective-permute-start.27) | collective-permute-done | bytes 393248 | tf_op jit(solution)/shard_map/ppermute | solution.py:16
  83.5 4.6 %shard_map.82.hidden_ref = bf16[512,2688]{1,0:T(8,128)(2,1)S(1)} custom-call(s32[2]{0:T(128)S(1)} %pad_add_fusion.1.me_ref, s32[4,1,384]{2,1,0:T(1,128)S(1)} %get-tuple-element.75.slot_ref, bf16[384,512]{1,0:T(8,128)(2,1)S(1)} %collective-permute-done.15.refs_0_, bf16[384,512]{1,0:T(8,128)(2,1)S(1)} %collective-permute-done.16.refs_1_, ...), custom_call_target="tpu_custom_call" | custom-call | flops 2818572288 | bytes 9836544 | tf_op jit(solution)/shard_map/pallas_call | solution.py:30
  88.2 2.7 %shard_map.83 = bf16[384,1024]{1,0:T(8,128)(2,1)S(1)} custom-call(s32[2]{0:T(128)S(1)} %pad_add_fusion.1.me_ref, s32[4,1,384]{2,1,0:T(1,128)S(1)} %get-tuple-element.75.slot_ref, f32[4,1,384]{2,1,0:T(1,128)S(1)} %get-tuple-element.59.weight_ref, bf16[512,2688]{1,0:T(8,128)(2,1)S(1)} %shard_map.82.hidden_ref, bf16[2688,1024]{1,0:T(8,128)(2,1)S(1)} %bitcast.9), custom_call_target="tpu_custom_call" | custom-call | flops 1409286144 | bytes 9056256 | tf_op jit(solution)/shard_map/pallas_call | solution.py:30
  91.4 2.7 %shard_map.84.refs_0_ = bf16[384,1024]{1,0:T(8,128)(2,1)S(1)} custom-call(s32[2]{0:T(128)S(1)} %pad_add_fusion.1.me_ref, s32[4,1,384]{2,1,0:T(1,128)S(1)} %get-tuple-element.75.slot_ref, f32[4,1,384]{2,1,0:T(1,128)S(1)} %get-tuple-element.59.weight_ref, bf16[512,2688]{1,0:T(8,128)(2,1)S(1)} %shard_map.82.hidden_ref, bf16[2688,1024]{1,0:T(8,128)(2,1)S(1)} %bitcast.10), custom_call_target="tpu_custom_call" | custom-call | flops 1409286144 | bytes 9056256 | tf_op jit(solution)/shard_map/pallas_call | solution.py:30
  94.1 0.7 shard_map.85
  95.4 1.5 collective-permute-start.33
  96.9 9.9 %collective-permute-done.29.refs_2_ = bf16[384,512]{1,0:T(8,128)(2,1)S(1)} collective-permute-done((bf16[384,512]{1,0:T(8,128)(2,1)S(1)}, bf16[384,512]{1,0:T(8,128)(2,1)S(1)}, u32[]{:S(2)}, u32[]{:S(2)}) %collective-permute-start.29) | collective-permute-done | bytes 393248 | tf_op jit(solution)/shard_map/ppermute | solution.py:16
  107.5 1.1 collective-permute-start.30
  108.7 1.6 collective-permute-start.31
  110.2 2.0 %collective-permute-done.30.refs_1_ = bf16[96,512]{1,0:T(8,128)(2,1)S(1)} collective-permute-done((bf16[96,512]{1,0:T(8,128)(2,1)S(1)}, bf16[96,512]{1,0:T(8,128)(2,1)S(1)}, u32[]{:S(2)}, u32[]{:S(2)}) %collective-permute-start.30) | collective-permute-done | bytes 98336 | tf_op jit(solution)/shard_map/ppermute | solution.py:16
  112.2 2.1 %collective-permute-start.32 = (bf16[96,512]{1,0:T(8,128)(2,1)S(1)}, bf16[96,512]{1,0:T(8,128)(2,1)S(1)}, u32[]{:S(2)}, u32[]{:S(2)}) collective-permute-start(bf16[96,512]{1,0:T(8,128)(2,1)S(1)} %get-tuple-element.80), channel_id=1, source_target_pairs={{0,3},{1,2},{2,1},{3,0},{4,7},{5,6},{6,5},{7,4},{8,11},{9,10},{10,... | collective-permute-start | bytes 294920 | tf_op jit(solution)/shard_map/ppermute | solution.py:16
  114.3 5.1 %collective-permute-done.31.refs_2_ = bf16[96,512]{1,0:T(8,128)(2,1)S(1)} collective-permute-done((bf16[96,512]{1,0:T(8,128)(2,1)S(1)}, bf16[96,512]{1,0:T(8,128)(2,1)S(1)}, u32[]{:S(2)}, u32[]{:S(2)}) %collective-permute-start.31) | collective-permute-done | bytes 98336 | tf_op jit(solution)/shard_map/ppermute | solution.py:16
  119.4 0.9 shard_map.87.refs_0_
  120.2 0.7 shard_map.88
  120.9 2.4 %collective-permute-start.34 = (bf16[96,512]{1,0:T(8,128)(2,1)S(1)}, bf16[96,512]{1,0:T(8,128)(2,1)S(1)}, u32[]{:S(2)}, u32[]{:S(2)}) collective-permute-start(bf16[96,512]{1,0:T(8,128)(2,1)S(1)} %get-tuple-element.84), channel_id=1, source_target_pairs={{0,1},{1,0},{2,3},{3,2},{4,5},{5,4},{6,7},{7,6},{8,9},{9,8},{10,11... | collective-permute-start | bytes 294920 | tf_op jit(solution)/shard_map/ppermute | solution.py:16
  123.3 0.9 collective-permute-start.35
  124.2 1.6 collective-permute-start.36
  125.7 0.8 collective-permute-done.34.refs_1_
  126.5 3.3 %collective-permute-start.41 = (bf16[128,512]{1,0:T(8,128)(2,1)S(1)}, bf16[128,512]{1,0:T(8,128)(2,1)S(1)}, u32[]{:S(2)}, u32[]{:S(2)}) collective-permute-start(bf16[128,512]{1,0:T(8,128)(2,1)S(1)} %shard_map.87.refs_0_), channel_id=1, source_target_pairs={{0,2},{1,3},{2,0},{3,1},{4,6},{5,7},{6,4},{7,5},{8,10},{9,11},{10,... | collective-permute-start | bytes 393224 | tf_op jit(solution)/shard_map/ppermute | solution.py:16
  129.8 6.7 %collective-permute-done.35.refs_2_ = bf16[96,512]{1,0:T(8,128)(2,1)S(1)} collective-permute-done((bf16[96,512]{1,0:T(8,128)(2,1)S(1)}, bf16[96,512]{1,0:T(8,128)(2,1)S(1)}, u32[]{:S(2)}, u32[]{:S(2)}) %collective-permute-start.35) | collective-permute-done | bytes 98336 | tf_op jit(solution)/shard_map/ppermute | solution.py:16
  136.5 0.9 shard_map.89.refs_0_
  137.3 3.1 %collective-permute-start.38 = (bf16[128,512]{1,0:T(8,128)(2,1)S(1)}, bf16[128,512]{1,0:T(8,128)(2,1)S(1)}, u32[]{:S(2)}, u32[]{:S(2)}) collective-permute-start(bf16[128,512]{1,0:T(8,128)(2,1)S(1)} %shard_map.89.refs_0_), channel_id=1, source_target_pairs={{0,2},{1,3},{2,0},{3,1},{4,6},{5,7},{6,4},{7,5},{8,10},{9,11},{10,... | collective-permute-start | bytes 393224 | tf_op jit(solution)/shard_map/ppermute | solution.py:16
  140.5 2.0 %collective-permute-start.42 = (bf16[128,512]{1,0:T(8,128)(2,1)S(1)}, bf16[128,512]{1,0:T(8,128)(2,1)S(1)}, u32[]{:S(2)}, u32[]{:S(2)}) collective-permute-start(bf16[128,512]{1,0:T(8,128)(2,1)S(1)} %collective-permute-done.41.refs_2_), channel_id=1, source_target_pairs={{0,1},{1,0},{2,3},{3,2},{4,5},{5,4},{6,7},{7,6},{8,9},{9,8},{10,11... | collective-permute-start | bytes 393224 | tf_op jit(solution)/shard_map/ppermute | solution.py:16
  142.6 2.5 %collective-permute-done.38.refs_2_ = bf16[128,512]{1,0:T(8,128)(2,1)S(1)} collective-permute-done((bf16[128,512]{1,0:T(8,128)(2,1)S(1)}, bf16[128,512]{1,0:T(8,128)(2,1)S(1)}, u32[]{:S(2)}, u32[]{:S(2)}) %collective-permute-start.38) | collective-permute-done | bytes 131104 | tf_op jit(solution)/shard_map/ppermute | solution.py:16
  145.0 2.4 %collective-permute-start.39 = (bf16[128,512]{1,0:T(8,128)(2,1)S(1)}, bf16[128,512]{1,0:T(8,128)(2,1)S(1)}, u32[]{:S(2)}, u32[]{:S(2)}) collective-permute-start(bf16[128,512]{1,0:T(8,128)(2,1)S(1)} %collective-permute-done.38.refs_2_), channel_id=1, source_target_pairs={{0,1},{1,0},{2,3},{3,2},{4,5},{5,4},{6,7},{7,6},{8,9},{9,8},{10,11... | collective-permute-start | bytes 393224 | tf_op jit(solution)/shard_map/ppermute | solution.py:16
  148.1 2.2 %collective-permute-done.42.refs_3_ = bf16[128,512]{1,0:T(8,128)(2,1)S(1)} collective-permute-done((bf16[128,512]{1,0:T(8,128)(2,1)S(1)}, bf16[128,512]{1,0:T(8,128)(2,1)S(1)}, u32[]{:S(2)}, u32[]{:S(2)}) %collective-permute-start.42) | collective-permute-done | bytes 131104 | tf_op jit(solution)/shard_map/ppermute | solution.py:16
  150.3 1.3 shard_map.90.refs_4_
  151.5 1.5 collective-permute-done.37.refs_1_
  153.1 2.0 %collective-permute-done.39.refs_3_ = bf16[128,512]{1,0:T(8,128)(2,1)S(1)} collective-permute-done((bf16[128,512]{1,0:T(8,128)(2,1)S(1)}, bf16[128,512]{1,0:T(8,128)(2,1)S(1)}, u32[]{:S(2)}, u32[]{:S(2)}) %collective-permute-start.39) | collective-permute-done | bytes 131104 | tf_op jit(solution)/shard_map/ppermute | solution.py:16
  155.1 2.3 %shard_map.91 = bf16[512,1024]{1,0:T(8,128)(2,1)} custom-call(s32[2]{0:T(128)S(1)} %pad_add_fusion.1.me_ref, bf16[1024,1024]{1,0:T(8,128)(2,1)S(1)} %shard_map.74.weights_ref, bf16[128,512]{1,0:T(8,128)(2,1)S(1)} %shard_map.89.refs_0_, bf16[128,512]{1,0:T(8,128)(2,1)S(1)} %collective-permute-done.37.refs_1_, ...), custom_call_target="tpu_custom_call" | custom-call | flops 536870912 | bytes 5767168 | tf_op jit(solution)/shard_map/pallas_call | solution.py:30
  (73 shorter events, 7.4 us)
Async XLA Ops:
  0.0 3.0 %collective-permute-start.2 = (bf16[256,1024]{1,0:T(8,128)(2,1)}, bf16[256,1024]{1,0:T(8,128)(2,1)S(1)}, u32[]{:S(2)}, u32[]{:S(2)}) collective-permute-start(bf16[256,1024]{1,0:T(8,128)(2,1)} %refs_0_.2), channel_id=1, source_target_pairs={{0,4},{4,0},{8,12},{12,8},{1,5},{5,1},{9,13},{13,9},{2,6},{6,2},{1... | collective-permute-start | bytes 1572872 | tf_op jit(solution)/shard_map/ppermute | solution.py:16
  0.5 15.3 %collective-permute-start.1 = (bf16[256,1024]{1,0:T(8,128)(2,1)}, bf16[256,1024]{1,0:T(8,128)(2,1)S(1)}, u32[]{:S(2)}, u32[]{:S(2)}) collective-permute-start(bf16[256,1024]{1,0:T(8,128)(2,1)} %refs_0_.2), channel_id=1, source_target_pairs={{0,8},{4,12},{8,0},{12,4},{1,9},{5,13},{9,1},{13,5},{2,10},{6,14},... | collective-permute-start | bytes 1572872 | tf_op jit(solution)/shard_map/ppermute | solution.py:16
  3.0 1.2 copy-start
  4.3 1.0 copy-start.2
  6.7 9.1 %collective-permute-start.3 = (bf16[128,512]{1,0:T(8,128)(2,1)S(1)}, bf16[128,512]{1,0:T(8,128)(2,1)S(1)}, u32[]{:S(2)}, u32[]{:S(2)}) collective-permute-start(bf16[128,512]{1,0:T(8,128)(2,1)S(1)} %get-tuple-element.47), channel_id=1, source_target_pairs={{0,1},{1,0},{2,3},{3,2},{4,5},{5,4},{6,7},{7,6},{8,9},{9,8},{10,11... | collective-permute-start | bytes 393224 | tf_op jit(solution)/shard_map/ppermute | solution.py:16
  8.9 12.9 %collective-permute-start.4 = (bf16[128,512]{1,0:T(8,128)(2,1)S(1)}, bf16[128,512]{1,0:T(8,128)(2,1)S(1)}, u32[]{:S(2)}, u32[]{:S(2)}) collective-permute-start(bf16[128,512]{1,0:T(8,128)(2,1)S(1)} %get-tuple-element.48), channel_id=1, source_target_pairs={{0,2},{1,3},{2,0},{3,1},{4,6},{5,7},{6,4},{7,5},{8,10},{9,11},{10,... | collective-permute-start | bytes 393224 | tf_op jit(solution)/shard_map/ppermute | solution.py:16
  11.5 10.3 %collective-permute-start.5 = (bf16[128,512]{1,0:T(8,128)(2,1)S(1)}, bf16[128,512]{1,0:T(8,128)(2,1)S(1)}, u32[]{:S(2)}, u32[]{:S(2)}) collective-permute-start(bf16[128,512]{1,0:T(8,128)(2,1)S(1)} %get-tuple-element.49), channel_id=1, source_target_pairs={{0,3},{1,2},{2,1},{3,0},{4,7},{5,6},{6,5},{7,4},{8,11},{9,10},{10,... | collective-permute-start | bytes 393224 | tf_op jit(solution)/shard_map/ppermute | solution.py:16
  21.8 6.3 %collective-permute-start.8 = (bf16[256,1024]{1,0:T(8,128)(2,1)S(1)}, bf16[256,1024]{1,0:T(8,128)(2,1)S(1)}, u32[]{:S(2)}, u32[]{:S(2)}) collective-permute-start(bf16[256,1024]{1,0:T(8,128)(2,1)S(1)} %collective-permute-done.1.refs_0_), channel_id=1, source_target_pairs={{0,4},{4,0},{8,12},{12,8},{1,5},{5,1},{9,13},{13,9},{2,6},{6,2},{1... | collective-permute-start | bytes 1572872 | tf_op jit(solution)/shard_map/ppermute | solution.py:16
  22.5 4.0 %collective-permute-start.10 = (s32[12,512]{1,0:T(8,128)S(1)}, s32[12,512]{1,0:T(8,128)S(1)}, u32[]{:S(2)}, u32[]{:S(2)}) collective-permute-start(s32[12,512]{1,0:T(8,128)S(1)} %pad_add_fusion.refs_0_), channel_id=1, source_target_pairs={{0,8},{4,12},{8,0},{12,4},{1,9},{5,13},{9,1},{13,5},{2,10},{6,14},... | collective-permute-start | bytes 73736 | tf_op jit(solution)/shard_map/ppermute | solution.py:16
  24.1 0.7 copy-start.4
  25.5 18.2 %collective-permute-start.9 = (s32[12,512]{1,0:T(8,128)S(1)}, s32[12,512]{1,0:T(8,128)S(1)}, u32[]{:S(2)}, u32[]{:S(2)}) collective-permute-start(s32[12,512]{1,0:T(8,128)S(1)} %pad_add_fusion.refs_0_), channel_id=1, source_target_pairs={{0,4},{4,0},{8,12},{12,8},{1,5},{5,1},{9,13},{13,9},{2,6},{6,2},{1... | collective-permute-start | bytes 73736 | tf_op jit(solution)/shard_map/ppermute | solution.py:16
  26.5 21.7 %collective-permute-start.11 = (s32[12,512]{1,0:T(8,128)S(1)}, s32[12,512]{1,0:T(8,128)S(1)}, u32[]{:S(2)}, u32[]{:S(2)}) collective-permute-start(s32[12,512]{1,0:T(8,128)S(1)} %collective-permute-done.10.refs_2_), channel_id=1, source_target_pairs={{0,4},{4,0},{8,12},{12,8},{1,5},{5,1},{9,13},{13,9},{2,6},{6,2},{1... | collective-permute-start | bytes 73736 | tf_op jit(solution)/shard_map/ppermute | solution.py:16
  26.5 25.8 %collective-permute-start.6 = (bf16[256,1024]{1,0:T(8,128)(2,1)}, bf16[256,1024]{1,0:T(8,128)(2,1)S(1)}, u32[]{:S(2)}, u32[]{:S(2)}) collective-permute-start(bf16[256,1024]{1,0:T(8,128)(2,1)} %refs_0_.3), channel_id=1, source_target_pairs={{0,8},{4,12},{8,0},{12,4},{1,9},{5,13},{9,1},{13,5},{2,10},{6,14},... | collective-permute-start | bytes 1572872 | tf_op jit(solution)/shard_map/ppermute | solution.py:16
  28.0 1.2 copy-start.1
  31.5 5.5 %collective-permute-start.12 = (bf16[96,512]{1,0:T(8,128)(2,1)S(1)}, bf16[96,512]{1,0:T(8,128)(2,1)S(1)}, u32[]{:S(2)}, u32[]{:S(2)}) collective-permute-start(bf16[96,512]{1,0:T(8,128)(2,1)S(1)} %get-tuple-element.60), channel_id=1, source_target_pairs={{0,1},{1,0},{2,3},{3,2},{4,5},{5,4},{6,7},{7,6},{8,9},{9,8},{10,11... | collective-permute-start | bytes 294920 | tf_op jit(solution)/shard_map/ppermute | solution.py:16
  33.9 9.9 %collective-permute-start.13 = (bf16[96,512]{1,0:T(8,128)(2,1)S(1)}, bf16[96,512]{1,0:T(8,128)(2,1)S(1)}, u32[]{:S(2)}, u32[]{:S(2)}) collective-permute-start(bf16[96,512]{1,0:T(8,128)(2,1)S(1)} %get-tuple-element.61), channel_id=1, source_target_pairs={{0,2},{1,3},{2,0},{3,1},{4,6},{5,7},{6,4},{7,5},{8,10},{9,11},{10,... | collective-permute-start | bytes 294920 | tf_op jit(solution)/shard_map/ppermute | solution.py:16
  37.1 10.3 %collective-permute-start.14 = (bf16[96,512]{1,0:T(8,128)(2,1)S(1)}, bf16[96,512]{1,0:T(8,128)(2,1)S(1)}, u32[]{:S(2)}, u32[]{:S(2)}) collective-permute-start(bf16[96,512]{1,0:T(8,128)(2,1)S(1)} %get-tuple-element.62), channel_id=1, source_target_pairs={{0,3},{1,2},{2,1},{3,0},{4,7},{5,6},{6,5},{7,4},{8,11},{9,10},{10,... | collective-permute-start | bytes 294920 | tf_op jit(solution)/shard_map/ppermute | solution.py:16
  43.7 8.7 %collective-permute-start.18 = (bf16[128,512]{1,0:T(8,128)(2,1)S(1)}, bf16[128,512]{1,0:T(8,128)(2,1)S(1)}, u32[]{:S(2)}, u32[]{:S(2)}) collective-permute-start(bf16[128,512]{1,0:T(8,128)(2,1)S(1)} %get-tuple-element.65), channel_id=1, source_target_pairs={{0,1},{1,0},{2,3},{3,2},{4,5},{5,4},{6,7},{7,6},{8,9},{9,8},{10,11... | collective-permute-start | bytes 393224 | tf_op jit(solution)/shard_map/ppermute | solution.py:16
  43.8 11.7 %collective-permute-start.19 = (bf16[128,512]{1,0:T(8,128)(2,1)S(1)}, bf16[128,512]{1,0:T(8,128)(2,1)S(1)}, u32[]{:S(2)}, u32[]{:S(2)}) collective-permute-start(bf16[128,512]{1,0:T(8,128)(2,1)S(1)} %get-tuple-element.66), channel_id=1, source_target_pairs={{0,2},{1,3},{2,0},{3,1},{4,6},{5,7},{6,4},{7,5},{8,10},{9,11},{10,... | collective-permute-start | bytes 393224 | tf_op jit(solution)/shard_map/ppermute | solution.py:16
  47.3 8.1 %collective-permute-start.20 = (bf16[128,512]{1,0:T(8,128)(2,1)S(1)}, bf16[128,512]{1,0:T(8,128)(2,1)S(1)}, u32[]{:S(2)}, u32[]{:S(2)}) collective-permute-start(bf16[128,512]{1,0:T(8,128)(2,1)S(1)} %get-tuple-element.67), channel_id=1, source_target_pairs={{0,3},{1,2},{2,1},{3,0},{4,7},{5,6},{6,5},{7,4},{8,11},{9,10},{10,... | collective-permute-start | bytes 393224 | tf_op jit(solution)/shard_map/ppermute | solution.py:16
  48.2 19.8 %collective-permute-start.15 = (bf16[384,512]{1,0:T(8,128)(2,1)S(1)}, bf16[384,512]{1,0:T(8,128)(2,1)S(1)}, u32[]{:S(2)}, u32[]{:S(2)}) collective-permute-start(bf16[384,512]{1,0:T(8,128)(2,1)S(1)} %constant_dynamic-update-slice_fusion.refs_0_), channel_id=1, source_target_pairs={{0,8},{4,12},{8,0},{12,4},{1,9},{5,13},{9,1},{13,5},{2,10},{6,14},... | collective-permute-start | bytes 1179656 | tf_op jit(solution)/shard_map/ppermute | solution.py:16
  52.4 17.4 %collective-permute-start.17 = (bf16[384,512]{1,0:T(8,128)(2,1)S(1)}, bf16[384,512]{1,0:T(8,128)(2,1)S(1)}, u32[]{:S(2)}, u32[]{:S(2)}) collective-permute-start(bf16[384,512]{1,0:T(8,128)(2,1)S(1)} %constant_dynamic-update-slice_fusion.refs_0_), channel_id=1, source_target_pairs={{0,4},{4,0},{8,12},{12,8},{1,5},{5,1},{9,13},{13,9},{2,6},{6,2},{1... | collective-permute-start | bytes 1179656 | tf_op jit(solution)/shard_map/ppermute | solution.py:16
  56.3 5.8 %collective-permute-start.21 = (bf16[96,512]{1,0:T(8,128)(2,1)S(1)}, bf16[96,512]{1,0:T(8,128)(2,1)S(1)}, u32[]{:S(2)}, u32[]{:S(2)}) collective-permute-start(bf16[96,512]{1,0:T(8,128)(2,1)S(1)} %get-tuple-element.69), channel_id=1, source_target_pairs={{0,1},{1,0},{2,3},{3,2},{4,5},{5,4},{6,7},{7,6},{8,9},{9,8},{10,11... | collective-permute-start | bytes 294920 | tf_op jit(solution)/shard_map/ppermute | solution.py:16
  58.5 9.5 %collective-permute-start.22 = (bf16[96,512]{1,0:T(8,128)(2,1)S(1)}, bf16[96,512]{1,0:T(8,128)(2,1)S(1)}, u32[]{:S(2)}, u32[]{:S(2)}) collective-permute-start(bf16[96,512]{1,0:T(8,128)(2,1)S(1)} %get-tuple-element.70), channel_id=1, source_target_pairs={{0,2},{1,3},{2,0},{3,1},{4,6},{5,7},{6,4},{7,5},{8,10},{9,11},{10,... | collective-permute-start | bytes 294920 | tf_op jit(solution)/shard_map/ppermute | solution.py:16
  59.6 8.5 %collective-permute-start.23 = (bf16[96,512]{1,0:T(8,128)(2,1)S(1)}, bf16[96,512]{1,0:T(8,128)(2,1)S(1)}, u32[]{:S(2)}, u32[]{:S(2)}) collective-permute-start(bf16[96,512]{1,0:T(8,128)(2,1)S(1)} %get-tuple-element.71), channel_id=1, source_target_pairs={{0,3},{1,2},{2,1},{3,0},{4,7},{5,6},{6,5},{7,4},{8,11},{9,10},{10,... | collective-permute-start | bytes 294920 | tf_op jit(solution)/shard_map/ppermute | solution.py:16
  68.0 1.8 %collective-permute-start.16 = (bf16[384,512]{1,0:T(8,128)(2,1)S(1)}, bf16[384,512]{1,0:T(8,128)(2,1)S(1)}, u32[]{:S(2)}, u32[]{:S(2)}) collective-permute-start(bf16[384,512]{1,0:T(8,128)(2,1)S(1)} %collective-permute-done.15.refs_0_), channel_id=1, source_target_pairs={{0,4},{4,0},{8,12},{12,8},{1,5},{5,1},{9,13},{13,9},{2,6},{6,2},{1... | collective-permute-start | bytes 1179656 | tf_op jit(solution)/shard_map/ppermute | solution.py:16
  68.1 9.3 %slice-start = ((s8[5505024]{0:T(1024)(128)(4,1)}), s8[4194304]{0:T(1024)(128)(4,1)S(1)}, s32[]{:S(2)}) async-start(s8[5505024]{0:T(1024)(128)(4,1)} %bitcast.6), calls=%async_computation | async-start | bytes 8388608
  68.1 2.2 %collective-permute-start.24 = (bf16[384,512]{1,0:T(8,128)(2,1)S(1)}, bf16[384,512]{1,0:T(8,128)(2,1)S(1)}, u32[]{:S(2)}, u32[]{:S(2)}) collective-permute-start(bf16[384,512]{1,0:T(8,128)(2,1)S(1)} %constant_dynamic-update-slice_fusion.4.refs_2_), channel_id=1, source_target_pairs={{0,4},{4,0},{8,12},{12,8},{1,5},{5,1},{9,13},{13,9},{2,6},{6,2},{1... | collective-permute-start | bytes 1179656 | tf_op jit(solution)/shard_map/ppermute | solution.py:16
  68.7 13.1 %collective-permute-start.26 = (bf16[384,512]{1,0:T(8,128)(2,1)S(1)}, bf16[384,512]{1,0:T(8,128)(2,1)S(1)}, u32[]{:S(2)}, u32[]{:S(2)}) collective-permute-start(bf16[384,512]{1,0:T(8,128)(2,1)S(1)} %constant_dynamic-update-slice_fusion.4.refs_2_), channel_id=1, source_target_pairs={{0,8},{4,12},{8,0},{12,4},{1,9},{5,13},{9,1},{13,5},{2,10},{6,14},... | collective-permute-start | bytes 1179656 | tf_op jit(solution)/shard_map/ppermute | solution.py:16
  70.4 2.6 %copy-start.5 = (bf16[1,1024,2688]{2,1,0:T(8,128)(2,1)S(1)}, bf16[1,1024,2688]{2,1,0:T(8,128)(2,1)}, u32[]{:S(2)}) copy-start(bf16[1,1024,2688]{2,1,0:T(8,128)(2,1)} %param.10) | copy-start | bytes 16515076
  72.9 4.5 %slice-start.1 = ((s8[5505024]{0:T(1024)(128)(4,1)}), s8[1310720]{0:T(1024)(128)(4,1)S(1)}, s32[]{:S(2)}) async-start(s8[5505024]{0:T(1024)(128)(4,1)} %bitcast.6), calls=%async_computation.1 | async-start | bytes 2621440
  72.9 10.6 %slice-start.2 = ((s8[5505024]{0:T(1024)(128)(4,1)}), s8[4194304]{0:T(1024)(128)(4,1)S(1)}, s32[]{:S(2)}) async-start(s8[5505024]{0:T(1024)(128)(4,1)} %bitcast.14), calls=%async_computation.2 | async-start | bytes 8388608
  77.4 6.2 %slice-start.3 = ((s8[5505024]{0:T(1024)(128)(4,1)}), s8[1310720]{0:T(1024)(128)(4,1)S(1)}, s32[]{:S(2)}) async-start(s8[5505024]{0:T(1024)(128)(4,1)} %bitcast.14), calls=%async_computation.3 | async-start | bytes 2621440
  81.8 1.8 %collective-permute-start.27 = (bf16[384,512]{1,0:T(8,128)(2,1)S(1)}, bf16[384,512]{1,0:T(8,128)(2,1)S(1)}, u32[]{:S(2)}, u32[]{:S(2)}) collective-permute-start(bf16[384,512]{1,0:T(8,128)(2,1)S(1)} %collective-permute-done.26.refs_2_), channel_id=1, source_target_pairs={{0,4},{4,0},{8,12},{12,8},{1,5},{5,1},{9,13},{13,9},{2,6},{6,2},{1... | collective-permute-start | bytes 1179656 | tf_op jit(solution)/shard_map/ppermute | solution.py:16
  90.8 6.1 %copy-start.3 = (bf16[256,1024]{1,0:T(8,128)(2,1)S(1)}, bf16[256,1024]{1,0:T(8,128)(2,1)}, u32[]{:S(2)}) copy-start(bf16[256,1024]{1,0:T(8,128)(2,1)} %refs_0_.3) | copy-start | bytes 1572868
  90.8 3.2 %collective-permute-start.28 = (bf16[384,1024]{1,0:T(8,128)(2,1)S(1)}, bf16[384,1024]{1,0:T(8,128)(2,1)S(1)}, u32[]{:S(2)}, u32[]{:S(2)}) collective-permute-start(bf16[384,1024]{1,0:T(8,128)(2,1)S(1)} %shard_map.83), channel_id=1, source_target_pairs={{0,4},{4,0},{8,12},{12,8},{1,5},{5,1},{9,13},{13,9},{2,6},{6,2},{1... | collective-permute-start | bytes 2359304 | tf_op jit(solution)/shard_map/ppermute | solution.py:16
  91.0 5.9 %collective-permute-start.25 = (bf16[384,1024]{1,0:T(8,128)(2,1)S(1)}, bf16[384,1024]{1,0:T(8,128)(2,1)S(1)}, u32[]{:S(2)}, u32[]{:S(2)}) collective-permute-start(bf16[384,1024]{1,0:T(8,128)(2,1)S(1)} %get-tuple-element.73), channel_id=1, source_target_pairs={{0,4},{4,0},{8,12},{12,8},{1,5},{5,1},{9,13},{13,9},{2,6},{6,2},{1... | collective-permute-start | bytes 2359304 | tf_op jit(solution)/shard_map/ppermute | solution.py:16
  94.8 12.0 %collective-permute-start.29 = (bf16[384,512]{1,0:T(8,128)(2,1)S(1)}, bf16[384,512]{1,0:T(8,128)(2,1)S(1)}, u32[]{:S(2)}, u32[]{:S(2)}) collective-permute-start(bf16[384,512]{1,0:T(8,128)(2,1)S(1)} %get-tuple-element.76), channel_id=1, source_target_pairs={{0,8},{4,12},{8,0},{12,4},{1,9},{5,13},{9,1},{13,5},{2,10},{6,14},... | collective-permute-start | bytes 1179656 | tf_op jit(solution)/shard_map/ppermute | solution.py:16
  95.4 24.8 %collective-permute-start.33 = (bf16[384,512]{1,0:T(8,128)(2,1)S(1)}, bf16[384,512]{1,0:T(8,128)(2,1)S(1)}, u32[]{:S(2)}, u32[]{:S(2)}) collective-permute-start(bf16[384,512]{1,0:T(8,128)(2,1)S(1)} %get-tuple-element.82), channel_id=1, source_target_pairs={{0,8},{4,12},{8,0},{12,4},{1,9},{5,13},{9,1},{13,5},{2,10},{6,14},... | collective-permute-start | bytes 1179656 | tf_op jit(solution)/shard_map/ppermute | solution.py:16
  96.9 45.6 %collective-permute-start = (bf16[256,1024]{1,0:T(8,128)(2,1)S(1)}, bf16[256,1024]{1,0:T(8,128)(2,1)S(1)}, u32[]{:S(2)}, u32[]{:S(2)}) collective-permute-start(bf16[256,1024]{1,0:T(8,128)(2,1)S(1)} %copy-done.3), channel_id=1, source_target_pairs={{0,4},{4,0},{8,12},{12,8},{1,5},{5,1},{9,13},{13,9},{2,6},{6,2},{1... | collective-permute-start | bytes 1572872 | tf_op jit(solution)/shard_map/ppermute | solution.py:16
  107.5 4.7 %collective-permute-start.30 = (bf16[96,512]{1,0:T(8,128)(2,1)S(1)}, bf16[96,512]{1,0:T(8,128)(2,1)S(1)}, u32[]{:S(2)}, u32[]{:S(2)}) collective-permute-start(bf16[96,512]{1,0:T(8,128)(2,1)S(1)} %get-tuple-element.78), channel_id=1, source_target_pairs={{0,1},{1,0},{2,3},{3,2},{4,5},{5,4},{6,7},{7,6},{8,9},{9,8},{10,11... | collective-permute-start | bytes 294920 | tf_op jit(solution)/shard_map/ppermute | solution.py:16
  108.7 38.7 %collective-permute-start.7 = (bf16[256,1024]{1,0:T(8,128)(2,1)S(1)}, bf16[256,1024]{1,0:T(8,128)(2,1)S(1)}, u32[]{:S(2)}, u32[]{:S(2)}) collective-permute-start(bf16[256,1024]{1,0:T(8,128)(2,1)S(1)} %collective-permute-done.6.refs_2_), channel_id=1, source_target_pairs={{0,4},{4,0},{8,12},{12,8},{1,5},{5,1},{9,13},{13,9},{2,6},{6,2},{1... | collective-permute-start | bytes 1572872 | tf_op jit(solution)/shard_map/ppermute | solution.py:16
  108.7 10.7 %collective-permute-start.31 = (bf16[96,512]{1,0:T(8,128)(2,1)S(1)}, bf16[96,512]{1,0:T(8,128)(2,1)S(1)}, u32[]{:S(2)}, u32[]{:S(2)}) collective-permute-start(bf16[96,512]{1,0:T(8,128)(2,1)S(1)} %get-tuple-element.79), channel_id=1, source_target_pairs={{0,2},{1,3},{2,0},{3,1},{4,6},{5,7},{6,4},{7,5},{8,10},{9,11},{10,... | collective-permute-start | bytes 294920 | tf_op jit(solution)/shard_map/ppermute | solution.py:16
  112.2 7.1 %collective-permute-start.32 = (bf16[96,512]{1,0:T(8,128)(2,1)S(1)}, bf16[96,512]{1,0:T(8,128)(2,1)S(1)}, u32[]{:S(2)}, u32[]{:S(2)}) collective-permute-start(bf16[96,512]{1,0:T(8,128)(2,1)S(1)} %get-tuple-element.80), channel_id=1, source_target_pairs={{0,3},{1,2},{2,1},{3,0},{4,7},{5,6},{6,5},{7,4},{8,11},{9,10},{10,... | collective-permute-start | bytes 294920 | tf_op jit(solution)/shard_map/ppermute | solution.py:16
  120.9 5.6 %collective-permute-start.34 = (bf16[96,512]{1,0:T(8,128)(2,1)S(1)}, bf16[96,512]{1,0:T(8,128)(2,1)S(1)}, u32[]{:S(2)}, u32[]{:S(2)}) collective-permute-start(bf16[96,512]{1,0:T(8,128)(2,1)S(1)} %get-tuple-element.84), channel_id=1, source_target_pairs={{0,1},{1,0},{2,3},{3,2},{4,5},{5,4},{6,7},{7,6},{8,9},{9,8},{10,11... | collective-permute-start | bytes 294920 | tf_op jit(solution)/shard_map/ppermute | solution.py:16
  123.3 13.2 %collective-permute-start.35 = (bf16[96,512]{1,0:T(8,128)(2,1)S(1)}, bf16[96,512]{1,0:T(8,128)(2,1)S(1)}, u32[]{:S(2)}, u32[]{:S(2)}) collective-permute-start(bf16[96,512]{1,0:T(8,128)(2,1)S(1)} %get-tuple-element.85), channel_id=1, source_target_pairs={{0,2},{1,3},{2,0},{3,1},{4,6},{5,7},{6,4},{7,5},{8,10},{9,11},{10,... | collective-permute-start | bytes 294920 | tf_op jit(solution)/shard_map/ppermute | solution.py:16
  124.2 12.3 %collective-permute-start.36 = (bf16[96,512]{1,0:T(8,128)(2,1)S(1)}, bf16[96,512]{1,0:T(8,128)(2,1)S(1)}, u32[]{:S(2)}, u32[]{:S(2)}) collective-permute-start(bf16[96,512]{1,0:T(8,128)(2,1)S(1)} %get-tuple-element.86), channel_id=1, source_target_pairs={{0,3},{1,2},{2,1},{3,0},{4,7},{5,6},{6,5},{7,4},{8,11},{9,10},{10,... | collective-permute-start | bytes 294920 | tf_op jit(solution)/shard_map/ppermute | solution.py:16
  126.5 14.0 %collective-permute-start.41 = (bf16[128,512]{1,0:T(8,128)(2,1)S(1)}, bf16[128,512]{1,0:T(8,128)(2,1)S(1)}, u32[]{:S(2)}, u32[]{:S(2)}) collective-permute-start(bf16[128,512]{1,0:T(8,128)(2,1)S(1)} %shard_map.87.refs_0_), channel_id=1, source_target_pairs={{0,2},{1,3},{2,0},{3,1},{4,6},{5,7},{6,4},{7,5},{8,10},{9,11},{10,... | collective-permute-start | bytes 393224 | tf_op jit(solution)/shard_map/ppermute | solution.py:16
  137.3 7.7 %collective-permute-start.38 = (bf16[128,512]{1,0:T(8,128)(2,1)S(1)}, bf16[128,512]{1,0:T(8,128)(2,1)S(1)}, u32[]{:S(2)}, u32[]{:S(2)}) collective-permute-start(bf16[128,512]{1,0:T(8,128)(2,1)S(1)} %shard_map.89.refs_0_), channel_id=1, source_target_pairs={{0,2},{1,3},{2,0},{3,1},{4,6},{5,7},{6,4},{7,5},{8,10},{9,11},{10,... | collective-permute-start | bytes 393224 | tf_op jit(solution)/shard_map/ppermute | solution.py:16
  140.5 7.6 %collective-permute-start.40 = (bf16[128,512]{1,0:T(8,128)(2,1)S(1)}, bf16[128,512]{1,0:T(8,128)(2,1)S(1)}, u32[]{:S(2)}, u32[]{:S(2)}) collective-permute-start(bf16[128,512]{1,0:T(8,128)(2,1)S(1)} %shard_map.87.refs_0_), channel_id=1, source_target_pairs={{0,1},{1,0},{2,3},{3,2},{4,5},{5,4},{6,7},{7,6},{8,9},{9,8},{10,11... | collective-permute-start | bytes 393224 | tf_op jit(solution)/shard_map/ppermute | solution.py:16
  140.5 9.8 %collective-permute-start.42 = (bf16[128,512]{1,0:T(8,128)(2,1)S(1)}, bf16[128,512]{1,0:T(8,128)(2,1)S(1)}, u32[]{:S(2)}, u32[]{:S(2)}) collective-permute-start(bf16[128,512]{1,0:T(8,128)(2,1)S(1)} %collective-permute-done.41.refs_2_), channel_id=1, source_target_pairs={{0,1},{1,0},{2,3},{3,2},{4,5},{5,4},{6,7},{7,6},{8,9},{9,8},{10,11... | collective-permute-start | bytes 393224 | tf_op jit(solution)/shard_map/ppermute | solution.py:16
  142.5 10.6 %collective-permute-start.37 = (bf16[128,512]{1,0:T(8,128)(2,1)S(1)}, bf16[128,512]{1,0:T(8,128)(2,1)S(1)}, u32[]{:S(2)}, u32[]{:S(2)}) collective-permute-start(bf16[128,512]{1,0:T(8,128)(2,1)S(1)} %shard_map.89.refs_0_), channel_id=1, source_target_pairs={{0,1},{1,0},{2,3},{3,2},{4,5},{5,4},{6,7},{7,6},{8,9},{9,8},{10,11... | collective-permute-start | bytes 393224 | tf_op jit(solution)/shard_map/ppermute | solution.py:16
  145.0 10.0 %collective-permute-start.39 = (bf16[128,512]{1,0:T(8,128)(2,1)S(1)}, bf16[128,512]{1,0:T(8,128)(2,1)S(1)}, u32[]{:S(2)}, u32[]{:S(2)}) collective-permute-start(bf16[128,512]{1,0:T(8,128)(2,1)S(1)} %collective-permute-done.38.refs_2_), channel_id=1, source_target_pairs={{0,1},{1,0},{2,3},{3,2},{4,5},{5,4},{6,7},{7,6},{8,9},{9,8},{10,11... | collective-permute-start | bytes 393224 | tf_op jit(solution)/shard_map/ppermute | solution.py:16

commit v3 on v2

--- a/solution.py
+++ b/solution.py
@@ -20,7 +20,7 @@
     return lax.optimization_barrier((x, *earlier))[0]
 
 
-def call(kernel, me, operands, outs, scratch=(), flops=1, room=4):
+def call(kernel, me, operands, outs, scratch=(), flops=1, room=4, told=True):
     vmem = pl.BlockSpec(memory_space=pltpu.VMEM)
     def size(arrays):
         return sum(math.prod(x.shape) * jnp.dtype(x.dtype).itemsize for x in arrays)
@@ -34,15 +34,15 @@
         out_specs=tuple(vmem for _ in outs),
         scratch_shapes=list(scratch),
         cost_estimate=pl.CostEstimate(
-            flops=flops, bytes_accessed=moved, transcendentals=0
+            flops=flops if told else 1, bytes_accessed=moved if told else 1, transcendentals=0
         ),
         compiler_params=pltpu.CompilerParams(vmem_limit_bytes=limit),
     )(me, *operands)
 
 
 def partial_kernel(n_rows, me_ref, tokens_ref, *refs):
-    n_blocks = len(refs) - 2 - n_rows
-    rows, outs, (weights, product) = refs[:n_rows], refs[n_rows:-2], refs[-2:]
+    rows, outs, (kept_ref, weights, product) = refs[:n_rows], refs[n_rows:-3], refs[-3:]
+    n_blocks = len(outs)
     high = rows[0].shape[0]
     core, grp = me_ref[0] & 1, me_ref[1]
     for q in range(n_rows):
@@ -53,6 +53,7 @@
         product[:, start : start + tile] = lax.dot_general(
             tokens_ref[...], weights[start : start + tile, :], (((1,), (1,)), ((), ())), preferred_element_type=F32
         ).astype(BF16)
+    kept_ref[...] = tokens_ref[: kept_ref.shape[0], :]
     block = product.shape[0] // n_blocks
     for k, out in enumerate(outs):
         out[...] = product[pl.ds(pl.multiple_of((grp ^ k) * block, block), block), :]
@@ -255,16 +256,17 @@
     rows_near = [proj_in, hop(proj_in, "ep", 1)]
     rows_far = [hop(proj_in, "ep", 2 * k) for k in steps]
 
-    def partial(rows):
+    def partial(tokens, rows, kept):
         columns = high * len(rows)
-        return call(
+        *cut, again = call(
             functools.partial(partial_kernel, len(rows)),
             me,
             [tokens, *rows],
-            [shape((block, columns), BF16)] * n_grp,
+            [shape((block, columns), BF16)] * n_grp + [shape((kept, depth), BF16)],
             [pltpu.VMEM((columns, depth), BF16), pltpu.VMEM((tokens.shape[0], columns), BF16)],
             flops=2 * tokens.shape[0] * columns * depth,
         )
+        return cut, again
 
     def swap(cut):
         return [cut[0]] + [hop(cut[k], "grp", k) for k in range(1, n_grp)]
@@ -273,34 +275,40 @@
         columns = arrived[0].shape[1]
         return call(dispatch_kernel, me, [ranks, *arrived], [shape((hits, columns), BF16)] * n_grp)
 
-    cut_near = partial(rows_near)
+    cut_near, kept = partial(tokens, rows_near, tokens.shape[0])
     meta_own = after(meta_own, cut_near[0])
     arrived_near = swap(cut_near)
-    rows_far = [after(part, *arrived_near) for part in rows_far]
     metas = [meta_own, hop(meta_own, "ep", 1)]
-    for k in steps:
-        part = after(hop(meta_own, "ep", 2 * k), *arrived_near)
+    meta_far = [hop(meta_own, "ep", 2 * k) for k in steps]
+    for part in meta_far:
         metas += [part, hop(part, "ep", 1)]
-    crossed_out = [hop(after(proj_out, *rows_far), "ep", 2 * k) for k in steps]
-    cut_far = partial([x for part in rows_far for x in (part, hop(part, "ep", 1))])
-    chosen_near = choose(after(ranks, cut_far[0]), arrived_near)
-    arrived_far, near_own = swap(cut_far), jnp.concatenate(swap(chosen_near), axis=0)
-    near = [near_own, hop(near_own, "ep", 1)]
-    crossed_near = [hop(near_own, "ep", 2 * k) for k in steps]
     line_slot, line_weight = call(
         functools.partial(route_kernel, n_grp, picks, cap),
-        after(me, chosen_near[0]),
+        me,
         metas,
         [shape((n_ep, 1, lines), I32), shape((n_ep, 1, lines), F32)],
         room=3 * n_ep,
     )
-    chosen_far = choose(after(ranks, near_own, line_slot, *crossed_out), arrived_far)
+    rows_far = [after(part, *arrived_near, ranks, line_slot) for part in rows_far]
+    cut_far, _ = partial(kept, [x for part in rows_far for x in (part, hop(part, "ep", 1))], 16)
+    chosen_near = choose(ranks, arrived_near)
+    arrived_far, pieces = swap(cut_far), swap(chosen_near)
+    pieces = lax.optimization_barrier((*pieces, *arrived_far))[:n_grp]
+    near_own = jnp.concatenate(pieces, axis=0)
+    rows_out = [proj_out, hop(proj_out, "ep", 1)]
+    for k in steps:
+        part = hop(after(proj_out, *rows_far), "ep", 2 * k)
+        rows_out += [part, hop(part, "ep", 1)]
+    [rows_out] = call(rows_kernel, me, rows_out, [shape((width, depth), BF16)])
+    near = [near_own, hop(near_own, "ep", 1)]
+    crossed_near = [hop(near_own, "ep", 2 * k) for k in steps]
+    chosen_far = choose(after(ranks, pieces[0], rows_out), arrived_far)
     far_own = jnp.concatenate(swap(chosen_far), axis=0)
     crossed_side = [hop(part, "ep", 1) for part in crossed_near]
     far = [far_own, hop(far_own, "ep", 1)]
     crossed_far = [hop(far_own, "ep", 2 * k) for k in steps]
 
-    def up(sources, *deps):
+    def up(sources, *deps, told=True):
         n = len(sources) * slots
         return call(
             functools.partial(up_kernel, sources, slots, 512),
@@ -309,9 +317,10 @@
             [shape((n, wide), BF16)],
             [pltpu.VMEM((n, width), BF16)],
             flops=2 * n * width * wide,
+            told=told,
         )[0]
 
-    def down(sources, hidden, first, stride, *deps, hides=1):
+    def down(sources, hidden, first, stride, *deps, told=True):
         n = len(sources) * slots
         return call(
             functools.partial(down_kernel, sources, slots, width // 2, first, stride),
@@ -319,7 +328,8 @@
             [after(line_slot, *deps), line_weight, hidden, expert_down[0]],
             [shape((lines, width), BF16)] * len(sources),
             [pltpu.VMEM((n, wide), BF16), pltpu.VMEM((n, width), BF16)],
-            flops=hides * 2 * n * width * wide,
+            flops=2 * n * width * wide,
+            told=told,
         )
 
     here, there = list(range(2)), list(range(2, n_ep))
@@ -330,24 +340,20 @@
     for k in steps:
         near += [crossed_near[k - 1], crossed_side[k - 1]]
         far += [crossed_far[k - 1], hop(crossed_far[k - 1], "ep", 1)]
-    hidden_there = up(there)
-    rows_out = [proj_out, hop(proj_out, "ep", 1)]
-    for part in crossed_out:
-        rows_out += [part, hop(part, "ep", 1)]
-    odd = down(there[1::2], hidden_there, 1, 2)
+    hidden_there = up(there, told=False)
+    odd = down(there[1::2], hidden_there, 1, 2, told=False)
     other = [hop(part, "ep", 1) for part in odd]
-    even = down(there[::2], hidden_there, 0, 2, *odd)
+    even = down(there[::2], hidden_there, 0, 2, *odd, told=False)
     sums = call(add_kernel, me, [*even, *other], [shape((lines, width // 2), BF16)] * (2 * len(even)))
     half = width // 2
     returned = [[hop(sums[2 * k + h], "ep", 2 * k + 2) for k in range(len(even))] for h in range(2)]
-    [rows_out] = call(rows_kernel, me, rows_out, [shape((width, depth), BF16)])
 
     def join(h, arrived):
         parts = [*local, *returned[h]]
         kernel = functools.partial(join_kernel, len(parts), h)
         return call(kernel, after(me, *arrived), parts, [shape((hits, half), BF16)] * n_grp)
 
-    def combine(arrived):
+    def combine(ranks, arrived):
         return call(combine_kernel, me, [ranks, *arrived], [shape((block, half), BF16)])[0]
 
     def gather(latent_out):
@@ -368,10 +374,12 @@
         )
 
     arrived = swap(join(0, ()))
-    latent_out = combine(arrived)
-    cut = join(1, (latent_out,))
-    total = mix(0, gather(latent_out), ())
-    return mix(1, gather(combine(swap(cut))), total)[0]
+    cut = join(1, arrived[1:2])
+    latent_out = combine(after(ranks, cut[0]), arrived)
+    first = gather(latent_out)
+    ranks = after(ranks, *(first[1 << i] for i in range(n_grp.bit_length() - 1)))
+    second = gather(combine(ranks, swap(cut)))
+    return mix(1, second, mix(0, first, ()))[0]
 
 
 def solution(mesh):

time: 158 us -> 147 us (0.930)
  waiting for transfers between devices: 62.8 us -> 56.1 us
  local copies, waits for them, and re-layouts: 6.86 us -> 3.07 us
    ppermute x43, waiting for transfers between devices: 62.8 us -> 56.1 us  [hop(): return lax.ppermute(x, axis, [(i, i ^ step) for i in range(count)])]
    unnamed x26 -> x20, local copies, waits for them, and re-layouts: 6.84 us -> 3.05 us
  transfers between devices with their start and end apart: 43 -> 43, of which waited for: 20 -> 21; matrix products, arithmetic and copies ran while one was open for 1% -> 1% of each run, Pallas kernels for 16% -> 17%
where the time goes in v3:
time: 147 us; the launch traced here: 146 us
  waiting for transfers between devices  56.1 us (38%)
  starting transfers between devices  50.3 us (34%)
  Pallas kernels  35.8 us (24%)
  local copies, waits for them, and re-layouts  3.07 us (2%)
    ppermute x43, waiting for transfers between devices, hop(): return lax.ppermute(x, axis, [(i, i ^ step) for i in range(count)])  56.1 us
    ppermute x43, starting transfers between devices, hop(): return lax.ppermute(x, axis, [(i, i ^ step) for i in range(count)])  50.3 us
    pallas_call x19, Pallas kernels, call(): pl.pallas_call(kernel, out_shape=tuple(outs), in_specs=[pl.BlockSpec(memo...  35.8 us
    unnamed x20, local copies, waits for them, and re-layouts  3.05 us
  transfers between devices with their start and end apart: 43, of which 21 were waited for; matrix products, arithmetic and copies ran while one was open for 1% of the time, Pallas kernels for 17%

profile of v3, /device:TPU:0, one launch (start us, length us, event | category | flops | bytes accessed | tf_op | source)
XLA Modules:
  0.0 146.4 jit_solution(14395284968597884441)
XLA Ops:
  0.5 2.5 %collective-permute-start.1 = (bf16[256,1024]{1,0:T(8,128)(2,1)}, bf16[256,1024]{1,0:T(8,128)(2,1)S(1)}, u32[]{:S(2)}, u32[]{:S(2)}) collective-permute-start(bf16[256,1024]{1,0:T(8,128)(2,1)} %refs_0_.2), channel_id=1, source_target_pairs={{0,8},{4,12},{8,0},{12,4},{1,9},{5,13},{9,1},{13,5},{2,10},{6,14},... | collective-permute-start | bytes 1572872 | tf_op jit(solution)/shard_map/ppermute | solution.py:16
  3.1 1.2 copy-done.1
  4.3 1.0 copy-done.2
  5.3 1.4 shard_map.73
  6.7 2.2 %collective-permute-start.3 = (bf16[128,512]{1,0:T(8,128)(2,1)S(1)}, bf16[128,512]{1,0:T(8,128)(2,1)S(1)}, u32[]{:S(2)}, u32[]{:S(2)}) collective-permute-start(bf16[128,512]{1,0:T(8,128)(2,1)S(1)} %get-tuple-element.51), channel_id=1, source_target_pairs={{0,1},{1,0},{2,3},{3,2},{4,5},{5,4},{6,7},{7,6},{8,9},{9,8},{10,11... | collective-permute-start | bytes 393224 | tf_op jit(solution)/shard_map/ppermute | solution.py:16
  8.9 2.6 %collective-permute-start.4 = (bf16[128,512]{1,0:T(8,128)(2,1)S(1)}, bf16[128,512]{1,0:T(8,128)(2,1)S(1)}, u32[]{:S(2)}, u32[]{:S(2)}) collective-permute-start(bf16[128,512]{1,0:T(8,128)(2,1)S(1)} %get-tuple-element.52), channel_id=1, source_target_pairs={{0,2},{1,3},{2,0},{3,1},{4,6},{5,7},{6,4},{7,5},{8,10},{9,11},{10,... | collective-permute-start | bytes 393224 | tf_op jit(solution)/shard_map/ppermute | solution.py:16
  11.5 0.7 pad_add_fusion.refs_0_
  12.2 1.8 %collective-permute-start.7 = (s32[12,512]{1,0:T(8,128)S(1)}, s32[12,512]{1,0:T(8,128)S(1)}, u32[]{:S(2)}, u32[]{:S(2)}) collective-permute-start(s32[12,512]{1,0:T(8,128)S(1)} %pad_add_fusion.refs_0_), channel_id=1, source_target_pairs={{0,8},{4,12},{8,0},{12,4},{1,9},{5,13},{9,1},{13,5},{2,10},{6,14},... | collective-permute-start | bytes 73736 | tf_op jit(solution)/shard_map/ppermute | solution.py:16
  14.0 2.4 %collective-permute-done.7.refs_2_ = s32[12,512]{1,0:T(8,128)S(1)} collective-permute-done((s32[12,512]{1,0:T(8,128)S(1)}, s32[12,512]{1,0:T(8,128)S(1)}, u32[]{:S(2)}, u32[]{:S(2)}) %collective-permute-start.7) | collective-permute-done | bytes 24608 | tf_op jit(solution)/shard_map/ppermute | solution.py:16
  16.5 1.2 collective-permute-done.6.refs_1_
  17.9 0.7 copy-done.4
  19.2 3.5 %shard_map.75 = (s32[4,1,384]{2,1,0:T(1,128)S(1)}, f32[4,1,384]{2,1,0:T(1,128)S(1)}) custom-call(s32[2]{0:T(128)S(1)} %pad_add_fusion.1.me_ref, s32[12,512]{1,0:T(8,128)S(1)} %pad_add_fusion.refs_0_, s32[12,512]{1,0:T(8,128)S(1)} %collective-permute-done.6.refs_1_, s32[12,512]{1,0:T(8,128)S(1)} %collective-permute-done.7.refs_2_, ...), custom_call_target="tpu_custom_call" | custom-call | flops 1 | bytes 110592 | tf_op jit(solution)/shard_map/pallas_call | solution.py:30
  23.3 1.7 %collective-permute-start.9 = (bf16[256,1024]{1,0:T(8,128)(2,1)}, bf16[256,1024]{1,0:T(8,128)(2,1)S(1)}, u32[]{:S(2)}, u32[]{:S(2)}) collective-permute-start(bf16[256,1024]{1,0:T(8,128)(2,1)} %refs_0_.3), channel_id=1, source_target_pairs={{0,8},{4,12},{8,0},{12,4},{1,9},{5,13},{9,1},{13,5},{2,10},{6,14},... | collective-permute-start | bytes 1572872 | tf_op jit(solution)/shard_map/ppermute | solution.py:16
  25.0 0.8 shard_map.77
  25.8 1.6 %collective-permute-start.11 = (bf16[96,512]{1,0:T(8,128)(2,1)S(1)}, bf16[96,512]{1,0:T(8,128)(2,1)S(1)}, u32[]{:S(2)}, u32[]{:S(2)}) collective-permute-start(bf16[96,512]{1,0:T(8,128)(2,1)S(1)} %get-tuple-element.60), channel_id=1, source_target_pairs={{0,1},{1,0},{2,3},{3,2},{4,5},{5,4},{6,7},{7,6},{8,9},{9,8},{10,11... | collective-permute-start | bytes 294920 | tf_op jit(solution)/shard_map/ppermute | solution.py:16
  27.5 2.6 %collective-permute-start.12 = (bf16[96,512]{1,0:T(8,128)(2,1)S(1)}, bf16[96,512]{1,0:T(8,128)(2,1)S(1)}, u32[]{:S(2)}, u32[]{:S(2)}) collective-permute-start(bf16[96,512]{1,0:T(8,128)(2,1)S(1)} %get-tuple-element.61), channel_id=1, source_target_pairs={{0,2},{1,3},{2,0},{3,1},{4,6},{5,7},{6,4},{7,5},{8,10},{9,11},{10,... | collective-permute-start | bytes 294920 | tf_op jit(solution)/shard_map/ppermute | solution.py:16
  30.1 1.9 %shard_map.78 = (bf16[128,512]{1,0:T(8,128)(2,1)S(1)}, bf16[128,512]{1,0:T(8,128)(2,1)S(1)}, bf16[128,512]{1,0:T(8,128)(2,1)S(1)}, bf16[128,512]{1,0:T(8,128)(2,1)S(1)}, bf16[16,1024]{1,0:T(8,128)(2,1)}) custom-call(s32[2]{0:T(128)S(1)} %pad_add_fusion.1.me_ref, bf16[512,1024]{1,0:T(8,128)(2,1)S(1)} %get-tuple-element.63.tokens_ref, ...), custom_call_target="tpu_custom_call" | custom-call | flops 536870912 | bytes 2654208 | tf_op jit(solution)/shard_map/pallas_call | solution.py:30
  32.8 3.9 %collective-permute-start.17 = (bf16[128,512]{1,0:T(8,128)(2,1)S(1)}, bf16[128,512]{1,0:T(8,128)(2,1)S(1)}, u32[]{:S(2)}, u32[]{:S(2)}) collective-permute-start(bf16[128,512]{1,0:T(8,128)(2,1)S(1)} %get-tuple-element.67), channel_id=1, source_target_pairs={{0,3},{1,2},{2,1},{3,0},{4,7},{5,6},{6,5},{7,4},{8,11},{9,10},{10,... | collective-permute-start | bytes 393224 | tf_op jit(solution)/shard_map/ppermute | solution.py:16
  36.7 1.3 collective-permute-start.13
  37.9 7.3 %collective-permute-done.13 = bf16[96,512]{1,0:T(8,128)(2,1)S(1)} collective-permute-done((bf16[96,512]{1,0:T(8,128)(2,1)S(1)}, bf16[96,512]{1,0:T(8,128)(2,1)S(1)}, u32[]{:S(2)}, u32[]{:S(2)}) %collective-permute-start.13) | collective-permute-done | bytes 98336 | tf_op jit(solution)/shard_map/ppermute | solution.py:16
  45.8 1.5 %collective-permute-done.16.refs_2_ = bf16[128,512]{1,0:T(8,128)(2,1)S(1)} collective-permute-done((bf16[128,512]{1,0:T(8,128)(2,1)S(1)}, bf16[128,512]{1,0:T(8,128)(2,1)S(1)}, u32[]{:S(2)}, u32[]{:S(2)}) %collective-permute-start.16) | collective-permute-done | bytes 131104 | tf_op jit(solution)/shard_map/ppermute | solution.py:16
  48.0 0.7 shard_map.76.weights_ref
  48.7 0.8 shard_map.79
  49.5 6.0 %collective-permute-start.21 = (bf16[96,512]{1,0:T(8,128)(2,1)S(1)}, bf16[96,512]{1,0:T(8,128)(2,1)S(1)}, u32[]{:S(2)}, u32[]{:S(2)}) collective-permute-start(bf16[96,512]{1,0:T(8,128)(2,1)S(1)} %get-tuple-element.75), channel_id=1, source_target_pairs={{0,1},{1,0},{2,3},{3,2},{4,5},{5,4},{6,7},{7,6},{8,9},{9,8},{10,11... | collective-permute-start | bytes 294920 | tf_op jit(solution)/shard_map/ppermute | solution.py:16
  56.2 1.8 %collective-permute-start.23 = (bf16[96,512]{1,0:T(8,128)(2,1)S(1)}, bf16[96,512]{1,0:T(8,128)(2,1)S(1)}, u32[]{:S(2)}, u32[]{:S(2)}) collective-permute-start(bf16[96,512]{1,0:T(8,128)(2,1)S(1)} %get-tuple-element.77), channel_id=1, source_target_pairs={{0,3},{1,2},{2,1},{3,0},{4,7},{5,6},{6,5},{7,4},{8,11},{9,10},{10,... | collective-permute-start | bytes 294920 | tf_op jit(solution)/shard_map/ppermute | solution.py:16
  58.0 0.7 collective-permute-done.21
  58.7 7.4 %collective-permute-done.22 = bf16[96,512]{1,0:T(8,128)(2,1)S(1)} collective-permute-done((bf16[96,512]{1,0:T(8,128)(2,1)S(1)}, bf16[96,512]{1,0:T(8,128)(2,1)S(1)}, u32[]{:S(2)}, u32[]{:S(2)}) %collective-permute-start.22) | collective-permute-done | bytes 98336 | tf_op jit(solution)/shard_map/ppermute | solution.py:16
  66.8 1.1 collective-permute-done.24.refs_3_
  68.0 4.4 %shard_map.80.hidden_ref = bf16[512,2688]{1,0:T(8,128)(2,1)S(1)} custom-call(s32[2]{0:T(128)S(1)} %pad_add_fusion.1.me_ref, s32[4,1,384]{2,1,0:T(1,128)S(1)} %get-tuple-element.81.slot_ref, bf16[384,512]{1,0:T(8,128)(2,1)S(1)} %constant_dynamic-update-slice_fusion.refs_0_, bf16[384,512]{1,0:T(8,128)(2,1)S(1)} %collective-permute-done.20.refs_1_, ...), custom_call_target="tpu_custom_call" | custom-call | flops 2818572288 | bytes 9836544 | tf_op jit(solution)/shard_map/pallas_call | solution.py:30
  72.4 4.5 %shard_map.81 = (bf16[384,1024]{1,0:T(8,128)(2,1)S(1)}, bf16[384,1024]{1,0:T(8,128)(2,1)S(1)}) custom-call(s32[2]{0:T(128)S(1)} %pad_add_fusion.1.me_ref, s32[4,1,384]{2,1,0:T(1,128)S(1)} %get-tuple-element.81.slot_ref, f32[4,1,384]{2,1,0:T(1,128)S(1)} %get-tuple-element.58.weight_ref, bf16[512,2688]{1,0:T(8,128)(2,1)S(1)} %shard_map.80.hidden_ref, ...), custom_call_target="tpu_custom_call" | custom-call | flops 2818572288 | bytes 9842688 | tf_op jit(solution)/shard_map/pallas_call | solution.py:30
  76.9 0.9 collective-permute-done.26.refs_2_
  77.8 1.7 %collective-permute-done.27.refs_3_ = bf16[384,512]{1,0:T(8,128)(2,1)S(1)} collective-permute-done((bf16[384,512]{1,0:T(8,128)(2,1)S(1)}, bf16[384,512]{1,0:T(8,128)(2,1)S(1)}, u32[]{:S(2)}, u32[]{:S(2)}) %collective-permute-start.27) | collective-permute-done | bytes 393248 | tf_op jit(solution)/shard_map/ppermute | solution.py:16
  79.5 4.4 %shard_map.82.hidden_ref = bf16[512,2688]{1,0:T(8,128)(2,1)S(1)} custom-call(s32[2]{0:T(128)S(1)} %pad_add_fusion.1.me_ref, s32[4,1,384]{2,1,0:T(1,128)S(1)} %get-tuple-element.81.slot_ref, bf16[384,512]{1,0:T(8,128)(2,1)S(1)} %collective-permute-done.18.refs_0_, bf16[384,512]{1,0:T(8,128)(2,1)S(1)} %collective-permute-done.19.refs_1_, ...), custom_call_target="tpu_custom_call" | custom-call | flops 1 | bytes 1 | tf_op jit(solution)/shard_map/pallas_call | solution.py:30
  83.9 2.7 %shard_map.83 = bf16[384,1024]{1,0:T(8,128)(2,1)S(1)} custom-call(s32[2]{0:T(128)S(1)} %pad_add_fusion.1.me_ref, s32[4,1,384]{2,1,0:T(1,128)S(1)} %get-tuple-element.81.slot_ref, f32[4,1,384]{2,1,0:T(1,128)S(1)} %get-tuple-element.58.weight_ref, bf16[512,2688]{1,0:T(8,128)(2,1)S(1)} %shard_map.82.hidden_ref, bf16[2688,1024]{1,0:T(8,128)(2,1)S(1)} %bitcast.9), custom_call_target="tpu_custom_call" | custom-call | flops 1 | bytes 1 | tf_op jit(solution)/shard_map/pallas_call | solution.py:30
  87.1 2.6 %shard_map.84.refs_0_ = bf16[384,1024]{1,0:T(8,128)(2,1)S(1)} custom-call(s32[2]{0:T(128)S(1)} %pad_add_fusion.1.me_ref, s32[4,1,384]{2,1,0:T(1,128)S(1)} %get-tuple-element.81.slot_ref, f32[4,1,384]{2,1,0:T(1,128)S(1)} %get-tuple-element.58.weight_ref, bf16[512,2688]{1,0:T(8,128)(2,1)S(1)} %shard_map.82.hidden_ref, bf16[2688,1024]{1,0:T(8,128)(2,1)S(1)} %bitcast.10), custom_call_target="tpu_custom_call" | custom-call | flops 1 | bytes 1 | tf_op jit(solution)/shard_map/pallas_call | solution.py:30
  89.8 0.7 shard_map.85
  91.1 1.5 %collective-permute-start.31 = (bf16[384,512]{1,0:T(8,128)(2,1)S(1)}, bf16[384,512]{1,0:T(8,128)(2,1)S(1)}, u32[]{:S(2)}, u32[]{:S(2)}) collective-permute-start(bf16[384,512]{1,0:T(8,128)(2,1)S(1)} %get-tuple-element.85), channel_id=1, source_target_pairs={{0,8},{4,12},{8,0},{12,4},{1,9},{5,13},{9,1},{13,5},{2,10},{6,14},... | collective-permute-start | bytes 1179656 | tf_op jit(solution)/shard_map/ppermute | solution.py:16
  92.6 9.9 %collective-permute-done.29.refs_2_ = bf16[384,512]{1,0:T(8,128)(2,1)S(1)} collective-permute-done((bf16[384,512]{1,0:T(8,128)(2,1)S(1)}, bf16[384,512]{1,0:T(8,128)(2,1)S(1)}, u32[]{:S(2)}, u32[]{:S(2)}) %collective-permute-start.29) | collective-permute-done | bytes 393248 | tf_op jit(solution)/shard_map/ppermute | solution.py:16
  102.5 0.7 shard_map.86
  103.2 1.8 %collective-permute-start.30 = (bf16[96,512]{1,0:T(8,128)(2,1)S(1)}, bf16[96,512]{1,0:T(8,128)(2,1)S(1)}, u32[]{:S(2)}, u32[]{:S(2)}) collective-permute-start(bf16[96,512]{1,0:T(8,128)(2,1)S(1)} %get-tuple-element.83), channel_id=1, source_target_pairs={{0,1},{1,0},{2,3},{3,2},{4,5},{5,4},{6,7},{7,6},{8,9},{9,8},{10,11... | collective-permute-start | bytes 294920 | tf_op jit(solution)/shard_map/ppermute | solution.py:16
  105.1 0.7 collective-permute-start.32
  105.8 1.9 %collective-permute-start.33 = (bf16[96,512]{1,0:T(8,128)(2,1)S(1)}, bf16[96,512]{1,0:T(8,128)(2,1)S(1)}, u32[]{:S(2)}, u32[]{:S(2)}) collective-permute-start(bf16[96,512]{1,0:T(8,128)(2,1)S(1)} %get-tuple-element.90), channel_id=1, source_target_pairs={{0,3},{1,2},{2,1},{3,0},{4,7},{5,6},{6,5},{7,4},{8,11},{9,10},{10,... | collective-permute-start | bytes 294920 | tf_op jit(solution)/shard_map/ppermute | solution.py:16
  108.3 1.8 %collective-permute-done.31.refs_2_ = bf16[384,512]{1,0:T(8,128)(2,1)S(1)} collective-permute-done((bf16[384,512]{1,0:T(8,128)(2,1)S(1)}, bf16[384,512]{1,0:T(8,128)(2,1)S(1)}, u32[]{:S(2)}, u32[]{:S(2)}) %collective-permute-start.31) | collective-permute-done | bytes 393248 | tf_op jit(solution)/shard_map/ppermute | solution.py:16
  110.2 0.7 shard_map.87
  110.9 3.2 %collective-permute-done.32.refs_2_ = bf16[96,512]{1,0:T(8,128)(2,1)S(1)} collective-permute-done((bf16[96,512]{1,0:T(8,128)(2,1)S(1)}, bf16[96,512]{1,0:T(8,128)(2,1)S(1)}, u32[]{:S(2)}, u32[]{:S(2)}) %collective-permute-start.32) | collective-permute-done | bytes 98336 | tf_op jit(solution)/shard_map/ppermute | solution.py:16
  114.1 0.9 shard_map.88.refs_0_
  114.9 2.3 %collective-permute-start.35 = (bf16[128,512]{1,0:T(8,128)(2,1)S(1)}, bf16[128,512]{1,0:T(8,128)(2,1)S(1)}, u32[]{:S(2)}, u32[]{:S(2)}) collective-permute-start(bf16[128,512]{1,0:T(8,128)(2,1)S(1)} %shard_map.88.refs_0_), channel_id=1, source_target_pairs={{0,2},{1,3},{2,0},{3,1},{4,6},{5,7},{6,4},{7,5},{8,10},{9,11},{10,... | collective-permute-start | bytes 393224 | tf_op jit(solution)/shard_map/ppermute | solution.py:16
  117.5 1.8 %collective-permute-start.36 = (bf16[96,512]{1,0:T(8,128)(2,1)S(1)}, bf16[96,512]{1,0:T(8,128)(2,1)S(1)}, u32[]{:S(2)}, u32[]{:S(2)}) collective-permute-start(bf16[96,512]{1,0:T(8,128)(2,1)S(1)} %get-tuple-element.92), channel_id=1, source_target_pairs={{0,1},{1,0},{2,3},{3,2},{4,5},{5,4},{6,7},{7,6},{8,9},{9,8},{10,11... | collective-permute-start | bytes 294920 | tf_op jit(solution)/shard_map/ppermute | solution.py:16
  119.2 0.7 collective-permute-start.37
  120.0 1.9 %collective-permute-start.38 = (bf16[96,512]{1,0:T(8,128)(2,1)S(1)}, bf16[96,512]{1,0:T(8,128)(2,1)S(1)}, u32[]{:S(2)}, u32[]{:S(2)}) collective-permute-start(bf16[96,512]{1,0:T(8,128)(2,1)S(1)} %get-tuple-element.94), channel_id=1, source_target_pairs={{0,3},{1,2},{2,1},{3,0},{4,7},{5,6},{6,5},{7,4},{8,11},{9,10},{10,... | collective-permute-start | bytes 294920 | tf_op jit(solution)/shard_map/ppermute | solution.py:16
  121.9 1.7 %collective-permute-done.35.refs_2_ = bf16[128,512]{1,0:T(8,128)(2,1)S(1)} collective-permute-done((bf16[128,512]{1,0:T(8,128)(2,1)S(1)}, bf16[128,512]{1,0:T(8,128)(2,1)S(1)}, u32[]{:S(2)}, u32[]{:S(2)}) %collective-permute-start.35) | collective-permute-done | bytes 131104 | tf_op jit(solution)/shard_map/ppermute | solution.py:16
  123.6 2.2 %collective-permute-done.34.refs_1_ = bf16[128,512]{1,0:T(8,128)(2,1)S(1)} collective-permute-done((bf16[128,512]{1,0:T(8,128)(2,1)S(1)}, bf16[128,512]{1,0:T(8,128)(2,1)S(1)}, u32[]{:S(2)}, u32[]{:S(2)}) %collective-permute-start.34) | collective-permute-done | bytes 131104 | tf_op jit(solution)/shard_map/ppermute | solution.py:16
  125.8 1.9 %collective-permute-done.36.refs_1_ = bf16[96,512]{1,0:T(8,128)(2,1)S(1)} collective-permute-done((bf16[96,512]{1,0:T(8,128)(2,1)S(1)}, bf16[96,512]{1,0:T(8,128)(2,1)S(1)}, u32[]{:S(2)}, u32[]{:S(2)}) %collective-permute-start.36) | collective-permute-done | bytes 98336 | tf_op jit(solution)/shard_map/ppermute | solution.py:16
  127.7 3.1 %collective-permute-done.38.refs_3_ = bf16[96,512]{1,0:T(8,128)(2,1)S(1)} collective-permute-done((bf16[96,512]{1,0:T(8,128)(2,1)S(1)}, bf16[96,512]{1,0:T(8,128)(2,1)S(1)}, u32[]{:S(2)}, u32[]{:S(2)}) %collective-permute-start.38) | collective-permute-done | bytes 98336 | tf_op jit(solution)/shard_map/ppermute | solution.py:16
  130.8 0.9 shard_map.89.refs_0_
  131.7 1.8 %collective-permute-start.40 = (bf16[128,512]{1,0:T(8,128)(2,1)S(1)}, bf16[128,512]{1,0:T(8,128)(2,1)S(1)}, u32[]{:S(2)}, u32[]{:S(2)}) collective-permute-start(bf16[128,512]{1,0:T(8,128)(2,1)S(1)} %shard_map.89.refs_0_), channel_id=1, source_target_pairs={{0,2},{1,3},{2,0},{3,1},{4,6},{5,7},{6,4},{7,5},{8,10},{9,11},{10,... | collective-permute-start | bytes 393224 | tf_op jit(solution)/shard_map/ppermute | solution.py:16
  133.5 0.9 collective-permute-start.42
  134.4 1.2 collective-permute-start.39
  135.5 3.6 %collective-permute-done.40.refs_2_ = bf16[128,512]{1,0:T(8,128)(2,1)S(1)} collective-permute-done((bf16[128,512]{1,0:T(8,128)(2,1)S(1)}, bf16[128,512]{1,0:T(8,128)(2,1)S(1)}, u32[]{:S(2)}, u32[]{:S(2)}) %collective-permute-start.40) | collective-permute-done | bytes 131104 | tf_op jit(solution)/shard_map/ppermute | solution.py:16
  139.3 1.3 collective-permute-done.42.refs_3_
  140.6 1.3 shard_map.90.refs_4_
  141.8 0.9 collective-permute-done.39.refs_1_
  142.8 1.4 collective-permute-done.41.refs_3_
  144.2 2.3 %shard_map.91 = bf16[512,1024]{1,0:T(8,128)(2,1)} custom-call(s32[2]{0:T(128)S(1)} %pad_add_fusion.1.me_ref, bf16[1024,1024]{1,0:T(8,128)(2,1)S(1)} %shard_map.76.weights_ref, bf16[128,512]{1,0:T(8,128)(2,1)S(1)} %shard_map.89.refs_0_, bf16[128,512]{1,0:T(8,128)(2,1)S(1)} %collective-permute-done.39.refs_1_, ...), custom_call_target="tpu_custom_call" | custom-call | flops 536870912 | bytes 5767168 | tf_op jit(solution)/shard_map/pallas_call | solution.py:30
  (66 shorter events, 7.3 us)
Async XLA Ops:
  0.0 3.0 %collective-permute-start.2 = (bf16[256,1024]{1,0:T(8,128)(2,1)}, bf16[256,1024]{1,0:T(8,128)(2,1)S(1)}, u32[]{:S(2)}, u32[]{:S(2)}) collective-permute-start(bf16[256,1024]{1,0:T(8,128)(2,1)} %refs_0_.2), channel_id=1, source_target_pairs={{0,4},{4,0},{8,12},{12,8},{1,5},{5,1},{9,13},{13,9},{2,6},{6,2},{1... | collective-permute-start | bytes 1572872 | tf_op jit(solution)/shard_map/ppermute | solution.py:16
  0.5 22.3 %collective-permute-start.1 = (bf16[256,1024]{1,0:T(8,128)(2,1)}, bf16[256,1024]{1,0:T(8,128)(2,1)S(1)}, u32[]{:S(2)}, u32[]{:S(2)}) collective-permute-start(bf16[256,1024]{1,0:T(8,128)(2,1)} %refs_0_.2), channel_id=1, source_target_pairs={{0,8},{4,12},{8,0},{12,4},{1,9},{5,13},{9,1},{13,5},{2,10},{6,14},... | collective-permute-start | bytes 1572872 | tf_op jit(solution)/shard_map/ppermute | solution.py:16
  3.0 1.2 copy-start.1
  4.3 1.0 copy-start.2
  5.3 39.9 %copy-start.3 = (bf16[256,1024]{1,0:T(8,128)(2,1)S(1)}, bf16[256,1024]{1,0:T(8,128)(2,1)}, u32[]{:S(2)}) copy-start(bf16[256,1024]{1,0:T(8,128)(2,1)} %refs_0_.3) | copy-start | bytes 1572868
  6.7 16.1 %collective-permute-start.3 = (bf16[128,512]{1,0:T(8,128)(2,1)S(1)}, bf16[128,512]{1,0:T(8,128)(2,1)S(1)}, u32[]{:S(2)}, u32[]{:S(2)}) collective-permute-start(bf16[128,512]{1,0:T(8,128)(2,1)S(1)} %get-tuple-element.51), channel_id=1, source_target_pairs={{0,1},{1,0},{2,3},{3,2},{4,5},{5,4},{6,7},{7,6},{8,9},{9,8},{10,11... | collective-permute-start | bytes 393224 | tf_op jit(solution)/shard_map/ppermute | solution.py:16
  8.9 13.9 %collective-permute-start.4 = (bf16[128,512]{1,0:T(8,128)(2,1)S(1)}, bf16[128,512]{1,0:T(8,128)(2,1)S(1)}, u32[]{:S(2)}, u32[]{:S(2)}) collective-permute-start(bf16[128,512]{1,0:T(8,128)(2,1)S(1)} %get-tuple-element.52), channel_id=1, source_target_pairs={{0,2},{1,3},{2,0},{3,1},{4,6},{5,7},{6,4},{7,5},{8,10},{9,11},{10,... | collective-permute-start | bytes 393224 | tf_op jit(solution)/shard_map/ppermute | solution.py:16
  11.5 11.3 %collective-permute-start.5 = (bf16[128,512]{1,0:T(8,128)(2,1)S(1)}, bf16[128,512]{1,0:T(8,128)(2,1)S(1)}, u32[]{:S(2)}, u32[]{:S(2)}) collective-permute-start(bf16[128,512]{1,0:T(8,128)(2,1)S(1)} %get-tuple-element.53), channel_id=1, source_target_pairs={{0,3},{1,2},{2,1},{3,0},{4,7},{5,6},{6,5},{7,4},{8,11},{9,10},{10,... | collective-permute-start | bytes 393224 | tf_op jit(solution)/shard_map/ppermute | solution.py:16
  12.2 4.2 %collective-permute-start.7 = (s32[12,512]{1,0:T(8,128)S(1)}, s32[12,512]{1,0:T(8,128)S(1)}, u32[]{:S(2)}, u32[]{:S(2)}) collective-permute-start(s32[12,512]{1,0:T(8,128)S(1)} %pad_add_fusion.refs_0_), channel_id=1, source_target_pairs={{0,8},{4,12},{8,0},{12,4},{1,9},{5,13},{9,1},{13,5},{2,10},{6,14},... | collective-permute-start | bytes 73736 | tf_op jit(solution)/shard_map/ppermute | solution.py:16
  16.5 1.2 collective-permute-start.6
  17.7 1.6 %collective-permute-start.8 = (s32[12,512]{1,0:T(8,128)S(1)}, s32[12,512]{1,0:T(8,128)S(1)}, u32[]{:S(2)}, u32[]{:S(2)}) collective-permute-start(s32[12,512]{1,0:T(8,128)S(1)} %collective-permute-done.7.refs_2_), channel_id=1, source_target_pairs={{0,4},{4,0},{8,12},{12,8},{1,5},{5,1},{9,13},{13,9},{2,6},{6,2},{1... | collective-permute-start | bytes 73736 | tf_op jit(solution)/shard_map/ppermute | solution.py:16
  17.8 0.7 copy-start.4
  22.8 7.2 %collective-permute-start.14 = (bf16[256,1024]{1,0:T(8,128)(2,1)S(1)}, bf16[256,1024]{1,0:T(8,128)(2,1)S(1)}, u32[]{:S(2)}, u32[]{:S(2)}) collective-permute-start(bf16[256,1024]{1,0:T(8,128)(2,1)S(1)} %collective-permute-done.1.refs_0_), channel_id=1, source_target_pairs={{0,4},{4,0},{8,12},{12,8},{1,5},{5,1},{9,13},{13,9},{2,6},{6,2},{1... | collective-permute-start | bytes 1572872 | tf_op jit(solution)/shard_map/ppermute | solution.py:16
  23.3 22.0 %collective-permute-start.9 = (bf16[256,1024]{1,0:T(8,128)(2,1)}, bf16[256,1024]{1,0:T(8,128)(2,1)S(1)}, u32[]{:S(2)}, u32[]{:S(2)}) collective-permute-start(bf16[256,1024]{1,0:T(8,128)(2,1)} %refs_0_.3), channel_id=1, source_target_pairs={{0,8},{4,12},{8,0},{12,4},{1,9},{5,13},{9,1},{13,5},{2,10},{6,14},... | collective-permute-start | bytes 1572872 | tf_op jit(solution)/shard_map/ppermute | solution.py:16
  25.8 6.9 %collective-permute-start.11 = (bf16[96,512]{1,0:T(8,128)(2,1)S(1)}, bf16[96,512]{1,0:T(8,128)(2,1)S(1)}, u32[]{:S(2)}, u32[]{:S(2)}) collective-permute-start(bf16[96,512]{1,0:T(8,128)(2,1)S(1)} %get-tuple-element.60), channel_id=1, source_target_pairs={{0,1},{1,0},{2,3},{3,2},{4,5},{5,4},{6,7},{7,6},{8,9},{9,8},{10,11... | collective-permute-start | bytes 294920 | tf_op jit(solution)/shard_map/ppermute | solution.py:16
  27.5 9.2 %collective-permute-start.12 = (bf16[96,512]{1,0:T(8,128)(2,1)S(1)}, bf16[96,512]{1,0:T(8,128)(2,1)S(1)}, u32[]{:S(2)}, u32[]{:S(2)}) collective-permute-start(bf16[96,512]{1,0:T(8,128)(2,1)S(1)} %get-tuple-element.61), channel_id=1, source_target_pairs={{0,2},{1,3},{2,0},{3,1},{4,6},{5,7},{6,4},{7,5},{8,10},{9,11},{10,... | collective-permute-start | bytes 294920 | tf_op jit(solution)/shard_map/ppermute | solution.py:16
  32.0 13.8 %collective-permute-start.15 = (bf16[128,512]{1,0:T(8,128)(2,1)S(1)}, bf16[128,512]{1,0:T(8,128)(2,1)S(1)}, u32[]{:S(2)}, u32[]{:S(2)}) collective-permute-start(bf16[128,512]{1,0:T(8,128)(2,1)S(1)} %get-tuple-element.65), channel_id=1, source_target_pairs={{0,1},{1,0},{2,3},{3,2},{4,5},{5,4},{6,7},{7,6},{8,9},{9,8},{10,11... | collective-permute-start | bytes 393224 | tf_op jit(solution)/shard_map/ppermute | solution.py:16
  32.4 14.9 %collective-permute-start.16 = (bf16[128,512]{1,0:T(8,128)(2,1)S(1)}, bf16[128,512]{1,0:T(8,128)(2,1)S(1)}, u32[]{:S(2)}, u32[]{:S(2)}) collective-permute-start(bf16[128,512]{1,0:T(8,128)(2,1)S(1)} %get-tuple-element.66), channel_id=1, source_target_pairs={{0,2},{1,3},{2,0},{3,1},{4,6},{5,7},{6,4},{7,5},{8,10},{9,11},{10,... | collective-permute-start | bytes 393224 | tf_op jit(solution)/shard_map/ppermute | solution.py:16
  32.8 14.6 %collective-permute-start.17 = (bf16[128,512]{1,0:T(8,128)(2,1)S(1)}, bf16[128,512]{1,0:T(8,128)(2,1)S(1)}, u32[]{:S(2)}, u32[]{:S(2)}) collective-permute-start(bf16[128,512]{1,0:T(8,128)(2,1)S(1)} %get-tuple-element.67), channel_id=1, source_target_pairs={{0,3},{1,2},{2,1},{3,0},{4,7},{5,6},{6,5},{7,4},{8,11},{9,10},{10,... | collective-permute-start | bytes 393224 | tf_op jit(solution)/shard_map/ppermute | solution.py:16
  36.7 8.6 %collective-permute-start.13 = (bf16[96,512]{1,0:T(8,128)(2,1)S(1)}, bf16[96,512]{1,0:T(8,128)(2,1)S(1)}, u32[]{:S(2)}, u32[]{:S(2)}) collective-permute-start(bf16[96,512]{1,0:T(8,128)(2,1)S(1)} %get-tuple-element.62), channel_id=1, source_target_pairs={{0,3},{1,2},{2,1},{3,0},{4,7},{5,6},{6,5},{7,4},{8,11},{9,10},{10,... | collective-permute-start | bytes 294920 | tf_op jit(solution)/shard_map/ppermute | solution.py:16
  45.3 2.7 %collective-permute-start = (bf16[256,1024]{1,0:T(8,128)(2,1)S(1)}, bf16[256,1024]{1,0:T(8,128)(2,1)S(1)}, u32[]{:S(2)}, u32[]{:S(2)}) collective-permute-start(bf16[256,1024]{1,0:T(8,128)(2,1)S(1)} %copy-done.3), channel_id=1, source_target_pairs={{0,4},{4,0},{8,12},{12,8},{1,5},{5,1},{9,13},{13,9},{2,6},{6,2},{1... | collective-permute-start | bytes 1572872 | tf_op jit(solution)/shard_map/ppermute | solution.py:16
  45.3 2.7 %collective-permute-start.10 = (bf16[256,1024]{1,0:T(8,128)(2,1)S(1)}, bf16[256,1024]{1,0:T(8,128)(2,1)S(1)}, u32[]{:S(2)}, u32[]{:S(2)}) collective-permute-start(bf16[256,1024]{1,0:T(8,128)(2,1)S(1)} %collective-permute-done.9.refs_2_), channel_id=1, source_target_pairs={{0,4},{4,0},{8,12},{12,8},{1,5},{5,1},{9,13},{13,9},{2,6},{6,2},{1... | collective-permute-start | bytes 1572872 | tf_op jit(solution)/shard_map/ppermute | solution.py:16
  47.4 20.6 %copy-start = (bf16[1,1024,2688]{2,1,0:T(8,128)(2,1)S(1)}, bf16[1,1024,2688]{2,1,0:T(8,128)(2,1)}, u32[]{:S(2)}) copy-start(bf16[1,1024,2688]{2,1,0:T(8,128)(2,1)} %param.10) | copy-start | bytes 16515076
  47.4 10.6 %collective-permute-start.18 = (bf16[384,512]{1,0:T(8,128)(2,1)S(1)}, bf16[384,512]{1,0:T(8,128)(2,1)S(1)}, u32[]{:S(2)}, u32[]{:S(2)}) collective-permute-start(bf16[384,512]{1,0:T(8,128)(2,1)S(1)} %constant_dynamic-update-slice_fusion.refs_0_), channel_id=1, source_target_pairs={{0,8},{4,12},{8,0},{12,4},{1,9},{5,13},{9,1},{13,5},{2,10},{6,14},... | collective-permute-start | bytes 1179656 | tf_op jit(solution)/shard_map/ppermute | solution.py:16
  48.0 18.8 %collective-permute-start.20 = (bf16[384,512]{1,0:T(8,128)(2,1)S(1)}, bf16[384,512]{1,0:T(8,128)(2,1)S(1)}, u32[]{:S(2)}, u32[]{:S(2)}) collective-permute-start(bf16[384,512]{1,0:T(8,128)(2,1)S(1)} %constant_dynamic-update-slice_fusion.refs_0_), channel_id=1, source_target_pairs={{0,4},{4,0},{8,12},{12,8},{1,5},{5,1},{9,13},{13,9},{2,6},{6,2},{1... | collective-permute-start | bytes 1179656 | tf_op jit(solution)/shard_map/ppermute | solution.py:16
  49.5 9.2 %collective-permute-start.21 = (bf16[96,512]{1,0:T(8,128)(2,1)S(1)}, bf16[96,512]{1,0:T(8,128)(2,1)S(1)}, u32[]{:S(2)}, u32[]{:S(2)}) collective-permute-start(bf16[96,512]{1,0:T(8,128)(2,1)S(1)} %get-tuple-element.75), channel_id=1, source_target_pairs={{0,1},{1,0},{2,3},{3,2},{4,5},{5,4},{6,7},{7,6},{8,9},{9,8},{10,11... | collective-permute-start | bytes 294920 | tf_op jit(solution)/shard_map/ppermute | solution.py:16
  55.6 10.6 %collective-permute-start.22 = (bf16[96,512]{1,0:T(8,128)(2,1)S(1)}, bf16[96,512]{1,0:T(8,128)(2,1)S(1)}, u32[]{:S(2)}, u32[]{:S(2)}) collective-permute-start(bf16[96,512]{1,0:T(8,128)(2,1)S(1)} %get-tuple-element.76), channel_id=1, source_target_pairs={{0,2},{1,3},{2,0},{3,1},{4,6},{5,7},{6,4},{7,5},{8,10},{9,11},{10,... | collective-permute-start | bytes 294920 | tf_op jit(solution)/shard_map/ppermute | solution.py:16
  56.2 10.0 %collective-permute-start.23 = (bf16[96,512]{1,0:T(8,128)(2,1)S(1)}, bf16[96,512]{1,0:T(8,128)(2,1)S(1)}, u32[]{:S(2)}, u32[]{:S(2)}) collective-permute-start(bf16[96,512]{1,0:T(8,128)(2,1)S(1)} %get-tuple-element.77), channel_id=1, source_target_pairs={{0,3},{1,2},{2,1},{3,0},{4,7},{5,6},{6,5},{7,4},{8,11},{9,10},{10,... | collective-permute-start | bytes 294920 | tf_op jit(solution)/shard_map/ppermute | solution.py:16
  58.0 8.8 %collective-permute-start.19 = (bf16[384,512]{1,0:T(8,128)(2,1)S(1)}, bf16[384,512]{1,0:T(8,128)(2,1)S(1)}, u32[]{:S(2)}, u32[]{:S(2)}) collective-permute-start(bf16[384,512]{1,0:T(8,128)(2,1)S(1)} %collective-permute-done.18.refs_0_), channel_id=1, source_target_pairs={{0,4},{4,0},{8,12},{12,8},{1,5},{5,1},{9,13},{13,9},{2,6},{6,2},{1... | collective-permute-start | bytes 1179656 | tf_op jit(solution)/shard_map/ppermute | solution.py:16
  66.1 6.2 %slice-start = ((s8[5505024]{0:T(1024)(128)(4,1)}), s8[4194304]{0:T(1024)(128)(4,1)S(1)}, s32[]{:S(2)}) async-start(s8[5505024]{0:T(1024)(128)(4,1)} %bitcast.6), calls=%async_computation | async-start | bytes 8388608
  66.2 1.8 %collective-permute-start.24 = (bf16[384,512]{1,0:T(8,128)(2,1)S(1)}, bf16[384,512]{1,0:T(8,128)(2,1)S(1)}, u32[]{:S(2)}, u32[]{:S(2)}) collective-permute-start(bf16[384,512]{1,0:T(8,128)(2,1)S(1)} %constant_dynamic-update-slice_fusion.4.refs_2_), channel_id=1, source_target_pairs={{0,4},{4,0},{8,12},{12,8},{1,5},{5,1},{9,13},{13,9},{2,6},{6,2},{1... | collective-permute-start | bytes 1179656 | tf_op jit(solution)/shard_map/ppermute | solution.py:16
  66.2 11.5 %collective-permute-start.26 = (bf16[384,512]{1,0:T(8,128)(2,1)S(1)}, bf16[384,512]{1,0:T(8,128)(2,1)S(1)}, u32[]{:S(2)}, u32[]{:S(2)}) collective-permute-start(bf16[384,512]{1,0:T(8,128)(2,1)S(1)} %constant_dynamic-update-slice_fusion.4.refs_2_), channel_id=1, source_target_pairs={{0,8},{4,12},{8,0},{12,4},{1,9},{5,13},{9,1},{13,5},{2,10},{6,14},... | collective-permute-start | bytes 1179656 | tf_op jit(solution)/shard_map/ppermute | solution.py:16
  68.0 4.4 %slice-start.1 = ((s8[5505024]{0:T(1024)(128)(4,1)}), s8[1310720]{0:T(1024)(128)(4,1)S(1)}, s32[]{:S(2)}) async-start(s8[5505024]{0:T(1024)(128)(4,1)} %bitcast.6), calls=%async_computation.1 | async-start | bytes 2621440
  77.8 1.7 %collective-permute-start.27 = (bf16[384,512]{1,0:T(8,128)(2,1)S(1)}, bf16[384,512]{1,0:T(8,128)(2,1)S(1)}, u32[]{:S(2)}, u32[]{:S(2)}) collective-permute-start(bf16[384,512]{1,0:T(8,128)(2,1)S(1)} %collective-permute-done.26.refs_2_), channel_id=1, source_target_pairs={{0,4},{4,0},{8,12},{12,8},{1,5},{5,1},{9,13},{13,9},{2,6},{6,2},{1... | collective-permute-start | bytes 1179656 | tf_op jit(solution)/shard_map/ppermute | solution.py:16
  86.5 3.2 %collective-permute-start.28 = (bf16[384,1024]{1,0:T(8,128)(2,1)S(1)}, bf16[384,1024]{1,0:T(8,128)(2,1)S(1)}, u32[]{:S(2)}, u32[]{:S(2)}) collective-permute-start(bf16[384,1024]{1,0:T(8,128)(2,1)S(1)} %shard_map.83), channel_id=1, source_target_pairs={{0,4},{4,0},{8,12},{12,8},{1,5},{5,1},{9,13},{13,9},{2,6},{6,2},{1... | collective-permute-start | bytes 2359304 | tf_op jit(solution)/shard_map/ppermute | solution.py:16
  86.7 5.9 %collective-permute-start.25 = (bf16[384,1024]{1,0:T(8,128)(2,1)S(1)}, bf16[384,1024]{1,0:T(8,128)(2,1)S(1)}, u32[]{:S(2)}, u32[]{:S(2)}) collective-permute-start(bf16[384,1024]{1,0:T(8,128)(2,1)S(1)} %get-tuple-element.79), channel_id=1, source_target_pairs={{0,4},{4,0},{8,12},{12,8},{1,5},{5,1},{9,13},{13,9},{2,6},{6,2},{1... | collective-permute-start | bytes 2359304 | tf_op jit(solution)/shard_map/ppermute | solution.py:16
  90.5 12.0 %collective-permute-start.29 = (bf16[384,512]{1,0:T(8,128)(2,1)S(1)}, bf16[384,512]{1,0:T(8,128)(2,1)S(1)}, u32[]{:S(2)}, u32[]{:S(2)}) collective-permute-start(bf16[384,512]{1,0:T(8,128)(2,1)S(1)} %get-tuple-element.82), channel_id=1, source_target_pairs={{0,8},{4,12},{8,0},{12,4},{1,9},{5,13},{9,1},{13,5},{2,10},{6,14},... | collective-permute-start | bytes 1179656 | tf_op jit(solution)/shard_map/ppermute | solution.py:16
  91.1 19.1 %collective-permute-start.31 = (bf16[384,512]{1,0:T(8,128)(2,1)S(1)}, bf16[384,512]{1,0:T(8,128)(2,1)S(1)}, u32[]{:S(2)}, u32[]{:S(2)}) collective-permute-start(bf16[384,512]{1,0:T(8,128)(2,1)S(1)} %get-tuple-element.85), channel_id=1, source_target_pairs={{0,8},{4,12},{8,0},{12,4},{1,9},{5,13},{9,1},{13,5},{2,10},{6,14},... | collective-permute-start | bytes 1179656 | tf_op jit(solution)/shard_map/ppermute | solution.py:16
  103.2 5.1 %collective-permute-start.30 = (bf16[96,512]{1,0:T(8,128)(2,1)S(1)}, bf16[96,512]{1,0:T(8,128)(2,1)S(1)}, u32[]{:S(2)}, u32[]{:S(2)}) collective-permute-start(bf16[96,512]{1,0:T(8,128)(2,1)S(1)} %get-tuple-element.83), channel_id=1, source_target_pairs={{0,1},{1,0},{2,3},{3,2},{4,5},{5,4},{6,7},{7,6},{8,9},{9,8},{10,11... | collective-permute-start | bytes 294920 | tf_op jit(solution)/shard_map/ppermute | solution.py:16
  105.1 9.0 %collective-permute-start.32 = (bf16[96,512]{1,0:T(8,128)(2,1)S(1)}, bf16[96,512]{1,0:T(8,128)(2,1)S(1)}, u32[]{:S(2)}, u32[]{:S(2)}) collective-permute-start(bf16[96,512]{1,0:T(8,128)(2,1)S(1)} %get-tuple-element.89), channel_id=1, source_target_pairs={{0,2},{1,3},{2,0},{3,1},{4,6},{5,7},{6,4},{7,5},{8,10},{9,11},{10,... | collective-permute-start | bytes 294920 | tf_op jit(solution)/shard_map/ppermute | solution.py:16
  105.8 8.3 %collective-permute-start.33 = (bf16[96,512]{1,0:T(8,128)(2,1)S(1)}, bf16[96,512]{1,0:T(8,128)(2,1)S(1)}, u32[]{:S(2)}, u32[]{:S(2)}) collective-permute-start(bf16[96,512]{1,0:T(8,128)(2,1)S(1)} %get-tuple-element.90), channel_id=1, source_target_pairs={{0,3},{1,2},{2,1},{3,0},{4,7},{5,6},{6,5},{7,4},{8,11},{9,10},{10,... | collective-permute-start | bytes 294920 | tf_op jit(solution)/shard_map/ppermute | solution.py:16
  114.9 8.6 %collective-permute-start.35 = (bf16[128,512]{1,0:T(8,128)(2,1)S(1)}, bf16[128,512]{1,0:T(8,128)(2,1)S(1)}, u32[]{:S(2)}, u32[]{:S(2)}) collective-permute-start(bf16[128,512]{1,0:T(8,128)(2,1)S(1)} %shard_map.88.refs_0_), channel_id=1, source_target_pairs={{0,2},{1,3},{2,0},{3,1},{4,6},{5,7},{6,4},{7,5},{8,10},{9,11},{10,... | collective-permute-start | bytes 393224 | tf_op jit(solution)/shard_map/ppermute | solution.py:16
  117.2 8.6 %collective-permute-start.34 = (bf16[128,512]{1,0:T(8,128)(2,1)S(1)}, bf16[128,512]{1,0:T(8,128)(2,1)S(1)}, u32[]{:S(2)}, u32[]{:S(2)}) collective-permute-start(bf16[128,512]{1,0:T(8,128)(2,1)S(1)} %shard_map.88.refs_0_), channel_id=1, source_target_pairs={{0,1},{1,0},{2,3},{3,2},{4,5},{5,4},{6,7},{7,6},{8,9},{9,8},{10,11... | collective-permute-start | bytes 393224 | tf_op jit(solution)/shard_map/ppermute | solution.py:16
  117.5 10.2 %collective-permute-start.36 = (bf16[96,512]{1,0:T(8,128)(2,1)S(1)}, bf16[96,512]{1,0:T(8,128)(2,1)S(1)}, u32[]{:S(2)}, u32[]{:S(2)}) collective-permute-start(bf16[96,512]{1,0:T(8,128)(2,1)S(1)} %get-tuple-element.92), channel_id=1, source_target_pairs={{0,1},{1,0},{2,3},{3,2},{4,5},{5,4},{6,7},{7,6},{8,9},{9,8},{10,11... | collective-permute-start | bytes 294920 | tf_op jit(solution)/shard_map/ppermute | solution.py:16
  119.2 8.4 %collective-permute-start.37 = (bf16[96,512]{1,0:T(8,128)(2,1)S(1)}, bf16[96,512]{1,0:T(8,128)(2,1)S(1)}, u32[]{:S(2)}, u32[]{:S(2)}) collective-permute-start(bf16[96,512]{1,0:T(8,128)(2,1)S(1)} %get-tuple-element.93), channel_id=1, source_target_pairs={{0,2},{1,3},{2,0},{3,1},{4,6},{5,7},{6,4},{7,5},{8,10},{9,11},{10,... | collective-permute-start | bytes 294920 | tf_op jit(solution)/shard_map/ppermute | solution.py:16
  120.0 10.8 %collective-permute-start.38 = (bf16[96,512]{1,0:T(8,128)(2,1)S(1)}, bf16[96,512]{1,0:T(8,128)(2,1)S(1)}, u32[]{:S(2)}, u32[]{:S(2)}) collective-permute-start(bf16[96,512]{1,0:T(8,128)(2,1)S(1)} %get-tuple-element.94), channel_id=1, source_target_pairs={{0,3},{1,2},{2,1},{3,0},{4,7},{5,6},{6,5},{7,4},{8,11},{9,10},{10,... | collective-permute-start | bytes 294920 | tf_op jit(solution)/shard_map/ppermute | solution.py:16
  131.7 7.4 %collective-permute-start.40 = (bf16[128,512]{1,0:T(8,128)(2,1)S(1)}, bf16[128,512]{1,0:T(8,128)(2,1)S(1)}, u32[]{:S(2)}, u32[]{:S(2)}) collective-permute-start(bf16[128,512]{1,0:T(8,128)(2,1)S(1)} %shard_map.89.refs_0_), channel_id=1, source_target_pairs={{0,2},{1,3},{2,0},{3,1},{4,6},{5,7},{6,4},{7,5},{8,10},{9,11},{10,... | collective-permute-start | bytes 393224 | tf_op jit(solution)/shard_map/ppermute | solution.py:16
  133.5 7.1 %collective-permute-start.42 = (bf16[128,512]{1,0:T(8,128)(2,1)S(1)}, bf16[128,512]{1,0:T(8,128)(2,1)S(1)}, u32[]{:S(2)}, u32[]{:S(2)}) collective-permute-start(bf16[128,512]{1,0:T(8,128)(2,1)S(1)} %collective-permute-done.35.refs_2_), channel_id=1, source_target_pairs={{0,1},{1,0},{2,3},{3,2},{4,5},{5,4},{6,7},{7,6},{8,9},{9,8},{10,11... | collective-permute-start | bytes 393224 | tf_op jit(solution)/shard_map/ppermute | solution.py:16
  134.4 8.4 %collective-permute-start.39 = (bf16[128,512]{1,0:T(8,128)(2,1)S(1)}, bf16[128,512]{1,0:T(8,128)(2,1)S(1)}, u32[]{:S(2)}, u32[]{:S(2)}) collective-permute-start(bf16[128,512]{1,0:T(8,128)(2,1)S(1)} %shard_map.89.refs_0_), channel_id=1, source_target_pairs={{0,1},{1,0},{2,3},{3,2},{4,5},{5,4},{6,7},{7,6},{8,9},{9,8},{10,11... | collective-permute-start | bytes 393224 | tf_op jit(solution)/shard_map/ppermute | solution.py:16
  139.1 5.1 %collective-permute-start.41 = (bf16[128,512]{1,0:T(8,128)(2,1)S(1)}, bf16[128,512]{1,0:T(8,128)(2,1)S(1)}, u32[]{:S(2)}, u32[]{:S(2)}) collective-permute-start(bf16[128,512]{1,0:T(8,128)(2,1)S(1)} %collective-permute-done.40.refs_2_), channel_id=1, source_target_pairs={{0,1},{1,0},{2,3},{3,2},{4,5},{5,4},{6,7},{7,6},{8,9},{9,8},{10,11... | collective-permute-start | bytes 393224 | tf_op jit(solution)/shard_map/ppermute | solution.py:16

commit v4 on v3

--- a/solution.py
+++ b/solution.py
@@ -151,18 +151,15 @@
         hidden_ref[:, span] = jnp.square(jnp.maximum(hidden, 0.0)).astype(BF16)
 
 
-def down_kernel(sources, slots, tile, first, stride, me_ref, slot_ref, weight_ref, hidden_ref, down_ref, *refs):
-    outs, picked, scaled = refs[:-2], refs[-2], refs[-1]
+def down_kernel(sources, slots, tile, me_ref, slot_ref, weight_ref, hidden_ref, down_ref, *refs):
+    outs, scaled = refs[:-1], refs[-1]
     picks = [one_hot(slot_ref[r], slots) for r in sources]
     scale = jnp.concatenate(
         [jnp.sum(pick.astype(F32) * weight_ref[r], axis=1, keepdims=True) for pick, r in zip(picks, sources)], axis=0
     )
-    for i in range(len(sources)):
-        at = (first + i * stride) * slots
-        picked[i * slots : (i + 1) * slots, :] = hidden_ref[at : at + slots, :]
     for start in range(0, scaled.shape[1], tile):
         span = slice(start, start + tile)
-        result = jnp.dot(picked[...], down_ref[:, span], preferred_element_type=F32)
+        result = jnp.dot(hidden_ref[...], down_ref[:, span], preferred_element_type=F32)
         scaled[:, span] = (result * scale).astype(BF16)
         for i, out in enumerate(outs):
             out[:, span] = lax.dot_general(
@@ -269,7 +266,8 @@
         return cut, again
 
     def swap(cut):
-        return [cut[0]] + [hop(cut[k], "grp", k) for k in range(1, n_grp)]
+        far_first = [hop(cut[k], "grp", k) for k in range(n_grp - 1, 0, -1)]
+        return [cut[0], *far_first[::-1]]
 
     def choose(ranks, arrived):
         columns = arrived[0].shape[1]
@@ -297,7 +295,7 @@
     near_own = jnp.concatenate(pieces, axis=0)
     rows_out = [proj_out, hop(proj_out, "ep", 1)]
     for k in steps:
-        part = hop(after(proj_out, *rows_far), "ep", 2 * k)
+        part = hop(after(proj_out, *rows_far, chosen_near[0]), "ep", 2 * k)
         rows_out += [part, hop(part, "ep", 1)]
     [rows_out] = call(rows_kernel, me, rows_out, [shape((width, depth), BF16)])
     near = [near_own, hop(near_own, "ep", 1)]
@@ -320,30 +318,31 @@
             told=told,
         )[0]
 
-    def down(sources, hidden, first, stride, *deps, told=True):
+    def down(sources, hidden, *deps, told=True):
         n = len(sources) * slots
         return call(
-            functools.partial(down_kernel, sources, slots, width // 2, first, stride),
+            functools.partial(down_kernel, sources, slots, width // 2),
             me,
             [after(line_slot, *deps), line_weight, hidden, expert_down[0]],
             [shape((lines, width), BF16)] * len(sources),
-            [pltpu.VMEM((n, wide), BF16), pltpu.VMEM((n, width), BF16)],
+            [pltpu.VMEM((n, width), BF16)],
             flops=2 * n * width * wide,
             told=told,
         )
 
     here, there = list(range(2)), list(range(2, n_ep))
     hidden_here = up(here, *crossed_side)
-    local = down(here, hidden_here, 0, 1)
+    local = down(here, hidden_here)
     crossed_far = [after(part, *local) for part in crossed_far]
     local = [local[0], hop(local[1], "ep", 1)]
     for k in steps:
         near += [crossed_near[k - 1], crossed_side[k - 1]]
         far += [crossed_far[k - 1], hop(crossed_far[k - 1], "ep", 1)]
-    hidden_there = up(there, told=False)
-    odd = down(there[1::2], hidden_there, 1, 2, told=False)
+    hidden_even = up(there[::2])
+    hidden_odd = up(there[1::2], hidden_even, told=False)
+    odd = down(there[1::2], hidden_odd, told=False)
     other = [hop(part, "ep", 1) for part in odd]
-    even = down(there[::2], hidden_there, 0, 2, *odd, told=False)
+    even = down(there[::2], hidden_even, *odd, told=False)
     sums = call(add_kernel, me, [*even, *other], [shape((lines, width // 2), BF16)] * (2 * len(even)))
     half = width // 2
     returned = [[hop(sums[2 * k + h], "ep", 2 * k + 2) for k in range(len(even))] for h in range(2)]
@@ -353,8 +352,8 @@
         kernel = functools.partial(join_kernel, len(parts), h)
         return call(kernel, after(me, *arrived), parts, [shape((hits, half), BF16)] * n_grp)
 
-    def combine(ranks, arrived):
-        return call(combine_kernel, me, [ranks, *arrived], [shape((block, half), BF16)])[0]
+    def combine(ranks, arrived, flops=1):
+        return call(combine_kernel, me, [ranks, *arrived], [shape((block, half), BF16)], flops=flops)[0]
 
     def gather(latent_out):
         blocks = [latent_out]
@@ -375,7 +374,7 @@
 
     arrived = swap(join(0, ()))
     cut = join(1, arrived[1:2])
-    latent_out = combine(after(ranks, cut[0]), arrived)
+    latent_out = combine(after(ranks, cut[0]), arrived, flops=20 * 10**9)
     first = gather(latent_out)
     ranks = after(ranks, *(first[1 << i] for i in range(n_grp.bit_length() - 1)))
     second = gather(combine(ranks, swap(cut)))

time: 147 us -> 146 us (level)
    unnamed x20 -> x22, local copies, waits for them, and re-layouts: 3.05 us -> 2.34 us
    pallas_call x19 -> x20, Pallas kernels: 35.8 us -> 36.4 us  [call(): pl.pallas_call(kernel, out_shape=tuple(outs), in_specs=[pl.BlockSpec(memo...]
  transfers between devices with their start and end apart: 43 -> 43, of which waited for: 21 -> 21; matrix products, arithmetic and copies ran while one was open for 1% -> 0% of each run, Pallas kernels for 17% -> 19%
where the time goes in v4:
time: 146 us
  waiting for transfers between devices  55.3 us (38%)
  starting transfers between devices  51.7 us (35%)
  Pallas kernels  36.4 us (25%)
  local copies, waits for them, and re-layouts  2.36 us (2%)
    ppermute x43, waiting for transfers between devices, hop(): return lax.ppermute(x, axis, [(i, i ^ step) for i in range(count)])  55.3 us
    ppermute x43, starting transfers between devices, hop(): return lax.ppermute(x, axis, [(i, i ^ step) for i in range(count)])  51.7 us
    pallas_call x20, Pallas kernels, call(): pl.pallas_call(kernel, out_shape=tuple(outs), in_specs=[pl.BlockSpec(memo...  36.4 us
  transfers between devices with their start and end apart: 43, of which 21 were waited for; matrix products, arithmetic and copies ran while one was open for 0% of the time, Pallas kernels for 19%

profile of v4, /device:TPU:0, one launch (start us, length us, event | category | flops | bytes accessed | tf_op | source)
XLA Modules:
  0.0 146.2 jit_solution(10963187987186359582)
XLA Ops:
  0.5 2.6 %collective-permute-start.1 = (bf16[256,1024]{1,0:T(8,128)(2,1)}, bf16[256,1024]{1,0:T(8,128)(2,1)S(1)}, u32[]{:S(2)}, u32[]{:S(2)}) collective-permute-start(bf16[256,1024]{1,0:T(8,128)(2,1)} %refs_0_.2), channel_id=1, source_target_pairs={{0,8},{4,12},{8,0},{12,4},{1,9},{5,13},{9,1},{13,5},{2,10},{6,14},... | collective-permute-start | bytes 1572872 | tf_op jit(solution)/shard_map/ppermute | solution.py:16
  3.1 1.2 copy-done.1
  4.3 1.0 copy-done.2
  5.4 1.4 shard_map.73
  6.8 2.1 %collective-permute-start.3 = (bf16[128,512]{1,0:T(8,128)(2,1)S(1)}, bf16[128,512]{1,0:T(8,128)(2,1)S(1)}, u32[]{:S(2)}, u32[]{:S(2)}) collective-permute-start(bf16[128,512]{1,0:T(8,128)(2,1)S(1)} %get-tuple-element.52), channel_id=1, source_target_pairs={{0,1},{1,0},{2,3},{3,2},{4,5},{5,4},{6,7},{7,6},{8,9},{9,8},{10,11... | collective-permute-start | bytes 393224 | tf_op jit(solution)/shard_map/ppermute | solution.py:16
  8.9 2.6 %collective-permute-start.4 = (bf16[128,512]{1,0:T(8,128)(2,1)S(1)}, bf16[128,512]{1,0:T(8,128)(2,1)S(1)}, u32[]{:S(2)}, u32[]{:S(2)}) collective-permute-start(bf16[128,512]{1,0:T(8,128)(2,1)S(1)} %get-tuple-element.53), channel_id=1, source_target_pairs={{0,2},{1,3},{2,0},{3,1},{4,6},{5,7},{6,4},{7,5},{8,10},{9,11},{10,... | collective-permute-start | bytes 393224 | tf_op jit(solution)/shard_map/ppermute | solution.py:16
  11.5 1.8 %collective-permute-start.7 = (s32[12,512]{1,0:T(8,128)S(1)}, s32[12,512]{1,0:T(8,128)S(1)}, u32[]{:S(2)}, u32[]{:S(2)}) collective-permute-start(s32[12,512]{1,0:T(8,128)S(1)} %pad_add_fusion.refs_0_), channel_id=1, source_target_pairs={{0,8},{4,12},{8,0},{12,4},{1,9},{5,13},{9,1},{13,5},{2,10},{6,14},... | collective-permute-start | bytes 73736 | tf_op jit(solution)/shard_map/ppermute | solution.py:16
  13.3 3.2 %collective-permute-done.7.refs_2_ = s32[12,512]{1,0:T(8,128)S(1)} collective-permute-done((s32[12,512]{1,0:T(8,128)S(1)}, s32[12,512]{1,0:T(8,128)S(1)}, u32[]{:S(2)}, u32[]{:S(2)}) %collective-permute-start.7) | collective-permute-done | bytes 24608 | tf_op jit(solution)/shard_map/ppermute | solution.py:16
  16.5 1.2 collective-permute-done.6.refs_1_
  17.9 0.7 shard_map.74.ranks_ref
  18.9 3.5 %shard_map.75 = (s32[4,1,384]{2,1,0:T(1,128)S(1)}, f32[4,1,384]{2,1,0:T(1,128)S(1)}) custom-call(s32[2]{0:T(128)S(1)} %pad_add_fusion.1.me_ref, s32[12,512]{1,0:T(8,128)S(1)} %pad_add_fusion.refs_0_, s32[12,512]{1,0:T(8,128)S(1)} %collective-permute-done.6.refs_1_, s32[12,512]{1,0:T(8,128)S(1)} %collective-permute-done.7.refs_2_, ...), custom_call_target="tpu_custom_call" | custom-call | flops 1 | bytes 110592 | tf_op jit(solution)/shard_map/pallas_call | solution.py:30
  22.7 0.8 shard_map.76
  23.6 1.8 %collective-permute-start.9 = (bf16[256,1024]{1,0:T(8,128)(2,1)S(1)}, bf16[256,1024]{1,0:T(8,128)(2,1)S(1)}, u32[]{:S(2)}, u32[]{:S(2)}) collective-permute-start(bf16[256,1024]{1,0:T(8,128)(2,1)S(1)} %copy-done.3), channel_id=1, source_target_pairs={{0,8},{4,12},{8,0},{12,4},{1,9},{5,13},{9,1},{13,5},{2,10},{6,14},... | collective-permute-start | bytes 1572872 | tf_op jit(solution)/shard_map/ppermute | solution.py:16
  25.4 1.6 %collective-permute-start.11 = (bf16[96,512]{1,0:T(8,128)(2,1)S(1)}, bf16[96,512]{1,0:T(8,128)(2,1)S(1)}, u32[]{:S(2)}, u32[]{:S(2)}) collective-permute-start(bf16[96,512]{1,0:T(8,128)(2,1)S(1)} %get-tuple-element.61), channel_id=1, source_target_pairs={{0,1},{1,0},{2,3},{3,2},{4,5},{5,4},{6,7},{7,6},{8,9},{9,8},{10,11... | collective-permute-start | bytes 294920 | tf_op jit(solution)/shard_map/ppermute | solution.py:16
  27.0 2.6 %collective-permute-start.12 = (bf16[96,512]{1,0:T(8,128)(2,1)S(1)}, bf16[96,512]{1,0:T(8,128)(2,1)S(1)}, u32[]{:S(2)}, u32[]{:S(2)}) collective-permute-start(bf16[96,512]{1,0:T(8,128)(2,1)S(1)} %get-tuple-element.62), channel_id=1, source_target_pairs={{0,2},{1,3},{2,0},{3,1},{4,6},{5,7},{6,4},{7,5},{8,10},{9,11},{10,... | collective-permute-start | bytes 294920 | tf_op jit(solution)/shard_map/ppermute | solution.py:16
  29.6 1.9 %shard_map.78 = (bf16[128,512]{1,0:T(8,128)(2,1)S(1)}, bf16[128,512]{1,0:T(8,128)(2,1)S(1)}, bf16[128,512]{1,0:T(8,128)(2,1)S(1)}, bf16[128,512]{1,0:T(8,128)(2,1)S(1)}, bf16[16,1024]{1,0:T(8,128)(2,1)}) custom-call(s32[2]{0:T(128)S(1)} %pad_add_fusion.1.me_ref, bf16[512,1024]{1,0:T(8,128)(2,1)S(1)} %get-tuple-element.64.tokens_ref, ...), custom_call_target="tpu_custom_call" | custom-call | flops 536870912 | bytes 2654208 | tf_op jit(solution)/shard_map/pallas_call | solution.py:30
  32.3 3.6 %collective-permute-start.17 = (bf16[128,512]{1,0:T(8,128)(2,1)S(1)}, bf16[128,512]{1,0:T(8,128)(2,1)S(1)}, u32[]{:S(2)}, u32[]{:S(2)}) collective-permute-start(bf16[128,512]{1,0:T(8,128)(2,1)S(1)} %get-tuple-element.68), channel_id=1, source_target_pairs={{0,3},{1,2},{2,1},{3,0},{4,7},{5,6},{6,5},{7,4},{8,11},{9,10},{10,... | collective-permute-start | bytes 393224 | tf_op jit(solution)/shard_map/ppermute | solution.py:16
  35.9 2.5 %collective-permute-start.13 = (bf16[96,512]{1,0:T(8,128)(2,1)S(1)}, bf16[96,512]{1,0:T(8,128)(2,1)S(1)}, u32[]{:S(2)}, u32[]{:S(2)}) collective-permute-start(bf16[96,512]{1,0:T(8,128)(2,1)S(1)} %get-tuple-element.63), channel_id=1, source_target_pairs={{0,3},{1,2},{2,1},{3,0},{4,7},{5,6},{6,5},{7,4},{8,11},{9,10},{10,... | collective-permute-start | bytes 294920 | tf_op jit(solution)/shard_map/ppermute | solution.py:16
  38.4 6.6 %collective-permute-done.13 = bf16[96,512]{1,0:T(8,128)(2,1)S(1)} collective-permute-done((bf16[96,512]{1,0:T(8,128)(2,1)S(1)}, bf16[96,512]{1,0:T(8,128)(2,1)S(1)}, u32[]{:S(2)}, u32[]{:S(2)}) %collective-permute-start.13) | collective-permute-done | bytes 98336 | tf_op jit(solution)/shard_map/ppermute | solution.py:16
  45.4 1.5 collective-permute-done.16.refs_2_
  47.6 0.7 shard_map.77.weights_ref
  48.3 0.8 shard_map.79
  49.1 6.1 %collective-permute-start.21 = (bf16[96,512]{1,0:T(8,128)(2,1)S(1)}, bf16[96,512]{1,0:T(8,128)(2,1)S(1)}, u32[]{:S(2)}, u32[]{:S(2)}) collective-permute-start(bf16[96,512]{1,0:T(8,128)(2,1)S(1)} %get-tuple-element.76), channel_id=1, source_target_pairs={{0,1},{1,0},{2,3},{3,2},{4,5},{5,4},{6,7},{7,6},{8,9},{9,8},{10,11... | collective-permute-start | bytes 294920 | tf_op jit(solution)/shard_map/ppermute | solution.py:16
  55.2 0.6 collective-permute-start.22
  55.9 1.8 %collective-permute-start.23 = (bf16[96,512]{1,0:T(8,128)(2,1)S(1)}, bf16[96,512]{1,0:T(8,128)(2,1)S(1)}, u32[]{:S(2)}, u32[]{:S(2)}) collective-permute-start(bf16[96,512]{1,0:T(8,128)(2,1)S(1)} %get-tuple-element.78), channel_id=1, source_target_pairs={{0,3},{1,2},{2,1},{3,0},{4,7},{5,6},{6,5},{7,4},{8,11},{9,10},{10,... | collective-permute-start | bytes 294920 | tf_op jit(solution)/shard_map/ppermute | solution.py:16
  57.7 0.7 collective-permute-done.21
  58.4 7.4 %collective-permute-done.22 = bf16[96,512]{1,0:T(8,128)(2,1)S(1)} collective-permute-done((bf16[96,512]{1,0:T(8,128)(2,1)S(1)}, bf16[96,512]{1,0:T(8,128)(2,1)S(1)}, u32[]{:S(2)}, u32[]{:S(2)}) %collective-permute-start.22) | collective-permute-done | bytes 98336 | tf_op jit(solution)/shard_map/ppermute | solution.py:16
  66.5 1.1 collective-permute-done.24.refs_3_
  67.6 4.4 %shard_map.80.hidden_ref = bf16[512,2688]{1,0:T(8,128)(2,1)S(1)} custom-call(s32[2]{0:T(128)S(1)} %pad_add_fusion.1.me_ref, s32[4,1,384]{2,1,0:T(1,128)S(1)} %get-tuple-element.83.slot_ref, bf16[384,512]{1,0:T(8,128)(2,1)S(1)} %constant_dynamic-update-slice_fusion.refs_0_, bf16[384,512]{1,0:T(8,128)(2,1)S(1)} %collective-permute-done.20.refs_1_, ...), custom_call_target="tpu_custom_call" | custom-call | flops 2818572288 | bytes 9836544 | tf_op jit(solution)/shard_map/pallas_call | solution.py:30
  72.0 4.3 %shard_map.81 = (bf16[384,1024]{1,0:T(8,128)(2,1)S(1)}, bf16[384,1024]{1,0:T(8,128)(2,1)S(1)}) custom-call(s32[2]{0:T(128)S(1)} %pad_add_fusion.1.me_ref, s32[4,1,384]{2,1,0:T(1,128)S(1)} %get-tuple-element.83.slot_ref, f32[4,1,384]{2,1,0:T(1,128)S(1)} %get-tuple-element.60.weight_ref, bf16[512,2688]{1,0:T(8,128)(2,1)S(1)} %shard_map.80.hidden_ref, ...), custom_call_target="tpu_custom_call" | custom-call | flops 2818572288 | bytes 9842688 | tf_op jit(solution)/shard_map/pallas_call | solution.py:30
  76.3 1.1 collective-permute-done.26.refs_1_
  77.5 2.6 %shard_map.82.hidden_ref = bf16[256,2688]{1,0:T(8,128)(2,1)S(1)} custom-call(s32[2]{0:T(128)S(1)} %pad_add_fusion.1.me_ref, s32[4,1,384]{2,1,0:T(1,128)S(1)} %get-tuple-element.83.slot_ref, bf16[384,512]{1,0:T(8,128)(2,1)S(1)} %collective-permute-done.18.refs_0_, bf16[384,512]{1,0:T(8,128)(2,1)S(1)} %collective-permute-done.26.refs_1_, ...), custom_call_target="tpu_custom_call" | custom-call | flops 1409286144 | bytes 7673856 | tf_op jit(solution)/shard_map/pallas_call | solution.py:30
  80.1 2.6 %shard_map.83.hidden_ref = bf16[256,2688]{1,0:T(8,128)(2,1)S(1)} custom-call(s32[2]{0:T(128)S(1)} %pad_add_fusion.1.me_ref, s32[4,1,384]{2,1,0:T(1,128)S(1)} %get-tuple-element.83.slot_ref, bf16[384,512]{1,0:T(8,128)(2,1)S(1)} %collective-permute-done.19.refs_0_, bf16[384,512]{1,0:T(8,128)(2,1)S(1)} %collective-permute-done.27.refs_1_, ...), custom_call_target="tpu_custom_call" | custom-call | flops 1 | bytes 1 | tf_op jit(solution)/shard_map/pallas_call | solution.py:30
  82.7 2.7 %shard_map.84 = bf16[384,1024]{1,0:T(8,128)(2,1)S(1)} custom-call(s32[2]{0:T(128)S(1)} %pad_add_fusion.1.me_ref, s32[4,1,384]{2,1,0:T(1,128)S(1)} %get-tuple-element.83.slot_ref, f32[4,1,384]{2,1,0:T(1,128)S(1)} %get-tuple-element.60.weight_ref, bf16[256,2688]{1,0:T(8,128)(2,1)S(1)} %shard_map.83.hidden_ref, bf16[2688,1024]{1,0:T(8,128)(2,1)S(1)} %bitcast.12), custom_call_target="tpu_custom_call" | custom-call | flops 1 | bytes 1 | tf_op jit(solution)/shard_map/pallas_call | solution.py:30
  86.0 2.6 %shard_map.85.refs_0_ = bf16[384,1024]{1,0:T(8,128)(2,1)S(1)} custom-call(s32[2]{0:T(128)S(1)} %pad_add_fusion.1.me_ref, s32[4,1,384]{2,1,0:T(1,128)S(1)} %get-tuple-element.83.slot_ref, f32[4,1,384]{2,1,0:T(1,128)S(1)} %get-tuple-element.60.weight_ref, bf16[256,2688]{1,0:T(8,128)(2,1)S(1)} %shard_map.82.hidden_ref, bf16[2688,1024]{1,0:T(8,128)(2,1)S(1)} %bitcast.13), custom_call_target="tpu_custom_call" | custom-call | flops 1 | bytes 1 | tf_op jit(solution)/shard_map/pallas_call | solution.py:30
  88.7 0.7 shard_map.86
  90.0 1.5 %collective-permute-start.31 = (bf16[384,512]{1,0:T(8,128)(2,1)S(1)}, bf16[384,512]{1,0:T(8,128)(2,1)S(1)}, u32[]{:S(2)}, u32[]{:S(2)}) collective-permute-start(bf16[384,512]{1,0:T(8,128)(2,1)S(1)} %get-tuple-element.87), channel_id=1, source_target_pairs={{0,8},{4,12},{8,0},{12,4},{1,9},{5,13},{9,1},{13,5},{2,10},{6,14},... | collective-permute-start | bytes 1179656 | tf_op jit(solution)/shard_map/ppermute | solution.py:16
  91.5 9.9 %collective-permute-done.29.refs_2_ = bf16[384,512]{1,0:T(8,128)(2,1)S(1)} collective-permute-done((bf16[384,512]{1,0:T(8,128)(2,1)S(1)}, bf16[384,512]{1,0:T(8,128)(2,1)S(1)}, u32[]{:S(2)}, u32[]{:S(2)}) %collective-permute-start.29) | collective-permute-done | bytes 393248 | tf_op jit(solution)/shard_map/ppermute | solution.py:16
  101.4 0.7 shard_map.87
  102.1 1.8 %collective-permute-start.30 = (bf16[96,512]{1,0:T(8,128)(2,1)S(1)}, bf16[96,512]{1,0:T(8,128)(2,1)S(1)}, u32[]{:S(2)}, u32[]{:S(2)}) collective-permute-start(bf16[96,512]{1,0:T(8,128)(2,1)S(1)} %get-tuple-element.85), channel_id=1, source_target_pairs={{0,1},{1,0},{2,3},{3,2},{4,5},{5,4},{6,7},{7,6},{8,9},{9,8},{10,11... | collective-permute-start | bytes 294920 | tf_op jit(solution)/shard_map/ppermute | solution.py:16
  103.9 0.7 collective-permute-start.32
  104.6 1.9 %collective-permute-start.33 = (bf16[96,512]{1,0:T(8,128)(2,1)S(1)}, bf16[96,512]{1,0:T(8,128)(2,1)S(1)}, u32[]{:S(2)}, u32[]{:S(2)}) collective-permute-start(bf16[96,512]{1,0:T(8,128)(2,1)S(1)} %get-tuple-element.92), channel_id=1, source_target_pairs={{0,3},{1,2},{2,1},{3,0},{4,7},{5,6},{6,5},{7,4},{8,11},{9,10},{10,... | collective-permute-start | bytes 294920 | tf_op jit(solution)/shard_map/ppermute | solution.py:16
  106.5 0.8 collective-permute-done.30.refs_1_
  107.3 2.0 %collective-permute-done.31.refs_2_ = bf16[384,512]{1,0:T(8,128)(2,1)S(1)} collective-permute-done((bf16[384,512]{1,0:T(8,128)(2,1)S(1)}, bf16[384,512]{1,0:T(8,128)(2,1)S(1)}, u32[]{:S(2)}, u32[]{:S(2)}) %collective-permute-start.31) | collective-permute-done | bytes 393248 | tf_op jit(solution)/shard_map/ppermute | solution.py:16
  109.4 0.7 shard_map.88
  110.1 3.5 %collective-permute-done.32.refs_2_ = bf16[96,512]{1,0:T(8,128)(2,1)S(1)} collective-permute-done((bf16[96,512]{1,0:T(8,128)(2,1)S(1)}, bf16[96,512]{1,0:T(8,128)(2,1)S(1)}, u32[]{:S(2)}, u32[]{:S(2)}) %collective-permute-start.32) | collective-permute-done | bytes 98336 | tf_op jit(solution)/shard_map/ppermute | solution.py:16
  113.5 0.9 shard_map.89.refs_0_
  114.4 2.4 %collective-permute-start.35 = (bf16[128,512]{1,0:T(8,128)(2,1)S(1)}, bf16[128,512]{1,0:T(8,128)(2,1)S(1)}, u32[]{:S(2)}, u32[]{:S(2)}) collective-permute-start(bf16[128,512]{1,0:T(8,128)(2,1)S(1)} %shard_map.89.refs_0_), channel_id=1, source_target_pairs={{0,2},{1,3},{2,0},{3,1},{4,6},{5,7},{6,4},{7,5},{8,10},{9,11},{10,... | collective-permute-start | bytes 393224 | tf_op jit(solution)/shard_map/ppermute | solution.py:16
  116.9 1.9 %collective-permute-start.36 = (bf16[96,512]{1,0:T(8,128)(2,1)S(1)}, bf16[96,512]{1,0:T(8,128)(2,1)S(1)}, u32[]{:S(2)}, u32[]{:S(2)}) collective-permute-start(bf16[96,512]{1,0:T(8,128)(2,1)S(1)} %get-tuple-element.94), channel_id=1, source_target_pairs={{0,1},{1,0},{2,3},{3,2},{4,5},{5,4},{6,7},{7,6},{8,9},{9,8},{10,11... | collective-permute-start | bytes 294920 | tf_op jit(solution)/shard_map/ppermute | solution.py:16
  119.4 1.9 %collective-permute-start.38 = (bf16[96,512]{1,0:T(8,128)(2,1)S(1)}, bf16[96,512]{1,0:T(8,128)(2,1)S(1)}, u32[]{:S(2)}, u32[]{:S(2)}) collective-permute-start(bf16[96,512]{1,0:T(8,128)(2,1)S(1)} %get-tuple-element.96), channel_id=1, source_target_pairs={{0,3},{1,2},{2,1},{3,0},{4,7},{5,6},{6,5},{7,4},{8,11},{9,10},{10,... | collective-permute-start | bytes 294920 | tf_op jit(solution)/shard_map/ppermute | solution.py:16
  121.3 1.9 %collective-permute-done.35.refs_2_ = bf16[128,512]{1,0:T(8,128)(2,1)S(1)} collective-permute-done((bf16[128,512]{1,0:T(8,128)(2,1)S(1)}, bf16[128,512]{1,0:T(8,128)(2,1)S(1)}, u32[]{:S(2)}, u32[]{:S(2)}) %collective-permute-start.35) | collective-permute-done | bytes 131104 | tf_op jit(solution)/shard_map/ppermute | solution.py:16
  123.2 2.3 %collective-permute-done.34.refs_1_ = bf16[128,512]{1,0:T(8,128)(2,1)S(1)} collective-permute-done((bf16[128,512]{1,0:T(8,128)(2,1)S(1)}, bf16[128,512]{1,0:T(8,128)(2,1)S(1)}, u32[]{:S(2)}, u32[]{:S(2)}) %collective-permute-start.34) | collective-permute-done | bytes 131104 | tf_op jit(solution)/shard_map/ppermute | solution.py:16
  125.5 1.8 %collective-permute-done.36.refs_1_ = bf16[96,512]{1,0:T(8,128)(2,1)S(1)} collective-permute-done((bf16[96,512]{1,0:T(8,128)(2,1)S(1)}, bf16[96,512]{1,0:T(8,128)(2,1)S(1)}, u32[]{:S(2)}, u32[]{:S(2)}) %collective-permute-start.36) | collective-permute-done | bytes 98336 | tf_op jit(solution)/shard_map/ppermute | solution.py:16
  127.3 3.1 %collective-permute-done.38.refs_3_ = bf16[96,512]{1,0:T(8,128)(2,1)S(1)} collective-permute-done((bf16[96,512]{1,0:T(8,128)(2,1)S(1)}, bf16[96,512]{1,0:T(8,128)(2,1)S(1)}, u32[]{:S(2)}, u32[]{:S(2)}) %collective-permute-start.38) | collective-permute-done | bytes 98336 | tf_op jit(solution)/shard_map/ppermute | solution.py:16
  130.4 0.9 shard_map.90.refs_0_
  131.2 1.9 %collective-permute-start.40 = (bf16[128,512]{1,0:T(8,128)(2,1)S(1)}, bf16[128,512]{1,0:T(8,128)(2,1)S(1)}, u32[]{:S(2)}, u32[]{:S(2)}) collective-permute-start(bf16[128,512]{1,0:T(8,128)(2,1)S(1)} %shard_map.90.refs_0_), channel_id=1, source_target_pairs={{0,2},{1,3},{2,0},{3,1},{4,6},{5,7},{6,4},{7,5},{8,10},{9,11},{10,... | collective-permute-start | bytes 393224 | tf_op jit(solution)/shard_map/ppermute | solution.py:16
  133.2 0.9 collective-permute-start.42
  134.0 1.2 collective-permute-start.39
  135.2 3.4 %collective-permute-done.40.refs_2_ = bf16[128,512]{1,0:T(8,128)(2,1)S(1)} collective-permute-done((bf16[128,512]{1,0:T(8,128)(2,1)S(1)}, bf16[128,512]{1,0:T(8,128)(2,1)S(1)}, u32[]{:S(2)}, u32[]{:S(2)}) %collective-permute-start.40) | collective-permute-done | bytes 131104 | tf_op jit(solution)/shard_map/ppermute | solution.py:16
  139.2 1.0 collective-permute-done.42.refs_3_
  140.2 1.3 shard_map.91.refs_4_
  141.5 1.0 collective-permute-done.39.refs_1_
  142.5 1.4 collective-permute-done.41.refs_3_
  143.9 2.3 %shard_map.92 = bf16[512,1024]{1,0:T(8,128)(2,1)} custom-call(s32[2]{0:T(128)S(1)} %pad_add_fusion.1.me_ref, bf16[1024,1024]{1,0:T(8,128)(2,1)S(1)} %shard_map.77.weights_ref, bf16[128,512]{1,0:T(8,128)(2,1)S(1)} %shard_map.90.refs_0_, bf16[128,512]{1,0:T(8,128)(2,1)S(1)} %collective-permute-done.39.refs_1_, ...), custom_call_target="tpu_custom_call" | custom-call | flops 536870912 | bytes 5767168 | tf_op jit(solution)/shard_map/pallas_call | solution.py:30
  (69 shorter events, 6.6 us)
Async XLA Ops:
  0.0 11.5 %copy-start.4 = (s32[512,6]{0,1:T(8,128)S(1)}, s32[512,6]{0,1:T(8,128)}, u32[]{:S(2)}) copy-start(s32[512,6]{0,1:T(8,128)} %param.12) | copy-start | bytes 36868
  0.0 3.1 %collective-permute-start.2 = (bf16[256,1024]{1,0:T(8,128)(2,1)}, bf16[256,1024]{1,0:T(8,128)(2,1)S(1)}, u32[]{:S(2)}, u32[]{:S(2)}) collective-permute-start(bf16[256,1024]{1,0:T(8,128)(2,1)} %refs_0_.2), channel_id=1, source_target_pairs={{0,4},{4,0},{8,12},{12,8},{1,5},{5,1},{9,13},{13,9},{2,6},{6,2},{1... | collective-permute-start | bytes 1572872 | tf_op jit(solution)/shard_map/ppermute | solution.py:16
  0.5 22.0 %collective-permute-start.1 = (bf16[256,1024]{1,0:T(8,128)(2,1)}, bf16[256,1024]{1,0:T(8,128)(2,1)S(1)}, u32[]{:S(2)}, u32[]{:S(2)}) collective-permute-start(bf16[256,1024]{1,0:T(8,128)(2,1)} %refs_0_.2), channel_id=1, source_target_pairs={{0,8},{4,12},{8,0},{12,4},{1,9},{5,13},{9,1},{13,5},{2,10},{6,14},... | collective-permute-start | bytes 1572872 | tf_op jit(solution)/shard_map/ppermute | solution.py:16
  3.1 1.2 copy-start.1
  4.3 1.0 copy-start.2
  5.4 6.1 %copy-start.5 = (s32[512,6]{0,1:T(8,128)S(1)}, s32[512,6]{0,1:T(8,128)}, u32[]{:S(2)}) copy-start(s32[512,6]{0,1:T(8,128)} %param.13) | copy-start | bytes 36868
  5.4 18.2 %copy-start.3 = (bf16[256,1024]{1,0:T(8,128)(2,1)S(1)}, bf16[256,1024]{1,0:T(8,128)(2,1)}, u32[]{:S(2)}) copy-start(bf16[256,1024]{1,0:T(8,128)(2,1)} %refs_0_.3) | copy-start | bytes 1572868
  6.8 15.7 %collective-permute-start.3 = (bf16[128,512]{1,0:T(8,128)(2,1)S(1)}, bf16[128,512]{1,0:T(8,128)(2,1)S(1)}, u32[]{:S(2)}, u32[]{:S(2)}) collective-permute-start(bf16[128,512]{1,0:T(8,128)(2,1)S(1)} %get-tuple-element.52), channel_id=1, source_target_pairs={{0,1},{1,0},{2,3},{3,2},{4,5},{5,4},{6,7},{7,6},{8,9},{9,8},{10,11... | collective-permute-start | bytes 393224 | tf_op jit(solution)/shard_map/ppermute | solution.py:16
  8.9 13.6 %collective-permute-start.4 = (bf16[128,512]{1,0:T(8,128)(2,1)S(1)}, bf16[128,512]{1,0:T(8,128)(2,1)S(1)}, u32[]{:S(2)}, u32[]{:S(2)}) collective-permute-start(bf16[128,512]{1,0:T(8,128)(2,1)S(1)} %get-tuple-element.53), channel_id=1, source_target_pairs={{0,2},{1,3},{2,0},{3,1},{4,6},{5,7},{6,4},{7,5},{8,10},{9,11},{10,... | collective-permute-start | bytes 393224 | tf_op jit(solution)/shard_map/ppermute | solution.py:16
  11.5 11.0 %collective-permute-start.5 = (bf16[128,512]{1,0:T(8,128)(2,1)S(1)}, bf16[128,512]{1,0:T(8,128)(2,1)S(1)}, u32[]{:S(2)}, u32[]{:S(2)}) collective-permute-start(bf16[128,512]{1,0:T(8,128)(2,1)S(1)} %get-tuple-element.54), channel_id=1, source_target_pairs={{0,3},{1,2},{2,1},{3,0},{4,7},{5,6},{6,5},{7,4},{8,11},{9,10},{10,... | collective-permute-start | bytes 393224 | tf_op jit(solution)/shard_map/ppermute | solution.py:16
  11.5 5.0 %collective-permute-start.7 = (s32[12,512]{1,0:T(8,128)S(1)}, s32[12,512]{1,0:T(8,128)S(1)}, u32[]{:S(2)}, u32[]{:S(2)}) collective-permute-start(s32[12,512]{1,0:T(8,128)S(1)} %pad_add_fusion.refs_0_), channel_id=1, source_target_pairs={{0,8},{4,12},{8,0},{12,4},{1,9},{5,13},{9,1},{13,5},{2,10},{6,14},... | collective-permute-start | bytes 73736 | tf_op jit(solution)/shard_map/ppermute | solution.py:16
  16.5 1.2 collective-permute-start.6
  17.7 1.2 collective-permute-start.8
  22.5 7.1 %collective-permute-start.14 = (bf16[256,1024]{1,0:T(8,128)(2,1)S(1)}, bf16[256,1024]{1,0:T(8,128)(2,1)S(1)}, u32[]{:S(2)}, u32[]{:S(2)}) collective-permute-start(bf16[256,1024]{1,0:T(8,128)(2,1)S(1)} %collective-permute-done.1.refs_0_), channel_id=1, source_target_pairs={{0,4},{4,0},{8,12},{12,8},{1,5},{5,1},{9,13},{13,9},{2,6},{6,2},{1... | collective-permute-start | bytes 1572872 | tf_op jit(solution)/shard_map/ppermute | solution.py:16
  23.6 21.4 %collective-permute-start.9 = (bf16[256,1024]{1,0:T(8,128)(2,1)S(1)}, bf16[256,1024]{1,0:T(8,128)(2,1)S(1)}, u32[]{:S(2)}, u32[]{:S(2)}) collective-permute-start(bf16[256,1024]{1,0:T(8,128)(2,1)S(1)} %copy-done.3), channel_id=1, source_target_pairs={{0,8},{4,12},{8,0},{12,4},{1,9},{5,13},{9,1},{13,5},{2,10},{6,14},... | collective-permute-start | bytes 1572872 | tf_op jit(solution)/shard_map/ppermute | solution.py:16
  25.4 6.9 %collective-permute-start.11 = (bf16[96,512]{1,0:T(8,128)(2,1)S(1)}, bf16[96,512]{1,0:T(8,128)(2,1)S(1)}, u32[]{:S(2)}, u32[]{:S(2)}) collective-permute-start(bf16[96,512]{1,0:T(8,128)(2,1)S(1)} %get-tuple-element.61), channel_id=1, source_target_pairs={{0,1},{1,0},{2,3},{3,2},{4,5},{5,4},{6,7},{7,6},{8,9},{9,8},{10,11... | collective-permute-start | bytes 294920 | tf_op jit(solution)/shard_map/ppermute | solution.py:16
  27.0 8.9 %collective-permute-start.12 = (bf16[96,512]{1,0:T(8,128)(2,1)S(1)}, bf16[96,512]{1,0:T(8,128)(2,1)S(1)}, u32[]{:S(2)}, u32[]{:S(2)}) collective-permute-start(bf16[96,512]{1,0:T(8,128)(2,1)S(1)} %get-tuple-element.62), channel_id=1, source_target_pairs={{0,2},{1,3},{2,0},{3,1},{4,6},{5,7},{6,4},{7,5},{8,10},{9,11},{10,... | collective-permute-start | bytes 294920 | tf_op jit(solution)/shard_map/ppermute | solution.py:16
  31.5 14.0 %collective-permute-start.15 = (bf16[128,512]{1,0:T(8,128)(2,1)S(1)}, bf16[128,512]{1,0:T(8,128)(2,1)S(1)}, u32[]{:S(2)}, u32[]{:S(2)}) collective-permute-start(bf16[128,512]{1,0:T(8,128)(2,1)S(1)} %get-tuple-element.66), channel_id=1, source_target_pairs={{0,1},{1,0},{2,3},{3,2},{4,5},{5,4},{6,7},{7,6},{8,9},{9,8},{10,11... | collective-permute-start | bytes 393224 | tf_op jit(solution)/shard_map/ppermute | solution.py:16
  31.9 15.0 %collective-permute-start.16 = (bf16[128,512]{1,0:T(8,128)(2,1)S(1)}, bf16[128,512]{1,0:T(8,128)(2,1)S(1)}, u32[]{:S(2)}, u32[]{:S(2)}) collective-permute-start(bf16[128,512]{1,0:T(8,128)(2,1)S(1)} %get-tuple-element.67), channel_id=1, source_target_pairs={{0,2},{1,3},{2,0},{3,1},{4,6},{5,7},{6,4},{7,5},{8,10},{9,11},{10,... | collective-permute-start | bytes 393224 | tf_op jit(solution)/shard_map/ppermute | solution.py:16
  32.3 14.6 %collective-permute-start.17 = (bf16[128,512]{1,0:T(8,128)(2,1)S(1)}, bf16[128,512]{1,0:T(8,128)(2,1)S(1)}, u32[]{:S(2)}, u32[]{:S(2)}) collective-permute-start(bf16[128,512]{1,0:T(8,128)(2,1)S(1)} %get-tuple-element.68), channel_id=1, source_target_pairs={{0,3},{1,2},{2,1},{3,0},{4,7},{5,6},{6,5},{7,4},{8,11},{9,10},{10,... | collective-permute-start | bytes 393224 | tf_op jit(solution)/shard_map/ppermute | solution.py:16
  35.9 9.1 %collective-permute-start.13 = (bf16[96,512]{1,0:T(8,128)(2,1)S(1)}, bf16[96,512]{1,0:T(8,128)(2,1)S(1)}, u32[]{:S(2)}, u32[]{:S(2)}) collective-permute-start(bf16[96,512]{1,0:T(8,128)(2,1)S(1)} %get-tuple-element.63), channel_id=1, source_target_pairs={{0,3},{1,2},{2,1},{3,0},{4,7},{5,6},{6,5},{7,4},{8,11},{9,10},{10,... | collective-permute-start | bytes 294920 | tf_op jit(solution)/shard_map/ppermute | solution.py:16
  44.9 2.6 %collective-permute-start = (bf16[256,1024]{1,0:T(8,128)(2,1)S(1)}, bf16[256,1024]{1,0:T(8,128)(2,1)S(1)}, u32[]{:S(2)}, u32[]{:S(2)}) collective-permute-start(bf16[256,1024]{1,0:T(8,128)(2,1)S(1)} %copy-done.3), channel_id=1, source_target_pairs={{0,4},{4,0},{8,12},{12,8},{1,5},{5,1},{9,13},{13,9},{2,6},{6,2},{1... | collective-permute-start | bytes 1572872 | tf_op jit(solution)/shard_map/ppermute | solution.py:16
  44.9 2.7 %collective-permute-start.10 = (bf16[256,1024]{1,0:T(8,128)(2,1)S(1)}, bf16[256,1024]{1,0:T(8,128)(2,1)S(1)}, u32[]{:S(2)}, u32[]{:S(2)}) collective-permute-start(bf16[256,1024]{1,0:T(8,128)(2,1)S(1)} %collective-permute-done.9.refs_2_), channel_id=1, source_target_pairs={{0,4},{4,0},{8,12},{12,8},{1,5},{5,1},{9,13},{13,9},{2,6},{6,2},{1... | collective-permute-start | bytes 1572872 | tf_op jit(solution)/shard_map/ppermute | solution.py:16
  47.0 20.7 %copy-start = (bf16[1,1024,2688]{2,1,0:T(8,128)(2,1)S(1)}, bf16[1,1024,2688]{2,1,0:T(8,128)(2,1)}, u32[]{:S(2)}) copy-start(bf16[1,1024,2688]{2,1,0:T(8,128)(2,1)} %param.10) | copy-start | bytes 16515076
  47.0 10.7 %collective-permute-start.18 = (bf16[384,512]{1,0:T(8,128)(2,1)S(1)}, bf16[384,512]{1,0:T(8,128)(2,1)S(1)}, u32[]{:S(2)}, u32[]{:S(2)}) collective-permute-start(bf16[384,512]{1,0:T(8,128)(2,1)S(1)} %constant_dynamic-update-slice_fusion.refs_0_), channel_id=1, source_target_pairs={{0,8},{4,12},{8,0},{12,4},{1,9},{5,13},{9,1},{13,5},{2,10},{6,14},... | collective-permute-start | bytes 1179656 | tf_op jit(solution)/shard_map/ppermute | solution.py:16
  47.5 19.0 %collective-permute-start.20 = (bf16[384,512]{1,0:T(8,128)(2,1)S(1)}, bf16[384,512]{1,0:T(8,128)(2,1)S(1)}, u32[]{:S(2)}, u32[]{:S(2)}) collective-permute-start(bf16[384,512]{1,0:T(8,128)(2,1)S(1)} %constant_dynamic-update-slice_fusion.refs_0_), channel_id=1, source_target_pairs={{0,4},{4,0},{8,12},{12,8},{1,5},{5,1},{9,13},{13,9},{2,6},{6,2},{1... | collective-permute-start | bytes 1179656 | tf_op jit(solution)/shard_map/ppermute | solution.py:16
  49.1 9.3 %collective-permute-start.21 = (bf16[96,512]{1,0:T(8,128)(2,1)S(1)}, bf16[96,512]{1,0:T(8,128)(2,1)S(1)}, u32[]{:S(2)}, u32[]{:S(2)}) collective-permute-start(bf16[96,512]{1,0:T(8,128)(2,1)S(1)} %get-tuple-element.76), channel_id=1, source_target_pairs={{0,1},{1,0},{2,3},{3,2},{4,5},{5,4},{6,7},{7,6},{8,9},{9,8},{10,11... | collective-permute-start | bytes 294920 | tf_op jit(solution)/shard_map/ppermute | solution.py:16
  55.2 10.6 %collective-permute-start.22 = (bf16[96,512]{1,0:T(8,128)(2,1)S(1)}, bf16[96,512]{1,0:T(8,128)(2,1)S(1)}, u32[]{:S(2)}, u32[]{:S(2)}) collective-permute-start(bf16[96,512]{1,0:T(8,128)(2,1)S(1)} %get-tuple-element.77), channel_id=1, source_target_pairs={{0,2},{1,3},{2,0},{3,1},{4,6},{5,7},{6,4},{7,5},{8,10},{9,11},{10,... | collective-permute-start | bytes 294920 | tf_op jit(solution)/shard_map/ppermute | solution.py:16
  55.9 10.0 %collective-permute-start.23 = (bf16[96,512]{1,0:T(8,128)(2,1)S(1)}, bf16[96,512]{1,0:T(8,128)(2,1)S(1)}, u32[]{:S(2)}, u32[]{:S(2)}) collective-permute-start(bf16[96,512]{1,0:T(8,128)(2,1)S(1)} %get-tuple-element.78), channel_id=1, source_target_pairs={{0,3},{1,2},{2,1},{3,0},{4,7},{5,6},{6,5},{7,4},{8,11},{9,10},{10,... | collective-permute-start | bytes 294920 | tf_op jit(solution)/shard_map/ppermute | solution.py:16
  57.7 8.8 %collective-permute-start.19 = (bf16[384,512]{1,0:T(8,128)(2,1)S(1)}, bf16[384,512]{1,0:T(8,128)(2,1)S(1)}, u32[]{:S(2)}, u32[]{:S(2)}) collective-permute-start(bf16[384,512]{1,0:T(8,128)(2,1)S(1)} %collective-permute-done.18.refs_0_), channel_id=1, source_target_pairs={{0,4},{4,0},{8,12},{12,8},{1,5},{5,1},{9,13},{13,9},{2,6},{6,2},{1... | collective-permute-start | bytes 1179656 | tf_op jit(solution)/shard_map/ppermute | solution.py:16
  65.8 6.2 %slice-start = ((s8[5505024]{0:T(1024)(128)(4,1)}), s8[4194304]{0:T(1024)(128)(4,1)S(1)}, s32[]{:S(2)}) async-start(s8[5505024]{0:T(1024)(128)(4,1)} %bitcast.9), calls=%async_computation | async-start | bytes 8388608
  65.9 1.8 %collective-permute-start.24 = (bf16[384,512]{1,0:T(8,128)(2,1)S(1)}, bf16[384,512]{1,0:T(8,128)(2,1)S(1)}, u32[]{:S(2)}, u32[]{:S(2)}) collective-permute-start(bf16[384,512]{1,0:T(8,128)(2,1)S(1)} %constant_dynamic-update-slice_fusion.4.refs_2_), channel_id=1, source_target_pairs={{0,4},{4,0},{8,12},{12,8},{1,5},{5,1},{9,13},{13,9},{2,6},{6,2},{1... | collective-permute-start | bytes 1179656 | tf_op jit(solution)/shard_map/ppermute | solution.py:16
  65.9 11.5 %collective-permute-start.26 = (bf16[384,512]{1,0:T(8,128)(2,1)S(1)}, bf16[384,512]{1,0:T(8,128)(2,1)S(1)}, u32[]{:S(2)}, u32[]{:S(2)}) collective-permute-start(bf16[384,512]{1,0:T(8,128)(2,1)S(1)} %constant_dynamic-update-slice_fusion.4.refs_2_), channel_id=1, source_target_pairs={{0,8},{4,12},{8,0},{12,4},{1,9},{5,13},{9,1},{13,5},{2,10},{6,14},... | collective-permute-start | bytes 1179656 | tf_op jit(solution)/shard_map/ppermute | solution.py:16
  67.6 4.4 %slice-start.1 = ((s8[5505024]{0:T(1024)(128)(4,1)}), s8[1310720]{0:T(1024)(128)(4,1)S(1)}, s32[]{:S(2)}) async-start(s8[5505024]{0:T(1024)(128)(4,1)} %bitcast.9), calls=%async_computation.1 | async-start | bytes 2621440
  77.5 2.6 %collective-permute-start.27 = (bf16[384,512]{1,0:T(8,128)(2,1)S(1)}, bf16[384,512]{1,0:T(8,128)(2,1)S(1)}, u32[]{:S(2)}, u32[]{:S(2)}) collective-permute-start(bf16[384,512]{1,0:T(8,128)(2,1)S(1)} %collective-permute-done.26.refs_1_), channel_id=1, source_target_pairs={{0,4},{4,0},{8,12},{12,8},{1,5},{5,1},{9,13},{13,9},{2,6},{6,2},{1... | collective-permute-start | bytes 1179656 | tf_op jit(solution)/shard_map/ppermute | solution.py:16
  85.4 3.3 %collective-permute-start.28 = (bf16[384,1024]{1,0:T(8,128)(2,1)S(1)}, bf16[384,1024]{1,0:T(8,128)(2,1)S(1)}, u32[]{:S(2)}, u32[]{:S(2)}) collective-permute-start(bf16[384,1024]{1,0:T(8,128)(2,1)S(1)} %shard_map.84), channel_id=1, source_target_pairs={{0,4},{4,0},{8,12},{12,8},{1,5},{5,1},{9,13},{13,9},{2,6},{6,2},{1... | collective-permute-start | bytes 2359304 | tf_op jit(solution)/shard_map/ppermute | solution.py:16
  85.9 5.6 %collective-permute-start.25 = (bf16[384,1024]{1,0:T(8,128)(2,1)S(1)}, bf16[384,1024]{1,0:T(8,128)(2,1)S(1)}, u32[]{:S(2)}, u32[]{:S(2)}) collective-permute-start(bf16[384,1024]{1,0:T(8,128)(2,1)S(1)} %get-tuple-element.80), channel_id=1, source_target_pairs={{0,4},{4,0},{8,12},{12,8},{1,5},{5,1},{9,13},{13,9},{2,6},{6,2},{1... | collective-permute-start | bytes 2359304 | tf_op jit(solution)/shard_map/ppermute | solution.py:16
  89.4 12.0 %collective-permute-start.29 = (bf16[384,512]{1,0:T(8,128)(2,1)S(1)}, bf16[384,512]{1,0:T(8,128)(2,1)S(1)}, u32[]{:S(2)}, u32[]{:S(2)}) collective-permute-start(bf16[384,512]{1,0:T(8,128)(2,1)S(1)} %get-tuple-element.84), channel_id=1, source_target_pairs={{0,8},{4,12},{8,0},{12,4},{1,9},{5,13},{9,1},{13,5},{2,10},{6,14},... | collective-permute-start | bytes 1179656 | tf_op jit(solution)/shard_map/ppermute | solution.py:16
  90.0 19.4 %collective-permute-start.31 = (bf16[384,512]{1,0:T(8,128)(2,1)S(1)}, bf16[384,512]{1,0:T(8,128)(2,1)S(1)}, u32[]{:S(2)}, u32[]{:S(2)}) collective-permute-start(bf16[384,512]{1,0:T(8,128)(2,1)S(1)} %get-tuple-element.87), channel_id=1, source_target_pairs={{0,8},{4,12},{8,0},{12,4},{1,9},{5,13},{9,1},{13,5},{2,10},{6,14},... | collective-permute-start | bytes 1179656 | tf_op jit(solution)/shard_map/ppermute | solution.py:16
  102.1 5.2 %collective-permute-start.30 = (bf16[96,512]{1,0:T(8,128)(2,1)S(1)}, bf16[96,512]{1,0:T(8,128)(2,1)S(1)}, u32[]{:S(2)}, u32[]{:S(2)}) collective-permute-start(bf16[96,512]{1,0:T(8,128)(2,1)S(1)} %get-tuple-element.85), channel_id=1, source_target_pairs={{0,1},{1,0},{2,3},{3,2},{4,5},{5,4},{6,7},{7,6},{8,9},{9,8},{10,11... | collective-permute-start | bytes 294920 | tf_op jit(solution)/shard_map/ppermute | solution.py:16
  103.9 9.6 %collective-permute-start.32 = (bf16[96,512]{1,0:T(8,128)(2,1)S(1)}, bf16[96,512]{1,0:T(8,128)(2,1)S(1)}, u32[]{:S(2)}, u32[]{:S(2)}) collective-permute-start(bf16[96,512]{1,0:T(8,128)(2,1)S(1)} %get-tuple-element.91), channel_id=1, source_target_pairs={{0,2},{1,3},{2,0},{3,1},{4,6},{5,7},{6,4},{7,5},{8,10},{9,11},{10,... | collective-permute-start | bytes 294920 | tf_op jit(solution)/shard_map/ppermute | solution.py:16
  104.6 8.9 %collective-permute-start.33 = (bf16[96,512]{1,0:T(8,128)(2,1)S(1)}, bf16[96,512]{1,0:T(8,128)(2,1)S(1)}, u32[]{:S(2)}, u32[]{:S(2)}) collective-permute-start(bf16[96,512]{1,0:T(8,128)(2,1)S(1)} %get-tuple-element.92), channel_id=1, source_target_pairs={{0,3},{1,2},{2,1},{3,0},{4,7},{5,6},{6,5},{7,4},{8,11},{9,10},{10,... | collective-permute-start | bytes 294920 | tf_op jit(solution)/shard_map/ppermute | solution.py:16
  114.4 8.8 %collective-permute-start.35 = (bf16[128,512]{1,0:T(8,128)(2,1)S(1)}, bf16[128,512]{1,0:T(8,128)(2,1)S(1)}, u32[]{:S(2)}, u32[]{:S(2)}) collective-permute-start(bf16[128,512]{1,0:T(8,128)(2,1)S(1)} %shard_map.89.refs_0_), channel_id=1, source_target_pairs={{0,2},{1,3},{2,0},{3,1},{4,6},{5,7},{6,4},{7,5},{8,10},{9,11},{10,... | collective-permute-start | bytes 393224 | tf_op jit(solution)/shard_map/ppermute | solution.py:16
  116.8 8.7 %collective-permute-start.34 = (bf16[128,512]{1,0:T(8,128)(2,1)S(1)}, bf16[128,512]{1,0:T(8,128)(2,1)S(1)}, u32[]{:S(2)}, u32[]{:S(2)}) collective-permute-start(bf16[128,512]{1,0:T(8,128)(2,1)S(1)} %shard_map.89.refs_0_), channel_id=1, source_target_pairs={{0,1},{1,0},{2,3},{3,2},{4,5},{5,4},{6,7},{7,6},{8,9},{9,8},{10,11... | collective-permute-start | bytes 393224 | tf_op jit(solution)/shard_map/ppermute | solution.py:16
  116.9 10.4 %collective-permute-start.36 = (bf16[96,512]{1,0:T(8,128)(2,1)S(1)}, bf16[96,512]{1,0:T(8,128)(2,1)S(1)}, u32[]{:S(2)}, u32[]{:S(2)}) collective-permute-start(bf16[96,512]{1,0:T(8,128)(2,1)S(1)} %get-tuple-element.94), channel_id=1, source_target_pairs={{0,1},{1,0},{2,3},{3,2},{4,5},{5,4},{6,7},{7,6},{8,9},{9,8},{10,11... | collective-permute-start | bytes 294920 | tf_op jit(solution)/shard_map/ppermute | solution.py:16
  118.8 8.5 %collective-permute-start.37 = (bf16[96,512]{1,0:T(8,128)(2,1)S(1)}, bf16[96,512]{1,0:T(8,128)(2,1)S(1)}, u32[]{:S(2)}, u32[]{:S(2)}) collective-permute-start(bf16[96,512]{1,0:T(8,128)(2,1)S(1)} %get-tuple-element.95), channel_id=1, source_target_pairs={{0,2},{1,3},{2,0},{3,1},{4,6},{5,7},{6,4},{7,5},{8,10},{9,11},{10,... | collective-permute-start | bytes 294920 | tf_op jit(solution)/shard_map/ppermute | solution.py:16
  119.4 11.0 %collective-permute-start.38 = (bf16[96,512]{1,0:T(8,128)(2,1)S(1)}, bf16[96,512]{1,0:T(8,128)(2,1)S(1)}, u32[]{:S(2)}, u32[]{:S(2)}) collective-permute-start(bf16[96,512]{1,0:T(8,128)(2,1)S(1)} %get-tuple-element.96), channel_id=1, source_target_pairs={{0,3},{1,2},{2,1},{3,0},{4,7},{5,6},{6,5},{7,4},{8,11},{9,10},{10,... | collective-permute-start | bytes 294920 | tf_op jit(solution)/shard_map/ppermute | solution.py:16
  131.2 7.3 %collective-permute-start.40 = (bf16[128,512]{1,0:T(8,128)(2,1)S(1)}, bf16[128,512]{1,0:T(8,128)(2,1)S(1)}, u32[]{:S(2)}, u32[]{:S(2)}) collective-permute-start(bf16[128,512]{1,0:T(8,128)(2,1)S(1)} %shard_map.90.refs_0_), channel_id=1, source_target_pairs={{0,2},{1,3},{2,0},{3,1},{4,6},{5,7},{6,4},{7,5},{8,10},{9,11},{10,... | collective-permute-start | bytes 393224 | tf_op jit(solution)/shard_map/ppermute | solution.py:16
  133.2 7.0 %collective-permute-start.42 = (bf16[128,512]{1,0:T(8,128)(2,1)S(1)}, bf16[128,512]{1,0:T(8,128)(2,1)S(1)}, u32[]{:S(2)}, u32[]{:S(2)}) collective-permute-start(bf16[128,512]{1,0:T(8,128)(2,1)S(1)} %collective-permute-done.35.refs_2_), channel_id=1, source_target_pairs={{0,1},{1,0},{2,3},{3,2},{4,5},{5,4},{6,7},{7,6},{8,9},{9,8},{10,11... | collective-permute-start | bytes 393224 | tf_op jit(solution)/shard_map/ppermute | solution.py:16
  134.0 8.5 %collective-permute-start.39 = (bf16[128,512]{1,0:T(8,128)(2,1)S(1)}, bf16[128,512]{1,0:T(8,128)(2,1)S(1)}, u32[]{:S(2)}, u32[]{:S(2)}) collective-permute-start(bf16[128,512]{1,0:T(8,128)(2,1)S(1)} %shard_map.90.refs_0_), channel_id=1, source_target_pairs={{0,1},{1,0},{2,3},{3,2},{4,5},{5,4},{6,7},{7,6},{8,9},{9,8},{10,11... | collective-permute-start | bytes 393224 | tf_op jit(solution)/shard_map/ppermute | solution.py:16
  138.6 5.3 %collective-permute-start.41 = (bf16[128,512]{1,0:T(8,128)(2,1)S(1)}, bf16[128,512]{1,0:T(8,128)(2,1)S(1)}, u32[]{:S(2)}, u32[]{:S(2)}) collective-permute-start(bf16[128,512]{1,0:T(8,128)(2,1)S(1)} %collective-permute-done.40.refs_2_), channel_id=1, source_target_pairs={{0,1},{1,0},{2,3},{3,2},{4,5},{5,4},{6,7},{7,6},{8,9},{9,8},{10,11... | collective-permute-start | bytes 393224 | tf_op jit(solution)/shard_map/ppermute | solution.py:16

commit v5 on v4

--- a/solution.py
+++ b/solution.py
@@ -110,13 +110,17 @@
             [jnp.where(picked[i] > 0.0, slots[i : i + 1, :] + (k * cap + 1), 0.0) for k, i in enumerate(rows)], axis=1
         )
         weight = jnp.concatenate([weights[i] for i in rows], axis=1)
-        at = jnp.where(lax.broadcasted_iota(I32, (lines, line.shape[1]), 0) == line, 1.0, 0.0)
+        high = weight.astype(BF16)
+        middle = (weight - high.astype(F32)).astype(BF16)
+        low = (weight - high.astype(F32) - middle.astype(F32)).astype(BF16)
         moved = lax.dot_general(
-            jnp.concatenate([slot, weight], axis=0), at, (((1,), (1,)), ((), ())),
-            precision=lax.Precision.HIGHEST, preferred_element_type=F32,
+            jnp.concatenate([slot.astype(BF16), high, middle, low], axis=0),
+            one_hot(line, lines),
+            (((1,), (1,)), ((), ())),
+            preferred_element_type=F32,
         )
         slot_ref[r] = moved[:1, :].astype(I32) - 1
-        weight_ref[r] = moved[1:, :]
+        weight_ref[r] = moved[1:2, :] + (moved[2:3, :] + moved[3:4, :])
 
 
 def dispatch_kernel(me_ref, ranks_ref, *refs):

time: 146 us -> 146 us (level)
  Pallas kernels: 36.4 us -> 34.3 us
  waiting for transfers between devices: 55.3 us -> 57.1 us
    pallas_call x20, Pallas kernels: 36.4 us -> 34.3 us  [call(): pl.pallas_call(kernel, out_shape=tuple(outs), in_specs=[pl.BlockSpec(memo...]
    ppermute x43, waiting for transfers between devices: 55.3 us -> 57.1 us  [hop(): return lax.ppermute(x, axis, [(i, i ^ step) for i in range(count)])]
  transfers between devices with their start and end apart: 43 -> 43, of which waited for: 21 -> 23; matrix products, arithmetic and copies ran while one was open for 0% -> 0% of each run, Pallas kernels for 19% -> 17%
where the time goes in v5:
time: 146 us
  waiting for transfers between devices  57.1 us (39%)
  starting transfers between devices  51.9 us (36%)
  Pallas kernels  34.3 us (23%)
  local copies, waits for them, and re-layouts  2.36 us (2%)
    ppermute x43, waiting for transfers between devices, hop(): return lax.ppermute(x, axis, [(i, i ^ step) for i in range(count)])  57.1 us
    ppermute x43, starting transfers between devices, hop(): return lax.ppermute(x, axis, [(i, i ^ step) for i in range(count)])  51.9 us
    pallas_call x20, Pallas kernels, call(): pl.pallas_call(kernel, out_shape=tuple(outs), in_specs=[pl.BlockSpec(memo...  34.3 us
  transfers between devices with their start and end apart: 43, of which 23 were waited for; matrix products, arithmetic and copies ran while one was open for 0% of the time, Pallas kernels for 17%

profile of v5, /device:TPU:0, one launch (start us, length us, event | category | flops | bytes accessed | tf_op | source)
XLA Modules:
  0.0 146.1 jit_solution(10574608579808075301)
XLA Ops:
  0.5 2.6 %collective-permute-start.1 = (bf16[256,1024]{1,0:T(8,128)(2,1)}, bf16[256,1024]{1,0:T(8,128)(2,1)S(1)}, u32[]{:S(2)}, u32[]{:S(2)}) collective-permute-start(bf16[256,1024]{1,0:T(8,128)(2,1)} %refs_0_.2), channel_id=1, source_target_pairs={{0,8},{4,12},{8,0},{12,4},{1,9},{5,13},{9,1},{13,5},{2,10},{6,14},... | collective-permute-start | bytes 1572872 | tf_op jit(solution)/shard_map/ppermute | solution.py:16
  3.1 1.2 copy-done.1
  4.3 1.0 copy-done.2
  5.4 1.4 shard_map.73
  6.8 2.1 %collective-permute-start.3 = (bf16[128,512]{1,0:T(8,128)(2,1)S(1)}, bf16[128,512]{1,0:T(8,128)(2,1)S(1)}, u32[]{:S(2)}, u32[]{:S(2)}) collective-permute-start(bf16[128,512]{1,0:T(8,128)(2,1)S(1)} %get-tuple-element.52), channel_id=1, source_target_pairs={{0,1},{1,0},{2,3},{3,2},{4,5},{5,4},{6,7},{7,6},{8,9},{9,8},{10,11... | collective-permute-start | bytes 393224 | tf_op jit(solution)/shard_map/ppermute | solution.py:16
  8.9 2.6 %collective-permute-start.4 = (bf16[128,512]{1,0:T(8,128)(2,1)S(1)}, bf16[128,512]{1,0:T(8,128)(2,1)S(1)}, u32[]{:S(2)}, u32[]{:S(2)}) collective-permute-start(bf16[128,512]{1,0:T(8,128)(2,1)S(1)} %get-tuple-element.53), channel_id=1, source_target_pairs={{0,2},{1,3},{2,0},{3,1},{4,6},{5,7},{6,4},{7,5},{8,10},{9,11},{10,... | collective-permute-start | bytes 393224 | tf_op jit(solution)/shard_map/ppermute | solution.py:16
  11.5 1.8 %collective-permute-start.7 = (s32[12,512]{1,0:T(8,128)S(1)}, s32[12,512]{1,0:T(8,128)S(1)}, u32[]{:S(2)}, u32[]{:S(2)}) collective-permute-start(s32[12,512]{1,0:T(8,128)S(1)} %pad_add_fusion.refs_0_), channel_id=1, source_target_pairs={{0,8},{4,12},{8,0},{12,4},{1,9},{5,13},{9,1},{13,5},{2,10},{6,14},... | collective-permute-start | bytes 73736 | tf_op jit(solution)/shard_map/ppermute | solution.py:16
  13.3 3.2 %collective-permute-done.7.refs_2_ = s32[12,512]{1,0:T(8,128)S(1)} collective-permute-done((s32[12,512]{1,0:T(8,128)S(1)}, s32[12,512]{1,0:T(8,128)S(1)}, u32[]{:S(2)}, u32[]{:S(2)}) %collective-permute-start.7) | collective-permute-done | bytes 24608 | tf_op jit(solution)/shard_map/ppermute | solution.py:16
  16.5 1.2 collective-permute-done.6.refs_1_
  18.9 1.2 shard_map.75
  20.1 1.7 %collective-permute-done.4.refs_2_ = bf16[128,512]{1,0:T(8,128)(2,1)S(1)} collective-permute-done((bf16[128,512]{1,0:T(8,128)(2,1)S(1)}, bf16[128,512]{1,0:T(8,128)(2,1)S(1)}, u32[]{:S(2)}, u32[]{:S(2)}) %collective-permute-start.4) | collective-permute-done | bytes 131104 | tf_op jit(solution)/shard_map/ppermute | solution.py:16
  21.8 0.8 shard_map.76
  22.7 1.6 %collective-permute-start.9 = (bf16[256,1024]{1,0:T(8,128)(2,1)S(1)}, bf16[256,1024]{1,0:T(8,128)(2,1)S(1)}, u32[]{:S(2)}, u32[]{:S(2)}) collective-permute-start(bf16[256,1024]{1,0:T(8,128)(2,1)S(1)} %copy-done.3), channel_id=1, source_target_pairs={{0,8},{4,12},{8,0},{12,4},{1,9},{5,13},{9,1},{13,5},{2,10},{6,14},... | collective-permute-start | bytes 1572872 | tf_op jit(solution)/shard_map/ppermute | solution.py:16
  24.3 2.3 %collective-permute-start.11 = (bf16[96,512]{1,0:T(8,128)(2,1)S(1)}, bf16[96,512]{1,0:T(8,128)(2,1)S(1)}, u32[]{:S(2)}, u32[]{:S(2)}) collective-permute-start(bf16[96,512]{1,0:T(8,128)(2,1)S(1)} %get-tuple-element.61), channel_id=1, source_target_pairs={{0,1},{1,0},{2,3},{3,2},{4,5},{5,4},{6,7},{7,6},{8,9},{9,8},{10,11... | collective-permute-start | bytes 294920 | tf_op jit(solution)/shard_map/ppermute | solution.py:16
  26.5 1.0 collective-permute-start.12
  27.6 1.9 %shard_map.78 = (bf16[128,512]{1,0:T(8,128)(2,1)S(1)}, bf16[128,512]{1,0:T(8,128)(2,1)S(1)}, bf16[128,512]{1,0:T(8,128)(2,1)S(1)}, bf16[128,512]{1,0:T(8,128)(2,1)S(1)}, bf16[16,1024]{1,0:T(8,128)(2,1)}) custom-call(s32[2]{0:T(128)S(1)} %pad_add_fusion.1.me_ref, bf16[512,1024]{1,0:T(8,128)(2,1)S(1)} %get-tuple-element.64.tokens_ref, ...), custom_call_target="tpu_custom_call" | custom-call | flops 536870912 | bytes 2654208 | tf_op jit(solution)/shard_map/pallas_call | solution.py:30
  29.5 2.0 %collective-permute-start.15 = (bf16[128,512]{1,0:T(8,128)(2,1)S(1)}, bf16[128,512]{1,0:T(8,128)(2,1)S(1)}, u32[]{:S(2)}, u32[]{:S(2)}) collective-permute-start(bf16[128,512]{1,0:T(8,128)(2,1)S(1)} %get-tuple-element.66), channel_id=1, source_target_pairs={{0,1},{1,0},{2,3},{3,2},{4,5},{5,4},{6,7},{7,6},{8,9},{9,8},{10,11... | collective-permute-start | bytes 393224 | tf_op jit(solution)/shard_map/ppermute | solution.py:16
  31.5 2.4 %collective-permute-start.17 = (bf16[128,512]{1,0:T(8,128)(2,1)S(1)}, bf16[128,512]{1,0:T(8,128)(2,1)S(1)}, u32[]{:S(2)}, u32[]{:S(2)}) collective-permute-start(bf16[128,512]{1,0:T(8,128)(2,1)S(1)} %get-tuple-element.68), channel_id=1, source_target_pairs={{0,3},{1,2},{2,1},{3,0},{4,7},{5,6},{6,5},{7,4},{8,11},{9,10},{10,... | collective-permute-start | bytes 393224 | tf_op jit(solution)/shard_map/ppermute | solution.py:16
  33.9 3.7 %collective-permute-start.13 = (bf16[96,512]{1,0:T(8,128)(2,1)S(1)}, bf16[96,512]{1,0:T(8,128)(2,1)S(1)}, u32[]{:S(2)}, u32[]{:S(2)}) collective-permute-start(bf16[96,512]{1,0:T(8,128)(2,1)S(1)} %get-tuple-element.63), channel_id=1, source_target_pairs={{0,3},{1,2},{2,1},{3,0},{4,7},{5,6},{6,5},{7,4},{8,11},{9,10},{10,... | collective-permute-start | bytes 294920 | tf_op jit(solution)/shard_map/ppermute | solution.py:16
  37.5 7.1 %collective-permute-done.13 = bf16[96,512]{1,0:T(8,128)(2,1)S(1)} collective-permute-done((bf16[96,512]{1,0:T(8,128)(2,1)S(1)}, bf16[96,512]{1,0:T(8,128)(2,1)S(1)}, u32[]{:S(2)}, u32[]{:S(2)}) %collective-permute-start.13) | collective-permute-done | bytes 98336 | tf_op jit(solution)/shard_map/ppermute | solution.py:16
  45.2 1.4 collective-permute-done.16.refs_2_
  48.0 0.8 shard_map.79
  48.9 6.0 %collective-permute-start.21 = (bf16[96,512]{1,0:T(8,128)(2,1)S(1)}, bf16[96,512]{1,0:T(8,128)(2,1)S(1)}, u32[]{:S(2)}, u32[]{:S(2)}) collective-permute-start(bf16[96,512]{1,0:T(8,128)(2,1)S(1)} %get-tuple-element.76), channel_id=1, source_target_pairs={{0,1},{1,0},{2,3},{3,2},{4,5},{5,4},{6,7},{7,6},{8,9},{9,8},{10,11... | collective-permute-start | bytes 294920 | tf_op jit(solution)/shard_map/ppermute | solution.py:16
  54.9 0.7 collective-permute-start.22
  55.6 1.7 %collective-permute-start.23 = (bf16[96,512]{1,0:T(8,128)(2,1)S(1)}, bf16[96,512]{1,0:T(8,128)(2,1)S(1)}, u32[]{:S(2)}, u32[]{:S(2)}) collective-permute-start(bf16[96,512]{1,0:T(8,128)(2,1)S(1)} %get-tuple-element.78), channel_id=1, source_target_pairs={{0,3},{1,2},{2,1},{3,0},{4,7},{5,6},{6,5},{7,4},{8,11},{9,10},{10,... | collective-permute-start | bytes 294920 | tf_op jit(solution)/shard_map/ppermute | solution.py:16
  57.3 0.7 collective-permute-done.21
  58.1 7.5 %collective-permute-done.22 = bf16[96,512]{1,0:T(8,128)(2,1)S(1)} collective-permute-done((bf16[96,512]{1,0:T(8,128)(2,1)S(1)}, bf16[96,512]{1,0:T(8,128)(2,1)S(1)}, u32[]{:S(2)}, u32[]{:S(2)}) %collective-permute-start.22) | collective-permute-done | bytes 98336 | tf_op jit(solution)/shard_map/ppermute | solution.py:16
  66.2 1.2 collective-permute-done.24.refs_3_
  67.3 4.4 %shard_map.80.hidden_ref = bf16[512,2688]{1,0:T(8,128)(2,1)S(1)} custom-call(s32[2]{0:T(128)S(1)} %pad_add_fusion.1.me_ref, s32[4,1,384]{2,1,0:T(1,128)S(1)} %get-tuple-element.83.slot_ref, bf16[384,512]{1,0:T(8,128)(2,1)S(1)} %constant_dynamic-update-slice_fusion.refs_0_, bf16[384,512]{1,0:T(8,128)(2,1)S(1)} %collective-permute-done.20.refs_1_, ...), custom_call_target="tpu_custom_call" | custom-call | flops 2818572288 | bytes 9836544 | tf_op jit(solution)/shard_map/pallas_call | solution.py:30
  71.7 4.3 %shard_map.81 = (bf16[384,1024]{1,0:T(8,128)(2,1)S(1)}, bf16[384,1024]{1,0:T(8,128)(2,1)S(1)}) custom-call(s32[2]{0:T(128)S(1)} %pad_add_fusion.1.me_ref, s32[4,1,384]{2,1,0:T(1,128)S(1)} %get-tuple-element.83.slot_ref, f32[4,1,384]{2,1,0:T(1,128)S(1)} %get-tuple-element.60.weight_ref, bf16[512,2688]{1,0:T(8,128)(2,1)S(1)} %shard_map.80.hidden_ref, ...), custom_call_target="tpu_custom_call" | custom-call | flops 2818572288 | bytes 9842688 | tf_op jit(solution)/shard_map/pallas_call | solution.py:30
  76.0 1.1 collective-permute-done.26.refs_1_
  77.2 2.6 %shard_map.82.hidden_ref = bf16[256,2688]{1,0:T(8,128)(2,1)S(1)} custom-call(s32[2]{0:T(128)S(1)} %pad_add_fusion.1.me_ref, s32[4,1,384]{2,1,0:T(1,128)S(1)} %get-tuple-element.83.slot_ref, bf16[384,512]{1,0:T(8,128)(2,1)S(1)} %collective-permute-done.18.refs_0_, bf16[384,512]{1,0:T(8,128)(2,1)S(1)} %collective-permute-done.26.refs_1_, ...), custom_call_target="tpu_custom_call" | custom-call | flops 1409286144 | bytes 7673856 | tf_op jit(solution)/shard_map/pallas_call | solution.py:30
  79.8 2.8 %shard_map.83.hidden_ref = bf16[256,2688]{1,0:T(8,128)(2,1)S(1)} custom-call(s32[2]{0:T(128)S(1)} %pad_add_fusion.1.me_ref, s32[4,1,384]{2,1,0:T(1,128)S(1)} %get-tuple-element.83.slot_ref, bf16[384,512]{1,0:T(8,128)(2,1)S(1)} %collective-permute-done.19.refs_0_, bf16[384,512]{1,0:T(8,128)(2,1)S(1)} %collective-permute-done.27.refs_1_, ...), custom_call_target="tpu_custom_call" | custom-call | flops 1 | bytes 1 | tf_op jit(solution)/shard_map/pallas_call | solution.py:30
  82.6 2.7 %shard_map.84 = bf16[384,1024]{1,0:T(8,128)(2,1)S(1)} custom-call(s32[2]{0:T(128)S(1)} %pad_add_fusion.1.me_ref, s32[4,1,384]{2,1,0:T(1,128)S(1)} %get-tuple-element.83.slot_ref, f32[4,1,384]{2,1,0:T(1,128)S(1)} %get-tuple-element.60.weight_ref, bf16[256,2688]{1,0:T(8,128)(2,1)S(1)} %shard_map.83.hidden_ref, bf16[2688,1024]{1,0:T(8,128)(2,1)S(1)} %bitcast.12), custom_call_target="tpu_custom_call" | custom-call | flops 1 | bytes 1 | tf_op jit(solution)/shard_map/pallas_call | solution.py:30
  85.9 2.7 %shard_map.85.refs_0_ = bf16[384,1024]{1,0:T(8,128)(2,1)S(1)} custom-call(s32[2]{0:T(128)S(1)} %pad_add_fusion.1.me_ref, s32[4,1,384]{2,1,0:T(1,128)S(1)} %get-tuple-element.83.slot_ref, f32[4,1,384]{2,1,0:T(1,128)S(1)} %get-tuple-element.60.weight_ref, bf16[256,2688]{1,0:T(8,128)(2,1)S(1)} %shard_map.82.hidden_ref, bf16[2688,1024]{1,0:T(8,128)(2,1)S(1)} %bitcast.13), custom_call_target="tpu_custom_call" | custom-call | flops 1 | bytes 1 | tf_op jit(solution)/shard_map/pallas_call | solution.py:30
  88.6 0.7 shard_map.86
  89.9 1.5 %collective-permute-start.31 = (bf16[384,512]{1,0:T(8,128)(2,1)S(1)}, bf16[384,512]{1,0:T(8,128)(2,1)S(1)}, u32[]{:S(2)}, u32[]{:S(2)}) collective-permute-start(bf16[384,512]{1,0:T(8,128)(2,1)S(1)} %get-tuple-element.87), channel_id=1, source_target_pairs={{0,8},{4,12},{8,0},{12,4},{1,9},{5,13},{9,1},{13,5},{2,10},{6,14},... | collective-permute-start | bytes 1179656 | tf_op jit(solution)/shard_map/ppermute | solution.py:16
  91.4 9.9 %collective-permute-done.29.refs_2_ = bf16[384,512]{1,0:T(8,128)(2,1)S(1)} collective-permute-done((bf16[384,512]{1,0:T(8,128)(2,1)S(1)}, bf16[384,512]{1,0:T(8,128)(2,1)S(1)}, u32[]{:S(2)}, u32[]{:S(2)}) %collective-permute-start.29) | collective-permute-done | bytes 393248 | tf_op jit(solution)/shard_map/ppermute | solution.py:16
  101.3 0.7 shard_map.87
  102.0 1.8 %collective-permute-start.30 = (bf16[96,512]{1,0:T(8,128)(2,1)S(1)}, bf16[96,512]{1,0:T(8,128)(2,1)S(1)}, u32[]{:S(2)}, u32[]{:S(2)}) collective-permute-start(bf16[96,512]{1,0:T(8,128)(2,1)S(1)} %get-tuple-element.85), channel_id=1, source_target_pairs={{0,1},{1,0},{2,3},{3,2},{4,5},{5,4},{6,7},{7,6},{8,9},{9,8},{10,11... | collective-permute-start | bytes 294920 | tf_op jit(solution)/shard_map/ppermute | solution.py:16
  103.8 0.8 collective-permute-start.32
  104.5 1.9 %collective-permute-start.33 = (bf16[96,512]{1,0:T(8,128)(2,1)S(1)}, bf16[96,512]{1,0:T(8,128)(2,1)S(1)}, u32[]{:S(2)}, u32[]{:S(2)}) collective-permute-start(bf16[96,512]{1,0:T(8,128)(2,1)S(1)} %get-tuple-element.92), channel_id=1, source_target_pairs={{0,3},{1,2},{2,1},{3,0},{4,7},{5,6},{6,5},{7,4},{8,11},{9,10},{10,... | collective-permute-start | bytes 294920 | tf_op jit(solution)/shard_map/ppermute | solution.py:16
  106.4 0.8 collective-permute-done.30.refs_1_
  107.3 2.0 %collective-permute-done.31.refs_2_ = bf16[384,512]{1,0:T(8,128)(2,1)S(1)} collective-permute-done((bf16[384,512]{1,0:T(8,128)(2,1)S(1)}, bf16[384,512]{1,0:T(8,128)(2,1)S(1)}, u32[]{:S(2)}, u32[]{:S(2)}) %collective-permute-start.31) | collective-permute-done | bytes 393248 | tf_op jit(solution)/shard_map/ppermute | solution.py:16
  109.3 0.7 shard_map.88
  109.9 3.5 %collective-permute-done.32.refs_2_ = bf16[96,512]{1,0:T(8,128)(2,1)S(1)} collective-permute-done((bf16[96,512]{1,0:T(8,128)(2,1)S(1)}, bf16[96,512]{1,0:T(8,128)(2,1)S(1)}, u32[]{:S(2)}, u32[]{:S(2)}) %collective-permute-start.32) | collective-permute-done | bytes 98336 | tf_op jit(solution)/shard_map/ppermute | solution.py:16
  113.4 0.9 shard_map.89.refs_0_
  114.3 2.4 %collective-permute-start.35 = (bf16[128,512]{1,0:T(8,128)(2,1)S(1)}, bf16[128,512]{1,0:T(8,128)(2,1)S(1)}, u32[]{:S(2)}, u32[]{:S(2)}) collective-permute-start(bf16[128,512]{1,0:T(8,128)(2,1)S(1)} %shard_map.89.refs_0_), channel_id=1, source_target_pairs={{0,2},{1,3},{2,0},{3,1},{4,6},{5,7},{6,4},{7,5},{8,10},{9,11},{10,... | collective-permute-start | bytes 393224 | tf_op jit(solution)/shard_map/ppermute | solution.py:16
  116.8 1.9 %collective-permute-start.36 = (bf16[96,512]{1,0:T(8,128)(2,1)S(1)}, bf16[96,512]{1,0:T(8,128)(2,1)S(1)}, u32[]{:S(2)}, u32[]{:S(2)}) collective-permute-start(bf16[96,512]{1,0:T(8,128)(2,1)S(1)} %get-tuple-element.94), channel_id=1, source_target_pairs={{0,1},{1,0},{2,3},{3,2},{4,5},{5,4},{6,7},{7,6},{8,9},{9,8},{10,11... | collective-permute-start | bytes 294920 | tf_op jit(solution)/shard_map/ppermute | solution.py:16
  119.3 1.9 %collective-permute-start.38 = (bf16[96,512]{1,0:T(8,128)(2,1)S(1)}, bf16[96,512]{1,0:T(8,128)(2,1)S(1)}, u32[]{:S(2)}, u32[]{:S(2)}) collective-permute-start(bf16[96,512]{1,0:T(8,128)(2,1)S(1)} %get-tuple-element.96), channel_id=1, source_target_pairs={{0,3},{1,2},{2,1},{3,0},{4,7},{5,6},{6,5},{7,4},{8,11},{9,10},{10,... | collective-permute-start | bytes 294920 | tf_op jit(solution)/shard_map/ppermute | solution.py:16
  121.2 2.0 %collective-permute-done.35.refs_2_ = bf16[128,512]{1,0:T(8,128)(2,1)S(1)} collective-permute-done((bf16[128,512]{1,0:T(8,128)(2,1)S(1)}, bf16[128,512]{1,0:T(8,128)(2,1)S(1)}, u32[]{:S(2)}, u32[]{:S(2)}) %collective-permute-start.35) | collective-permute-done | bytes 131104 | tf_op jit(solution)/shard_map/ppermute | solution.py:16
  123.3 2.3 %collective-permute-done.34.refs_1_ = bf16[128,512]{1,0:T(8,128)(2,1)S(1)} collective-permute-done((bf16[128,512]{1,0:T(8,128)(2,1)S(1)}, bf16[128,512]{1,0:T(8,128)(2,1)S(1)}, u32[]{:S(2)}, u32[]{:S(2)}) %collective-permute-start.34) | collective-permute-done | bytes 131104 | tf_op jit(solution)/shard_map/ppermute | solution.py:16
  125.6 2.0 %collective-permute-done.36.refs_1_ = bf16[96,512]{1,0:T(8,128)(2,1)S(1)} collective-permute-done((bf16[96,512]{1,0:T(8,128)(2,1)S(1)}, bf16[96,512]{1,0:T(8,128)(2,1)S(1)}, u32[]{:S(2)}, u32[]{:S(2)}) %collective-permute-start.36) | collective-permute-done | bytes 98336 | tf_op jit(solution)/shard_map/ppermute | solution.py:16
  127.6 2.6 %collective-permute-done.38.refs_3_ = bf16[96,512]{1,0:T(8,128)(2,1)S(1)} collective-permute-done((bf16[96,512]{1,0:T(8,128)(2,1)S(1)}, bf16[96,512]{1,0:T(8,128)(2,1)S(1)}, u32[]{:S(2)}, u32[]{:S(2)}) %collective-permute-start.38) | collective-permute-done | bytes 98336 | tf_op jit(solution)/shard_map/ppermute | solution.py:16
  130.2 0.9 shard_map.90.refs_0_
  131.1 2.0 %collective-permute-start.40 = (bf16[128,512]{1,0:T(8,128)(2,1)S(1)}, bf16[128,512]{1,0:T(8,128)(2,1)S(1)}, u32[]{:S(2)}, u32[]{:S(2)}) collective-permute-start(bf16[128,512]{1,0:T(8,128)(2,1)S(1)} %shard_map.90.refs_0_), channel_id=1, source_target_pairs={{0,2},{1,3},{2,0},{3,1},{4,6},{5,7},{6,4},{7,5},{8,10},{9,11},{10,... | collective-permute-start | bytes 393224 | tf_op jit(solution)/shard_map/ppermute | solution.py:16
  133.1 0.9 collective-permute-start.42
  134.0 1.2 collective-permute-start.39
  135.2 3.7 %collective-permute-done.40.refs_2_ = bf16[128,512]{1,0:T(8,128)(2,1)S(1)} collective-permute-done((bf16[128,512]{1,0:T(8,128)(2,1)S(1)}, bf16[128,512]{1,0:T(8,128)(2,1)S(1)}, u32[]{:S(2)}, u32[]{:S(2)}) %collective-permute-start.40) | collective-permute-done | bytes 131104 | tf_op jit(solution)/shard_map/ppermute | solution.py:16
  138.8 1.0 collective-permute-start.41
  139.8 0.8 collective-permute-done.42.refs_3_
  140.6 1.3 shard_map.91.refs_4_
  142.5 1.4 collective-permute-done.41.refs_3_
  143.9 2.3 %shard_map.92 = bf16[512,1024]{1,0:T(8,128)(2,1)} custom-call(s32[2]{0:T(128)S(1)} %pad_add_fusion.1.me_ref, bf16[1024,1024]{1,0:T(8,128)(2,1)S(1)} %shard_map.77.weights_ref, bf16[128,512]{1,0:T(8,128)(2,1)S(1)} %shard_map.90.refs_0_, bf16[128,512]{1,0:T(8,128)(2,1)S(1)} %collective-permute-done.39.refs_1_, ...), custom_call_target="tpu_custom_call" | custom-call | flops 536870912 | bytes 5767168 | tf_op jit(solution)/shard_map/pallas_call | solution.py:30
  (69 shorter events, 6.8 us)
Async XLA Ops:
  0.0 11.5 %copy-start.4 = (s32[512,6]{0,1:T(8,128)S(1)}, s32[512,6]{0,1:T(8,128)}, u32[]{:S(2)}) copy-start(s32[512,6]{0,1:T(8,128)} %param.12) | copy-start | bytes 36868
  0.0 3.1 %collective-permute-start.2 = (bf16[256,1024]{1,0:T(8,128)(2,1)}, bf16[256,1024]{1,0:T(8,128)(2,1)S(1)}, u32[]{:S(2)}, u32[]{:S(2)}) collective-permute-start(bf16[256,1024]{1,0:T(8,128)(2,1)} %refs_0_.2), channel_id=1, source_target_pairs={{0,4},{4,0},{8,12},{12,8},{1,5},{5,1},{9,13},{13,9},{2,6},{6,2},{1... | collective-permute-start | bytes 1572872 | tf_op jit(solution)/shard_map/ppermute | solution.py:16
  0.5 19.7 %collective-permute-start.1 = (bf16[256,1024]{1,0:T(8,128)(2,1)}, bf16[256,1024]{1,0:T(8,128)(2,1)S(1)}, u32[]{:S(2)}, u32[]{:S(2)}) collective-permute-start(bf16[256,1024]{1,0:T(8,128)(2,1)} %refs_0_.2), channel_id=1, source_target_pairs={{0,8},{4,12},{8,0},{12,4},{1,9},{5,13},{9,1},{13,5},{2,10},{6,14},... | collective-permute-start | bytes 1572872 | tf_op jit(solution)/shard_map/ppermute | solution.py:16
  3.1 1.2 copy-start.1
  4.3 1.0 copy-start.2
  5.4 6.1 %copy-start.5 = (s32[512,6]{0,1:T(8,128)S(1)}, s32[512,6]{0,1:T(8,128)}, u32[]{:S(2)}) copy-start(s32[512,6]{0,1:T(8,128)} %param.13) | copy-start | bytes 36868
  5.4 17.3 %copy-start.3 = (bf16[256,1024]{1,0:T(8,128)(2,1)S(1)}, bf16[256,1024]{1,0:T(8,128)(2,1)}, u32[]{:S(2)}) copy-start(bf16[256,1024]{1,0:T(8,128)(2,1)} %refs_0_.3) | copy-start | bytes 1572868
  6.8 13.3 %collective-permute-start.3 = (bf16[128,512]{1,0:T(8,128)(2,1)S(1)}, bf16[128,512]{1,0:T(8,128)(2,1)S(1)}, u32[]{:S(2)}, u32[]{:S(2)}) collective-permute-start(bf16[128,512]{1,0:T(8,128)(2,1)S(1)} %get-tuple-element.52), channel_id=1, source_target_pairs={{0,1},{1,0},{2,3},{3,2},{4,5},{5,4},{6,7},{7,6},{8,9},{9,8},{10,11... | collective-permute-start | bytes 393224 | tf_op jit(solution)/shard_map/ppermute | solution.py:16
  8.9 12.9 %collective-permute-start.4 = (bf16[128,512]{1,0:T(8,128)(2,1)S(1)}, bf16[128,512]{1,0:T(8,128)(2,1)S(1)}, u32[]{:S(2)}, u32[]{:S(2)}) collective-permute-start(bf16[128,512]{1,0:T(8,128)(2,1)S(1)} %get-tuple-element.53), channel_id=1, source_target_pairs={{0,2},{1,3},{2,0},{3,1},{4,6},{5,7},{6,4},{7,5},{8,10},{9,11},{10,... | collective-permute-start | bytes 393224 | tf_op jit(solution)/shard_map/ppermute | solution.py:16
  11.5 10.3 %collective-permute-start.5 = (bf16[128,512]{1,0:T(8,128)(2,1)S(1)}, bf16[128,512]{1,0:T(8,128)(2,1)S(1)}, u32[]{:S(2)}, u32[]{:S(2)}) collective-permute-start(bf16[128,512]{1,0:T(8,128)(2,1)S(1)} %get-tuple-element.54), channel_id=1, source_target_pairs={{0,3},{1,2},{2,1},{3,0},{4,7},{5,6},{6,5},{7,4},{8,11},{9,10},{10,... | collective-permute-start | bytes 393224 | tf_op jit(solution)/shard_map/ppermute | solution.py:16
  11.5 5.0 %collective-permute-start.7 = (s32[12,512]{1,0:T(8,128)S(1)}, s32[12,512]{1,0:T(8,128)S(1)}, u32[]{:S(2)}, u32[]{:S(2)}) collective-permute-start(s32[12,512]{1,0:T(8,128)S(1)} %pad_add_fusion.refs_0_), channel_id=1, source_target_pairs={{0,8},{4,12},{8,0},{12,4},{1,9},{5,13},{9,1},{13,5},{2,10},{6,14},... | collective-permute-start | bytes 73736 | tf_op jit(solution)/shard_map/ppermute | solution.py:16
  16.5 1.2 collective-permute-start.6
  17.7 1.2 collective-permute-start.8
  21.8 5.8 %collective-permute-start.14 = (bf16[256,1024]{1,0:T(8,128)(2,1)S(1)}, bf16[256,1024]{1,0:T(8,128)(2,1)S(1)}, u32[]{:S(2)}, u32[]{:S(2)}) collective-permute-start(bf16[256,1024]{1,0:T(8,128)(2,1)S(1)} %collective-permute-done.1.refs_0_), channel_id=1, source_target_pairs={{0,4},{4,0},{8,12},{12,8},{1,5},{5,1},{9,13},{13,9},{2,6},{6,2},{1... | collective-permute-start | bytes 1572872 | tf_op jit(solution)/shard_map/ppermute | solution.py:16
  22.7 22.0 %collective-permute-start.9 = (bf16[256,1024]{1,0:T(8,128)(2,1)S(1)}, bf16[256,1024]{1,0:T(8,128)(2,1)S(1)}, u32[]{:S(2)}, u32[]{:S(2)}) collective-permute-start(bf16[256,1024]{1,0:T(8,128)(2,1)S(1)} %copy-done.3), channel_id=1, source_target_pairs={{0,8},{4,12},{8,0},{12,4},{1,9},{5,13},{9,1},{13,5},{2,10},{6,14},... | collective-permute-start | bytes 1572872 | tf_op jit(solution)/shard_map/ppermute | solution.py:16
  24.3 7.3 %collective-permute-start.11 = (bf16[96,512]{1,0:T(8,128)(2,1)S(1)}, bf16[96,512]{1,0:T(8,128)(2,1)S(1)}, u32[]{:S(2)}, u32[]{:S(2)}) collective-permute-start(bf16[96,512]{1,0:T(8,128)(2,1)S(1)} %get-tuple-element.61), channel_id=1, source_target_pairs={{0,1},{1,0},{2,3},{3,2},{4,5},{5,4},{6,7},{7,6},{8,9},{9,8},{10,11... | collective-permute-start | bytes 294920 | tf_op jit(solution)/shard_map/ppermute | solution.py:16
  26.5 7.3 %collective-permute-start.12 = (bf16[96,512]{1,0:T(8,128)(2,1)S(1)}, bf16[96,512]{1,0:T(8,128)(2,1)S(1)}, u32[]{:S(2)}, u32[]{:S(2)}) collective-permute-start(bf16[96,512]{1,0:T(8,128)(2,1)S(1)} %get-tuple-element.62), channel_id=1, source_target_pairs={{0,2},{1,3},{2,0},{3,1},{4,6},{5,7},{6,4},{7,5},{8,10},{9,11},{10,... | collective-permute-start | bytes 294920 | tf_op jit(solution)/shard_map/ppermute | solution.py:16
  29.5 15.7 %collective-permute-start.15 = (bf16[128,512]{1,0:T(8,128)(2,1)S(1)}, bf16[128,512]{1,0:T(8,128)(2,1)S(1)}, u32[]{:S(2)}, u32[]{:S(2)}) collective-permute-start(bf16[128,512]{1,0:T(8,128)(2,1)S(1)} %get-tuple-element.66), channel_id=1, source_target_pairs={{0,1},{1,0},{2,3},{3,2},{4,5},{5,4},{6,7},{7,6},{8,9},{9,8},{10,11... | collective-permute-start | bytes 393224 | tf_op jit(solution)/shard_map/ppermute | solution.py:16
  31.5 15.1 %collective-permute-start.16 = (bf16[128,512]{1,0:T(8,128)(2,1)S(1)}, bf16[128,512]{1,0:T(8,128)(2,1)S(1)}, u32[]{:S(2)}, u32[]{:S(2)}) collective-permute-start(bf16[128,512]{1,0:T(8,128)(2,1)S(1)} %get-tuple-element.67), channel_id=1, source_target_pairs={{0,2},{1,3},{2,0},{3,1},{4,6},{5,7},{6,4},{7,5},{8,10},{9,11},{10,... | collective-permute-start | bytes 393224 | tf_op jit(solution)/shard_map/ppermute | solution.py:16
  31.5 15.1 %collective-permute-start.17 = (bf16[128,512]{1,0:T(8,128)(2,1)S(1)}, bf16[128,512]{1,0:T(8,128)(2,1)S(1)}, u32[]{:S(2)}, u32[]{:S(2)}) collective-permute-start(bf16[128,512]{1,0:T(8,128)(2,1)S(1)} %get-tuple-element.68), channel_id=1, source_target_pairs={{0,3},{1,2},{2,1},{3,0},{4,7},{5,6},{6,5},{7,4},{8,11},{9,10},{10,... | collective-permute-start | bytes 393224 | tf_op jit(solution)/shard_map/ppermute | solution.py:16
  33.9 10.8 %collective-permute-start.13 = (bf16[96,512]{1,0:T(8,128)(2,1)S(1)}, bf16[96,512]{1,0:T(8,128)(2,1)S(1)}, u32[]{:S(2)}, u32[]{:S(2)}) collective-permute-start(bf16[96,512]{1,0:T(8,128)(2,1)S(1)} %get-tuple-element.63), channel_id=1, source_target_pairs={{0,3},{1,2},{2,1},{3,0},{4,7},{5,6},{6,5},{7,4},{8,11},{9,10},{10,... | collective-permute-start | bytes 294920 | tf_op jit(solution)/shard_map/ppermute | solution.py:16
  44.7 2.5 %collective-permute-start = (bf16[256,1024]{1,0:T(8,128)(2,1)S(1)}, bf16[256,1024]{1,0:T(8,128)(2,1)S(1)}, u32[]{:S(2)}, u32[]{:S(2)}) collective-permute-start(bf16[256,1024]{1,0:T(8,128)(2,1)S(1)} %copy-done.3), channel_id=1, source_target_pairs={{0,4},{4,0},{8,12},{12,8},{1,5},{5,1},{9,13},{13,9},{2,6},{6,2},{1... | collective-permute-start | bytes 1572872 | tf_op jit(solution)/shard_map/ppermute | solution.py:16
  44.7 2.7 %collective-permute-start.10 = (bf16[256,1024]{1,0:T(8,128)(2,1)S(1)}, bf16[256,1024]{1,0:T(8,128)(2,1)S(1)}, u32[]{:S(2)}, u32[]{:S(2)}) collective-permute-start(bf16[256,1024]{1,0:T(8,128)(2,1)S(1)} %collective-permute-done.9.refs_2_), channel_id=1, source_target_pairs={{0,4},{4,0},{8,12},{12,8},{1,5},{5,1},{9,13},{13,9},{2,6},{6,2},{1... | collective-permute-start | bytes 1572872 | tf_op jit(solution)/shard_map/ppermute | solution.py:16
  46.6 20.7 %copy-start = (bf16[1,1024,2688]{2,1,0:T(8,128)(2,1)S(1)}, bf16[1,1024,2688]{2,1,0:T(8,128)(2,1)}, u32[]{:S(2)}) copy-start(bf16[1,1024,2688]{2,1,0:T(8,128)(2,1)} %param.10) | copy-start | bytes 16515076
  46.6 10.7 %collective-permute-start.18 = (bf16[384,512]{1,0:T(8,128)(2,1)S(1)}, bf16[384,512]{1,0:T(8,128)(2,1)S(1)}, u32[]{:S(2)}, u32[]{:S(2)}) collective-permute-start(bf16[384,512]{1,0:T(8,128)(2,1)S(1)} %constant_dynamic-update-slice_fusion.refs_0_), channel_id=1, source_target_pairs={{0,8},{4,12},{8,0},{12,4},{1,9},{5,13},{9,1},{13,5},{2,10},{6,14},... | collective-permute-start | bytes 1179656 | tf_op jit(solution)/shard_map/ppermute | solution.py:16
  47.2 19.0 %collective-permute-start.20 = (bf16[384,512]{1,0:T(8,128)(2,1)S(1)}, bf16[384,512]{1,0:T(8,128)(2,1)S(1)}, u32[]{:S(2)}, u32[]{:S(2)}) collective-permute-start(bf16[384,512]{1,0:T(8,128)(2,1)S(1)} %constant_dynamic-update-slice_fusion.refs_0_), channel_id=1, source_target_pairs={{0,4},{4,0},{8,12},{12,8},{1,5},{5,1},{9,13},{13,9},{2,6},{6,2},{1... | collective-permute-start | bytes 1179656 | tf_op jit(solution)/shard_map/ppermute | solution.py:16
  48.9 9.2 %collective-permute-start.21 = (bf16[96,512]{1,0:T(8,128)(2,1)S(1)}, bf16[96,512]{1,0:T(8,128)(2,1)S(1)}, u32[]{:S(2)}, u32[]{:S(2)}) collective-permute-start(bf16[96,512]{1,0:T(8,128)(2,1)S(1)} %get-tuple-element.76), channel_id=1, source_target_pairs={{0,1},{1,0},{2,3},{3,2},{4,5},{5,4},{6,7},{7,6},{8,9},{9,8},{10,11... | collective-permute-start | bytes 294920 | tf_op jit(solution)/shard_map/ppermute | solution.py:16
  54.9 10.6 %collective-permute-start.22 = (bf16[96,512]{1,0:T(8,128)(2,1)S(1)}, bf16[96,512]{1,0:T(8,128)(2,1)S(1)}, u32[]{:S(2)}, u32[]{:S(2)}) collective-permute-start(bf16[96,512]{1,0:T(8,128)(2,1)S(1)} %get-tuple-element.77), channel_id=1, source_target_pairs={{0,2},{1,3},{2,0},{3,1},{4,6},{5,7},{6,4},{7,5},{8,10},{9,11},{10,... | collective-permute-start | bytes 294920 | tf_op jit(solution)/shard_map/ppermute | solution.py:16
  55.6 9.9 %collective-permute-start.23 = (bf16[96,512]{1,0:T(8,128)(2,1)S(1)}, bf16[96,512]{1,0:T(8,128)(2,1)S(1)}, u32[]{:S(2)}, u32[]{:S(2)}) collective-permute-start(bf16[96,512]{1,0:T(8,128)(2,1)S(1)} %get-tuple-element.78), channel_id=1, source_target_pairs={{0,3},{1,2},{2,1},{3,0},{4,7},{5,6},{6,5},{7,4},{8,11},{9,10},{10,... | collective-permute-start | bytes 294920 | tf_op jit(solution)/shard_map/ppermute | solution.py:16
  57.3 8.9 %collective-permute-start.19 = (bf16[384,512]{1,0:T(8,128)(2,1)S(1)}, bf16[384,512]{1,0:T(8,128)(2,1)S(1)}, u32[]{:S(2)}, u32[]{:S(2)}) collective-permute-start(bf16[384,512]{1,0:T(8,128)(2,1)S(1)} %collective-permute-done.18.refs_0_), channel_id=1, source_target_pairs={{0,4},{4,0},{8,12},{12,8},{1,5},{5,1},{9,13},{13,9},{2,6},{6,2},{1... | collective-permute-start | bytes 1179656 | tf_op jit(solution)/shard_map/ppermute | solution.py:16
  65.5 6.2 %slice-start = ((s8[5505024]{0:T(1024)(128)(4,1)}), s8[4194304]{0:T(1024)(128)(4,1)S(1)}, s32[]{:S(2)}) async-start(s8[5505024]{0:T(1024)(128)(4,1)} %bitcast.9), calls=%async_computation | async-start | bytes 8388608
  65.6 1.8 %collective-permute-start.24 = (bf16[384,512]{1,0:T(8,128)(2,1)S(1)}, bf16[384,512]{1,0:T(8,128)(2,1)S(1)}, u32[]{:S(2)}, u32[]{:S(2)}) collective-permute-start(bf16[384,512]{1,0:T(8,128)(2,1)S(1)} %constant_dynamic-update-slice_fusion.4.refs_2_), channel_id=1, source_target_pairs={{0,4},{4,0},{8,12},{12,8},{1,5},{5,1},{9,13},{13,9},{2,6},{6,2},{1... | collective-permute-start | bytes 1179656 | tf_op jit(solution)/shard_map/ppermute | solution.py:16
  65.6 11.5 %collective-permute-start.26 = (bf16[384,512]{1,0:T(8,128)(2,1)S(1)}, bf16[384,512]{1,0:T(8,128)(2,1)S(1)}, u32[]{:S(2)}, u32[]{:S(2)}) collective-permute-start(bf16[384,512]{1,0:T(8,128)(2,1)S(1)} %constant_dynamic-update-slice_fusion.4.refs_2_), channel_id=1, source_target_pairs={{0,8},{4,12},{8,0},{12,4},{1,9},{5,13},{9,1},{13,5},{2,10},{6,14},... | collective-permute-start | bytes 1179656 | tf_op jit(solution)/shard_map/ppermute | solution.py:16
  67.3 4.4 %slice-start.1 = ((s8[5505024]{0:T(1024)(128)(4,1)}), s8[1310720]{0:T(1024)(128)(4,1)S(1)}, s32[]{:S(2)}) async-start(s8[5505024]{0:T(1024)(128)(4,1)} %bitcast.9), calls=%async_computation.1 | async-start | bytes 2621440
  77.2 2.6 %collective-permute-start.27 = (bf16[384,512]{1,0:T(8,128)(2,1)S(1)}, bf16[384,512]{1,0:T(8,128)(2,1)S(1)}, u32[]{:S(2)}, u32[]{:S(2)}) collective-permute-start(bf16[384,512]{1,0:T(8,128)(2,1)S(1)} %collective-permute-done.26.refs_1_), channel_id=1, source_target_pairs={{0,4},{4,0},{8,12},{12,8},{1,5},{5,1},{9,13},{13,9},{2,6},{6,2},{1... | collective-permute-start | bytes 1179656 | tf_op jit(solution)/shard_map/ppermute | solution.py:16
  85.3 3.3 %collective-permute-start.28 = (bf16[384,1024]{1,0:T(8,128)(2,1)S(1)}, bf16[384,1024]{1,0:T(8,128)(2,1)S(1)}, u32[]{:S(2)}, u32[]{:S(2)}) collective-permute-start(bf16[384,1024]{1,0:T(8,128)(2,1)S(1)} %shard_map.84), channel_id=1, source_target_pairs={{0,4},{4,0},{8,12},{12,8},{1,5},{5,1},{9,13},{13,9},{2,6},{6,2},{1... | collective-permute-start | bytes 2359304 | tf_op jit(solution)/shard_map/ppermute | solution.py:16
  85.8 5.6 %collective-permute-start.25 = (bf16[384,1024]{1,0:T(8,128)(2,1)S(1)}, bf16[384,1024]{1,0:T(8,128)(2,1)S(1)}, u32[]{:S(2)}, u32[]{:S(2)}) collective-permute-start(bf16[384,1024]{1,0:T(8,128)(2,1)S(1)} %get-tuple-element.80), channel_id=1, source_target_pairs={{0,4},{4,0},{8,12},{12,8},{1,5},{5,1},{9,13},{13,9},{2,6},{6,2},{1... | collective-permute-start | bytes 2359304 | tf_op jit(solution)/shard_map/ppermute | solution.py:16
  89.3 12.0 %collective-permute-start.29 = (bf16[384,512]{1,0:T(8,128)(2,1)S(1)}, bf16[384,512]{1,0:T(8,128)(2,1)S(1)}, u32[]{:S(2)}, u32[]{:S(2)}) collective-permute-start(bf16[384,512]{1,0:T(8,128)(2,1)S(1)} %get-tuple-element.84), channel_id=1, source_target_pairs={{0,8},{4,12},{8,0},{12,4},{1,9},{5,13},{9,1},{13,5},{2,10},{6,14},... | collective-permute-start | bytes 1179656 | tf_op jit(solution)/shard_map/ppermute | solution.py:16
  89.9 19.4 %collective-permute-start.31 = (bf16[384,512]{1,0:T(8,128)(2,1)S(1)}, bf16[384,512]{1,0:T(8,128)(2,1)S(1)}, u32[]{:S(2)}, u32[]{:S(2)}) collective-permute-start(bf16[384,512]{1,0:T(8,128)(2,1)S(1)} %get-tuple-element.87), channel_id=1, source_target_pairs={{0,8},{4,12},{8,0},{12,4},{1,9},{5,13},{9,1},{13,5},{2,10},{6,14},... | collective-permute-start | bytes 1179656 | tf_op jit(solution)/shard_map/ppermute | solution.py:16
  102.0 5.3 %collective-permute-start.30 = (bf16[96,512]{1,0:T(8,128)(2,1)S(1)}, bf16[96,512]{1,0:T(8,128)(2,1)S(1)}, u32[]{:S(2)}, u32[]{:S(2)}) collective-permute-start(bf16[96,512]{1,0:T(8,128)(2,1)S(1)} %get-tuple-element.85), channel_id=1, source_target_pairs={{0,1},{1,0},{2,3},{3,2},{4,5},{5,4},{6,7},{7,6},{8,9},{9,8},{10,11... | collective-permute-start | bytes 294920 | tf_op jit(solution)/shard_map/ppermute | solution.py:16
  103.8 9.7 %collective-permute-start.32 = (bf16[96,512]{1,0:T(8,128)(2,1)S(1)}, bf16[96,512]{1,0:T(8,128)(2,1)S(1)}, u32[]{:S(2)}, u32[]{:S(2)}) collective-permute-start(bf16[96,512]{1,0:T(8,128)(2,1)S(1)} %get-tuple-element.91), channel_id=1, source_target_pairs={{0,2},{1,3},{2,0},{3,1},{4,6},{5,7},{6,4},{7,5},{8,10},{9,11},{10,... | collective-permute-start | bytes 294920 | tf_op jit(solution)/shard_map/ppermute | solution.py:16
  104.5 8.9 %collective-permute-start.33 = (bf16[96,512]{1,0:T(8,128)(2,1)S(1)}, bf16[96,512]{1,0:T(8,128)(2,1)S(1)}, u32[]{:S(2)}, u32[]{:S(2)}) collective-permute-start(bf16[96,512]{1,0:T(8,128)(2,1)S(1)} %get-tuple-element.92), channel_id=1, source_target_pairs={{0,3},{1,2},{2,1},{3,0},{4,7},{5,6},{6,5},{7,4},{8,11},{9,10},{10,... | collective-permute-start | bytes 294920 | tf_op jit(solution)/shard_map/ppermute | solution.py:16
  114.3 9.0 %collective-permute-start.35 = (bf16[128,512]{1,0:T(8,128)(2,1)S(1)}, bf16[128,512]{1,0:T(8,128)(2,1)S(1)}, u32[]{:S(2)}, u32[]{:S(2)}) collective-permute-start(bf16[128,512]{1,0:T(8,128)(2,1)S(1)} %shard_map.89.refs_0_), channel_id=1, source_target_pairs={{0,2},{1,3},{2,0},{3,1},{4,6},{5,7},{6,4},{7,5},{8,10},{9,11},{10,... | collective-permute-start | bytes 393224 | tf_op jit(solution)/shard_map/ppermute | solution.py:16
  116.7 8.9 %collective-permute-start.34 = (bf16[128,512]{1,0:T(8,128)(2,1)S(1)}, bf16[128,512]{1,0:T(8,128)(2,1)S(1)}, u32[]{:S(2)}, u32[]{:S(2)}) collective-permute-start(bf16[128,512]{1,0:T(8,128)(2,1)S(1)} %shard_map.89.refs_0_), channel_id=1, source_target_pairs={{0,1},{1,0},{2,3},{3,2},{4,5},{5,4},{6,7},{7,6},{8,9},{9,8},{10,11... | collective-permute-start | bytes 393224 | tf_op jit(solution)/shard_map/ppermute | solution.py:16
  116.8 10.8 %collective-permute-start.36 = (bf16[96,512]{1,0:T(8,128)(2,1)S(1)}, bf16[96,512]{1,0:T(8,128)(2,1)S(1)}, u32[]{:S(2)}, u32[]{:S(2)}) collective-permute-start(bf16[96,512]{1,0:T(8,128)(2,1)S(1)} %get-tuple-element.94), channel_id=1, source_target_pairs={{0,1},{1,0},{2,3},{3,2},{4,5},{5,4},{6,7},{7,6},{8,9},{9,8},{10,11... | collective-permute-start | bytes 294920 | tf_op jit(solution)/shard_map/ppermute | solution.py:16
  118.7 8.8 %collective-permute-start.37 = (bf16[96,512]{1,0:T(8,128)(2,1)S(1)}, bf16[96,512]{1,0:T(8,128)(2,1)S(1)}, u32[]{:S(2)}, u32[]{:S(2)}) collective-permute-start(bf16[96,512]{1,0:T(8,128)(2,1)S(1)} %get-tuple-element.95), channel_id=1, source_target_pairs={{0,2},{1,3},{2,0},{3,1},{4,6},{5,7},{6,4},{7,5},{8,10},{9,11},{10,... | collective-permute-start | bytes 294920 | tf_op jit(solution)/shard_map/ppermute | solution.py:16
  119.3 10.9 %collective-permute-start.38 = (bf16[96,512]{1,0:T(8,128)(2,1)S(1)}, bf16[96,512]{1,0:T(8,128)(2,1)S(1)}, u32[]{:S(2)}, u32[]{:S(2)}) collective-permute-start(bf16[96,512]{1,0:T(8,128)(2,1)S(1)} %get-tuple-element.96), channel_id=1, source_target_pairs={{0,3},{1,2},{2,1},{3,0},{4,7},{5,6},{6,5},{7,4},{8,11},{9,10},{10,... | collective-permute-start | bytes 294920 | tf_op jit(solution)/shard_map/ppermute | solution.py:16
  131.1 7.7 %collective-permute-start.40 = (bf16[128,512]{1,0:T(8,128)(2,1)S(1)}, bf16[128,512]{1,0:T(8,128)(2,1)S(1)}, u32[]{:S(2)}, u32[]{:S(2)}) collective-permute-start(bf16[128,512]{1,0:T(8,128)(2,1)S(1)} %shard_map.90.refs_0_), channel_id=1, source_target_pairs={{0,2},{1,3},{2,0},{3,1},{4,6},{5,7},{6,4},{7,5},{8,10},{9,11},{10,... | collective-permute-start | bytes 393224 | tf_op jit(solution)/shard_map/ppermute | solution.py:16
  133.1 7.5 %collective-permute-start.42 = (bf16[128,512]{1,0:T(8,128)(2,1)S(1)}, bf16[128,512]{1,0:T(8,128)(2,1)S(1)}, u32[]{:S(2)}, u32[]{:S(2)}) collective-permute-start(bf16[128,512]{1,0:T(8,128)(2,1)S(1)} %collective-permute-done.35.refs_2_), channel_id=1, source_target_pairs={{0,1},{1,0},{2,3},{3,2},{4,5},{5,4},{6,7},{7,6},{8,9},{9,8},{10,11... | collective-permute-start | bytes 393224 | tf_op jit(solution)/shard_map/ppermute | solution.py:16
  134.0 8.5 %collective-permute-start.39 = (bf16[128,512]{1,0:T(8,128)(2,1)S(1)}, bf16[128,512]{1,0:T(8,128)(2,1)S(1)}, u32[]{:S(2)}, u32[]{:S(2)}) collective-permute-start(bf16[128,512]{1,0:T(8,128)(2,1)S(1)} %shard_map.90.refs_0_), channel_id=1, source_target_pairs={{0,1},{1,0},{2,3},{3,2},{4,5},{5,4},{6,7},{7,6},{8,9},{9,8},{10,11... | collective-permute-start | bytes 393224 | tf_op jit(solution)/shard_map/ppermute | solution.py:16
  138.8 5.0 %collective-permute-start.41 = (bf16[128,512]{1,0:T(8,128)(2,1)S(1)}, bf16[128,512]{1,0:T(8,128)(2,1)S(1)}, u32[]{:S(2)}, u32[]{:S(2)}) collective-permute-start(bf16[128,512]{1,0:T(8,128)(2,1)S(1)} %collective-permute-done.40.refs_2_), channel_id=1, source_target_pairs={{0,1},{1,0},{2,3},{3,2},{4,5},{5,4},{6,7},{7,6},{8,9},{9,8},{10,11... | collective-permute-start | bytes 393224 | tf_op jit(solution)/shard_map/ppermute | solution.py:16

commit v6 on v4

--- a/solution.py
+++ b/solution.py
@@ -374,10 +374,11 @@
 
     arrived = swap(join(0, ()))
     cut = join(1, arrived[1:2])
-    latent_out = combine(after(ranks, cut[0]), arrived, flops=20 * 10**9)
+    arrived_last = swap(cut)
+    latent_out = combine(after(ranks, arrived_last[1]), arrived)
     first = gather(latent_out)
     ranks = after(ranks, *(first[1 << i] for i in range(n_grp.bit_length() - 1)))
-    second = gather(combine(ranks, swap(cut)))
+    second = gather(combine(ranks, arrived_last))
     return mix(1, second, mix(0, first, ()))[0]
 
 

time: 146 us -> 155 us (1.062)
  starting transfers between devices: 51.7 us -> 55.9 us
  waiting for transfers between devices: 55.3 us -> 59.4 us
    ppermute x43, starting transfers between devices: 51.7 us -> 55.9 us  [hop(): return lax.ppermute(x, axis, [(i, i ^ step) for i in range(count)])]
    ppermute x43, waiting for transfers between devices: 55.3 us -> 59.4 us  [hop(): return lax.ppermute(x, axis, [(i, i ^ step) for i in range(count)])]
  transfers between devices with their start and end apart: 43 -> 43, of which waited for: 21 -> 20; matrix products, arithmetic and copies ran while one was open for 0% -> 0% of each run, Pallas kernels for 19% -> 17%
where the time goes in v6:
time: 155 us; the launch traced here: 154 us
  waiting for transfers between devices  59.4 us (38%)
  starting transfers between devices  55.9 us (36%)
  Pallas kernels  36.4 us (23%)
  local copies, waits for them, and re-layouts  2.36 us (2%)
    ppermute x43, waiting for transfers between devices, hop(): return lax.ppermute(x, axis, [(i, i ^ step) for i in range(count)])  59.4 us
    ppermute x43, starting transfers between devices, hop(): return lax.ppermute(x, axis, [(i, i ^ step) for i in range(count)])  55.9 us
    pallas_call x20, Pallas kernels, call(): pl.pallas_call(kernel, out_shape=tuple(outs), in_specs=[pl.BlockSpec(memo...  36.4 us
  transfers between devices with their start and end apart: 43, of which 20 were waited for; matrix products, arithmetic and copies ran while one was open for 0% of the time, Pallas kernels for 17%

profile of v6, /device:TPU:0, one launch (start us, length us, event | category | flops | bytes accessed | tf_op | source)
XLA Modules:
  0.0 154.4 jit_solution(1008025471999681469)
XLA Ops:
  0.5 2.6 %collective-permute-start.1 = (bf16[256,1024]{1,0:T(8,128)(2,1)}, bf16[256,1024]{1,0:T(8,128)(2,1)S(1)}, u32[]{:S(2)}, u32[]{:S(2)}) collective-permute-start(bf16[256,1024]{1,0:T(8,128)(2,1)} %refs_0_.2), channel_id=1, source_target_pairs={{0,8},{4,12},{8,0},{12,4},{1,9},{5,13},{9,1},{13,5},{2,10},{6,14},... | collective-permute-start | bytes 1572872 | tf_op jit(solution)/shard_map/ppermute | solution.py:16
  3.1 1.2 copy-done.1
  4.3 1.0 copy-done.2
  5.4 1.4 shard_map.73
  6.8 2.1 %collective-permute-start.3 = (bf16[128,512]{1,0:T(8,128)(2,1)S(1)}, bf16[128,512]{1,0:T(8,128)(2,1)S(1)}, u32[]{:S(2)}, u32[]{:S(2)}) collective-permute-start(bf16[128,512]{1,0:T(8,128)(2,1)S(1)} %get-tuple-element.52), channel_id=1, source_target_pairs={{0,1},{1,0},{2,3},{3,2},{4,5},{5,4},{6,7},{7,6},{8,9},{9,8},{10,11... | collective-permute-start | bytes 393224 | tf_op jit(solution)/shard_map/ppermute | solution.py:16
  8.9 2.6 %collective-permute-start.4 = (bf16[128,512]{1,0:T(8,128)(2,1)S(1)}, bf16[128,512]{1,0:T(8,128)(2,1)S(1)}, u32[]{:S(2)}, u32[]{:S(2)}) collective-permute-start(bf16[128,512]{1,0:T(8,128)(2,1)S(1)} %get-tuple-element.53), channel_id=1, source_target_pairs={{0,2},{1,3},{2,0},{3,1},{4,6},{5,7},{6,4},{7,5},{8,10},{9,11},{10,... | collective-permute-start | bytes 393224 | tf_op jit(solution)/shard_map/ppermute | solution.py:16
  11.5 1.8 %collective-permute-start.7 = (s32[12,512]{1,0:T(8,128)S(1)}, s32[12,512]{1,0:T(8,128)S(1)}, u32[]{:S(2)}, u32[]{:S(2)}) collective-permute-start(s32[12,512]{1,0:T(8,128)S(1)} %pad_add_fusion.refs_0_), channel_id=1, source_target_pairs={{0,8},{4,12},{8,0},{12,4},{1,9},{5,13},{9,1},{13,5},{2,10},{6,14},... | collective-permute-start | bytes 73736 | tf_op jit(solution)/shard_map/ppermute | solution.py:16
  13.3 3.2 %collective-permute-done.7.refs_2_ = s32[12,512]{1,0:T(8,128)S(1)} collective-permute-done((s32[12,512]{1,0:T(8,128)S(1)}, s32[12,512]{1,0:T(8,128)S(1)}, u32[]{:S(2)}, u32[]{:S(2)}) %collective-permute-start.7) | collective-permute-done | bytes 24608 | tf_op jit(solution)/shard_map/ppermute | solution.py:16
  16.5 1.2 collective-permute-done.6.refs_1_
  17.9 0.7 shard_map.74.ranks_ref
  18.9 3.5 %shard_map.75 = (s32[4,1,384]{2,1,0:T(1,128)S(1)}, f32[4,1,384]{2,1,0:T(1,128)S(1)}) custom-call(s32[2]{0:T(128)S(1)} %pad_add_fusion.1.me_ref, s32[12,512]{1,0:T(8,128)S(1)} %pad_add_fusion.refs_0_, s32[12,512]{1,0:T(8,128)S(1)} %collective-permute-done.6.refs_1_, s32[12,512]{1,0:T(8,128)S(1)} %collective-permute-done.7.refs_2_, ...), custom_call_target="tpu_custom_call" | custom-call | flops 1 | bytes 110592 | tf_op jit(solution)/shard_map/pallas_call | solution.py:30
  22.7 0.8 shard_map.76
  23.6 1.8 %collective-permute-start.9 = (bf16[256,1024]{1,0:T(8,128)(2,1)S(1)}, bf16[256,1024]{1,0:T(8,128)(2,1)S(1)}, u32[]{:S(2)}, u32[]{:S(2)}) collective-permute-start(bf16[256,1024]{1,0:T(8,128)(2,1)S(1)} %copy-done.3), channel_id=1, source_target_pairs={{0,8},{4,12},{8,0},{12,4},{1,9},{5,13},{9,1},{13,5},{2,10},{6,14},... | collective-permute-start | bytes 1572872 | tf_op jit(solution)/shard_map/ppermute | solution.py:16
  25.4 1.6 %collective-permute-start.11 = (bf16[96,512]{1,0:T(8,128)(2,1)S(1)}, bf16[96,512]{1,0:T(8,128)(2,1)S(1)}, u32[]{:S(2)}, u32[]{:S(2)}) collective-permute-start(bf16[96,512]{1,0:T(8,128)(2,1)S(1)} %get-tuple-element.61), channel_id=1, source_target_pairs={{0,1},{1,0},{2,3},{3,2},{4,5},{5,4},{6,7},{7,6},{8,9},{9,8},{10,11... | collective-permute-start | bytes 294920 | tf_op jit(solution)/shard_map/ppermute | solution.py:16
  27.0 2.6 %collective-permute-start.12 = (bf16[96,512]{1,0:T(8,128)(2,1)S(1)}, bf16[96,512]{1,0:T(8,128)(2,1)S(1)}, u32[]{:S(2)}, u32[]{:S(2)}) collective-permute-start(bf16[96,512]{1,0:T(8,128)(2,1)S(1)} %get-tuple-element.62), channel_id=1, source_target_pairs={{0,2},{1,3},{2,0},{3,1},{4,6},{5,7},{6,4},{7,5},{8,10},{9,11},{10,... | collective-permute-start | bytes 294920 | tf_op jit(solution)/shard_map/ppermute | solution.py:16
  29.6 1.9 %shard_map.78 = (bf16[128,512]{1,0:T(8,128)(2,1)S(1)}, bf16[128,512]{1,0:T(8,128)(2,1)S(1)}, bf16[128,512]{1,0:T(8,128)(2,1)S(1)}, bf16[128,512]{1,0:T(8,128)(2,1)S(1)}, bf16[16,1024]{1,0:T(8,128)(2,1)}) custom-call(s32[2]{0:T(128)S(1)} %pad_add_fusion.1.me_ref, bf16[512,1024]{1,0:T(8,128)(2,1)S(1)} %get-tuple-element.64.tokens_ref, ...), custom_call_target="tpu_custom_call" | custom-call | flops 536870912 | bytes 2654208 | tf_op jit(solution)/shard_map/pallas_call | solution.py:30
  32.3 3.6 %collective-permute-start.17 = (bf16[128,512]{1,0:T(8,128)(2,1)S(1)}, bf16[128,512]{1,0:T(8,128)(2,1)S(1)}, u32[]{:S(2)}, u32[]{:S(2)}) collective-permute-start(bf16[128,512]{1,0:T(8,128)(2,1)S(1)} %get-tuple-element.68), channel_id=1, source_target_pairs={{0,3},{1,2},{2,1},{3,0},{4,7},{5,6},{6,5},{7,4},{8,11},{9,10},{10,... | collective-permute-start | bytes 393224 | tf_op jit(solution)/shard_map/ppermute | solution.py:16
  35.9 2.5 %collective-permute-start.13 = (bf16[96,512]{1,0:T(8,128)(2,1)S(1)}, bf16[96,512]{1,0:T(8,128)(2,1)S(1)}, u32[]{:S(2)}, u32[]{:S(2)}) collective-permute-start(bf16[96,512]{1,0:T(8,128)(2,1)S(1)} %get-tuple-element.63), channel_id=1, source_target_pairs={{0,3},{1,2},{2,1},{3,0},{4,7},{5,6},{6,5},{7,4},{8,11},{9,10},{10,... | collective-permute-start | bytes 294920 | tf_op jit(solution)/shard_map/ppermute | solution.py:16
  38.4 6.6 %collective-permute-done.13 = bf16[96,512]{1,0:T(8,128)(2,1)S(1)} collective-permute-done((bf16[96,512]{1,0:T(8,128)(2,1)S(1)}, bf16[96,512]{1,0:T(8,128)(2,1)S(1)}, u32[]{:S(2)}, u32[]{:S(2)}) %collective-permute-start.13) | collective-permute-done | bytes 98336 | tf_op jit(solution)/shard_map/ppermute | solution.py:16
  45.4 1.5 collective-permute-done.16.refs_2_
  47.6 0.7 shard_map.77.weights_ref
  48.3 0.8 shard_map.79
  49.1 6.1 %collective-permute-start.21 = (bf16[96,512]{1,0:T(8,128)(2,1)S(1)}, bf16[96,512]{1,0:T(8,128)(2,1)S(1)}, u32[]{:S(2)}, u32[]{:S(2)}) collective-permute-start(bf16[96,512]{1,0:T(8,128)(2,1)S(1)} %get-tuple-element.76), channel_id=1, source_target_pairs={{0,1},{1,0},{2,3},{3,2},{4,5},{5,4},{6,7},{7,6},{8,9},{9,8},{10,11... | collective-permute-start | bytes 294920 | tf_op jit(solution)/shard_map/ppermute | solution.py:16
  55.2 0.6 collective-permute-start.22
  55.9 1.8 %collective-permute-start.23 = (bf16[96,512]{1,0:T(8,128)(2,1)S(1)}, bf16[96,512]{1,0:T(8,128)(2,1)S(1)}, u32[]{:S(2)}, u32[]{:S(2)}) collective-permute-start(bf16[96,512]{1,0:T(8,128)(2,1)S(1)} %get-tuple-element.78), channel_id=1, source_target_pairs={{0,3},{1,2},{2,1},{3,0},{4,7},{5,6},{6,5},{7,4},{8,11},{9,10},{10,... | collective-permute-start | bytes 294920 | tf_op jit(solution)/shard_map/ppermute | solution.py:16
  57.7 0.7 collective-permute-done.21
  58.4 7.4 %collective-permute-done.22 = bf16[96,512]{1,0:T(8,128)(2,1)S(1)} collective-permute-done((bf16[96,512]{1,0:T(8,128)(2,1)S(1)}, bf16[96,512]{1,0:T(8,128)(2,1)S(1)}, u32[]{:S(2)}, u32[]{:S(2)}) %collective-permute-start.22) | collective-permute-done | bytes 98336 | tf_op jit(solution)/shard_map/ppermute | solution.py:16
  65.9 0.6 collective-permute-start.26
  66.5 1.1 collective-permute-done.24.refs_3_
  67.6 4.4 %shard_map.80.hidden_ref = bf16[512,2688]{1,0:T(8,128)(2,1)S(1)} custom-call(s32[2]{0:T(128)S(1)} %pad_add_fusion.1.me_ref, s32[4,1,384]{2,1,0:T(1,128)S(1)} %get-tuple-element.83.slot_ref, bf16[384,512]{1,0:T(8,128)(2,1)S(1)} %constant_dynamic-update-slice_fusion.refs_0_, bf16[384,512]{1,0:T(8,128)(2,1)S(1)} %collective-permute-done.20.refs_1_, ...), custom_call_target="tpu_custom_call" | custom-call | flops 2818572288 | bytes 9836544 | tf_op jit(solution)/shard_map/pallas_call | solution.py:30
  72.0 4.3 %shard_map.81 = (bf16[384,1024]{1,0:T(8,128)(2,1)S(1)}, bf16[384,1024]{1,0:T(8,128)(2,1)S(1)}) custom-call(s32[2]{0:T(128)S(1)} %pad_add_fusion.1.me_ref, s32[4,1,384]{2,1,0:T(1,128)S(1)} %get-tuple-element.83.slot_ref, f32[4,1,384]{2,1,0:T(1,128)S(1)} %get-tuple-element.60.weight_ref, bf16[512,2688]{1,0:T(8,128)(2,1)S(1)} %shard_map.80.hidden_ref, ...), custom_call_target="tpu_custom_call" | custom-call | flops 2818572288 | bytes 9842688 | tf_op jit(solution)/shard_map/pallas_call | solution.py:30
  76.3 1.1 collective-permute-done.26.refs_1_
  77.5 2.6 %shard_map.82.hidden_ref = bf16[256,2688]{1,0:T(8,128)(2,1)S(1)} custom-call(s32[2]{0:T(128)S(1)} %pad_add_fusion.1.me_ref, s32[4,1,384]{2,1,0:T(1,128)S(1)} %get-tuple-element.83.slot_ref, bf16[384,512]{1,0:T(8,128)(2,1)S(1)} %collective-permute-done.18.refs_0_, bf16[384,512]{1,0:T(8,128)(2,1)S(1)} %collective-permute-done.26.refs_1_, ...), custom_call_target="tpu_custom_call" | custom-call | flops 1409286144 | bytes 7673856 | tf_op jit(solution)/shard_map/pallas_call | solution.py:30
  80.1 2.6 %shard_map.83.hidden_ref = bf16[256,2688]{1,0:T(8,128)(2,1)S(1)} custom-call(s32[2]{0:T(128)S(1)} %pad_add_fusion.1.me_ref, s32[4,1,384]{2,1,0:T(1,128)S(1)} %get-tuple-element.83.slot_ref, bf16[384,512]{1,0:T(8,128)(2,1)S(1)} %collective-permute-done.19.refs_0_, bf16[384,512]{1,0:T(8,128)(2,1)S(1)} %collective-permute-done.27.refs_1_, ...), custom_call_target="tpu_custom_call" | custom-call | flops 1 | bytes 1 | tf_op jit(solution)/shard_map/pallas_call | solution.py:30
  82.7 2.7 %shard_map.84 = bf16[384,1024]{1,0:T(8,128)(2,1)S(1)} custom-call(s32[2]{0:T(128)S(1)} %pad_add_fusion.1.me_ref, s32[4,1,384]{2,1,0:T(1,128)S(1)} %get-tuple-element.83.slot_ref, f32[4,1,384]{2,1,0:T(1,128)S(1)} %get-tuple-element.60.weight_ref, bf16[256,2688]{1,0:T(8,128)(2,1)S(1)} %shard_map.83.hidden_ref, bf16[2688,1024]{1,0:T(8,128)(2,1)S(1)} %bitcast.12), custom_call_target="tpu_custom_call" | custom-call | flops 1 | bytes 1 | tf_op jit(solution)/shard_map/pallas_call | solution.py:30
  86.0 2.6 %shard_map.85.refs_0_ = bf16[384,1024]{1,0:T(8,128)(2,1)S(1)} custom-call(s32[2]{0:T(128)S(1)} %pad_add_fusion.1.me_ref, s32[4,1,384]{2,1,0:T(1,128)S(1)} %get-tuple-element.83.slot_ref, f32[4,1,384]{2,1,0:T(1,128)S(1)} %get-tuple-element.60.weight_ref, bf16[256,2688]{1,0:T(8,128)(2,1)S(1)} %shard_map.82.hidden_ref, bf16[2688,1024]{1,0:T(8,128)(2,1)S(1)} %bitcast.13), custom_call_target="tpu_custom_call" | custom-call | flops 1 | bytes 1 | tf_op jit(solution)/shard_map/pallas_call | solution.py:30
  88.7 0.7 shard_map.86
  89.4 0.6 collective-permute-start.29
  90.0 1.5 collective-permute-start.31
  91.5 9.9 %collective-permute-done.29.refs_2_ = bf16[384,512]{1,0:T(8,128)(2,1)S(1)} collective-permute-done((bf16[384,512]{1,0:T(8,128)(2,1)S(1)}, bf16[384,512]{1,0:T(8,128)(2,1)S(1)}, u32[]{:S(2)}, u32[]{:S(2)}) %collective-permute-start.29) | collective-permute-done | bytes 393248 | tf_op jit(solution)/shard_map/ppermute | solution.py:16
  101.4 0.7 shard_map.87
  102.1 1.8 %collective-permute-start.30 = (bf16[96,512]{1,0:T(8,128)(2,1)S(1)}, bf16[96,512]{1,0:T(8,128)(2,1)S(1)}, u32[]{:S(2)}, u32[]{:S(2)}) collective-permute-start(bf16[96,512]{1,0:T(8,128)(2,1)S(1)} %get-tuple-element.85), channel_id=1, source_target_pairs={{0,1},{1,0},{2,3},{3,2},{4,5},{5,4},{6,7},{7,6},{8,9},{9,8},{10,11... | collective-permute-start | bytes 294920 | tf_op jit(solution)/shard_map/ppermute | solution.py:16
  103.9 2.9 %collective-permute-done.30.refs_1_ = bf16[96,512]{1,0:T(8,128)(2,1)S(1)} collective-permute-done((bf16[96,512]{1,0:T(8,128)(2,1)S(1)}, bf16[96,512]{1,0:T(8,128)(2,1)S(1)}, u32[]{:S(2)}, u32[]{:S(2)}) %collective-permute-start.30) | collective-permute-done | bytes 98336 | tf_op jit(solution)/shard_map/ppermute | solution.py:16
  106.8 2.6 %collective-permute-done.31.refs_2_ = bf16[384,512]{1,0:T(8,128)(2,1)S(1)} collective-permute-done((bf16[384,512]{1,0:T(8,128)(2,1)S(1)}, bf16[384,512]{1,0:T(8,128)(2,1)S(1)}, u32[]{:S(2)}, u32[]{:S(2)}) %collective-permute-start.31) | collective-permute-done | bytes 393248 | tf_op jit(solution)/shard_map/ppermute | solution.py:16
  109.4 0.7 shard_map.88
  110.1 1.8 %collective-permute-start.32 = (bf16[96,512]{1,0:T(8,128)(2,1)S(1)}, bf16[96,512]{1,0:T(8,128)(2,1)S(1)}, u32[]{:S(2)}, u32[]{:S(2)}) collective-permute-start(bf16[96,512]{1,0:T(8,128)(2,1)S(1)} %get-tuple-element.88), channel_id=1, source_target_pairs={{0,1},{1,0},{2,3},{3,2},{4,5},{5,4},{6,7},{7,6},{8,9},{9,8},{10,11... | collective-permute-start | bytes 294920 | tf_op jit(solution)/shard_map/ppermute | solution.py:16
  111.8 0.7 collective-permute-start.33
  112.6 1.9 %collective-permute-start.34 = (bf16[96,512]{1,0:T(8,128)(2,1)S(1)}, bf16[96,512]{1,0:T(8,128)(2,1)S(1)}, u32[]{:S(2)}, u32[]{:S(2)}) collective-permute-start(bf16[96,512]{1,0:T(8,128)(2,1)S(1)} %get-tuple-element.92), channel_id=1, source_target_pairs={{0,3},{1,2},{2,1},{3,0},{4,7},{5,6},{6,5},{7,4},{8,11},{9,10},{10,... | collective-permute-start | bytes 294920 | tf_op jit(solution)/shard_map/ppermute | solution.py:16
  115.1 6.9 %collective-permute-done.33.refs_2_ = bf16[96,512]{1,0:T(8,128)(2,1)S(1)} collective-permute-done((bf16[96,512]{1,0:T(8,128)(2,1)S(1)}, bf16[96,512]{1,0:T(8,128)(2,1)S(1)}, u32[]{:S(2)}, u32[]{:S(2)}) %collective-permute-start.33) | collective-permute-done | bytes 98336 | tf_op jit(solution)/shard_map/ppermute | solution.py:16
  122.0 0.9 shard_map.89.refs_0_
  122.8 2.4 %collective-permute-start.36 = (bf16[128,512]{1,0:T(8,128)(2,1)S(1)}, bf16[128,512]{1,0:T(8,128)(2,1)S(1)}, u32[]{:S(2)}, u32[]{:S(2)}) collective-permute-start(bf16[128,512]{1,0:T(8,128)(2,1)S(1)} %shard_map.89.refs_0_), channel_id=1, source_target_pairs={{0,2},{1,3},{2,0},{3,1},{4,6},{5,7},{6,4},{7,5},{8,10},{9,11},{10,... | collective-permute-start | bytes 393224 | tf_op jit(solution)/shard_map/ppermute | solution.py:16
  125.4 2.2 %collective-permute-start.37 = (bf16[96,512]{1,0:T(8,128)(2,1)S(1)}, bf16[96,512]{1,0:T(8,128)(2,1)S(1)}, u32[]{:S(2)}, u32[]{:S(2)}) collective-permute-start(bf16[96,512]{1,0:T(8,128)(2,1)S(1)} %get-tuple-element.95), channel_id=1, source_target_pairs={{0,2},{1,3},{2,0},{3,1},{4,6},{5,7},{6,4},{7,5},{8,10},{9,11},{10,... | collective-permute-start | bytes 294920 | tf_op jit(solution)/shard_map/ppermute | solution.py:16
  127.6 2.0 %collective-permute-start.38 = (bf16[96,512]{1,0:T(8,128)(2,1)S(1)}, bf16[96,512]{1,0:T(8,128)(2,1)S(1)}, u32[]{:S(2)}, u32[]{:S(2)}) collective-permute-start(bf16[96,512]{1,0:T(8,128)(2,1)S(1)} %get-tuple-element.96), channel_id=1, source_target_pairs={{0,3},{1,2},{2,1},{3,0},{4,7},{5,6},{6,5},{7,4},{8,11},{9,10},{10,... | collective-permute-start | bytes 294920 | tf_op jit(solution)/shard_map/ppermute | solution.py:16
  129.6 4.6 %collective-permute-done.36.refs_2_ = bf16[128,512]{1,0:T(8,128)(2,1)S(1)} collective-permute-done((bf16[128,512]{1,0:T(8,128)(2,1)S(1)}, bf16[128,512]{1,0:T(8,128)(2,1)S(1)}, u32[]{:S(2)}, u32[]{:S(2)}) %collective-permute-start.36) | collective-permute-done | bytes 131104 | tf_op jit(solution)/shard_map/ppermute | solution.py:16
  134.2 4.2 %collective-permute-done.37.refs_2_ = bf16[96,512]{1,0:T(8,128)(2,1)S(1)} collective-permute-done((bf16[96,512]{1,0:T(8,128)(2,1)S(1)}, bf16[96,512]{1,0:T(8,128)(2,1)S(1)}, u32[]{:S(2)}, u32[]{:S(2)}) %collective-permute-start.37) | collective-permute-done | bytes 98336 | tf_op jit(solution)/shard_map/ppermute | solution.py:16
  138.3 0.9 shard_map.90.refs_0_
  139.2 2.3 %collective-permute-start.40 = (bf16[128,512]{1,0:T(8,128)(2,1)S(1)}, bf16[128,512]{1,0:T(8,128)(2,1)S(1)}, u32[]{:S(2)}, u32[]{:S(2)}) collective-permute-start(bf16[128,512]{1,0:T(8,128)(2,1)S(1)} %shard_map.90.refs_0_), channel_id=1, source_target_pairs={{0,2},{1,3},{2,0},{3,1},{4,6},{5,7},{6,4},{7,5},{8,10},{9,11},{10,... | collective-permute-start | bytes 393224 | tf_op jit(solution)/shard_map/ppermute | solution.py:16
  142.0 1.6 %collective-permute-start.39 = (bf16[128,512]{1,0:T(8,128)(2,1)S(1)}, bf16[128,512]{1,0:T(8,128)(2,1)S(1)}, u32[]{:S(2)}, u32[]{:S(2)}) collective-permute-start(bf16[128,512]{1,0:T(8,128)(2,1)S(1)} %shard_map.90.refs_0_), channel_id=1, source_target_pairs={{0,1},{1,0},{2,3},{3,2},{4,5},{5,4},{6,7},{7,6},{8,9},{9,8},{10,11... | collective-permute-start | bytes 393224 | tf_op jit(solution)/shard_map/ppermute | solution.py:16
  143.6 1.9 %collective-permute-done.40.refs_2_ = bf16[128,512]{1,0:T(8,128)(2,1)S(1)} collective-permute-done((bf16[128,512]{1,0:T(8,128)(2,1)S(1)}, bf16[128,512]{1,0:T(8,128)(2,1)S(1)}, u32[]{:S(2)}, u32[]{:S(2)}) %collective-permute-start.40) | collective-permute-done | bytes 131104 | tf_op jit(solution)/shard_map/ppermute | solution.py:16
  145.5 2.7 %collective-permute-start.41 = (bf16[128,512]{1,0:T(8,128)(2,1)S(1)}, bf16[128,512]{1,0:T(8,128)(2,1)S(1)}, u32[]{:S(2)}, u32[]{:S(2)}) collective-permute-start(bf16[128,512]{1,0:T(8,128)(2,1)S(1)} %collective-permute-done.40.refs_2_), channel_id=1, source_target_pairs={{0,1},{1,0},{2,3},{3,2},{4,5},{5,4},{6,7},{7,6},{8,9},{9,8},{10,11... | collective-permute-start | bytes 393224 | tf_op jit(solution)/shard_map/ppermute | solution.py:16
  148.3 1.3 shard_map.91.refs_4_
  149.6 1.1 collective-permute-done.39.refs_1_
  150.7 1.4 collective-permute-done.41.refs_3_
  152.1 2.3 %shard_map.92 = bf16[512,1024]{1,0:T(8,128)(2,1)} custom-call(s32[2]{0:T(128)S(1)} %pad_add_fusion.1.me_ref, bf16[1024,1024]{1,0:T(8,128)(2,1)S(1)} %shard_map.77.weights_ref, bf16[128,512]{1,0:T(8,128)(2,1)S(1)} %shard_map.90.refs_0_, bf16[128,512]{1,0:T(8,128)(2,1)S(1)} %collective-permute-done.39.refs_1_, ...), custom_call_target="tpu_custom_call" | custom-call | flops 536870912 | bytes 5767168 | tf_op jit(solution)/shard_map/pallas_call | solution.py:30
  (69 shorter events, 5.3 us)
Async XLA Ops:
  0.0 11.5 %copy-start.4 = (s32[512,6]{0,1:T(8,128)S(1)}, s32[512,6]{0,1:T(8,128)}, u32[]{:S(2)}) copy-start(s32[512,6]{0,1:T(8,128)} %param.12) | copy-start | bytes 36868
  0.0 3.1 %collective-permute-start.2 = (bf16[256,1024]{1,0:T(8,128)(2,1)}, bf16[256,1024]{1,0:T(8,128)(2,1)S(1)}, u32[]{:S(2)}, u32[]{:S(2)}) collective-permute-start(bf16[256,1024]{1,0:T(8,128)(2,1)} %refs_0_.2), channel_id=1, source_target_pairs={{0,4},{4,0},{8,12},{12,8},{1,5},{5,1},{9,13},{13,9},{2,6},{6,2},{1... | collective-permute-start | bytes 1572872 | tf_op jit(solution)/shard_map/ppermute | solution.py:16
  0.5 22.0 %collective-permute-start.1 = (bf16[256,1024]{1,0:T(8,128)(2,1)}, bf16[256,1024]{1,0:T(8,128)(2,1)S(1)}, u32[]{:S(2)}, u32[]{:S(2)}) collective-permute-start(bf16[256,1024]{1,0:T(8,128)(2,1)} %refs_0_.2), channel_id=1, source_target_pairs={{0,8},{4,12},{8,0},{12,4},{1,9},{5,13},{9,1},{13,5},{2,10},{6,14},... | collective-permute-start | bytes 1572872 | tf_op jit(solution)/shard_map/ppermute | solution.py:16
  3.1 1.2 copy-start.1
  4.3 1.0 copy-start.2
  5.4 6.1 %copy-start.5 = (s32[512,6]{0,1:T(8,128)S(1)}, s32[512,6]{0,1:T(8,128)}, u32[]{:S(2)}) copy-start(s32[512,6]{0,1:T(8,128)} %param.13) | copy-start | bytes 36868
  5.4 18.2 %copy-start.3 = (bf16[256,1024]{1,0:T(8,128)(2,1)S(1)}, bf16[256,1024]{1,0:T(8,128)(2,1)}, u32[]{:S(2)}) copy-start(bf16[256,1024]{1,0:T(8,128)(2,1)} %refs_0_.3) | copy-start | bytes 1572868
  6.8 15.7 %collective-permute-start.3 = (bf16[128,512]{1,0:T(8,128)(2,1)S(1)}, bf16[128,512]{1,0:T(8,128)(2,1)S(1)}, u32[]{:S(2)}, u32[]{:S(2)}) collective-permute-start(bf16[128,512]{1,0:T(8,128)(2,1)S(1)} %get-tuple-element.52), channel_id=1, source_target_pairs={{0,1},{1,0},{2,3},{3,2},{4,5},{5,4},{6,7},{7,6},{8,9},{9,8},{10,11... | collective-permute-start | bytes 393224 | tf_op jit(solution)/shard_map/ppermute | solution.py:16
  8.9 13.6 %collective-permute-start.4 = (bf16[128,512]{1,0:T(8,128)(2,1)S(1)}, bf16[128,512]{1,0:T(8,128)(2,1)S(1)}, u32[]{:S(2)}, u32[]{:S(2)}) collective-permute-start(bf16[128,512]{1,0:T(8,128)(2,1)S(1)} %get-tuple-element.53), channel_id=1, source_target_pairs={{0,2},{1,3},{2,0},{3,1},{4,6},{5,7},{6,4},{7,5},{8,10},{9,11},{10,... | collective-permute-start | bytes 393224 | tf_op jit(solution)/shard_map/ppermute | solution.py:16
  11.5 11.0 %collective-permute-start.5 = (bf16[128,512]{1,0:T(8,128)(2,1)S(1)}, bf16[128,512]{1,0:T(8,128)(2,1)S(1)}, u32[]{:S(2)}, u32[]{:S(2)}) collective-permute-start(bf16[128,512]{1,0:T(8,128)(2,1)S(1)} %get-tuple-element.54), channel_id=1, source_target_pairs={{0,3},{1,2},{2,1},{3,0},{4,7},{5,6},{6,5},{7,4},{8,11},{9,10},{10,... | collective-permute-start | bytes 393224 | tf_op jit(solution)/shard_map/ppermute | solution.py:16
  11.5 5.0 %collective-permute-start.7 = (s32[12,512]{1,0:T(8,128)S(1)}, s32[12,512]{1,0:T(8,128)S(1)}, u32[]{:S(2)}, u32[]{:S(2)}) collective-permute-start(s32[12,512]{1,0:T(8,128)S(1)} %pad_add_fusion.refs_0_), channel_id=1, source_target_pairs={{0,8},{4,12},{8,0},{12,4},{1,9},{5,13},{9,1},{13,5},{2,10},{6,14},... | collective-permute-start | bytes 73736 | tf_op jit(solution)/shard_map/ppermute | solution.py:16
  16.5 1.2 collective-permute-start.6
  17.7 1.2 collective-permute-start.8
  22.5 7.1 %collective-permute-start.14 = (bf16[256,1024]{1,0:T(8,128)(2,1)S(1)}, bf16[256,1024]{1,0:T(8,128)(2,1)S(1)}, u32[]{:S(2)}, u32[]{:S(2)}) collective-permute-start(bf16[256,1024]{1,0:T(8,128)(2,1)S(1)} %collective-permute-done.1.refs_0_), channel_id=1, source_target_pairs={{0,4},{4,0},{8,12},{12,8},{1,5},{5,1},{9,13},{13,9},{2,6},{6,2},{1... | collective-permute-start | bytes 1572872 | tf_op jit(solution)/shard_map/ppermute | solution.py:16
  23.6 21.4 %collective-permute-start.9 = (bf16[256,1024]{1,0:T(8,128)(2,1)S(1)}, bf16[256,1024]{1,0:T(8,128)(2,1)S(1)}, u32[]{:S(2)}, u32[]{:S(2)}) collective-permute-start(bf16[256,1024]{1,0:T(8,128)(2,1)S(1)} %copy-done.3), channel_id=1, source_target_pairs={{0,8},{4,12},{8,0},{12,4},{1,9},{5,13},{9,1},{13,5},{2,10},{6,14},... | collective-permute-start | bytes 1572872 | tf_op jit(solution)/shard_map/ppermute | solution.py:16
  25.4 6.9 %collective-permute-start.11 = (bf16[96,512]{1,0:T(8,128)(2,1)S(1)}, bf16[96,512]{1,0:T(8,128)(2,1)S(1)}, u32[]{:S(2)}, u32[]{:S(2)}) collective-permute-start(bf16[96,512]{1,0:T(8,128)(2,1)S(1)} %get-tuple-element.61), channel_id=1, source_target_pairs={{0,1},{1,0},{2,3},{3,2},{4,5},{5,4},{6,7},{7,6},{8,9},{9,8},{10,11... | collective-permute-start | bytes 294920 | tf_op jit(solution)/shard_map/ppermute | solution.py:16
  27.0 8.9 %collective-permute-start.12 = (bf16[96,512]{1,0:T(8,128)(2,1)S(1)}, bf16[96,512]{1,0:T(8,128)(2,1)S(1)}, u32[]{:S(2)}, u32[]{:S(2)}) collective-permute-start(bf16[96,512]{1,0:T(8,128)(2,1)S(1)} %get-tuple-element.62), channel_id=1, source_target_pairs={{0,2},{1,3},{2,0},{3,1},{4,6},{5,7},{6,4},{7,5},{8,10},{9,11},{10,... | collective-permute-start | bytes 294920 | tf_op jit(solution)/shard_map/ppermute | solution.py:16
  31.5 14.0 %collective-permute-start.15 = (bf16[128,512]{1,0:T(8,128)(2,1)S(1)}, bf16[128,512]{1,0:T(8,128)(2,1)S(1)}, u32[]{:S(2)}, u32[]{:S(2)}) collective-permute-start(bf16[128,512]{1,0:T(8,128)(2,1)S(1)} %get-tuple-element.66), channel_id=1, source_target_pairs={{0,1},{1,0},{2,3},{3,2},{4,5},{5,4},{6,7},{7,6},{8,9},{9,8},{10,11... | collective-permute-start | bytes 393224 | tf_op jit(solution)/shard_map/ppermute | solution.py:16
  31.9 15.0 %collective-permute-start.16 = (bf16[128,512]{1,0:T(8,128)(2,1)S(1)}, bf16[128,512]{1,0:T(8,128)(2,1)S(1)}, u32[]{:S(2)}, u32[]{:S(2)}) collective-permute-start(bf16[128,512]{1,0:T(8,128)(2,1)S(1)} %get-tuple-element.67), channel_id=1, source_target_pairs={{0,2},{1,3},{2,0},{3,1},{4,6},{5,7},{6,4},{7,5},{8,10},{9,11},{10,... | collective-permute-start | bytes 393224 | tf_op jit(solution)/shard_map/ppermute | solution.py:16
  32.3 14.6 %collective-permute-start.17 = (bf16[128,512]{1,0:T(8,128)(2,1)S(1)}, bf16[128,512]{1,0:T(8,128)(2,1)S(1)}, u32[]{:S(2)}, u32[]{:S(2)}) collective-permute-start(bf16[128,512]{1,0:T(8,128)(2,1)S(1)} %get-tuple-element.68), channel_id=1, source_target_pairs={{0,3},{1,2},{2,1},{3,0},{4,7},{5,6},{6,5},{7,4},{8,11},{9,10},{10,... | collective-permute-start | bytes 393224 | tf_op jit(solution)/shard_map/ppermute | solution.py:16
  35.9 9.1 %collective-permute-start.13 = (bf16[96,512]{1,0:T(8,128)(2,1)S(1)}, bf16[96,512]{1,0:T(8,128)(2,1)S(1)}, u32[]{:S(2)}, u32[]{:S(2)}) collective-permute-start(bf16[96,512]{1,0:T(8,128)(2,1)S(1)} %get-tuple-element.63), channel_id=1, source_target_pairs={{0,3},{1,2},{2,1},{3,0},{4,7},{5,6},{6,5},{7,4},{8,11},{9,10},{10,... | collective-permute-start | bytes 294920 | tf_op jit(solution)/shard_map/ppermute | solution.py:16
  44.9 2.6 %collective-permute-start = (bf16[256,1024]{1,0:T(8,128)(2,1)S(1)}, bf16[256,1024]{1,0:T(8,128)(2,1)S(1)}, u32[]{:S(2)}, u32[]{:S(2)}) collective-permute-start(bf16[256,1024]{1,0:T(8,128)(2,1)S(1)} %copy-done.3), channel_id=1, source_target_pairs={{0,4},{4,0},{8,12},{12,8},{1,5},{5,1},{9,13},{13,9},{2,6},{6,2},{1... | collective-permute-start | bytes 1572872 | tf_op jit(solution)/shard_map/ppermute | solution.py:16
  44.9 2.7 %collective-permute-start.10 = (bf16[256,1024]{1,0:T(8,128)(2,1)S(1)}, bf16[256,1024]{1,0:T(8,128)(2,1)S(1)}, u32[]{:S(2)}, u32[]{:S(2)}) collective-permute-start(bf16[256,1024]{1,0:T(8,128)(2,1)S(1)} %collective-permute-done.9.refs_2_), channel_id=1, source_target_pairs={{0,4},{4,0},{8,12},{12,8},{1,5},{5,1},{9,13},{13,9},{2,6},{6,2},{1... | collective-permute-start | bytes 1572872 | tf_op jit(solution)/shard_map/ppermute | solution.py:16
  47.0 20.7 %copy-start = (bf16[1,1024,2688]{2,1,0:T(8,128)(2,1)S(1)}, bf16[1,1024,2688]{2,1,0:T(8,128)(2,1)}, u32[]{:S(2)}) copy-start(bf16[1,1024,2688]{2,1,0:T(8,128)(2,1)} %param.10) | copy-start | bytes 16515076
  47.0 10.7 %collective-permute-start.18 = (bf16[384,512]{1,0:T(8,128)(2,1)S(1)}, bf16[384,512]{1,0:T(8,128)(2,1)S(1)}, u32[]{:S(2)}, u32[]{:S(2)}) collective-permute-start(bf16[384,512]{1,0:T(8,128)(2,1)S(1)} %constant_dynamic-update-slice_fusion.refs_0_), channel_id=1, source_target_pairs={{0,8},{4,12},{8,0},{12,4},{1,9},{5,13},{9,1},{13,5},{2,10},{6,14},... | collective-permute-start | bytes 1179656 | tf_op jit(solution)/shard_map/ppermute | solution.py:16
  47.5 19.0 %collective-permute-start.20 = (bf16[384,512]{1,0:T(8,128)(2,1)S(1)}, bf16[384,512]{1,0:T(8,128)(2,1)S(1)}, u32[]{:S(2)}, u32[]{:S(2)}) collective-permute-start(bf16[384,512]{1,0:T(8,128)(2,1)S(1)} %constant_dynamic-update-slice_fusion.refs_0_), channel_id=1, source_target_pairs={{0,4},{4,0},{8,12},{12,8},{1,5},{5,1},{9,13},{13,9},{2,6},{6,2},{1... | collective-permute-start | bytes 1179656 | tf_op jit(solution)/shard_map/ppermute | solution.py:16
  49.1 9.3 %collective-permute-start.21 = (bf16[96,512]{1,0:T(8,128)(2,1)S(1)}, bf16[96,512]{1,0:T(8,128)(2,1)S(1)}, u32[]{:S(2)}, u32[]{:S(2)}) collective-permute-start(bf16[96,512]{1,0:T(8,128)(2,1)S(1)} %get-tuple-element.76), channel_id=1, source_target_pairs={{0,1},{1,0},{2,3},{3,2},{4,5},{5,4},{6,7},{7,6},{8,9},{9,8},{10,11... | collective-permute-start | bytes 294920 | tf_op jit(solution)/shard_map/ppermute | solution.py:16
  55.2 10.6 %collective-permute-start.22 = (bf16[96,512]{1,0:T(8,128)(2,1)S(1)}, bf16[96,512]{1,0:T(8,128)(2,1)S(1)}, u32[]{:S(2)}, u32[]{:S(2)}) collective-permute-start(bf16[96,512]{1,0:T(8,128)(2,1)S(1)} %get-tuple-element.77), channel_id=1, source_target_pairs={{0,2},{1,3},{2,0},{3,1},{4,6},{5,7},{6,4},{7,5},{8,10},{9,11},{10,... | collective-permute-start | bytes 294920 | tf_op jit(solution)/shard_map/ppermute | solution.py:16
  55.9 10.0 %collective-permute-start.23 = (bf16[96,512]{1,0:T(8,128)(2,1)S(1)}, bf16[96,512]{1,0:T(8,128)(2,1)S(1)}, u32[]{:S(2)}, u32[]{:S(2)}) collective-permute-start(bf16[96,512]{1,0:T(8,128)(2,1)S(1)} %get-tuple-element.78), channel_id=1, source_target_pairs={{0,3},{1,2},{2,1},{3,0},{4,7},{5,6},{6,5},{7,4},{8,11},{9,10},{10,... | collective-permute-start | bytes 294920 | tf_op jit(solution)/shard_map/ppermute | solution.py:16
  57.7 8.8 %collective-permute-start.19 = (bf16[384,512]{1,0:T(8,128)(2,1)S(1)}, bf16[384,512]{1,0:T(8,128)(2,1)S(1)}, u32[]{:S(2)}, u32[]{:S(2)}) collective-permute-start(bf16[384,512]{1,0:T(8,128)(2,1)S(1)} %collective-permute-done.18.refs_0_), channel_id=1, source_target_pairs={{0,4},{4,0},{8,12},{12,8},{1,5},{5,1},{9,13},{13,9},{2,6},{6,2},{1... | collective-permute-start | bytes 1179656 | tf_op jit(solution)/shard_map/ppermute | solution.py:16
  65.8 6.2 %slice-start = ((s8[5505024]{0:T(1024)(128)(4,1)}), s8[4194304]{0:T(1024)(128)(4,1)S(1)}, s32[]{:S(2)}) async-start(s8[5505024]{0:T(1024)(128)(4,1)} %bitcast.9), calls=%async_computation | async-start | bytes 8388608
  65.9 1.8 %collective-permute-start.24 = (bf16[384,512]{1,0:T(8,128)(2,1)S(1)}, bf16[384,512]{1,0:T(8,128)(2,1)S(1)}, u32[]{:S(2)}, u32[]{:S(2)}) collective-permute-start(bf16[384,512]{1,0:T(8,128)(2,1)S(1)} %constant_dynamic-update-slice_fusion.4.refs_2_), channel_id=1, source_target_pairs={{0,4},{4,0},{8,12},{12,8},{1,5},{5,1},{9,13},{13,9},{2,6},{6,2},{1... | collective-permute-start | bytes 1179656 | tf_op jit(solution)/shard_map/ppermute | solution.py:16
  65.9 11.5 %collective-permute-start.26 = (bf16[384,512]{1,0:T(8,128)(2,1)S(1)}, bf16[384,512]{1,0:T(8,128)(2,1)S(1)}, u32[]{:S(2)}, u32[]{:S(2)}) collective-permute-start(bf16[384,512]{1,0:T(8,128)(2,1)S(1)} %constant_dynamic-update-slice_fusion.4.refs_2_), channel_id=1, source_target_pairs={{0,8},{4,12},{8,0},{12,4},{1,9},{5,13},{9,1},{13,5},{2,10},{6,14},... | collective-permute-start | bytes 1179656 | tf_op jit(solution)/shard_map/ppermute | solution.py:16
  67.6 4.4 %slice-start.1 = ((s8[5505024]{0:T(1024)(128)(4,1)}), s8[1310720]{0:T(1024)(128)(4,1)S(1)}, s32[]{:S(2)}) async-start(s8[5505024]{0:T(1024)(128)(4,1)} %bitcast.9), calls=%async_computation.1 | async-start | bytes 2621440
  77.5 2.6 %collective-permute-start.27 = (bf16[384,512]{1,0:T(8,128)(2,1)S(1)}, bf16[384,512]{1,0:T(8,128)(2,1)S(1)}, u32[]{:S(2)}, u32[]{:S(2)}) collective-permute-start(bf16[384,512]{1,0:T(8,128)(2,1)S(1)} %collective-permute-done.26.refs_1_), channel_id=1, source_target_pairs={{0,4},{4,0},{8,12},{12,8},{1,5},{5,1},{9,13},{13,9},{2,6},{6,2},{1... | collective-permute-start | bytes 1179656 | tf_op jit(solution)/shard_map/ppermute | solution.py:16
  85.4 3.3 %collective-permute-start.28 = (bf16[384,1024]{1,0:T(8,128)(2,1)S(1)}, bf16[384,1024]{1,0:T(8,128)(2,1)S(1)}, u32[]{:S(2)}, u32[]{:S(2)}) collective-permute-start(bf16[384,1024]{1,0:T(8,128)(2,1)S(1)} %shard_map.84), channel_id=1, source_target_pairs={{0,4},{4,0},{8,12},{12,8},{1,5},{5,1},{9,13},{13,9},{2,6},{6,2},{1... | collective-permute-start | bytes 2359304 | tf_op jit(solution)/shard_map/ppermute | solution.py:16
  85.9 5.6 %collective-permute-start.25 = (bf16[384,1024]{1,0:T(8,128)(2,1)S(1)}, bf16[384,1024]{1,0:T(8,128)(2,1)S(1)}, u32[]{:S(2)}, u32[]{:S(2)}) collective-permute-start(bf16[384,1024]{1,0:T(8,128)(2,1)S(1)} %get-tuple-element.80), channel_id=1, source_target_pairs={{0,4},{4,0},{8,12},{12,8},{1,5},{5,1},{9,13},{13,9},{2,6},{6,2},{1... | collective-permute-start | bytes 2359304 | tf_op jit(solution)/shard_map/ppermute | solution.py:16
  89.4 12.0 %collective-permute-start.29 = (bf16[384,512]{1,0:T(8,128)(2,1)S(1)}, bf16[384,512]{1,0:T(8,128)(2,1)S(1)}, u32[]{:S(2)}, u32[]{:S(2)}) collective-permute-start(bf16[384,512]{1,0:T(8,128)(2,1)S(1)} %get-tuple-element.84), channel_id=1, source_target_pairs={{0,8},{4,12},{8,0},{12,4},{1,9},{5,13},{9,1},{13,5},{2,10},{6,14},... | collective-permute-start | bytes 1179656 | tf_op jit(solution)/shard_map/ppermute | solution.py:16
  90.0 19.4 %collective-permute-start.31 = (bf16[384,512]{1,0:T(8,128)(2,1)S(1)}, bf16[384,512]{1,0:T(8,128)(2,1)S(1)}, u32[]{:S(2)}, u32[]{:S(2)}) collective-permute-start(bf16[384,512]{1,0:T(8,128)(2,1)S(1)} %get-tuple-element.87), channel_id=1, source_target_pairs={{0,8},{4,12},{8,0},{12,4},{1,9},{5,13},{9,1},{13,5},{2,10},{6,14},... | collective-permute-start | bytes 1179656 | tf_op jit(solution)/shard_map/ppermute | solution.py:16
  102.1 4.7 %collective-permute-start.30 = (bf16[96,512]{1,0:T(8,128)(2,1)S(1)}, bf16[96,512]{1,0:T(8,128)(2,1)S(1)}, u32[]{:S(2)}, u32[]{:S(2)}) collective-permute-start(bf16[96,512]{1,0:T(8,128)(2,1)S(1)} %get-tuple-element.85), channel_id=1, source_target_pairs={{0,1},{1,0},{2,3},{3,2},{4,5},{5,4},{6,7},{7,6},{8,9},{9,8},{10,11... | collective-permute-start | bytes 294920 | tf_op jit(solution)/shard_map/ppermute | solution.py:16
  110.1 5.0 %collective-permute-start.32 = (bf16[96,512]{1,0:T(8,128)(2,1)S(1)}, bf16[96,512]{1,0:T(8,128)(2,1)S(1)}, u32[]{:S(2)}, u32[]{:S(2)}) collective-permute-start(bf16[96,512]{1,0:T(8,128)(2,1)S(1)} %get-tuple-element.88), channel_id=1, source_target_pairs={{0,1},{1,0},{2,3},{3,2},{4,5},{5,4},{6,7},{7,6},{8,9},{9,8},{10,11... | collective-permute-start | bytes 294920 | tf_op jit(solution)/shard_map/ppermute | solution.py:16
  111.8 10.1 %collective-permute-start.33 = (bf16[96,512]{1,0:T(8,128)(2,1)S(1)}, bf16[96,512]{1,0:T(8,128)(2,1)S(1)}, u32[]{:S(2)}, u32[]{:S(2)}) collective-permute-start(bf16[96,512]{1,0:T(8,128)(2,1)S(1)} %get-tuple-element.91), channel_id=1, source_target_pairs={{0,2},{1,3},{2,0},{3,1},{4,6},{5,7},{6,4},{7,5},{8,10},{9,11},{10,... | collective-permute-start | bytes 294920 | tf_op jit(solution)/shard_map/ppermute | solution.py:16
  112.6 9.4 %collective-permute-start.34 = (bf16[96,512]{1,0:T(8,128)(2,1)S(1)}, bf16[96,512]{1,0:T(8,128)(2,1)S(1)}, u32[]{:S(2)}, u32[]{:S(2)}) collective-permute-start(bf16[96,512]{1,0:T(8,128)(2,1)S(1)} %get-tuple-element.92), channel_id=1, source_target_pairs={{0,3},{1,2},{2,1},{3,0},{4,7},{5,6},{6,5},{7,4},{8,11},{9,10},{10,... | collective-permute-start | bytes 294920 | tf_op jit(solution)/shard_map/ppermute | solution.py:16
  122.8 11.3 %collective-permute-start.36 = (bf16[128,512]{1,0:T(8,128)(2,1)S(1)}, bf16[128,512]{1,0:T(8,128)(2,1)S(1)}, u32[]{:S(2)}, u32[]{:S(2)}) collective-permute-start(bf16[128,512]{1,0:T(8,128)(2,1)S(1)} %shard_map.89.refs_0_), channel_id=1, source_target_pairs={{0,2},{1,3},{2,0},{3,1},{4,6},{5,7},{6,4},{7,5},{8,10},{9,11},{10,... | collective-permute-start | bytes 393224 | tf_op jit(solution)/shard_map/ppermute | solution.py:16
  125.2 9.0 %collective-permute-start.35 = (bf16[128,512]{1,0:T(8,128)(2,1)S(1)}, bf16[128,512]{1,0:T(8,128)(2,1)S(1)}, u32[]{:S(2)}, u32[]{:S(2)}) collective-permute-start(bf16[128,512]{1,0:T(8,128)(2,1)S(1)} %shard_map.89.refs_0_), channel_id=1, source_target_pairs={{0,1},{1,0},{2,3},{3,2},{4,5},{5,4},{6,7},{7,6},{8,9},{9,8},{10,11... | collective-permute-start | bytes 393224 | tf_op jit(solution)/shard_map/ppermute | solution.py:16
  125.4 13.0 %collective-permute-start.37 = (bf16[96,512]{1,0:T(8,128)(2,1)S(1)}, bf16[96,512]{1,0:T(8,128)(2,1)S(1)}, u32[]{:S(2)}, u32[]{:S(2)}) collective-permute-start(bf16[96,512]{1,0:T(8,128)(2,1)S(1)} %get-tuple-element.95), channel_id=1, source_target_pairs={{0,2},{1,3},{2,0},{3,1},{4,6},{5,7},{6,4},{7,5},{8,10},{9,11},{10,... | collective-permute-start | bytes 294920 | tf_op jit(solution)/shard_map/ppermute | solution.py:16
  127.6 10.8 %collective-permute-start.38 = (bf16[96,512]{1,0:T(8,128)(2,1)S(1)}, bf16[96,512]{1,0:T(8,128)(2,1)S(1)}, u32[]{:S(2)}, u32[]{:S(2)}) collective-permute-start(bf16[96,512]{1,0:T(8,128)(2,1)S(1)} %get-tuple-element.96), channel_id=1, source_target_pairs={{0,3},{1,2},{2,1},{3,0},{4,7},{5,6},{6,5},{7,4},{8,11},{9,10},{10,... | collective-permute-start | bytes 294920 | tf_op jit(solution)/shard_map/ppermute | solution.py:16
  139.2 6.3 %collective-permute-start.40 = (bf16[128,512]{1,0:T(8,128)(2,1)S(1)}, bf16[128,512]{1,0:T(8,128)(2,1)S(1)}, u32[]{:S(2)}, u32[]{:S(2)}) collective-permute-start(bf16[128,512]{1,0:T(8,128)(2,1)S(1)} %shard_map.90.refs_0_), channel_id=1, source_target_pairs={{0,2},{1,3},{2,0},{3,1},{4,6},{5,7},{6,4},{7,5},{8,10},{9,11},{10,... | collective-permute-start | bytes 393224 | tf_op jit(solution)/shard_map/ppermute | solution.py:16
  141.6 6.8 %collective-permute-start.42 = (bf16[128,512]{1,0:T(8,128)(2,1)S(1)}, bf16[128,512]{1,0:T(8,128)(2,1)S(1)}, u32[]{:S(2)}, u32[]{:S(2)}) collective-permute-start(bf16[128,512]{1,0:T(8,128)(2,1)S(1)} %collective-permute-done.36.refs_2_), channel_id=1, source_target_pairs={{0,1},{1,0},{2,3},{3,2},{4,5},{5,4},{6,7},{7,6},{8,9},{9,8},{10,11... | collective-permute-start | bytes 393224 | tf_op jit(solution)/shard_map/ppermute | solution.py:16
  142.0 8.8 %collective-permute-start.39 = (bf16[128,512]{1,0:T(8,128)(2,1)S(1)}, bf16[128,512]{1,0:T(8,128)(2,1)S(1)}, u32[]{:S(2)}, u32[]{:S(2)}) collective-permute-start(bf16[128,512]{1,0:T(8,128)(2,1)S(1)} %shard_map.90.refs_0_), channel_id=1, source_target_pairs={{0,1},{1,0},{2,3},{3,2},{4,5},{5,4},{6,7},{7,6},{8,9},{9,8},{10,11... | collective-permute-start | bytes 393224 | tf_op jit(solution)/shard_map/ppermute | solution.py:16
  145.5 6.6 %collective-permute-start.41 = (bf16[128,512]{1,0:T(8,128)(2,1)S(1)}, bf16[128,512]{1,0:T(8,128)(2,1)S(1)}, u32[]{:S(2)}, u32[]{:S(2)}) collective-permute-start(bf16[128,512]{1,0:T(8,128)(2,1)S(1)} %collective-permute-done.40.refs_2_), channel_id=1, source_target_pairs={{0,1},{1,0},{2,3},{3,2},{4,5},{5,4},{6,7},{7,6},{8,9},{9,8},{10,11... | collective-permute-start | bytes 393224 | tf_op jit(solution)/shard_map/ppermute | solution.py:16
